TPU v7x, 32 devices: a whole 2x2x4 slice. The times are simulated.
32 devices in a mesh: seq: 4 (over y, x), fsdp: 8 (over z, core).
Axes of the slice: x: 2, y: 2, z: 4, core: 2. Of those that a mesh axis runs over, the one named last changes fastest.
Arguments:
- latents: bfloat16 [8, 1024, 1408], P('fsdp', 'seq'), may hold values from -6 to 6
- skip_input: bfloat16 [8, 1024, 1408], P('fsdp', 'seq'), may hold values from -6 to 6
- text_tokens: bfloat16 [8, 333, 1024], P('fsdp'), may hold values from -6 to 6
- text_lengths: int32 [8], P('fsdp'), may hold values from 83 to 333, as said below
- condition: bfloat16 [8, 1408], P('fsdp'), may hold values from -6 to 6
- cotangent: bfloat16 [8, 1024, 1408], P('fsdp', 'seq'), may hold values from -6 to 6
- mod_weight: bfloat16 [2, 1408, 1408], P(None, 'fsdp'), may hold values from -0.15625 to 0.15625
- norm_gains: bfloat16 [2, 3, 1408], P(None, None, 'fsdp'), may hold values from 0.5 to 1.5
- qkv_weight: bfloat16 [2, 1408, 4224], P(None, 'fsdp'), may hold values from -0.15625 to 0.15625
- query_weight: bfloat16 [2, 1408, 1408], P(None, 'fsdp'), may hold values from -0.15625 to 0.15625
- text_kv_weight: bfloat16 [2, 1024, 2816], P(None, 'fsdp'), may hold values from -0.1875 to 0.1875
- self_out_weight: bfloat16 [2, 1408, 1408], P(None, 'fsdp'), may hold values from -3 to 3
- cross_out_weight: bfloat16 [2, 1408, 1408], P(None, 'fsdp'), may hold values from -1.25 to 1.25
- up_weight: bfloat16 [2, 1408, 6144], P(None, 'fsdp'), may hold values from -0.15625 to 0.15625
- down_weight: bfloat16 [2, 6144, 1408], P(None, 'fsdp'), may hold values from -0.078125 to 0.078125
- skip_gain: bfloat16 [2816], P('fsdp'), may hold values from 0.5 to 1.5
- skip_weight: bfloat16 [2816, 1408], P('fsdp'), may hold values from -0.109375 to 0.109375
Outputs:
- output: bfloat16 [8, 1024, 1408], P('fsdp', 'seq')
- grad_latents: float32 [8, 1024, 1408], P('fsdp', 'seq')
- grad_skip: float32 [8, 1024, 1408], P('fsdp', 'seq')
- grad_text: float32 [8, 333, 1024], P('fsdp')
- grad_condition: float32 [8, 1408], P('fsdp')
- grad_mod_weight: float32 [2, 1408, 1408], P(None, 'fsdp')
- grad_norm_gains: float32 [2, 3, 1408], P(None, None, 'fsdp')
- grad_qkv_weight: float32 [2, 1408, 4224], P(None, 'fsdp')
- grad_query_weight: float32 [2, 1408, 1408], P(None, 'fsdp')
- grad_text_kv_weight: float32 [2, 1024, 2816], P(None, 'fsdp')
- grad_self_out_weight: float32 [2, 1408, 1408], P(None, 'fsdp')
- grad_cross_out_weight: float32 [2, 1408, 1408], P(None, 'fsdp')
- grad_up_weight: float32 [2, 1408, 6144], P(None, 'fsdp')
- grad_down_weight: float32 [2, 6144, 1408], P(None, 'fsdp')
- grad_skip_gain: float32 [2816], P('fsdp')
- grad_skip_weight: float32 [2816, 1408], P('fsdp')
Inputs may be any that keep to these rules, and one draw needn't show every extreme that they name: `text_lengths`: some latent's text has all 333 tokens.
All inputs are finite; a program needn't handle non-finite values.
Results may differ from a plain program's by a relative error of at most 0.022.
Values may be sent and summed in bfloat16 or wider, within the bound.
No kernel may reach another device: no remote copies, remote signals or barrier semaphores. Data moves between devices by JAX's collectives and lax.ppermute only.
A program may use at most 576 MiB of HBM per device.

v0:
```python
import math

import jax
import jax.numpy as jnp
from jax import lax
from jax.sharding import PartitionSpec as P

H = 16


NORM_EPSILON = 1e-06
EXACT = lax.Precision.HIGHEST


def layer_norm(values, gain_vec):
    row_mean = jnp.mean(values, axis=-1, keepdims=True)
    centered = values - row_mean
    row_var = jnp.mean(centered * centered, axis=-1, keepdims=True)
    return centered * lax.rsqrt(row_var + NORM_EPSILON) * gain_vec


def norm_shift(values, gain_vec, shift_vec):
    return layer_norm(values, gain_vec) + shift_vec[:, None, :]


def modulate(cond_rows, mod_matrix):
    return jnp.dot(jax.nn.silu(cond_rows), mod_matrix, precision=EXACT)


def gelu_tanh(values):
    return jax.nn.gelu(values, approximate=True)


def product(left_in, right_in):
    return jnp.dot(left_in, right_in, preferred_element_type=jnp.float32)


def product_tn(left_in, right_in):
    return lax.dot_general(
        left_in, right_in, (((0,), (0,)), ((), ())), preferred_element_type=jnp.float32
    )


def product_nt(left_in, right_in):
    return lax.dot_general(
        left_in, right_in, (((1,), (1,)), ((), ())), preferred_element_type=jnp.float32
    )


def masked_scores(queries, key_rows, key_validity_mask, score_scale):
    scores = (
        jnp.einsum("qhd,khd->hqk", queries, key_rows, preferred_element_type=jnp.float32)
        * score_scale
    )
    return jnp.where(key_validity_mask[None, None, :], scores, -1e30)


def attend_forward(queries, key_rows, values, key_validity_mask, score_scale):
    scores = masked_scores(queries, key_rows, key_validity_mask, score_scale)
    top_score = jnp.max(scores, axis=-1, keepdims=True)
    exponent = jnp.exp(scores - top_score)
    row_total = jnp.sum(exponent, axis=-1, keepdims=True)
    weights = (exponent / row_total).astype(jnp.bfloat16)
    attended = jnp.einsum("hqk,khd->qhd", weights, values, preferred_element_type=jnp.float32)
    return (attended.astype(jnp.bfloat16), (top_score + jnp.log(row_total))[..., 0])


def attend_backward(
    queries, key_rows, values, key_validity_mask, grad_mixed, log_total, score_scale
):
    scores = masked_scores(queries, key_rows, key_validity_mask, score_scale)
    probability = jnp.exp(scores - log_total[..., None])
    weights = probability.astype(jnp.bfloat16)
    grad_values = jnp.einsum(
        "hqk,qhd->khd", weights, grad_mixed, preferred_element_type=jnp.float32
    )
    grad_probs = jnp.einsum("qhd,khd->hqk", grad_mixed, values, preferred_element_type=jnp.float32)
    row_delta = jnp.sum(grad_probs * probability, axis=-1, keepdims=True)
    grad_scores = (probability * (grad_probs - row_delta)).astype(jnp.bfloat16)
    grad_queries = (
        jnp.einsum("hqk,khd->qhd", grad_scores, key_rows, preferred_element_type=jnp.float32)
        * score_scale
    )
    grad_keys = (
        jnp.einsum("hqk,qhd->khd", grad_scores, queries, preferred_element_type=jnp.float32)
        * score_scale
    )
    return (
        grad_queries.astype(jnp.bfloat16),
        grad_keys.astype(jnp.bfloat16),
        grad_values.astype(jnp.bfloat16),
    )


def arrange_heads(tokens, groups):
    seq_count = lax.axis_size("seq")
    lat_count, tok_rows, full_width = tokens.shape
    return tokens.reshape(
        lat_count, tok_rows, groups, seq_count, full_width // (groups * seq_count)
    )


def finish_heads(arrived):
    seq_count = lax.axis_size("seq")
    return arrived.reshape(arrived.shape[0], arrived.shape[1], arrived.shape[2], H // seq_count, -1)


def arrange_tokens(head_data):
    return head_data.reshape(head_data.shape[0], head_data.shape[1], head_data.shape[2], 1, -1)


def finish_tokens(arrived):
    return arrived.reshape(arrived.shape[0], arrived.shape[1], -1)


def heads_forward(tokens, groups):
    arrived = lax.all_to_all(
        arrange_heads(tokens, groups), "seq", split_axis=3, concat_axis=1, tiled=True
    )
    return finish_heads(arrived)


def tokens_forward(head_data):
    arrived = lax.all_to_all(
        arrange_tokens(head_data), "seq", split_axis=1, concat_axis=3, tiled=True
    )
    return finish_tokens(arrived)


def heads_backward(tokens, groups):
    arrived = lax.all_to_all(
        arrange_heads(tokens, groups), "seq", split_axis=3, concat_axis=1, tiled=True
    )
    return finish_heads(arrived)


def tokens_backward(head_data):
    arrived = lax.all_to_all(
        arrange_tokens(head_data), "seq", split_axis=1, concat_axis=3, tiled=True
    )
    return finish_tokens(arrived)


def own_columns(kv_matrix):
    per_device = H // lax.axis_size("seq")
    split_view = kv_matrix.reshape(kv_matrix.shape[0], 2, H, -1)
    picked = lax.dynamic_slice_in_dim(split_view, lax.axis_index("seq") * per_device, per_device, 2)
    return picked.reshape(kv_matrix.shape[0], -1)


def place_columns(grad_columns):
    per_device = H // lax.axis_size("seq")
    in_width = grad_columns.shape[0]
    head_size = grad_columns.shape[1] // (2 * per_device)
    blank = jnp.zeros((in_width, 2, H, head_size), jnp.float32)
    placed = lax.dynamic_update_slice_in_dim(
        blank,
        grad_columns.reshape(in_width, 2, per_device, head_size),
        lax.axis_index("seq") * per_device,
        2,
    )
    return placed.reshape(in_width, -1)


def gather_forward(
    layer_index,
    mod_weight,
    norm_gains,
    qkv_weight,
    query_weight,
    text_kv_weight,
    self_out_weight,
    cross_out_weight,
    up_weight,
    down_weight,
):
    return (
        lax.all_gather(mod_weight[layer_index], "fsdp", axis=0, tiled=True),
        lax.all_gather(norm_gains[layer_index], "fsdp", axis=1, tiled=True),
        lax.all_gather(qkv_weight[layer_index], "fsdp", axis=0, tiled=True),
        lax.all_gather(query_weight[layer_index], "fsdp", axis=0, tiled=True),
        lax.all_gather(text_kv_weight[layer_index], "fsdp", axis=0, tiled=True),
        lax.all_gather(self_out_weight[layer_index], "fsdp", axis=0, tiled=True),
        lax.all_gather(cross_out_weight[layer_index], "fsdp", axis=0, tiled=True),
        lax.all_gather(up_weight[layer_index], "fsdp", axis=0, tiled=True),
        lax.all_gather(down_weight[layer_index], "fsdp", axis=0, tiled=True),
    )


def gather_backward(
    layer_index,
    mod_weight,
    norm_gains,
    qkv_weight,
    query_weight,
    text_kv_weight,
    self_out_weight,
    cross_out_weight,
    up_weight,
    down_weight,
):
    return (
        lax.all_gather(mod_weight[layer_index], "fsdp", axis=0, tiled=True),
        lax.all_gather(norm_gains[layer_index], "fsdp", axis=1, tiled=True),
        lax.all_gather(qkv_weight[layer_index], "fsdp", axis=0, tiled=True),
        lax.all_gather(query_weight[layer_index], "fsdp", axis=0, tiled=True),
        lax.all_gather(text_kv_weight[layer_index], "fsdp", axis=0, tiled=True),
        lax.all_gather(self_out_weight[layer_index], "fsdp", axis=0, tiled=True),
        lax.all_gather(cross_out_weight[layer_index], "fsdp", axis=0, tiled=True),
        lax.all_gather(up_weight[layer_index], "fsdp", axis=0, tiled=True),
        lax.all_gather(down_weight[layer_index], "fsdp", axis=0, tiled=True),
    )


def layer_forward(
    hidden_state, cond_rows, text_tokens, key_validity_mask, block_parameters, score_scale
):
    (
        mod_matrix,
        gain_block,
        qkv_matrix,
        query_matrix,
        kv_matrix,
        self_matrix,
        cross_matrix,
        up_matrix,
        down_matrix,
    ) = block_parameters
    lat_count, tok_rows, model_width = hidden_state.shape
    flat_rows = lat_count * tok_rows
    gain_rows = gain_block.astype(jnp.float32)
    shift_vec = modulate(cond_rows, mod_matrix.astype(jnp.float32))
    first_norm = norm_shift(hidden_state, gain_rows[0], shift_vec).astype(jnp.bfloat16)
    triples = product(first_norm.reshape(flat_rows, model_width), qkv_matrix).astype(jnp.bfloat16)
    self_heads = heads_forward(triples.reshape(lat_count, tok_rows, -1), 3)
    open_keys = jnp.ones((self_heads.shape[1],), jnp.bool_)

    def self_one(head_block):
        return attend_forward(
            head_block[:, 0], head_block[:, 1], head_block[:, 2], open_keys, score_scale
        )

    self_mixed, self_log = lax.map(self_one, self_heads)
    self_tokens = tokens_forward(self_mixed[:, :, None])
    after_self = hidden_state + product(
        self_tokens.reshape(flat_rows, model_width), self_matrix
    ).reshape(hidden_state.shape)
    cross_norm = layer_norm(after_self, gain_rows[1]).astype(jnp.bfloat16)
    queries = product(cross_norm.reshape(flat_rows, model_width), query_matrix).astype(jnp.bfloat16)
    query_heads = heads_forward(queries.reshape(lat_count, tok_rows, -1), 1)[:, :, 0]
    text_pairs = jnp.einsum(
        "btc,cw->btw", text_tokens, own_columns(kv_matrix), preferred_element_type=jnp.float32
    ).astype(jnp.bfloat16)
    text_pairs = text_pairs.reshape(lat_count, text_tokens.shape[1], 2, query_heads.shape[2], -1)

    def cross_one(items):
        query_block, pair_block, valid_row = items
        return attend_forward(
            query_block, pair_block[:, 0], pair_block[:, 1], valid_row, score_scale
        )

    cross_mixed, cross_log = lax.map(cross_one, (query_heads, text_pairs, key_validity_mask))
    cross_tokens = tokens_forward(cross_mixed[:, :, None])
    after_cross = after_self + product(
        cross_tokens.reshape(flat_rows, model_width), cross_matrix
    ).reshape(hidden_state.shape)
    mlp_norm = (
        layer_norm(after_cross, gain_rows[2]).astype(jnp.bfloat16).reshape(flat_rows, model_width)
    )
    up_rows = product(mlp_norm, up_matrix)
    activated = gelu_tanh(up_rows).astype(jnp.bfloat16)
    result = after_cross + product(activated, down_matrix).reshape(hidden_state.shape)
    saved = (
        hidden_state,
        shift_vec,
        first_norm,
        self_heads,
        self_log,
        self_tokens,
        after_self,
        cross_norm,
        query_heads,
        text_pairs,
        cross_log,
        cross_tokens,
        after_cross,
        mlp_norm,
        up_rows,
        activated,
    )
    return (result, saved)


def layer_backward(
    grad_out, saved, block_parameters, cond_rows, text_tokens, key_validity_mask, score_scale
):
    (
        mod_matrix,
        gain_block,
        qkv_matrix,
        query_matrix,
        kv_matrix,
        self_matrix,
        cross_matrix,
        up_matrix,
        down_matrix,
    ) = block_parameters
    (
        hidden_state,
        shift_vec,
        first_norm,
        self_heads,
        self_log,
        self_tokens,
        after_self,
        cross_norm,
        query_heads,
        text_pairs,
        cross_log,
        cross_tokens,
        after_cross,
        mlp_norm,
        up_rows,
        activated,
    ) = saved
    lat_count, tok_rows, model_width = hidden_state.shape
    flat_rows = lat_count * tok_rows
    gain_rows = gain_block.astype(jnp.float32)
    out_grad = grad_out.reshape(flat_rows, model_width).astype(jnp.bfloat16)
    grad_down = lax.psum_scatter(
        product_tn(activated, out_grad).astype(jnp.bfloat16),
        "fsdp",
        scatter_dimension=0,
        tiled=True,
    ).astype(jnp.float32)
    grad_activated = product_nt(out_grad, down_matrix)
    _, gelu_pull = jax.vjp(gelu_tanh, up_rows)
    grad_up_rows = gelu_pull(grad_activated)[0].astype(jnp.bfloat16)
    grad_up = lax.psum_scatter(
        product_tn(mlp_norm, grad_up_rows).astype(jnp.bfloat16),
        "fsdp",
        scatter_dimension=0,
        tiled=True,
    ).astype(jnp.float32)
    grad_mlp_norm = product_nt(grad_up_rows, up_matrix).reshape(hidden_state.shape)
    _, mlp_pull = jax.vjp(layer_norm, after_cross, gain_rows[2])
    grad_cross_res, grad_gain_mlp = mlp_pull(grad_mlp_norm)
    grad_cross_res = grad_cross_res + grad_out
    branch_grad = grad_cross_res.reshape(flat_rows, model_width).astype(jnp.bfloat16)
    grad_cross_w = product_tn(cross_tokens.reshape(flat_rows, model_width), branch_grad)
    grad_cross_tok = (
        product_nt(branch_grad, cross_matrix).astype(jnp.bfloat16).reshape(hidden_state.shape)
    )
    grad_cross_heads = heads_backward(grad_cross_tok, 1)[:, :, 0]

    def cross_back(items):
        query_block, pair_block, valid_row, grad_block, log_block = items
        return attend_backward(
            query_block,
            pair_block[:, 0],
            pair_block[:, 1],
            valid_row,
            grad_block,
            log_block,
            score_scale,
        )

    grad_query_heads, grad_text_keys, grad_text_values = lax.map(
        cross_back, (query_heads, text_pairs, key_validity_mask, grad_cross_heads, cross_log)
    )
    grad_queries = tokens_backward(grad_query_heads[:, :, None]).reshape(flat_rows, model_width)
    grad_query_w = product_tn(cross_norm.reshape(flat_rows, model_width), grad_queries)
    grad_cross_norm = product_nt(grad_queries, query_matrix).reshape(hidden_state.shape)
    grad_pairs = jnp.stack([grad_text_keys, grad_text_values], axis=2).reshape(
        lat_count, text_tokens.shape[1], -1
    )
    kv_columns = own_columns(kv_matrix)
    grad_text = jnp.einsum(
        "btw,cw->btc", grad_pairs, kv_columns, preferred_element_type=jnp.float32
    )
    grad_kv_columns = jnp.einsum(
        "btc,btw->cw", text_tokens, grad_pairs, preferred_element_type=jnp.float32
    )
    _, cross_pull = jax.vjp(layer_norm, after_self, gain_rows[1])
    grad_self_res, grad_gain_cross = cross_pull(grad_cross_norm)
    grad_self_res = grad_self_res + grad_cross_res
    branch_grad = grad_self_res.reshape(flat_rows, model_width).astype(jnp.bfloat16)
    grad_self_w = product_tn(self_tokens.reshape(flat_rows, model_width), branch_grad)
    grad_self_tok = (
        product_nt(branch_grad, self_matrix).astype(jnp.bfloat16).reshape(hidden_state.shape)
    )
    grad_self_heads = heads_backward(grad_self_tok, 1)[:, :, 0]
    open_keys = jnp.ones((self_heads.shape[1],), jnp.bool_)

    def self_back(items):
        head_block, grad_block, log_block = items
        grad_q, grad_k, grad_v = attend_backward(
            head_block[:, 0],
            head_block[:, 1],
            head_block[:, 2],
            open_keys,
            grad_block,
            log_block,
            score_scale,
        )
        return jnp.stack([grad_q, grad_k, grad_v], axis=1)

    grad_triples_heads = lax.map(self_back, (self_heads, grad_self_heads, self_log))
    grad_triples = tokens_backward(grad_triples_heads).reshape(flat_rows, -1)
    grad_qkv_w = product_tn(first_norm.reshape(flat_rows, model_width), grad_triples)
    grad_first_norm = product_nt(grad_triples, qkv_matrix).reshape(hidden_state.shape)
    _, shift_pull = jax.vjp(norm_shift, hidden_state, gain_rows[0], shift_vec)
    grad_hidden, grad_gain_self, grad_shift = shift_pull(grad_first_norm)
    grad_hidden = grad_hidden + grad_self_res
    mod_float = mod_matrix.astype(jnp.float32)

    def shift_of(cond_in):
        return modulate(cond_in, mod_float)

    _, cond_pull = jax.vjp(shift_of, cond_rows)
    grad_cond = cond_pull(grad_shift)[0]
    grad_mod = jnp.dot(jax.nn.silu(cond_rows).T, grad_shift, precision=EXACT)
    grad_gain_block = jnp.stack([grad_gain_self, grad_gain_cross, grad_gain_mlp])
    sent = (
        lax.psum_scatter(
            grad_mod.astype(jnp.bfloat16), "fsdp", scatter_dimension=0, tiled=True
        ).astype(jnp.float32),
        lax.psum_scatter(
            grad_gain_block.astype(jnp.bfloat16), "fsdp", scatter_dimension=1, tiled=True
        ).astype(jnp.float32),
        lax.psum_scatter(
            grad_qkv_w.astype(jnp.bfloat16), "fsdp", scatter_dimension=0, tiled=True
        ).astype(jnp.float32),
        lax.psum_scatter(
            grad_query_w.astype(jnp.bfloat16), "fsdp", scatter_dimension=0, tiled=True
        ).astype(jnp.float32),
        lax.psum_scatter(
            grad_kv_columns.astype(jnp.bfloat16), "fsdp", scatter_dimension=0, tiled=True
        ).astype(jnp.float32),
        lax.psum_scatter(
            grad_self_w.astype(jnp.bfloat16), "fsdp", scatter_dimension=0, tiled=True
        ).astype(jnp.float32),
        lax.psum_scatter(
            grad_cross_w.astype(jnp.bfloat16), "fsdp", scatter_dimension=0, tiled=True
        ).astype(jnp.float32),
    )
    block_shards = (
        sent[0],
        sent[1],
        sent[2],
        sent[3],
        sent[4],
        sent[5],
        sent[6],
        grad_up,
        grad_down,
    )
    return (grad_hidden, grad_text, grad_cond, block_shards)


def body(
    latents,
    skip_input,
    text_tokens,
    text_lengths,
    condition,
    cotangent,
    mod_weight,
    norm_gains,
    qkv_weight,
    query_weight,
    text_kv_weight,
    self_out_weight,
    cross_out_weight,
    up_weight,
    down_weight,
    skip_gain,
    skip_weight,
):
    lat_count, tok_rows, model_width = latents.shape
    flat_rows = lat_count * tok_rows
    score_scale = 1.0 / math.sqrt(model_width // H)
    cond_rows = condition.astype(jnp.float32)
    key_validity_mask = jnp.arange(text_tokens.shape[1])[None, :] < text_lengths[:, None]
    first_weights = gather_forward(
        0,
        mod_weight,
        norm_gains,
        qkv_weight,
        query_weight,
        text_kv_weight,
        self_out_weight,
        cross_out_weight,
        up_weight,
        down_weight,
    )
    first_out, first_saved = layer_forward(
        latents.astype(jnp.float32),
        cond_rows,
        text_tokens,
        key_validity_mask,
        first_weights,
        score_scale,
    )
    skip_pair = (
        lax.all_gather(skip_gain, "fsdp", axis=0, tiled=True),
        lax.all_gather(skip_weight, "fsdp", axis=0, tiled=True),
    )
    joined = jnp.concatenate([first_out, skip_input.astype(jnp.float32)], axis=-1)
    joined_norm = (
        layer_norm(joined, skip_pair[0].astype(jnp.float32))
        .astype(jnp.bfloat16)
        .reshape(flat_rows, 2 * model_width)
    )
    skip_out = product(joined_norm, skip_pair[1]).reshape(latents.shape)
    second_weights = gather_forward(
        1,
        mod_weight,
        norm_gains,
        qkv_weight,
        query_weight,
        text_kv_weight,
        self_out_weight,
        cross_out_weight,
        up_weight,
        down_weight,
    )
    final_out, second_saved = layer_forward(
        skip_out, cond_rows, text_tokens, key_validity_mask, second_weights, score_scale
    )
    output = final_out.astype(jnp.bfloat16)
    grad_skip_out, text_second, cond_second, shards_second = layer_backward(
        cotangent.astype(jnp.float32),
        second_saved,
        second_weights,
        cond_rows,
        text_tokens,
        key_validity_mask,
        score_scale,
    )
    branch_grad = grad_skip_out.reshape(flat_rows, model_width).astype(jnp.bfloat16)
    grad_skip_w = product_tn(joined_norm, branch_grad)
    grad_joined_norm = product_nt(branch_grad, skip_pair[1]).reshape(
        lat_count, tok_rows, 2 * model_width
    )
    _, joined_pull = jax.vjp(layer_norm, joined, skip_pair[0].astype(jnp.float32))
    grad_joined, grad_skip_g = joined_pull(grad_joined_norm)
    skip_shards = (
        lax.psum_scatter(
            grad_skip_g.astype(jnp.bfloat16), "fsdp", scatter_dimension=0, tiled=True
        ).astype(jnp.float32),
        lax.psum_scatter(
            grad_skip_w.astype(jnp.bfloat16), "fsdp", scatter_dimension=0, tiled=True
        ).astype(jnp.float32),
    )
    back_first = gather_backward(
        0,
        mod_weight,
        norm_gains,
        qkv_weight,
        query_weight,
        text_kv_weight,
        self_out_weight,
        cross_out_weight,
        up_weight,
        down_weight,
    )
    grad_latents, text_first, cond_first, shards_first = layer_backward(
        grad_joined[..., :model_width],
        first_saved,
        back_first,
        cond_rows,
        text_tokens,
        key_validity_mask,
        score_scale,
    )
    grad_skip = grad_joined[..., model_width:]

    def paired(index):
        return jnp.stack([shards_first[index], shards_second[index]])

    kv_pair = jnp.stack([place_columns(shards_first[4]), place_columns(shards_second[4])])
    summed = (
        lax.psum(paired(0).astype(jnp.bfloat16), "seq").astype(jnp.float32),
        lax.psum(paired(1).astype(jnp.bfloat16), "seq").astype(jnp.float32),
        lax.psum(paired(2).astype(jnp.bfloat16), "seq").astype(jnp.float32),
        lax.psum(paired(3).astype(jnp.bfloat16), "seq").astype(jnp.float32),
        lax.psum(kv_pair.astype(jnp.bfloat16), "seq").astype(jnp.float32),
        lax.psum(paired(5).astype(jnp.bfloat16), "seq").astype(jnp.float32),
        lax.psum(paired(6).astype(jnp.bfloat16), "seq").astype(jnp.float32),
        lax.psum(paired(7).astype(jnp.bfloat16), "seq").astype(jnp.float32),
        lax.psum(paired(8).astype(jnp.bfloat16), "seq").astype(jnp.float32),
        lax.psum(skip_shards[0].astype(jnp.bfloat16), "seq").astype(jnp.float32),
        lax.psum(skip_shards[1].astype(jnp.bfloat16), "seq").astype(jnp.float32),
    )
    grad_text, grad_cond = (
        lax.psum((text_first + text_second).astype(jnp.bfloat16), "seq").astype(jnp.float32),
        lax.psum((cond_first + cond_second).astype(jnp.bfloat16), "seq").astype(jnp.float32),
    )
    return (
        output,
        grad_latents,
        grad_skip,
        grad_text,
        grad_cond,
        summed[0],
        summed[1],
        summed[2],
        summed[3],
        summed[4],
        summed[5],
        summed[6],
        summed[7],
        summed[8],
        summed[9],
        summed[10],
    )


def solution(mesh):
    in_specs = (
        P("fsdp", "seq", None),
        P("fsdp", "seq", None),
        P("fsdp", None, None),
        P("fsdp"),
        P("fsdp", None),
        P("fsdp", "seq", None),
        P(None, "fsdp", None),
        P(None, None, "fsdp"),
        P(None, "fsdp", None),
        P(None, "fsdp", None),
        P(None, "fsdp", None),
        P(None, "fsdp", None),
        P(None, "fsdp", None),
        P(None, "fsdp", None),
        P(None, "fsdp", None),
        P("fsdp"),
        P("fsdp", None),
    )
    out_specs = (
        P("fsdp", "seq", None),
        P("fsdp", "seq", None),
        P("fsdp", "seq", None),
        P("fsdp", None, None),
        P("fsdp", None),
        P(None, "fsdp", None),
        P(None, None, "fsdp"),
        P(None, "fsdp", None),
        P(None, "fsdp", None),
        P(None, "fsdp", None),
        P(None, "fsdp", None),
        P(None, "fsdp", None),
        P(None, "fsdp", None),
        P(None, "fsdp", None),
        P("fsdp"),
        P("fsdp", None),
    )
    return jax.shard_map(body, mesh=mesh, in_specs=in_specs, out_specs=out_specs, check_vma=False)
```

profile of v0, /device:TPU:0, one launch (start us, length us, event | category | flops | bytes accessed | tf_op | source)
XLA Modules:
  0.0 3658.8 jit_solution(13534902531081952833)
XLA Ops:
  58.3 41.6 %slice_reduce_fusion.3 = (f32[1408]{0:T(1024)S(1)}, f32[1408]{0:T(1024)S(1)}, f32[1408]{0:T(1024)S(1)}) fusion(f32[1,3,1408]{1,0,2:T(1,128)S(1)} %convert_element_type.583), kind=kLoop, calls=%fused_computation.276 | loop fusion | bytes 33792 | tf_op jit(solution)/shard_map/slice | solution.py:268
  103.8 72.2 %all-gather.40.cloned.1.call-done = bf16[1,1408,4224]{2,1,0:T(8,128)(2,1)} async-done(((bf16[1,176,4224]{2,1,0:T(8,128)(2,1)}), bf16[1,1408,4224]{2,1,0:T(8,128)(2,1)}) %all-gather.40.cloned.1.call-update) | async-done | bytes 11894800 | tf_op jit(solution)/shard_map/all_gather | solution.py:180
  197.7 25.7 all-to-all-done
  278.3 25.0 all-gather.9
  335.0 61.1 %all-gather.44.cloned.1.call-done = bf16[1,1024,2816]{1,2,0:T(8,128)(2,1)} async-done(((bf16[1,128,2816]{1,2,0:T(8,128)(2,1)}), bf16[1,1024,2816]{1,2,0:T(8,128)(2,1)}) %all-gather.44.cloned.1.call-update) | async-done | bytes 5767184 | tf_op jit(solution)/shard_map/all_gather | solution.py:182
  428.3 41.2 %slice_reduce_fusion = (f32[1408]{0:T(1024)S(1)}, f32[1408]{0:T(1024)S(1)}, f32[1408]{0:T(1024)S(1)}) fusion(f32[1,3,1408]{1,0,2:T(1,128)S(1)} %copy-done.39), kind=kLoop, calls=%fused_computation.270 | loop fusion | bytes 33792 | tf_op jit(solution)/shard_map/slice | solution.py:268
  506.0 137.7 %all-gather.50.cloned.1.call-done = bf16[1,1408,6144]{2,1,0:T(8,128)(2,1)} async-done(((bf16[1,176,6144]{2,1,0:T(8,128)(2,1)}), bf16[1,1408,6144]{2,1,0:T(8,128)(2,1)}) %all-gather.50.cloned.1.call-update) | async-done | bytes 17301520 | tf_op jit(solution)/shard_map/all_gather | solution.py:185
  656.9 141.9 %all-gather.52.cloned.1.call-done = bf16[1,6144,1408]{2,1,0:T(8,128)(2,1)} async-done(((bf16[1,768,1408]{2,1,0:T(8,128)(2,1)}), bf16[1,6144,1408]{2,1,0:T(8,128)(2,1)}) %all-gather.52.cloned.1.call-update) | async-done | bytes 17301520 | tf_op jit(solution)/shard_map/all_gather | solution.py:186
  813.6 63.3 %all-gather.36.cloned.1.call-done = bf16[2816,1408]{1,0:T(8,128)(2,1)} async-done(((bf16[352,1408]{1,0:T(8,128)(2,1)}), bf16[2816,1408]{1,0:T(8,128)(2,1)}) %all-gather.36.cloned.1.call-update) | async-done | bytes 7929872 | tf_op jit(solution)/shard_map/all_gather | solution.py:507
  884.0 104.7 %all-gather.56.cloned.1.call-done = bf16[1,1408,4224]{2,1,0:T(8,128)(2,1)} async-done(((bf16[1,176,4224]{2,1,0:T(8,128)(2,1)}), bf16[1,1408,4224]{2,1,0:T(8,128)(2,1)}) %all-gather.56.cloned.1.call-update) | async-done | bytes 11894800 | tf_op jit(solution)/shard_map/all_gather | solution.py:180
  1004.2 30.2 all_to_all.240
  1156.3 124.0 %all-gather.66.cloned.1.call-done = bf16[1,1408,6144]{2,1,0:T(8,128)(2,1)} async-done(((bf16[1,176,6144]{2,1,0:T(8,128)(2,1)}), bf16[1,1408,6144]{2,1,0:T(8,128)(2,1)}) %all-gather.66.cloned.1.call-update) | async-done | bytes 17301520 | tf_op jit(solution)/shard_map/all_gather | solution.py:185
  1291.2 144.2 %all-gather.68.cloned.1.call-done = bf16[1,6144,1408]{2,1,0:T(8,128)(2,1)} async-done(((bf16[1,768,1408]{2,1,0:T(8,128)(2,1)}), bf16[1,6144,1408]{2,1,0:T(8,128)(2,1)}) %all-gather.68.cloned.1.call-update) | async-done | bytes 17301520 | tf_op jit(solution)/shard_map/all_gather | solution.py:186
  1916.8 33.2 all-to-all-done.15
  2082.6 46.2 %reduce-scatter.30.cloned.1.call-done = bf16[176,1408]{1,0:T(8,128)(2,1)} async-done(((bf16[1408,1408]{1,0:T(8,128)(2,1)}), bf16[176,1408]{1,0:T(8,128)(2,1)}) %reduce-scatter.30.cloned.1.call-update) | async-done | bytes 495632 | tf_op jit(solution)/shard_map/reduce_scatter | solution.py:425
  2128.8 49.1 %reduce-scatter.28.cloned.1.call-done = bf16[176,1408]{1,0:T(8,128)(2,1)} async-done(((bf16[1408,1408]{1,0:T(8,128)(2,1)}), bf16[176,1408]{1,0:T(8,128)(2,1)}) %reduce-scatter.28.cloned.1.call-update) | async-done | bytes 495632 | tf_op jit(solution)/shard_map/reduce_scatter | solution.py:425
  2180.1 121.2 %reduce-scatter.34.cloned.1.call-done = bf16[176,4224]{1,0:T(8,128)(2,1)} async-done(((bf16[1408,4224]{1,0:T(8,128)(2,1)}), bf16[176,4224]{1,0:T(8,128)(2,1)}) %reduce-scatter.34.cloned.1.call-update) | async-done | bytes 1486864 | tf_op jit(solution)/shard_map/reduce_scatter | solution.py:431
  2301.4 123.8 %reduce-scatter.32.cloned.1.call-done = bf16[176,4224]{1,0:T(8,128)(2,1)} async-done(((bf16[1408,4224]{1,0:T(8,128)(2,1)}), bf16[176,4224]{1,0:T(8,128)(2,1)}) %reduce-scatter.32.cloned.1.call-update) | async-done | bytes 1486864 | tf_op jit(solution)/shard_map/reduce_scatter | solution.py:431
  2428.9 170.0 %reduce-scatter.50.cloned.1.call-done = bf16[176,6144]{1,0:T(8,128)(2,1)} async-done(((bf16[1408,6144]{1,0:T(8,128)(2,1)}), bf16[176,6144]{1,0:T(8,128)(2,1)}) %reduce-scatter.50.cloned.1.call-update) | async-done | bytes 2162704 | tf_op jit(solution)/shard_map/reduce_scatter | solution.py:339
  2599.0 173.9 %reduce-scatter.48.cloned.1.call-done = bf16[176,6144]{1,0:T(8,128)(2,1)} async-done(((bf16[1408,6144]{1,0:T(8,128)(2,1)}), bf16[176,6144]{1,0:T(8,128)(2,1)}) %reduce-scatter.48.cloned.1.call-update) | async-done | bytes 2162704 | tf_op jit(solution)/shard_map/reduce_scatter | solution.py:339
  2777.6 169.2 %reduce-scatter.54.cloned.1.call-done = bf16[768,1408]{1,0:T(8,128)(2,1)} async-done(((bf16[6144,1408]{1,0:T(8,128)(2,1)}), bf16[768,1408]{1,0:T(8,128)(2,1)}) %reduce-scatter.54.cloned.1.call-update) | async-done | bytes 2162704 | tf_op jit(solution)/shard_map/reduce_scatter | solution.py:330
  2946.8 173.8 %reduce-scatter.52.cloned.1.call-done = bf16[768,1408]{1,0:T(8,128)(2,1)} async-done(((bf16[6144,1408]{1,0:T(8,128)(2,1)}), bf16[768,1408]{1,0:T(8,128)(2,1)}) %reduce-scatter.52.cloned.1.call-update) | async-done | bytes 2162704 | tf_op jit(solution)/shard_map/reduce_scatter | solution.py:330
  3125.4 81.8 %reduce-scatter.56.cloned.1.call-done = bf16[352,1408]{1,0:T(8,128)(2,1)} async-done(((bf16[2816,1408]{1,0:T(8,128)(2,1)}), bf16[352,1408]{1,0:T(8,128)(2,1)}) %reduce-scatter.56.cloned.1.call-update) | async-done | bytes 991248 | tf_op jit(solution)/shard_map/reduce_scatter | solution.py:552
  3289.4 332.4 %all-reduce.6.cloned.1.call-done = (bf16[1,333,1024]{2,1,0:T(8,128)(2,1)}, bf16[2,128,2816]{1,2,0:T(8,128)(2,1)}, bf16[2,176,1408]{2,1,0:T(8,128)(2,1)}, bf16[2,...) async-done(((bf16[1,333,1024]{2,1,0:T(8,128)(2,1)}, ...) | async-done | bytes 18704400 | tf_op jit(solution)/shard_map/psum | solution.py:597
  (756 shorter events, 1152.2 us)
Async XLA Ops:
  18.5 377.6 %all-gather.44.cloned.1.call-start = ((), (), s32[]{:S(2)}) async-start(), calls=%async_computation.54 | async-start | bytes 6488064 | tf_op jit(solution)/shard_map/all_gather | solution.py:182
  19.7 468.2 %all-gather.54.cloned.1.call-start = ((), (), s32[]{:S(2)}) async-start(), calls=%async_computation.59 | async-start | bytes 4460544 | tf_op jit(solution)/shard_map/all_gather | solution.py:178
  20.5 479.9 %all-gather.48.cloned.1.call-start = ((), (), s32[]{:S(2)}) async-start(), calls=%async_computation.56 | async-start | bytes 4460544 | tf_op jit(solution)/shard_map/all_gather | solution.py:184
  21.6 622.1 %all-gather.50.cloned.1.call-start = ((), (), s32[]{:S(2)}) async-start(), calls=%async_computation.57 | async-start | bytes 19464192 | tf_op jit(solution)/shard_map/all_gather | solution.py:185
  26.4 772.4 %all-gather.52.cloned.1.call-start = ((), (), s32[]{:S(2)}) async-start(), calls=%async_computation.58 | async-start | bytes 19464192 | tf_op jit(solution)/shard_map/all_gather | solution.py:186
  31.2 845.8 %all-gather.36.cloned.1.call-start = ((), (), s32[]{:S(2)}) async-start(), calls=%async_computation.35 | async-start | bytes 8921088 | tf_op jit(solution)/shard_map/all_gather | solution.py:507
  31.9 956.8 %all-gather.56.cloned.1.call-start = ((), (), s32[]{:S(2)}) async-start(), calls=%async_computation.60 | async-start | bytes 13381632 | tf_op jit(solution)/shard_map/all_gather | solution.py:180
  32.5 1060.1 %all-gather.58.cloned.1.call-start = ((), (), s32[]{:S(2)}) async-start(), calls=%async_computation.61 | async-start | bytes 4460544 | tf_op jit(solution)/shard_map/all_gather | solution.py:183
  33.2 1064.0 %all-gather.62.cloned.1.call-start = ((), (), s32[]{:S(2)}) async-start(), calls=%async_computation.63 | async-start | bytes 4460544 | tf_op jit(solution)/shard_map/all_gather | solution.py:181
  33.8 1117.0 %all-gather.64.cloned.1.call-start = ((), (), s32[]{:S(2)}) async-start(), calls=%async_computation.64 | async-start | bytes 4460544 | tf_op jit(solution)/shard_map/all_gather | solution.py:184
  34.4 1245.9 %all-gather.66.cloned.1.call-start = ((), (), s32[]{:S(2)}) async-start(), calls=%async_computation.65 | async-start | bytes 19464192 | tf_op jit(solution)/shard_map/all_gather | solution.py:185
  197.1 1238.3 %all-gather.68.cloned.1.call-start = ((), (), s32[]{:S(2)}) async-start(), calls=%async_computation.66 | async-start | bytes 19464192 | tf_op jit(solution)/shard_map/all_gather | solution.py:186
  1622.9 432.1 %reduce-scatter.64.cloned.1.call-start = ((), (), s32[]{:S(2)}) async-start(), calls=%async_computation.70 | async-start | bytes 1769472
  1729.4 334.2 %reduce-scatter.62.cloned.1.call-start = ((), (), s32[]{:S(2)}) async-start(), calls=%async_computation.69 | async-start | bytes 1769472
  1972.6 328.8 %reduce-scatter.34.cloned.1.call-start = ((), (), s32[]{:S(2)}) async-start(), calls=%async_computation.39 | async-start | bytes 13381632 | tf_op jit(solution)/shard_map/reduce_scatter | solution.py:431
  1983.0 442.2 %reduce-scatter.32.cloned.1.call-start = ((), (), s32[]{:S(2)}) async-start(), calls=%async_computation.38 | async-start | bytes 13381632 | tf_op jit(solution)/shard_map/reduce_scatter | solution.py:431
  1993.4 605.6 %reduce-scatter.50.cloned.1.call-start = ((), (), s32[]{:S(2)}) async-start(), calls=%async_computation.47 | async-start | bytes 19464192 | tf_op jit(solution)/shard_map/reduce_scatter | solution.py:339
  2007.4 765.5 %reduce-scatter.48.cloned.1.call-start = ((), (), s32[]{:S(2)}) async-start(), calls=%async_computation.46 | async-start | bytes 19464192 | tf_op jit(solution)/shard_map/reduce_scatter | solution.py:339
  2020.9 926.0 %reduce-scatter.54.cloned.1.call-start = ((), (), s32[]{:S(2)}) async-start(), calls=%async_computation.49 | async-start | bytes 19464192 | tf_op jit(solution)/shard_map/reduce_scatter | solution.py:330
  2032.5 1088.1 %reduce-scatter.52.cloned.1.call-start = ((), (), s32[]{:S(2)}) async-start(), calls=%async_computation.48 | async-start | bytes 19464192 | tf_op jit(solution)/shard_map/reduce_scatter | solution.py:330
  2044.5 1162.6 %reduce-scatter.56.cloned.1.call-start = ((), (), s32[]{:S(2)}) async-start(), calls=%async_computation.50 | async-start | bytes 8921088 | tf_op jit(solution)/shard_map/reduce_scatter | solution.py:552
  2053.1 1185.9 %reduce-scatter.60.cloned.1.call-start = ((), (), s32[]{:S(2)}) async-start(), calls=%async_computation.68 | async-start | bytes 405504
  2054.9 1215.2 %reduce-scatter.58.cloned.1.call-start = ((), (), s32[]{:S(2)}) async-start(), calls=%async_computation.67 | async-start | bytes 405504
  2063.4 1558.5 %all-reduce.6.cloned.1.call-start = ((), (), s32[]{:S(2)}) async-start(), calls=%async_computation.71 | async-start | bytes 37421056 | tf_op jit(solution)/shard_map/psum | solution.py:597
  (194 other events, 11250.3 us)
Sparse Core Ops, SparseCore 0:
  10.2 53.4 all-gather.37
  66.0 109.9 all-gather.39
  269.5 65.4 all-gather.59
  337.0 59.0 all-gather.43
  489.3 154.2 all-gather.49
  645.1 153.6 all-gather.51
  800.4 76.4 all-gather.35
  879.0 109.6 all-gather.55
  1126.0 154.2 all-gather.65
  1281.7 153.6 all-gather.67
  1839.6 46.2 reduce-scatter.43
  1888.2 46.2 reduce-scatter.37
  1985.4 46.2 reduce-scatter.41
  2034.1 46.2 reduce-scatter.39
  2082.5 46.2 reduce-scatter.29
  2131.6 46.2 reduce-scatter.27
  2180.2 121.0 reduce-scatter.33
  2303.8 121.3 reduce-scatter.31
  2427.4 171.5 reduce-scatter.49
  2601.4 171.5 reduce-scatter.47
  2775.3 171.5 reduce-scatter.53
  2949.1 171.5 reduce-scatter.51
  3123.5 83.6 reduce-scatter.55
  3276.5 345.3 all-reduce.5
  (13 shorter events, 519.7 us)
where the time goes:
time: 3670 us; the launch traced here: 3660 us
  waiting for transfers between devices  2450 us (67%)
  matrix products  451 us (12%)
  local copies, waits for them, and re-layouts  337 us (9%)
  other arithmetic  176 us (5%)
  blocking collectives  174 us (5%)
  starting transfers between devices  47.8 us (1%)
    reduce_scatter x2, waiting for transfers between devices, layer_backward(): lax.psum_scatter(product_tn(mlp_norm, grad_up_rows).astype(jnp.bfloat16),...  344 us
    reduce_scatter x2, waiting for transfers between devices, layer_backward(): lax.psum_scatter(product_tn(activated, out_grad).astype(jnp.bfloat16), 'f...  343 us
    psum x1, waiting for transfers between devices, body(): lax.psum((text_first + text_second).astype(jnp.bfloat16), 'seq')  332 us
    all_gather x2, waiting for transfers between devices, gather_forward(): lax.all_gather(down_weight[layer_index], 'fsdp', axis=0, tiled=True)  286 us
    all_gather x2, waiting for transfers between devices, gather_forward(): lax.all_gather(up_weight[layer_index], 'fsdp', axis=0, tiled=True)  262 us
    reduce_scatter x2, waiting for transfers between devices, layer_backward(): lax.psum_scatter(grad_qkv_w.astype(jnp.bfloat16), 'fsdp', scatter_dimensi...  245 us
    all_gather x2, waiting for transfers between devices, gather_forward(): lax.all_gather(qkv_weight[layer_index], 'fsdp', axis=0, tiled=True)  177 us
    dot_general x13, matrix products, product_nt(): lax.dot_general(left_in, right_in, (((1,), (1,)), ((), ())), preferred_el...  104 us
  transfers between devices with their start and end apart: 48, of which 30 were waited for; matrix products, arithmetic and copies ran while one was open for 21% of the time, Pallas kernels for 0%

commit v1 on v0

v1 whole, which is shorter than its diff:
```python
import math

import jax
import jax.numpy as jnp
from jax import lax
from jax.sharding import PartitionSpec as P

H = 16

NORM_EPSILON = 1e-06
EXACT = lax.Precision.HIGHEST
BF16 = jnp.bfloat16
F32 = jnp.float32


def layer_norm(values, gain_vec):
    row_mean = jnp.mean(values, axis=-1, keepdims=True)
    centered = values - row_mean
    row_var = jnp.mean(centered * centered, axis=-1, keepdims=True)
    return centered * lax.rsqrt(row_var + NORM_EPSILON) * gain_vec


def norm_shift(values, gain_vec, shift_vec):
    return layer_norm(values, gain_vec) + shift_vec


def gelu_tanh(values):
    return jax.nn.gelu(values, approximate=True)


def product(left_in, right_in):
    return jnp.dot(left_in, right_in, preferred_element_type=F32)


def product_tn(left_in, right_in):
    return lax.dot_general(
        left_in, right_in, (((0,), (0,)), ((), ())), preferred_element_type=F32
    )


def product_nt(left_in, right_in):
    return lax.dot_general(
        left_in, right_in, (((1,), (1,)), ((), ())), preferred_element_type=F32
    )


def masked_scores(queries, key_rows, key_mask, score_scale):
    scores = (
        jnp.einsum("qhd,khd->hqk", queries, key_rows, preferred_element_type=F32) * score_scale
    )
    if key_mask is None:
        return scores
    return jnp.where(key_mask[None, None, :], scores, -1e30)


def attend_forward(queries, key_rows, values, key_mask, score_scale):
    scores = masked_scores(queries, key_rows, key_mask, score_scale)
    top_score = jnp.max(scores, axis=-1, keepdims=True)
    exponent = jnp.exp(scores - top_score)
    row_total = jnp.sum(exponent, axis=-1, keepdims=True)
    weights = (exponent / row_total).astype(BF16)
    attended = jnp.einsum("hqk,khd->qhd", weights, values, preferred_element_type=F32)
    return (attended.astype(BF16), (top_score + jnp.log(row_total))[..., 0])


def attend_backward(queries, key_rows, values, key_mask, grad_mixed, log_total, score_scale):
    scores = masked_scores(queries, key_rows, key_mask, score_scale)
    probability = jnp.exp(scores - log_total[..., None])
    weights = probability.astype(BF16)
    grad_values = jnp.einsum("hqk,qhd->khd", weights, grad_mixed, preferred_element_type=F32)
    grad_probs = jnp.einsum("qhd,khd->hqk", grad_mixed, values, preferred_element_type=F32)
    row_delta = jnp.sum(grad_probs * probability, axis=-1, keepdims=True)
    grad_scores = (probability * (grad_probs - row_delta)).astype(BF16)
    grad_queries = (
        jnp.einsum("hqk,khd->qhd", grad_scores, key_rows, preferred_element_type=F32) * score_scale
    )
    grad_keys = (
        jnp.einsum("hqk,qhd->khd", grad_scores, queries, preferred_element_type=F32) * score_scale
    )
    return (grad_queries.astype(BF16), grad_keys.astype(BF16), grad_values.astype(BF16))


def swap_seq(block, bits):
    seq_count = lax.axis_size("seq")
    return lax.ppermute(block, "seq", [(i, i ^ bits) for i in range(seq_count)])


def swap_core(block):
    fsdp_count = lax.axis_size("fsdp")
    return lax.ppermute(block, "fsdp", [(i, i ^ 1) for i in range(fsdp_count)])


def swap_by_core(block, even_bits, odd_bits):
    seq_count, fsdp_count = lax.axis_size("seq"), lax.axis_size("fsdp")
    pairs = []
    for s in range(seq_count):
        for f in range(fsdp_count):
            other = s ^ (odd_bits if f % 2 else even_bits)
            pairs.append((s * fsdp_count + f, other * fsdp_count + f))
    return lax.ppermute(block, ("seq", "fsdp"), pairs)


def gather_rel(block):
    seq_count = lax.axis_size("seq")
    if seq_count != 4:
        return [block] + [swap_seq(block, j) for j in range(1, seq_count)]
    half = block.shape[0] // 2
    from_x, from_y = swap_seq(block, 1), swap_seq(block, 2)
    corner = jnp.concatenate([swap_seq(from_y[:half], 1), swap_seq(from_x[half:], 2)], axis=0)
    return [block, from_x, from_y, corner]


def scatter_rel(blocks):
    seq_count = lax.axis_size("seq")
    if seq_count != 4:
        total = blocks[0].astype(F32)
        for j in range(1, seq_count):
            total = total + swap_seq(blocks[j].astype(BF16), j).astype(F32)
        return total
    half = blocks[0].shape[0] // 2
    corner = blocks[3].astype(BF16)
    by_x, by_y = swap_seq(corner[:half], 1), swap_seq(corner[half:], 2)
    to_y = jnp.concatenate(
        [(blocks[2][:half].astype(F32) + by_x.astype(F32)).astype(BF16), blocks[2][half:].astype(BF16)]
    )
    to_x = jnp.concatenate(
        [blocks[1][:half].astype(BF16), (blocks[1][half:].astype(F32) + by_y.astype(F32)).astype(BF16)]
    )
    return blocks[0].astype(F32) + swap_seq(to_x, 1).astype(F32) + swap_seq(to_y, 2).astype(F32)


def exchange_rel(blocks):
    return [blocks[0]] + [swap_seq(blocks[j], j) for j in range(1, len(blocks))]


def list_order():
    s, seq_count = lax.axis_index("seq"), lax.axis_size("seq")
    if seq_count != 4:
        return [s ^ j for j in range(seq_count)]
    odd = lax.axis_index("fsdp") % 2
    return [s, s ^ (1 + odd), s ^ (2 - odd), s ^ 3]


def spread(block):
    seq_count = lax.axis_size("seq")
    if seq_count != 4:
        return [block] + [swap_seq(block, j) for j in range(1, seq_count)]
    odd = lax.axis_index("fsdp") % 2
    half = block.shape[0] // 2
    first = swap_by_core(block, 1, 2)
    part = swap_by_core(lax.dynamic_slice_in_dim(first, odd * half, half, 0), 2, 1)
    second, other_part = swap_core(first), swap_core(part)
    corner = jnp.where(
        odd == 0,
        jnp.concatenate([part, other_part], axis=0),
        jnp.concatenate([other_part, part], axis=0),
    )
    return [block, first, second, corner]


def add_bf16(left_in, right_in):
    return (left_in.astype(F32) + right_in.astype(F32)).astype(BF16)


def unspread(blocks):
    seq_count = lax.axis_size("seq")
    if seq_count != 4:
        return scatter_rel(blocks).astype(BF16)
    odd = lax.axis_index("fsdp") % 2
    half = blocks[0].shape[0] // 2
    to_send = add_bf16(blocks[1], swap_core(blocks[2].astype(BF16)))
    corner = blocks[3].astype(BF16)
    mine = lax.dynamic_slice_in_dim(corner, odd * half, half, 0)
    others = lax.dynamic_slice_in_dim(corner, (1 - odd) * half, half, 0)
    passed = swap_by_core(add_bf16(mine, swap_core(others)), 2, 1)
    part = lax.dynamic_slice_in_dim(to_send, odd * half, half, 0)
    to_send = lax.dynamic_update_slice_in_dim(to_send, add_bf16(part, passed), odd * half, 0)
    return add_bf16(blocks[0], swap_by_core(to_send, 1, 2))


def place(blocks, order):
    seq_count = lax.axis_size("seq")
    stacked = jnp.stack(blocks)
    inverse = sum(
        (jnp.arange(seq_count) == order[i]).astype(jnp.int32) * i for i in range(seq_count)
    )
    picked = [lax.dynamic_index_in_dim(stacked, inverse[a], 0, False) for a in range(seq_count)]
    return jnp.concatenate(picked, axis=-1)


def split(rows, order):
    seq_count = lax.axis_size("seq")
    width = rows.shape[-1] // seq_count
    stacked = jnp.stack([rows[:, a * width : (a + 1) * width] for a in range(seq_count)])
    return [lax.dynamic_index_in_dim(stacked, order[i], 0, False) for i in range(seq_count)]


def own_part(matrix, groups):
    s, seq_count = lax.axis_index("seq"), lax.axis_size("seq")
    width = matrix.shape[1] // (groups * seq_count)
    parts = [
        lax.dynamic_slice_in_dim(matrix, (g * seq_count + s) * width, width, 1)
        for g in range(groups)
    ]
    return jnp.concatenate(parts, axis=1)


def gather_fsdp(shard):
    return lax.all_gather(shard, "fsdp", axis=0, tiled=True)


def scatter_fsdp(full):
    return lax.psum_scatter(full.astype(BF16), "fsdp", scatter_dimension=0, tiled=True)


def weighted_nt(parts, matrices):
    total = product_nt(parts[0], matrices[0])
    for part, matrix in zip(parts[1:], matrices[1:]):
        total = total + product_nt(part, matrix)
    return total


def layer_forward(hidden, shift_vec, gain_rows, text_rows, key_mask, weights, score_scale):
    qkv_part, square_parts, kv_part, up_part, down_part = weights
    seq_count = lax.axis_size("seq")
    tok_rows, model_width = hidden.shape
    width = model_width // seq_count
    head_count = H // seq_count
    order = list_order()
    relative = [lax.axis_index("seq") ^ j for j in range(seq_count)]
    self_parts = [m[:, :width] for m in square_parts]
    query_parts = [m[:, width : 2 * width] for m in square_parts]
    cross_parts = [m[:, 2 * width :] for m in square_parts]

    first_norm = norm_shift(hidden, gain_rows[0], shift_vec).astype(BF16)
    first_all = jnp.concatenate(gather_rel(first_norm), axis=0)
    triples = product(first_all, qkv_part).astype(BF16)
    heads = triples.reshape(triples.shape[0], 3, head_count, -1)
    self_mixed, self_log = attend_forward(
        heads[:, 0], heads[:, 1], heads[:, 2], None, score_scale
    )
    self_blocks = self_mixed.reshape(seq_count, tok_rows, width)
    self_tokens = place(exchange_rel([self_blocks[j] for j in range(seq_count)]), relative)
    after_self = hidden + place([product(self_tokens, m) for m in self_parts], order)

    cross_norm = layer_norm(after_self, gain_rows[1]).astype(BF16)
    queries = place([product(cross_norm, m).astype(BF16) for m in query_parts], order)
    pairs = gather_text(product(text_rows, kv_part).astype(BF16))
    pairs = place_pairs(pairs, relative)
    cross_mixed, cross_log = attend_forward(
        queries.reshape(tok_rows, H, -1), pairs[:, 0], pairs[:, 1], key_mask, score_scale
    )
    cross_tokens = cross_mixed.reshape(tok_rows, model_width)
    after_cross = after_self + place([product(cross_tokens, m) for m in cross_parts], order)

    mlp_norm = layer_norm(after_cross, gain_rows[2]).astype(BF16)
    mlp_all = jnp.concatenate(gather_rel(mlp_norm), axis=0)
    up_rows = product(mlp_all, up_part)
    activated = gelu_tanh(up_rows).astype(BF16)
    down_rows = product(activated, down_part).reshape(seq_count, tok_rows, model_width)
    result = after_cross + scatter_rel([down_rows[j] for j in range(seq_count)])
    saved = (
        hidden,
        first_all,
        heads,
        self_log,
        self_tokens,
        after_self,
        cross_norm,
        queries,
        pairs,
        cross_log,
        cross_tokens,
        after_cross,
        mlp_all,
        up_rows,
        activated,
    )
    return (result, saved)


def gather_text(pairs):
    return gather_rel(jnp.pad(pairs, ((0, pairs.shape[0] % 2), (0, 0))))


def place_pairs(blocks, order):
    head_count = H // len(blocks)
    stacked = [m.reshape(m.shape[0], 2 * head_count, -1) for m in blocks]
    halves = [place([m[:, k * m.shape[1] // 2 : (k + 1) * m.shape[1] // 2] for m in blocks], order) for k in range(2)]
    del stacked
    return jnp.stack([m.reshape(m.shape[0], H, -1) for m in halves], axis=1)


def layer_backward(
    grad_out, saved, shift_vec, gain_rows, text_rows, key_mask, weights, score_scale
):
    qkv_part, square_parts, kv_part, up_part, down_part = weights
    (
        hidden,
        first_all,
        heads,
        self_log,
        self_tokens,
        after_self,
        cross_norm,
        queries,
        pairs,
        cross_log,
        cross_tokens,
        after_cross,
        mlp_all,
        up_rows,
        activated,
    ) = saved
    seq_count = lax.axis_size("seq")
    tok_rows, model_width = hidden.shape
    width = model_width // seq_count
    head_count = H // seq_count
    order = list_order()
    relative = [lax.axis_index("seq") ^ j for j in range(seq_count)]
    self_parts = [m[:, :width] for m in square_parts]
    query_parts = [m[:, width : 2 * width] for m in square_parts]
    cross_parts = [m[:, 2 * width :] for m in square_parts]

    out_all = jnp.concatenate(gather_rel(grad_out.astype(BF16)), axis=0)
    grad_activated = product_nt(out_all, down_part)
    _, gelu_pull = jax.vjp(gelu_tanh, up_rows)
    grad_up_rows = gelu_pull(grad_activated)[0].astype(BF16)
    grad_mlp = product_nt(grad_up_rows, up_part).reshape(seq_count, tok_rows, model_width)
    grad_mlp_norm = scatter_rel([grad_mlp[j] for j in range(seq_count)])
    down_shard = scatter_fsdp(product_tn(activated, out_all))
    up_shard = scatter_fsdp(product_tn(mlp_all, grad_up_rows))

    _, mlp_pull = jax.vjp(layer_norm, after_cross, gain_rows[2])
    grad_cross_res, grad_gain_mlp = mlp_pull(grad_mlp_norm)
    grad_cross_res = grad_cross_res + grad_out
    branch = split(grad_cross_res.astype(BF16), order)
    grad_cross_w = [product_tn(cross_tokens, m) for m in branch]
    grad_cross_tok = weighted_nt(branch, cross_parts).astype(BF16)
    grad_queries, grad_keys, grad_values = attend_backward(
        queries.reshape(tok_rows, H, -1),
        pairs[:, 0],
        pairs[:, 1],
        key_mask,
        grad_cross_tok.reshape(tok_rows, H, -1),
        cross_log,
        score_scale,
    )
    text_count = grad_keys.shape[0]
    keys_split = split(grad_keys.reshape(text_count, model_width), relative)
    values_split = split(grad_values.reshape(text_count, model_width), relative)
    grad_pairs = scatter_rel(
        [jnp.concatenate(m, axis=1) for m in zip(keys_split, values_split)]
    ).astype(BF16)
    grad_pairs = grad_pairs[: text_rows.shape[0]]
    grad_text = product_nt(grad_pairs, kv_part)
    kv_shard = scatter_fsdp(product_tn(text_rows, grad_pairs))
    query_split = split(grad_queries.reshape(tok_rows, model_width), order)
    grad_query_w = [product_tn(cross_norm, m) for m in query_split]
    grad_cross_norm = weighted_nt(query_split, query_parts)

    _, cross_pull = jax.vjp(layer_norm, after_self, gain_rows[1])
    grad_self_res, grad_gain_cross = cross_pull(grad_cross_norm)
    grad_self_res = grad_self_res + grad_cross_res
    branch = split(grad_self_res.astype(BF16), order)
    grad_self_w = [product_tn(self_tokens, m) for m in branch]
    grad_self_tok = split(weighted_nt(branch, self_parts).astype(BF16), relative)
    grad_mixed = jnp.concatenate(exchange_rel(grad_self_tok), axis=0)
    grad_triples = jnp.stack(
        attend_backward(
            heads[:, 0],
            heads[:, 1],
            heads[:, 2],
            None,
            grad_mixed.reshape(grad_mixed.shape[0], head_count, -1),
            self_log,
            score_scale,
        ),
        axis=1,
    ).reshape(grad_mixed.shape[0], -1)
    square_shard = scatter_fsdp(
        unspread(
            [
                jnp.concatenate(m, axis=1).astype(BF16)
                for m in zip(grad_self_w, grad_query_w, grad_cross_w)
            ]
        )
    )
    grad_first = product_nt(grad_triples, qkv_part).reshape(seq_count, tok_rows, model_width)
    grad_first_norm = scatter_rel([grad_first[j] for j in range(seq_count)])
    qkv_shard = scatter_fsdp(product_tn(first_all, grad_triples))
    _, shift_pull = jax.vjp(norm_shift, hidden, gain_rows[0], shift_vec)
    grad_hidden, grad_gain_self, grad_shift = shift_pull(grad_first_norm)
    grad_hidden = grad_hidden + grad_self_res
    vectors = jnp.stack([grad_shift, grad_gain_self, grad_gain_cross, grad_gain_mlp])
    shards = (qkv_shard, square_shard, kv_shard, up_shard, down_shard)
    return (grad_hidden, grad_text, vectors, shards)


def gather_block(layer, qkv, query, text_kv, self_out, cross_out, up, down):
    s, seq_count = lax.axis_index("seq"), lax.axis_size("seq")
    fsdp_count = lax.axis_size("fsdp")
    squares = jnp.concatenate(
        [own_part(self_out[layer], 1), own_part(query[layer], 1), own_part(cross_out[layer], 1)],
        axis=1,
    )
    rows = down.shape[1] // seq_count
    return (
        gather_fsdp(own_part(qkv[layer], 3)),
        spread(gather_fsdp(squares)),
        gather_fsdp(own_part(text_kv[layer], 2)),
        gather_fsdp(own_part(up[layer], fsdp_count)),
        gather_fsdp(lax.dynamic_slice_in_dim(down[layer], s * rows, rows, 0)),
    )


def unpart(blocks, groups):
    seq_count = lax.axis_size("seq")
    s = lax.axis_index("seq")
    stacked = jnp.stack(blocks)
    picked = [lax.dynamic_index_in_dim(stacked, a ^ s, 0, False) for a in range(seq_count)]
    width = picked[0].shape[1] // groups
    return jnp.concatenate(
        [picked[a][:, g * width : (g + 1) * width] for g in range(groups) for a in range(seq_count)],
        axis=1,
    ).astype(F32)


def finish_block(shards):
    qkv_shard, square_shard, kv_shard, up_shard, down_shard = shards
    s, seq_count, fsdp_count = lax.axis_index("seq"), lax.axis_size("seq"), lax.axis_size("fsdp")
    qkv_blocks, square_blocks = gather_rel(qkv_shard), gather_rel(square_shard)
    kv_blocks, up_blocks, down_blocks = (
        gather_rel(kv_shard),
        gather_rel(up_shard),
        gather_rel(down_shard),
    )
    width = square_shard.shape[1] // 3
    stacked = jnp.stack(down_blocks)
    down_full = jnp.concatenate(
        [lax.dynamic_index_in_dim(stacked, a ^ s, 0, False) for a in range(seq_count)], axis=0
    ).astype(F32)
    return (
        unpart(qkv_blocks, 3),
        unpart([m[:, width : 2 * width] for m in square_blocks], 1),
        unpart(kv_blocks, 2),
        unpart([m[:, :width] for m in square_blocks], 1),
        unpart([m[:, 2 * width :] for m in square_blocks], 1),
        unpart(up_blocks, fsdp_count),
        down_full,
    )


def body(
    latents,
    skip_input,
    text_tokens,
    text_lengths,
    condition,
    cotangent,
    mod_weight,
    norm_gains,
    qkv_weight,
    query_weight,
    text_kv_weight,
    self_out_weight,
    cross_out_weight,
    up_weight,
    down_weight,
    skip_gain,
    skip_weight,
):
    seq_count, fsdp_count = lax.axis_size("seq"), lax.axis_size("fsdp")
    f = lax.axis_index("fsdp")
    _, tok_rows, model_width = latents.shape
    shard_rows = mod_weight.shape[1]
    score_scale = 1.0 / math.sqrt(model_width // H)
    text_rows = text_tokens[0]
    padded = text_rows.shape[0] + text_rows.shape[0] % 2
    key_mask = jnp.arange(padded) < text_lengths[0]
    order = list_order()

    gain_columns = jnp.concatenate(
        [norm_gains.reshape(-1, shard_rows), skip_gain.reshape(-1, shard_rows)], axis=0
    )
    gains_all = lax.all_gather(gain_columns, "fsdp", axis=0).astype(F32)
    gains = jnp.swapaxes(gains_all[:, :6], 0, 1).reshape(2, 3, model_width)
    skip_gains = gains_all[:, 6:].reshape(-1)

    cond_part = lax.all_to_all(
        condition.astype(F32).reshape(fsdp_count, shard_rows), "fsdp", 0, 0, tiled=True
    )
    silu_part = jax.nn.silu(cond_part)
    shift_terms = jnp.einsum(
        "br,lrd->bld", silu_part, mod_weight.astype(F32), precision=EXACT
    )
    shifts = jnp.sum(lax.all_to_all(shift_terms, "fsdp", 0, 0, tiled=True), axis=0)

    stacks = (
        qkv_weight,
        query_weight,
        text_kv_weight,
        self_out_weight,
        cross_out_weight,
        up_weight,
        down_weight,
    )
    first_weights = gather_block(0, *stacks)
    first_out, first_saved = layer_forward(
        latents[0].astype(F32), shifts[0], gains[0], text_rows, key_mask, first_weights, score_scale
    )
    skip_parts = spread(gather_fsdp(own_part(skip_weight, 1)))
    joined = jnp.concatenate([first_out, skip_input[0].astype(F32)], axis=-1)
    joined_norm = layer_norm(joined, skip_gains).astype(BF16)
    skip_out = place([product(joined_norm, m) for m in skip_parts], order)
    second_weights = gather_block(1, *stacks)
    final_out, second_saved = layer_forward(
        skip_out, shifts[1], gains[1], text_rows, key_mask, second_weights, score_scale
    )
    output = final_out.astype(BF16)

    grad_skip_out, text_second, vectors_second, shards_second = layer_backward(
        cotangent[0].astype(F32),
        second_saved,
        shifts[1],
        gains[1],
        text_rows,
        key_mask,
        second_weights,
        score_scale,
    )
    branch = split(grad_skip_out.astype(BF16), order)
    grad_joined_norm = weighted_nt(branch, skip_parts)
    _, joined_pull = jax.vjp(layer_norm, joined, skip_gains)
    grad_joined, grad_skip_gains = joined_pull(grad_joined_norm)
    skip_shard = scatter_fsdp(
        unspread([product_tn(joined_norm, m).astype(BF16) for m in branch])
    )
    grad_latents, text_first, vectors_first, shards_first = layer_backward(
        grad_joined[:, :model_width],
        first_saved,
        shifts[0],
        gains[0],
        text_rows,
        key_mask,
        first_weights,
        score_scale,
    )
    grad_skip = grad_joined[:, model_width:]

    vectors = jnp.concatenate(
        [vectors_first, vectors_second, grad_skip_gains.reshape(-1, model_width)], axis=0
    )
    vectors_all = lax.all_gather(vectors, ("fsdp", "seq"), axis=0)
    vectors_all = vectors_all.reshape(fsdp_count, seq_count, -1, model_width).sum(axis=1)
    shift_grads = jnp.stack([vectors_all[:, 0], vectors_all[:, 4]], axis=1)
    gain_sums = vectors_all.sum(axis=0)
    grad_norm_gains = lax.dynamic_slice_in_dim(
        jnp.stack([gain_sums[1:4], gain_sums[5:8]]), f * shard_rows, shard_rows, 2
    )
    grad_skip_gain = lax.dynamic_slice_in_dim(
        gain_sums[8:].reshape(-1), f * skip_gain.shape[0], skip_gain.shape[0], 0
    )
    grad_mod = jnp.einsum("br,bld->lrd", silu_part, shift_grads, precision=EXACT)
    grad_silu = jnp.einsum("bld,lrd->br", shift_grads, mod_weight.astype(F32), precision=EXACT)
    _, silu_pull = jax.vjp(jax.nn.silu, cond_part)
    grad_cond_part = silu_pull(grad_silu)[0]
    grad_condition = lax.all_to_all(grad_cond_part, "fsdp", 0, 0, tiled=True).reshape(1, -1)

    grad_text = lax.psum((text_first + text_second).astype(BF16), "seq").astype(F32)[None]
    first_done, second_done = finish_block(shards_first), finish_block(shards_second)
    stacked = [jnp.stack(pair) for pair in zip(first_done, second_done)]
    grad_skip_weight = unpart(gather_rel(skip_shard), 1)
    return (
        output[None],
        grad_latents[None],
        grad_skip[None],
        grad_text,
        grad_condition,
        grad_mod,
        grad_norm_gains,
        *stacked,
        grad_skip_gain,
        grad_skip_weight,
    )


def solution(mesh):
    in_specs = (
        P("fsdp", "seq", None),
        P("fsdp", "seq", None),
        P("fsdp", None, None),
        P("fsdp"),
        P("fsdp", None),
        P("fsdp", "seq", None),
        P(None, "fsdp", None),
        P(None, None, "fsdp"),
        P(None, "fsdp", None),
        P(None, "fsdp", None),
        P(None, "fsdp", None),
        P(None, "fsdp", None),
        P(None, "fsdp", None),
        P(None, "fsdp", None),
        P(None, "fsdp", None),
        P("fsdp"),
        P("fsdp", None),
    )
    out_specs = (
        P("fsdp", "seq", None),
        P("fsdp", "seq", None),
        P("fsdp", "seq", None),
        P("fsdp", None, None),
        P("fsdp", None),
        P(None, "fsdp", None),
        P(None, None, "fsdp"),
        P(None, "fsdp", None),
        P(None, "fsdp", None),
        P(None, "fsdp", None),
        P(None, "fsdp", None),
        P(None, "fsdp", None),
        P(None, "fsdp", None),
        P(None, "fsdp", None),
        P("fsdp"),
        P("fsdp", None),
    )
    return jax.shard_map(body, mesh=mesh, in_specs=in_specs, out_specs=out_specs, check_vma=False)
```

time: 3670 us -> 1610 us (0.44)
  waiting for transfers between devices: 2450 us -> 402 us
  blocking collectives: 174 us -> 14.7 us
  starting transfers between devices: 47.8 us -> 167 us
  other arithmetic: 176 us -> 231 us
  matrix products: 451 us -> 404 us
    reduce_scatter x15 -> x9, waiting for transfers between devices: 1120 us -> 0.09 us  [scatter_fsdp(): lax.psum_scatter(full.astype(BF16), 'fsdp', scatter_dimension=0, tiled=True)]
    all_gather x17 -> x12, waiting for transfers between devices: 856 us -> 0.08 us  [the longest x11 0.08 us: gather_fsdp(): return lax.all_gather(shard, 'fsdp', axis=0, tiled=True)]
    ppermute x0 -> x144, waiting for transfers between devices: none -> 393 us  [the longest x120 340 us: swap_seq(): return lax.ppermute(block, 'seq', [(i, i ^ bits) for i in range(seq_count)])]
    psum x1, waiting for transfers between devices: 332 us -> 0.01 us  [body(): lax.psum((text_first + text_second).astype(BF16), 'seq').astype(F32)[None]]
    ppermute x0 -> x144, starting transfers between devices: none -> 150 us  [the longest x120 130 us: swap_seq(): return lax.ppermute(block, 'seq', [(i, i ^ bits) for i in range(seq_count)])]
    all_to_all x11 -> x3, waiting for transfers between devices: 120 us -> 8.6 us  [the longest x1 8.6 us: body(): lax.all_to_all(shift_terms, 'fsdp', 0, 0, tiled=True)]
    all_to_all x5 -> x0, blocking collectives: 81.2 us -> none  [the longest x1 30.2 us: heads_forward(): lax.all_to_all(arrange_heads(tokens, groups), 'seq', split_axis=3, concat...]
    dynamic_slice x1 -> x78, local copies, waits for them, and re-layouts: 3.27 us -> 64.5 us  [the longest x23 24.7 us: place(): lax.dynamic_index_in_dim(stacked, inverse[a], 0, False)]
  transfers between devices with their start and end apart: 48 -> 171, of which waited for: 30 -> 64; matrix products, arithmetic and copies ran while one was open for 21% -> 50% of each run, Pallas kernels for 0% -> 0%
where the time goes in v1:
time: 1610 us; the launch traced here: 1590 us
  matrix products  404 us (25%)
  waiting for transfers between devices  402 us (25%)
  local copies, waits for them, and re-layouts  339 us (21%)
  other arithmetic  231 us (14%)
  starting transfers between devices  167 us (10%)
  between operations  37.2 us (2%)
    ppermute x120, waiting for transfers between devices, swap_seq(): return lax.ppermute(block, 'seq', [(i, i ^ bits) for i in range(seq_count)])  340 us
    ppermute x120, starting transfers between devices, swap_seq(): return lax.ppermute(block, 'seq', [(i, i ^ bits) for i in range(seq_count)])  130 us
    unnamed x758, local copies, waits for them, and re-layouts  118 us
    dot_general x36, matrix products, product_tn(): lax.dot_general(left_in, right_in, (((0,), (0,)), ((), ())), preferred_el...  96.4 us
    dot_general x36, matrix products, product_nt(): lax.dot_general(left_in, right_in, (((1,), (1,)), ((), ())), preferred_el...  93.5 us
    dot_general x36, matrix products, product(): return jnp.dot(left_in, right_in, preferred_element_type=F32)  91.1 us
    ppermute x12, waiting for transfers between devices, swap_by_core(): return lax.ppermute(block, ('seq', 'fsdp'), pairs)  53.5 us
    convert_element_type x10, other arithmetic, add_bf16(): return (left_in.astype(F32) + right_in.astype(F32)).astype(BF16)  41 us
  transfers between devices with their start and end apart: 171, of which 64 were waited for; matrix products, arithmetic and copies ran while one was open for 50% of the time, Pallas kernels for 0%

profile of v1, /device:TPU:0, one launch (start us, length us, event | category | flops | bytes accessed | tf_op | source)
XLA Modules:
  0.0 1594.7 jit_solution(4132803571558881819)
XLA Ops:
  40.2 14.7 all-gather
  172.4 11.7 collective-permute-done.9
  206.5 16.6 %maximum_select_fusion = bf16[1408,1056]{0,1:T(8,128)(2,1)S(1)} fusion(bf16[704,1056]{0,1:T(8,128)(2,1)} %collective-permute-done.10, bf16[704,1056]{0,1:T(8,128)(2,1)} %collective-permute-done.9, pred[]{:T(512)S(6)} %eq.40), kind=kLoop, calls=%fused_computation.93 | loop fusion | flops 13381632 | bytes 5947393 | tf_op jit(solution)/shard_map/jit(_where)/select_n | solution.py:153
  271.4 50.9 %collective-permute-done.17 = bf16[128,1408]{0,1:T(8,128)(2,1)S(1)} collective-permute-done((bf16[128,1408]{0,1:T(8,128)(2,1)S(1)}, bf16[128,1408]{0,1:T(8,128)(2,1)S(1)}, u32[]{:S(2)}, u32[]{:S(2)}) %collective-permute-start.17) | collective-permute-done | bytes 360480 | tf_op jit(solution)/shard_map/ppermute | solution.py:85
  323.9 10.1 fusion.523
  334.1 11.5 fusion.516
  363.4 10.3 collective-permute-done.50
  374.8 10.0 collective-permute-done.38
  545.6 9.9 collective-permute-done.43
  577.2 11.8 fusion.23
  617.3 13.0 collective-permute-done.57
  631.6 13.2 collective-permute-done.49
  693.0 10.4 fusion.111
  703.4 13.2 multiply_reduce_fusion.1
  800.3 12.4 collective-permute-done.86
  833.2 12.2 fusion.16
  1004.5 14.6 multiply_reduce_fusion
  1067.6 9.8 collective-permute-done.79
  1094.7 22.0 %collective-permute-done.139 = bf16[2816,352]{0,1:T(8,128)(2,1)} collective-permute-done((bf16[2816,352]{0,1:T(8,128)(2,1)S(1)}, bf16[2816,352]{0,1:T(8,128)(2,1)}, u32[]{:S(2)}, u32[]{:S(2)}) %collective-permute-start.139) | collective-permute-done | bytes 1982496 | tf_op jit(solution)/shard_map/ppermute | solution.py:100
  1174.1 10.5 collective-permute-done.106
  1188.3 15.3 dynamic_update_slice.10
  1236.3 11.9 collective-permute-done.116
  1303.8 14.7 dynamic_update_slice.9
  1331.7 27.1 %collective-permute-done.112 = bf16[128,704]{0,1:T(8,128)(2,1)S(1)} collective-permute-done((bf16[128,704]{0,1:T(8,128)(2,1)S(1)}, bf16[128,704]{0,1:T(8,128)(2,1)S(1)}, u32[]{:S(2)}, u32[]{:S(2)}) %collective-permute-start.112) | collective-permute-done | bytes 180256 | tf_op jit(solution)/shard_map/ppermute | solution.py:85
  (1707 shorter events, 1199.5 us)
Async XLA Ops:
  16.7 233.9 %all-gather.26.cloned.1.call-start = ((), (), s32[]{:S(2)}) async-start(), calls=%async_computation.18 | async-start | bytes 2433024 | tf_op jit(solution)/shard_map/all_gather | solution.py:209
  17.7 237.7 %all-gather.30.cloned.1.call-start = ((), (), s32[]{:S(2)}) async-start(), calls=%async_computation.20 | async-start | bytes 3649536 | tf_op jit(solution)/shard_map/all_gather | solution.py:209
  19.9 304.0 %all-gather.24.cloned.1.call-start = ((), (), s32[]{:S(2)}) async-start(), calls=%async_computation.17 | async-start | bytes 4866048 | tf_op jit(solution)/shard_map/all_gather | solution.py:209
  24.8 309.3 %all-gather.36.cloned.1.call-start = ((), (), s32[]{:S(2)}) async-start(), calls=%async_computation.31 | async-start | bytes 4866048 | tf_op jit(solution)/shard_map/all_gather | solution.py:209
  29.7 320.1 %all-gather.32.cloned.1.call-start = ((), (), s32[]{:S(2)}) async-start(), calls=%async_computation.21 | async-start | bytes 1769472 | tf_op jit(solution)/shard_map/all_gather | solution.py:209
  30.6 429.0 %all-gather.28.cloned.1.call-start = ((), (), s32[]{:S(2)}) async-start(), calls=%async_computation.19 | async-start | bytes 3649536 | tf_op jit(solution)/shard_map/all_gather | solution.py:209
  31.6 536.2 %all-gather.34.cloned.1.call-start = ((), (), s32[]{:S(2)}) async-start(), calls=%async_computation.22 | async-start | bytes 4866048 | tf_op jit(solution)/shard_map/all_gather | solution.py:209
  61.9 515.3 %all-gather.38.cloned.1.call-start = ((), (), s32[]{:S(2)}) async-start(), calls=%async_computation.32 | async-start | bytes 4866048 | tf_op jit(solution)/shard_map/all_gather | solution.py:209
  76.9 1150.1 %reduce-scatter.40.cloned.1.call-start = ((), (), s32[]{:S(2)}) async-start(), calls=%async_computation.37 | async-start | bytes 1769472
  198.1 164.7 %collective-permute-start.51 = (bf16[256,1408]{1,0:T(8,128)(2,1)S(1)}, bf16[256,1408]{1,0:T(8,128)(2,1)}, u32[]{:S(2)}, u32[]{:S(2)}) collective-permute-start(bf16[256,1408]{1,0:T(8,128)(2,1)S(1)} %bitcast.1261), channel_id=1, source_target_pairs={{0,16},{8,24},{16,0},{24,8},{1,17},{9,25},{17,1},{25,9},{2,18},{10... | collective-permute-start | bytes 2162696 | tf_op jit(solution)/shard_map/ppermute | solution.py:85
  260.8 133.6 %collective-permute-start.34 = (bf16[1408,1056]{0,1:T(8,128)(2,1)}, bf16[1408,1056]{0,1:T(8,128)(2,1)}, u32[]{:S(2)}, u32[]{:S(2)}) collective-permute-start(bf16[1408,1056]{0,1:T(8,128)(2,1)} %copy.304), channel_id=1, source_target_pairs={{0,8},{1,17},{2,10},{3,19},{4,12},{5,21},{6,14},{7,23},{8,0},{9,25... | collective-permute-start | bytes 8921096 | tf_op jit(solution)/shard_map/ppermute | solution.py:100
  420.5 121.5 %collective-permute-start.52 = (bf16[128,1408]{1,0:T(8,128)(2,1)}, bf16[128,1408]{1,0:T(8,128)(2,1)}, u32[]{:S(2)}, u32[]{:S(2)}) collective-permute-start(bf16[128,1408]{1,0:T(8,128)(2,1)} %slice.1774), channel_id=1, source_target_pairs={{0,8},{8,0},{16,24},{24,16},{1,9},{9,1},{17,25},{25,17},{2,10},{10... | collective-permute-start | bytes 1081352 | tf_op jit(solution)/shard_map/ppermute | solution.py:85
  880.0 379.5 %all-reduce.4.cloned.1.call-start = ((), (), s32[]{:S(2)}) async-start(), calls=%async_computation.23 | async-start | bytes 1376256 | tf_op jit(solution)/shard_map/psum | solution.py:570
  939.6 342.0 %reduce-scatter.22.cloned.1.call-start = ((), (), s32[]{:S(2)}) async-start(), calls=%async_computation.25 | async-start | bytes 3649536 | tf_op jit(solution)/shard_map/reduce_scatter | solution.py:213
  947.8 373.9 %reduce-scatter.38.cloned.1.call-start = ((), (), s32[]{:S(2)}) async-start(), calls=%async_computation.36 | async-start | bytes 1769472
  952.2 413.5 %reduce-scatter.30.cloned.1.call-start = ((), (), s32[]{:S(2)}) async-start(), calls=%async_computation.29 | async-start | bytes 4866048 | tf_op jit(solution)/shard_map/reduce_scatter | solution.py:213
  962.1 404.3 %reduce-scatter.26.cloned.1.call-start = ((), (), s32[]{:S(2)}) async-start(), calls=%async_computation.27 | async-start | bytes 4866048 | tf_op jit(solution)/shard_map/reduce_scatter | solution.py:213
  972.4 423.2 %all-gather.40.cloned.1.call-start = ((), (), s32[]{:S(2)}) async-start(), calls=%async_computation.33 | async-start | bytes 2973696 | tf_op jit(solution)/shard_map/all_gather | solution.py:554
  1087.8 335.5 %reduce-scatter.32.cloned.1.call-start = ((), (), s32[]{:S(2)}) async-start(), calls=%async_computation.30 | async-start | bytes 2433024 | tf_op jit(solution)/shard_map/reduce_scatter | solution.py:213
  1124.6 310.8 %reduce-scatter.20.cloned.1.call-start = ((), (), s32[]{:S(2)}) async-start(), calls=%async_computation.24 | async-start | bytes 3649536 | tf_op jit(solution)/shard_map/reduce_scatter | solution.py:213
  1133.7 329.4 %reduce-scatter.24.cloned.1.call-start = ((), (), s32[]{:S(2)}) async-start(), calls=%async_computation.26 | async-start | bytes 4866048 | tf_op jit(solution)/shard_map/reduce_scatter | solution.py:213
  1143.4 328.8 %reduce-scatter.28.cloned.1.call-start = ((), (), s32[]{:S(2)}) async-start(), calls=%async_computation.28 | async-start | bytes 4866048 | tf_op jit(solution)/shard_map/reduce_scatter | solution.py:213
  1170.8 346.5 %reduce-scatter.36.cloned.1.call-start = ((), (), s32[]{:S(2)}) async-start(), calls=%async_computation.35 | async-start | bytes 3649536 | tf_op jit(solution)/shard_map/reduce_scatter | solution.py:213
  1402.6 143.0 %reduce-scatter.34.cloned.1.call-start = ((), (), s32[]{:S(2)}) async-start(), calls=%async_computation.34 | async-start | bytes 3649536 | tf_op jit(solution)/shard_map/reduce_scatter | solution.py:213
  (489 other events, 6694.4 us)
Sparse Core Ops, SparseCore 0:
  10.6 27.7 all-gather.21
  40.6 40.6 all-gather.19
  83.5 37.8 all-gather.17
  123.4 28.4 all-gather.25
  154.0 38.5 all-gather.29
  194.7 47.2 all-gather.23
  244.3 47.1 all-gather.35
  293.1 23.7 all-gather.31
  318.6 38.6 all-gather.27
  358.7 47.2 all-gather.33
  407.7 47.1 all-gather.37
  880.1 31.9 reduce-scatter.39
  939.7 44.3 all-reduce.3
  986.4 41.2 reduce-scatter.21
  1030.4 32.7 reduce-scatter.37
  1065.4 49.4 reduce-scatter.29
  1117.7 49.3 reduce-scatter.25
  1169.8 58.2 all-gather.39
  1230.4 35.0 reduce-scatter.31
  1267.6 39.9 reduce-scatter.19
  1310.6 50.0 reduce-scatter.23
  1363.5 49.5 reduce-scatter.27
  1415.5 39.4 reduce-scatter.35
  1457.2 40.0 reduce-scatter.33

commit v2 on v1

v2 whole, which is shorter than its diff:
```python
import functools
import math

import jax
import jax.numpy as jnp
from jax import lax
from jax.experimental import pallas as pl
from jax.experimental.pallas import tpu as pltpu
from jax.sharding import PartitionSpec as P

H = 16
NORM_EPSILON = 1e-06
BF16 = jnp.bfloat16
F32 = jnp.float32
LOG2_E = 1.4426950408889634
VMEM_LIMIT = 56 * 1024 * 1024


def dot_nn(a, b):
    return lax.dot_general(a, b, (((1,), (0,)), ((), ())), preferred_element_type=F32)


def dot_nt(a, b):
    return lax.dot_general(a, b, (((1,), (1,)), ((), ())), preferred_element_type=F32)


def dot_tn(a, b):
    return lax.dot_general(a, b, (((0,), (0,)), ((), ())), preferred_element_type=F32)


def whole(count):
    return [pl.BlockSpec(memory_space=pltpu.VMEM)] * count


def call(kernel, outs, scratch, cost, *operands, scalars=None):
    specs = whole(len(operands))
    if scalars is not None:
        specs = [pl.BlockSpec(memory_space=pltpu.SMEM)] + specs
        operands = (scalars,) + operands
    return pl.pallas_call(
        kernel,
        out_shape=tuple(jax.ShapeDtypeStruct(s, d) for s, d in outs),
        in_specs=specs,
        out_specs=tuple(whole(len(outs))),
        scratch_shapes=scratch,
        compiler_params=pltpu.CompilerParams(vmem_limit_bytes=VMEM_LIMIT),
        cost_estimate=pl.CostEstimate(flops=cost[0], bytes_accessed=cost[1], transcendentals=0),
    )(*operands)


def self_forward_kernel(width, head_size, step, triples_ref, mixed_ref):
    rows = triples_ref.shape[0]
    head_count = width // head_size
    factor = LOG2_E / math.sqrt(head_size)

    def block(i, carry):
        at = pl.ds(pl.multiple_of(i * step, step), step)
        for h in range(head_count):
            low = h * head_size
            q = triples_ref[at, low : low + head_size]
            k = triples_ref[:, width + low : width + low + head_size]
            v = triples_ref[:, 2 * width + low : 2 * width + low + head_size]
            scores = dot_nt(q, k)
            top = jnp.max(scores, axis=1, keepdims=True)
            weights = jnp.exp2((scores - top) * factor)
            total = jnp.sum(weights, axis=1, keepdims=True)
            mixed = dot_nn(weights.astype(BF16), v) * (1.0 / total)
            mixed_ref[at, low : low + head_size] = mixed.astype(BF16)
        return carry

    lax.fori_loop(0, rows // step, block, 0)


def self_forward(triples, head_size):
    rows, width = triples.shape[0], triples.shape[1] // 3
    (mixed,) = call(
        functools.partial(self_forward_kernel, width, head_size, 256),
        [((rows, width), BF16)],
        [],
        (4 * rows * rows * width, 8 * rows * width),
        triples,
    )
    return mixed


def attention_back(q, k, v, grad, valid, head_size):
    factor = LOG2_E / math.sqrt(head_size)
    scores = dot_nt(k, q)
    if valid is not None:
        scores = jnp.where(valid, scores, -1e30)
    top = jnp.max(scores, axis=0, keepdims=True)
    weights = jnp.exp2((scores - top) * factor)
    weights = weights * (1.0 / jnp.sum(weights, axis=0, keepdims=True))
    grad_weights = dot_nt(v, grad)
    delta = jnp.sum(grad_weights * weights, axis=0, keepdims=True)
    grad_scores = (weights * (grad_weights - delta)).astype(BF16)
    scale = 1.0 / math.sqrt(head_size)
    return (
        dot_tn(grad_scores, k) * scale,
        dot_nn(grad_scores, q) * scale,
        dot_nn(weights.astype(BF16), grad),
    )


def self_backward_kernel(width, head_size, step, triples_ref, *refs):
    grad_refs, (out_ref, keys_ref, values_ref) = refs[:-3], refs[-3:]
    rows = triples_ref.shape[0]
    part = grad_refs[0].shape[0]
    for h in range(width // head_size):
        low = h * head_size
        k = triples_ref[:, width + low : width + low + head_size]
        v = triples_ref[:, 2 * width + low : 2 * width + low + head_size]
        for i in range(rows // step):
            at = slice(i * step, (i + 1) * step)
            inside = (i * step) % part
            q = triples_ref[at, low : low + head_size]
            grad = grad_refs[i * step // part][inside : inside + step, low : low + head_size]
            grad_q, grad_k, grad_v = attention_back(q, k, v, grad, None, head_size)
            out_ref[at, low : low + head_size] = grad_q.astype(BF16)
            if i == 0:
                keys_ref[...] = grad_k
                values_ref[...] = grad_v
            else:
                keys_ref[...] += grad_k
                values_ref[...] += grad_v
        out_ref[:, width + low : width + low + head_size] = keys_ref[...].astype(BF16)
        out_ref[:, 2 * width + low : 2 * width + low + head_size] = values_ref[...].astype(BF16)


def self_backward(triples, grads, head_size):
    rows, width = triples.shape[0], triples.shape[1] // 3
    step = min(256, grads[0].shape[0])
    (out,) = call(
        functools.partial(self_backward_kernel, width, head_size, step),
        [((rows, 3 * width), BF16)],
        [pltpu.VMEM((rows, head_size), F32), pltpu.VMEM((rows, head_size), F32)],
        (10 * rows * rows * width, 16 * rows * width),
        triples,
        *grads,
    )
    return out


def norm_stats(values):
    mean = jnp.mean(values, axis=1, keepdims=True)
    centered = values - mean
    var = jnp.mean(centered * centered, axis=1, keepdims=True)
    scale = lax.rsqrt(var + NORM_EPSILON)
    return centered * scale, scale


def norm_back(values, gain, grad):
    unit, scale = norm_stats(values)
    grad_unit = grad * gain
    inner = jnp.mean(grad_unit * unit, axis=1, keepdims=True)
    grad_values = scale * (grad_unit - jnp.mean(grad_unit, axis=1, keepdims=True) - unit * inner)
    return grad_values, jnp.sum(grad * unit, axis=0, keepdims=True)


def fill_corner(count, matrix_refs, scalars_ref, corner_ref):
    if len(matrix_refs) == count:
        return list(matrix_refs)
    odd = scalars_ref[2 * count]
    half = matrix_refs[-1].shape[0]
    corner_ref[pl.ds(pl.multiple_of(odd * half, half), half), :] = matrix_refs[-2][...]
    corner_ref[pl.ds(pl.multiple_of((1 - odd) * half, half), half), :] = matrix_refs[-1][...]
    return list(matrix_refs[:-2]) + [corner_ref]


def middle_forward_kernel(count, parts, head_size, scalars_ref, *refs):
    mixed_refs, refs = refs[:count], refs[count:]
    matrix_refs, refs = refs[:parts], refs[parts:]
    pair_refs, refs = refs[:count], refs[count:]
    hidden_ref, gains_ref = refs[:2]
    (self_ref, after_self_ref, norm_ref, queries_ref, cross_ref, after_cross_ref, mlp_ref) = refs[2:9]
    wide_ref, narrow_ref, corner_ref = refs[9:]
    width = mixed_refs[0].shape[1]
    matrices = fill_corner(count, matrix_refs, scalars_ref, corner_ref)
    order = [scalars_ref[i] for i in range(count)]
    relative = [scalars_ref[count + j] for j in range(count)]
    length = scalars_ref[2 * count + 1]
    spans = [slice(a * width, (a + 1) * width) for a in range(count)]

    for j in range(count):
        narrow_ref[relative[j]] = mixed_refs[j][...]
    for a in range(count):
        self_ref[:, spans[a]] = narrow_ref[a]
    tokens = self_ref[...]
    for i in range(count):
        wide_ref[order[i]] = dot_nn(tokens, matrices[i][:, :width])
    for a in range(count):
        after_self_ref[:, spans[a]] = hidden_ref[:, spans[a]] + wide_ref[a]
    normed = (norm_stats(after_self_ref[...])[0] * gains_ref[1:2, :]).astype(BF16)
    norm_ref[...] = normed
    for i in range(count):
        found = dot_nn(normed, matrices[i][:, width : 2 * width])
        queries_ref[order[i] ^ relative[0]] = found.astype(BF16)

    factor = LOG2_E / math.sqrt(head_size)
    valid = lax.broadcasted_iota(jnp.int32, (1, pair_refs[0].shape[0]), 1) < length
    for j in range(count):
        for h in range(width // head_size):
            at = slice(h * head_size, (h + 1) * head_size)
            values_at = slice(width + h * head_size, width + (h + 1) * head_size)
            scores = dot_nt(queries_ref[j, :, at], pair_refs[j][:, at])
            scores = jnp.where(valid, scores, -1e30)
            top = jnp.max(scores, axis=1, keepdims=True)
            weights = jnp.exp2((scores - top) * factor)
            total = jnp.sum(weights, axis=1, keepdims=True)
            mixed = dot_nn(weights.astype(BF16), pair_refs[j][:, values_at]) * (1.0 / total)
            narrow_ref[relative[j], :, at] = mixed.astype(BF16)
    for a in range(count):
        cross_ref[:, spans[a]] = narrow_ref[a]
    tokens = cross_ref[...]
    for i in range(count):
        wide_ref[order[i]] = dot_nn(tokens, matrices[i][:, 2 * width :])
    for a in range(count):
        after_cross_ref[:, spans[a]] = after_self_ref[:, spans[a]] + wide_ref[a]
    mlp_ref[...] = (norm_stats(after_cross_ref[...])[0] * gains_ref[2:3, :]).astype(BF16)


def corner_scratch(count, matrices):
    rows, columns = matrices[0].shape
    return pltpu.VMEM((rows, columns) if len(matrices) > count else (16, 128), BF16)


def middle_forward(scalars, mixed, matrices, pairs, hidden, gains, head_size):
    count = len(mixed)
    rows, columns = hidden.shape
    width = columns // count
    return call(
        functools.partial(middle_forward_kernel, count, len(matrices), head_size),
        [
            ((rows, columns), BF16),
            ((rows, columns), F32),
            ((rows, columns), BF16),
            ((count, rows, width), BF16),
            ((rows, columns), BF16),
            ((rows, columns), F32),
            ((rows, columns), BF16),
        ],
        [
            pltpu.VMEM((count, rows, width), F32),
            pltpu.VMEM((count, rows, width), BF16),
            corner_scratch(count, matrices),
        ],
        (6 * rows * columns * columns, 6 * columns * columns + 24 * rows * columns),
        *mixed,
        *matrices,
        *pairs,
        hidden,
        gains,
        scalars=scalars,
    )


def middle_backward_kernel(count, parts, head_size, scalars_ref, *refs):
    matrix_refs, refs = refs[:parts], refs[parts:]
    pair_refs, refs = refs[:count], refs[count:]
    grad_norm_ref, grad_out_ref, after_cross_ref, after_self_ref, queries_ref, gains_ref = refs[:6]
    out_ref, self_branch_ref, query_branch_ref, cross_branch_ref, gain_ref = refs[6:11]
    pair_grad_refs, refs = refs[11 : 11 + count], refs[11 + count :]
    mixed_grad_refs, refs = refs[:count], refs[count:]
    wide_ref, narrow_ref, query_ref, corner_ref = refs
    width = queries_ref.shape[2]
    matrices = fill_corner(count, matrix_refs, scalars_ref, corner_ref)
    order = [scalars_ref[i] for i in range(count)]
    relative = [scalars_ref[count + j] for j in range(count)]
    length = scalars_ref[2 * count + 1]
    spans = [slice(a * width, (a + 1) * width) for a in range(count)]

    def back(branch_ref, columns):
        total = dot_nt(branch_ref[0], matrices[0][:, columns])
        for i in range(1, count):
            total = total + dot_nt(branch_ref[i], matrices[i][:, columns])
        return total

    def divide(values):
        for a in range(count):
            narrow_ref[a] = values[:, spans[a]].astype(BF16)

    grad, grad_gain = norm_back(after_cross_ref[...], gains_ref[2:3, :], grad_norm_ref[...])
    gain_ref[1:2, :] = grad_gain
    wide_ref[...] = grad + grad_out_ref[...]
    divide(wide_ref[...])
    for i in range(count):
        cross_branch_ref[i] = narrow_ref[order[i]]
    divide(back(cross_branch_ref, slice(2 * width, 3 * width)))

    valid = lax.broadcasted_iota(jnp.int32, (pair_refs[0].shape[0], 1), 0) < length
    for j in range(count):
        for h in range(width // head_size):
            at = slice(h * head_size, (h + 1) * head_size)
            values_at = slice(width + h * head_size, width + (h + 1) * head_size)
            grad_q, grad_k, grad_v = attention_back(
                queries_ref[j, :, at],
                pair_refs[j][:, at],
                pair_refs[j][:, values_at],
                narrow_ref[relative[j], :, at],
                valid,
                head_size,
            )
            query_ref[j, :, at] = grad_q.astype(BF16)
            pair_grad_refs[j][:, at] = grad_k.astype(BF16)
            pair_grad_refs[j][:, values_at] = grad_v.astype(BF16)
    for i in range(count):
        query_branch_ref[i] = query_ref[order[i] ^ relative[0]]
    grad, grad_gain = norm_back(
        after_self_ref[...], gains_ref[1:2, :], back(query_branch_ref, slice(width, 2 * width))
    )
    gain_ref[0:1, :] = grad_gain
    out_ref[...] = grad + wide_ref[...]
    divide(out_ref[...])
    for i in range(count):
        self_branch_ref[i] = narrow_ref[order[i]]
    divide(back(self_branch_ref, slice(0, width)))
    for j in range(count):
        mixed_grad_refs[j][...] = narrow_ref[relative[j]]


def middle_backward(
    scalars, matrices, pairs, grad_norm, grad_out, after_cross, after_self, queries, gains, head_size
):
    count = len(pairs)
    rows, columns = grad_out.shape
    width = columns // count
    branch = ((count, rows, width), BF16)
    found = call(
        functools.partial(middle_backward_kernel, count, len(matrices), head_size),
        [((rows, columns), F32), branch, branch, branch, ((2, columns), F32)]
        + [(m.shape, BF16) for m in pairs]
        + [((rows, width), BF16)] * count,
        [
            pltpu.VMEM((rows, columns), F32),
            pltpu.VMEM((count, rows, width), BF16),
            pltpu.VMEM((count, rows, width), BF16),
            corner_scratch(count, matrices),
        ],
        (10 * rows * columns * columns, 6 * columns * columns + 36 * rows * columns),
        *matrices,
        *pairs,
        grad_norm,
        grad_out,
        after_cross,
        after_self,
        queries,
        gains,
        scalars=scalars,
    )
    return found[:5] + (found[5 : 5 + count], found[5 + count :])


def outer_kernel(groups, *refs):
    rows_refs, branch_refs, out_refs = refs[:groups], refs[groups : 2 * groups], refs[2 * groups :]
    width = branch_refs[0].shape[2]
    for g in range(groups):
        turned = rows_refs[g][...].T
        for i, out_ref in enumerate(out_refs):
            out_ref[:, g * width : (g + 1) * width] = dot_nn(turned, branch_refs[g][i]).astype(BF16)


def outer(rows, branches):
    count, tokens, width = branches[0].shape
    groups, columns = len(rows), rows[0].shape[1]
    return call(
        functools.partial(outer_kernel, groups),
        [((columns, groups * width), BF16)] * count,
        [],
        (2 * groups * count * tokens * columns * width, 2 * groups * count * columns * width),
        *rows,
        *branches,
    )


def joined_stats(first, second):
    count = first.shape[1] + second.shape[1]
    mean = (jnp.sum(first, axis=1, keepdims=True) + jnp.sum(second, axis=1, keepdims=True)) / count
    first, second = first - mean, second - mean
    var = (
        jnp.sum(first * first, axis=1, keepdims=True)
        + jnp.sum(second * second, axis=1, keepdims=True)
    ) / count
    scale = lax.rsqrt(var + NORM_EPSILON)
    return first * scale, second * scale, scale


def skip_forward_kernel(count, parts, scalars_ref, *refs):
    matrix_refs, refs = refs[:parts], refs[parts:]
    first_ref, second_ref, gains_ref, joined_ref, out_ref, wide_ref, corner_ref = refs
    columns = first_ref.shape[1]
    width = columns // count
    matrices = fill_corner(count, matrix_refs, scalars_ref, corner_ref)
    first, second, _ = joined_stats(first_ref[...], second_ref[...].astype(F32))
    joined_ref[:, :columns] = (first * gains_ref[0:1, :]).astype(BF16)
    joined_ref[:, columns:] = (second * gains_ref[1:2, :]).astype(BF16)
    joined = joined_ref[...]
    for i in range(count):
        wide_ref[scalars_ref[i]] = dot_nn(joined, matrices[i][...])
    for a in range(count):
        out_ref[:, a * width : (a + 1) * width] = wide_ref[a]


def skip_forward(scalars, matrices, first, second, gains):
    rows, columns = first.shape
    count = columns // matrices[0].shape[1]
    return call(
        functools.partial(skip_forward_kernel, count, len(matrices)),
        [((rows, 2 * columns), BF16), ((rows, columns), F32)],
        [pltpu.VMEM((count, rows, columns // count), F32), corner_scratch(count, matrices)],
        (4 * rows * columns * columns, 4 * columns * columns + 16 * rows * columns),
        *matrices,
        first,
        second,
        gains,
        scalars=scalars,
    )


def skip_backward_kernel(count, parts, scalars_ref, *refs):
    matrix_refs, refs = refs[:parts], refs[parts:]
    first_ref, second_ref, gains_ref, grad_ref = refs[:4]
    branch_ref, grad_first_ref, grad_second_ref, gain_ref, narrow_ref, corner_ref = refs[4:]
    columns = first_ref.shape[1]
    width = columns // count
    matrices = fill_corner(count, matrix_refs, scalars_ref, corner_ref)
    for a in range(count):
        narrow_ref[a] = grad_ref[:, a * width : (a + 1) * width].astype(BF16)
    for i in range(count):
        branch_ref[i] = narrow_ref[scalars_ref[i]]

    def back(at):
        total = dot_nt(branch_ref[0], matrices[0][at, :])
        for i in range(1, count):
            total = total + dot_nt(branch_ref[i], matrices[i][at, :])
        return total

    grad_first_ref[...] = back(slice(0, columns))
    grad_second_ref[...] = back(slice(columns, 2 * columns))
    first, second, scale = joined_stats(first_ref[...], second_ref[...].astype(F32))
    gain_ref[0:1, :] = jnp.sum(grad_first_ref[...] * first, axis=0, keepdims=True)
    gain_ref[1:2, :] = jnp.sum(grad_second_ref[...] * second, axis=0, keepdims=True)
    grad_first = grad_first_ref[...] * gains_ref[0:1, :]
    grad_second = grad_second_ref[...] * gains_ref[1:2, :]
    mean = (
        jnp.sum(grad_first, axis=1, keepdims=True) + jnp.sum(grad_second, axis=1, keepdims=True)
    ) / (2 * columns)
    inner = (
        jnp.sum(grad_first * first, axis=1, keepdims=True)
        + jnp.sum(grad_second * second, axis=1, keepdims=True)
    ) / (2 * columns)
    grad_first_ref[...] = scale * (grad_first - mean - first * inner)
    grad_second_ref[...] = scale * (grad_second - mean - second * inner)


def skip_backward(scalars, matrices, first, second, gains, grad):
    rows, columns = first.shape
    count = columns // matrices[0].shape[1]
    narrow = (count, rows, columns // count)
    return call(
        functools.partial(skip_backward_kernel, count, len(matrices)),
        [
            (narrow, BF16),
            ((rows, columns), F32),
            ((rows, columns), F32),
            ((2, columns), F32),
        ],
        [pltpu.VMEM(narrow, BF16), corner_scratch(count, matrices)],
        (4 * rows * columns * columns, 4 * columns * columns + 20 * rows * columns),
        *matrices,
        first,
        second,
        gains,
        grad,
        scalars=scalars,
    )


def settle_kernel(count, parts, groups, pieces, scalars_ref, *refs):
    block_refs, refs = refs[:parts], refs[parts:]
    out_refs, stack_ref = refs[-pieces - 1 : -1], refs[-1]
    columns = stack_ref.shape[2] // pieces
    width = columns // groups
    for j in range(count):
        owner = scalars_ref[count + j]
        if j == count - 1 and parts > count:
            cut = block_refs[j].shape[0]
            stack_ref[owner, :cut] = block_refs[j][...]
            stack_ref[owner, cut:] = block_refs[j + 1][...]
        else:
            stack_ref[owner] = block_refs[j][...]
    for p in range(pieces):
        for g in range(groups):
            for a in range(count):
                low = p * columns + g * width
                at = (g * count + a) * width
                out_refs[p][0, :, at : at + width] = stack_ref[a, :, low : low + width].astype(F32)


def settle_rows_kernel(count, parts, scalars_ref, *refs):
    block_refs, out_ref = refs[:parts], refs[-1]
    rows = block_refs[0].shape[0]
    for j in range(count):
        low = pl.multiple_of(scalars_ref[count + j] * rows, rows)
        if j == count - 1 and parts > count:
            cut = block_refs[j].shape[0]
            out_ref[0, pl.ds(low, cut), :] = block_refs[j][...].astype(F32)
            out_ref[0, pl.ds(low + cut, rows - cut), :] = block_refs[j + 1][...].astype(F32)
        else:
            out_ref[0, pl.ds(low, rows), :] = block_refs[j][...].astype(F32)


def settle_call(kernel, scalars, blocks, shape, pieces, layer, layer_count, before, scratch):
    held = [] if before is None else list(before)
    inputs = whole(len(blocks)) + [pl.BlockSpec(memory_space=pl.ANY)] * len(held)
    found = pl.pallas_call(
        kernel,
        grid=(1,),
        out_shape=[jax.ShapeDtypeStruct((layer_count,) + shape, F32)] * pieces,
        in_specs=[pl.BlockSpec(memory_space=pltpu.SMEM)] + inputs,
        out_specs=[pl.BlockSpec((1,) + shape, lambda i: (layer, 0, 0))] * pieces,
        scratch_shapes=scratch,
        input_output_aliases={1 + len(blocks) + i: i for i in range(len(held))},
        compiler_params=pltpu.CompilerParams(vmem_limit_bytes=VMEM_LIMIT),
        cost_estimate=pl.CostEstimate(
            flops=0, bytes_accessed=6 * pieces * shape[0] * shape[1], transcendentals=0
        ),
    )(scalars, *blocks, *held)
    return list(found)


def settle(scalars, blocks, groups, pieces, layer, layer_count, before=None):
    count = lax.axis_size("seq")
    rows, columns = blocks[0].shape
    return settle_call(
        functools.partial(settle_kernel, count, len(blocks), groups, pieces),
        scalars,
        blocks,
        (rows, count * columns // pieces),
        pieces,
        layer,
        layer_count,
        before,
        [pltpu.VMEM((count, rows, columns), BF16)],
    )


def settle_rows(scalars, blocks, layer, layer_count, before=None):
    count = lax.axis_size("seq")
    rows, columns = blocks[0].shape
    return settle_call(
        functools.partial(settle_rows_kernel, count, len(blocks)),
        scalars,
        blocks,
        (count * rows, columns),
        1,
        layer,
        layer_count,
        before,
        [],
    )


EXACT = lax.Precision.HIGHEST


def layer_norm(values, gain_vec):
    row_mean = jnp.mean(values, axis=-1, keepdims=True)
    centered = values - row_mean
    row_var = jnp.mean(centered * centered, axis=-1, keepdims=True)
    return centered * lax.rsqrt(row_var + NORM_EPSILON) * gain_vec


def norm_shift(values, gain_vec, shift_vec):
    return layer_norm(values, gain_vec) + shift_vec


def gelu_tanh(values):
    return jax.nn.gelu(values, approximate=True)


def swap_seq(block, bits):
    seq_count = lax.axis_size("seq")
    return lax.ppermute(block, "seq", [(i, i ^ bits) for i in range(seq_count)])


def swap_fsdp(block, bits):
    fsdp_count = lax.axis_size("fsdp")
    return lax.ppermute(block, "fsdp", [(i, i ^ bits) for i in range(fsdp_count)])


def swap_core(block):
    return swap_fsdp(block, 1)


def swap_by_core(block, even_bits, odd_bits):
    seq_count, fsdp_count = lax.axis_size("seq"), lax.axis_size("fsdp")
    pairs = []
    for s in range(seq_count):
        for f in range(fsdp_count):
            other = s ^ (odd_bits if f % 2 else even_bits)
            pairs.append((s * fsdp_count + f, other * fsdp_count + f))
    return lax.ppermute(block, ("seq", "fsdp"), pairs)


def gather_parts(block):
    seq_count = lax.axis_size("seq")
    if seq_count != 4:
        return [block] + [swap_seq(block, j) for j in range(1, seq_count)]
    cut = block.shape[0] // 32 * 16
    from_x, from_y = swap_seq(block, 1), swap_seq(block, 2)
    return [block, from_x, from_y, swap_seq(from_y[:cut], 1), swap_seq(from_x[cut:], 2)]


def gather_rel(block):
    parts = gather_parts(block)
    if len(parts) == 5:
        parts = parts[:3] + [jnp.concatenate(parts[3:], axis=0)]
    return parts


def add_bf16(left_in, right_in):
    return (left_in.astype(F32) + right_in.astype(F32)).astype(BF16)


def scatter_rel(blocks):
    seq_count = lax.axis_size("seq")
    if seq_count != 4:
        total = blocks[0].astype(F32)
        for j in range(1, seq_count):
            total = total + swap_seq(blocks[j].astype(BF16), j).astype(F32)
        return total
    cut = blocks[0].shape[0] // 32 * 16
    corner = blocks[3].astype(BF16)
    by_x, by_y = swap_seq(corner[:cut], 1), swap_seq(corner[cut:], 2)
    to_y = jnp.concatenate([add_bf16(blocks[2][:cut], by_x), blocks[2][cut:].astype(BF16)])
    to_x = jnp.concatenate([blocks[1][:cut].astype(BF16), add_bf16(blocks[1][cut:], by_y)])
    return blocks[0].astype(F32) + swap_seq(to_x, 1).astype(F32) + swap_seq(to_y, 2).astype(F32)


def exchange_rel(blocks):
    return [blocks[0]] + [swap_seq(blocks[j], j) for j in range(1, len(blocks))]


def list_order():
    s, seq_count = lax.axis_index("seq"), lax.axis_size("seq")
    if seq_count != 4:
        return [s ^ j for j in range(seq_count)]
    odd = lax.axis_index("fsdp") % 2
    return [s, s ^ (1 + odd), s ^ (2 - odd), s ^ 3]


def spread(block):
    seq_count = lax.axis_size("seq")
    if seq_count != 4:
        return [block] + [swap_seq(block, j) for j in range(1, seq_count)]
    odd = lax.axis_index("fsdp") % 2
    half = block.shape[0] // 2
    first = swap_by_core(block, 1, 2)
    part = swap_by_core(lax.dynamic_slice_in_dim(first, odd * half, half, 0), 2, 1)
    return [block, first, swap_core(first), part, swap_core(part)]


def unspread(blocks):
    seq_count = lax.axis_size("seq")
    if seq_count != 4:
        return scatter_rel(blocks).astype(BF16)
    odd = lax.axis_index("fsdp") % 2
    half = blocks[0].shape[0] // 2
    mine = lax.dynamic_slice_in_dim(blocks[3], odd * half, half, 0)
    others = lax.dynamic_slice_in_dim(blocks[3], (1 - odd) * half, half, 0)
    passed = swap_by_core(add_bf16(mine, swap_core(others)), 2, 1).astype(F32)
    from_core = swap_core(blocks[2])
    to_send = jnp.concatenate(
        [
            (
                blocks[1][k * half : (k + 1) * half].astype(F32)
                + from_core[k * half : (k + 1) * half].astype(F32)
                + jnp.where(odd == k, passed, 0.0)
            ).astype(BF16)
            for k in range(2)
        ]
    )
    return add_bf16(blocks[0], swap_by_core(to_send, 1, 2))


def own_part(matrix, groups):
    s, seq_count = lax.axis_index("seq"), lax.axis_size("seq")
    width = matrix.shape[1] // (groups * seq_count)
    parts = [
        lax.dynamic_slice_in_dim(matrix, (g * seq_count + s) * width, width, 1)
        for g in range(groups)
    ]
    return jnp.concatenate(parts, axis=1)


def gather_fsdp(shard):
    return lax.all_gather(shard, "fsdp", axis=0, tiled=True)


def scatter_fsdp(full):
    return lax.psum_scatter(full.astype(BF16), "fsdp", scatter_dimension=0, tiled=True)


def after(values, *others):
    for other in others:
        values = values + 0.0 * other[(slice(0, 1),) * other.ndim].reshape(()).astype(F32)
    return values


def layer_forward(first_all, hidden, scalars, gain_rows, pairs, weights):
    qkv_part, square_parts, _, up_part, down_part = weights
    seq_count = lax.axis_size("seq")
    tok_rows, model_width = hidden.shape
    head_size = model_width // H
    triples = dot_nn(first_all, qkv_part).astype(BF16)
    mixed = self_forward(triples, head_size).reshape(seq_count, tok_rows, -1)
    mixed = exchange_rel([mixed[j] for j in range(seq_count)])
    self_tokens, after_self, cross_norm, queries, cross_tokens, after_cross, mlp_norm = (
        middle_forward(scalars, mixed, square_parts, pairs, hidden, gain_rows, head_size)
    )
    mlp_all = jnp.concatenate(gather_rel(mlp_norm), axis=0)
    up_rows = dot_nn(mlp_all, up_part)
    activated = gelu_tanh(up_rows).astype(BF16)
    down_rows = [
        dot_nn(activated[j * tok_rows : (j + 1) * tok_rows], down_part) for j in range(seq_count)
    ]
    result = after_cross + scatter_rel(down_rows)
    saved = (
        first_all,
        triples,
        self_tokens,
        after_self,
        cross_norm,
        queries,
        cross_tokens,
        after_cross,
        mlp_all,
        up_rows,
        activated,
    )
    return (result, saved)


def layer_backward(grad_out, saved, hidden, shift_vec, scalars, gain_rows, text_rows, pairs, weights, earlier):
    qkv_part, square_parts, kv_part, up_part, down_part = weights
    (
        first_all,
        triples,
        self_tokens,
        after_self,
        cross_norm,
        queries,
        cross_tokens,
        after_cross,
        mlp_all,
        up_rows,
        activated,
    ) = saved
    seq_count = lax.axis_size("seq")
    tok_rows, model_width = grad_out.shape
    head_size = model_width // H

    out_all = jnp.concatenate(gather_rel(grad_out.astype(BF16)), axis=0)
    grad_activated = dot_nt(out_all, down_part)
    _, gelu_pull = jax.vjp(gelu_tanh, up_rows)
    grad_up_rows = gelu_pull(grad_activated)[0].astype(BF16)
    grad_mlp_norm = scatter_rel(
        [
            dot_nt(grad_up_rows[j * tok_rows : (j + 1) * tok_rows], up_part)
            for j in range(seq_count)
        ]
    )
    down_shard = scatter_fsdp(dot_tn(activated, out_all))
    up_shard = scatter_fsdp(dot_tn(mlp_all, grad_up_rows))

    grad_self_res, self_branch, query_branch, cross_branch, gain_grads, pair_grads, mixed_grads = (
        middle_backward(
            scalars,
            square_parts,
            pairs,
            grad_mlp_norm,
            grad_out,
            after_cross,
            after_self,
            queries,
            after(gain_rows, *earlier[0]),
            head_size,
        )
    )
    grad_triples = self_backward(triples, exchange_rel(mixed_grads), head_size)
    grad_first = [
        dot_nt(grad_triples[j * tok_rows : (j + 1) * tok_rows], qkv_part) for j in range(seq_count)
    ]
    grad_first_norm = scatter_rel(grad_first)
    grad_pairs = scatter_rel(pair_grads).astype(BF16)
    grad_text = dot_nt(grad_pairs, kv_part)
    kv_shard = scatter_fsdp(dot_tn(text_rows, grad_pairs))
    square_shard = scatter_fsdp(
        unspread(
            outer([self_tokens, cross_norm, cross_tokens], [self_branch, query_branch, cross_branch])
        )
    )
    qkv_shard = scatter_fsdp(dot_tn(first_all, grad_triples))
    _, shift_pull = jax.vjp(norm_shift, hidden, after(gain_rows[0], *earlier[1], down_shard), shift_vec)
    grad_hidden, grad_gain_self, grad_shift = shift_pull(grad_first_norm)
    grad_hidden = grad_hidden + grad_self_res
    vectors = jnp.concatenate([jnp.stack([grad_shift, grad_gain_self]), gain_grads])
    return (grad_hidden, grad_text, vectors, (qkv_shard, square_shard, kv_shard, up_shard, down_shard))


def gather_block(layer, qkv, query, text_kv, self_out, cross_out, up, down):
    s, seq_count = lax.axis_index("seq"), lax.axis_size("seq")
    fsdp_count = lax.axis_size("fsdp")
    squares = jnp.concatenate(
        [own_part(self_out[layer], 1), own_part(query[layer], 1), own_part(cross_out[layer], 1)],
        axis=1,
    )
    rows = down.shape[1] // seq_count
    return (
        gather_fsdp(own_part(qkv[layer], 3)),
        spread(gather_fsdp(squares)),
        gather_fsdp(own_part(text_kv[layer], 2)),
        gather_fsdp(own_part(up[layer], fsdp_count)),
        gather_fsdp(lax.dynamic_slice_in_dim(down[layer], s * rows, rows, 0)),
    )


def finish_block(scalars, shards, layer, before):
    qkv_shard, square_shard, kv_shard, up_shard, down_shard = shards
    fsdp_count = lax.axis_size("fsdp")
    if before is None:
        before = [None] * 5
    return [
        settle(scalars, gather_parts(qkv_shard), 3, 1, layer, 2, before[0]),
        settle(scalars, gather_parts(square_shard), 1, 3, layer, 2, before[1]),
        settle(scalars, gather_parts(kv_shard), 2, 1, layer, 2, before[2]),
        settle(scalars, gather_parts(up_shard), fsdp_count, 1, layer, 2, before[3]),
        settle_rows(scalars, gather_parts(down_shard), layer, 2, before[4]),
    ]


def sum_vectors(vectors):
    bits = 1
    while bits < lax.axis_size("seq"):
        vectors = vectors + swap_seq(vectors, bits)
        bits *= 2
    found, bits = vectors[None], 1
    while bits < lax.axis_size("fsdp"):
        found = jnp.concatenate([found, swap_fsdp(found, bits)], axis=0)
        bits *= 2
    return found


def body(
    latents,
    skip_input,
    text_tokens,
    text_lengths,
    condition,
    cotangent,
    mod_weight,
    norm_gains,
    qkv_weight,
    query_weight,
    text_kv_weight,
    self_out_weight,
    cross_out_weight,
    up_weight,
    down_weight,
    skip_gain,
    skip_weight,
):
    seq_count, fsdp_count = lax.axis_size("seq"), lax.axis_size("fsdp")
    s, f = lax.axis_index("seq"), lax.axis_index("fsdp")
    _, tok_rows, model_width = latents.shape
    shard_rows = mod_weight.shape[1]
    text_count = text_tokens.shape[1]
    padded = -(-text_count // 32) * 32
    text_rows = jnp.pad(text_tokens[0], ((0, padded - text_count), (0, 0)))
    scalars = jnp.stack(
        [*list_order(), *[s ^ j for j in range(seq_count)], f % 2, text_lengths[0]]
    ).astype(jnp.int32)

    gain_rows = jnp.concatenate(
        [norm_gains.reshape(-1, shard_rows), skip_gain.reshape(-1, shard_rows)], axis=0
    )
    small = jnp.concatenate(
        [
            condition.reshape(fsdp_count, 1, shard_rows),
            jnp.broadcast_to(gain_rows[None], (fsdp_count,) + gain_rows.shape),
        ],
        axis=1,
    ).astype(F32)
    small = lax.all_to_all(small, "fsdp", 0, 0, tiled=True)
    cond_part = small[:, 0]
    gains = jnp.swapaxes(small[:, 1:7], 0, 1).reshape(2, 3, model_width)
    skip_gains = small[:, 7:].reshape(2, model_width)
    silu_part = jax.nn.silu(cond_part)
    shift_terms = jnp.einsum("br,lrd->bld", silu_part, mod_weight.astype(F32), precision=EXACT)
    shifts = jnp.sum(lax.all_to_all(shift_terms, "fsdp", 0, 0, tiled=True), axis=0)

    stacks = (
        qkv_weight,
        query_weight,
        text_kv_weight,
        self_out_weight,
        cross_out_weight,
        up_weight,
        down_weight,
    )
    hidden = latents[0].astype(F32)
    all_hidden = jnp.concatenate(gather_rel(latents[0]), axis=0).astype(F32)
    first_weights = gather_block(0, *stacks)
    first_pairs = gather_rel(dot_nn(text_rows, first_weights[2]).astype(BF16))
    first_norm = norm_shift(all_hidden, gains[0, 0], shifts[0]).astype(BF16)
    first_out, first_saved = layer_forward(
        first_norm, hidden, scalars, gains[0], first_pairs, first_weights
    )
    skip_parts = spread(gather_fsdp(own_part(skip_weight, 1)))
    joined_norm, skip_out = skip_forward(scalars, skip_parts, first_out, skip_input[0], skip_gains)
    second_weights = gather_block(1, *stacks)
    second_pairs = gather_rel(dot_nn(text_rows, second_weights[2]).astype(BF16))
    second_norm = norm_shift(skip_out, gains[1, 0], shifts[1]).astype(BF16)
    second_norm = jnp.concatenate(gather_rel(second_norm), axis=0)
    final_out, second_saved = layer_forward(
        second_norm, skip_out, scalars, gains[1], second_pairs, second_weights
    )
    output = final_out.astype(BF16)

    grad_skip_out, text_second, vectors_second, shards_second = layer_backward(
        cotangent[0].astype(F32),
        second_saved,
        skip_out,
        shifts[1],
        scalars,
        gains[1],
        text_rows,
        second_pairs,
        second_weights,
        ((), ()),
    )
    skip_branch, grad_first_out, grad_skip, skip_gain_grads = skip_backward(
        scalars,
        skip_parts,
        first_out,
        skip_input[0],
        after(skip_gains, shards_second[3]),
        grad_skip_out,
    )
    skip_shard = scatter_fsdp(unspread(outer([joined_norm], [skip_branch])))
    second_done = finish_block(scalars, shards_second, 1, None)
    grad_latents, text_first, vectors_first, shards_first = layer_backward(
        grad_first_out,
        first_saved,
        hidden,
        shifts[0],
        scalars,
        gains[0],
        text_rows,
        first_pairs,
        first_weights,
        (
            (shards_second[2], shards_second[1]),
            (skip_shard, second_done[4][0], second_done[3][0], second_done[0][0]),
        ),
    )
    first_done = finish_block(scalars, shards_first, 0, second_done)
    (grad_qkv,), (grad_self_out, grad_query, grad_cross_out), (grad_kv,), (grad_up,), (grad_down,) = (
        first_done
    )
    (grad_skip_weight,) = settle(scalars, gather_parts(skip_shard), 1, 1, 0, 1)

    second_sums = sum_vectors(jnp.concatenate([vectors_second, skip_gain_grads]))
    first_sums = sum_vectors(vectors_first)
    shift_grads = jnp.stack([first_sums[:, 0], second_sums[:, 0]], axis=1)
    gain_sums = jnp.stack([first_sums[:, 1:4].sum(axis=0), second_sums[:, 1:4].sum(axis=0)])
    grad_norm_gains = lax.dynamic_slice_in_dim(gain_sums, f * shard_rows, shard_rows, 2)
    grad_skip_gain = lax.dynamic_slice_in_dim(
        second_sums[:, 4:].sum(axis=0).reshape(-1), f * skip_gain.shape[0], skip_gain.shape[0], 0
    )
    turned = jnp.stack(
        [lax.dynamic_index_in_dim(silu_part, f ^ j, 0, False) for j in range(fsdp_count)]
    )
    grad_mod = jnp.einsum("br,bld->lrd", turned, shift_grads, precision=EXACT)
    grad_silu = jnp.einsum("bld,lrd->br", shift_grads, mod_weight.astype(F32), precision=EXACT)
    grad_silu = jnp.stack(
        [lax.dynamic_index_in_dim(grad_silu, f ^ j, 0, False) for j in range(fsdp_count)]
    )
    _, silu_pull = jax.vjp(jax.nn.silu, cond_part)
    grad_cond_part = silu_pull(grad_silu)[0]
    grad_condition = lax.all_to_all(grad_cond_part, "fsdp", 0, 0, tiled=True).reshape(1, -1)

    text_sum = text_first + text_second
    width = text_sum.shape[1] // seq_count
    text_blocks = [
        lax.dynamic_slice_in_dim(text_sum, (s ^ j) * width, width, 1) for j in range(seq_count)
    ]
    (grad_text,) = settle(
        scalars, gather_parts(scatter_rel(text_blocks).astype(BF16)), 1, 1, 0, 1
    )
    return (
        output[None],
        grad_latents[None],
        grad_skip[None],
        grad_text[:, :text_count],
        grad_condition,
        grad_mod,
        grad_norm_gains,
        grad_qkv,
        grad_query,
        grad_kv,
        grad_self_out,
        grad_cross_out,
        grad_up,
        grad_down,
        grad_skip_gain,
        grad_skip_weight[0],
    )


def solution(mesh):
    in_specs = (
        P("fsdp", "seq", None),
        P("fsdp", "seq", None),
        P("fsdp", None, None),
        P("fsdp"),
        P("fsdp", None),
        P("fsdp", "seq", None),
        P(None, "fsdp", None),
        P(None, None, "fsdp"),
        P(None, "fsdp", None),
        P(None, "fsdp", None),
        P(None, "fsdp", None),
        P(None, "fsdp", None),
        P(None, "fsdp", None),
        P(None, "fsdp", None),
        P(None, "fsdp", None),
        P("fsdp"),
        P("fsdp", None),
    )
    out_specs = (
        P("fsdp", "seq", None),
        P("fsdp", "seq", None),
        P("fsdp", "seq", None),
        P("fsdp", None, None),
        P("fsdp", None),
        P(None, "fsdp", None),
        P(None, None, "fsdp"),
        P(None, "fsdp", None),
        P(None, "fsdp", None),
        P(None, "fsdp", None),
        P(None, "fsdp", None),
        P(None, "fsdp", None),
        P(None, "fsdp", None),
        P(None, "fsdp", None),
        P("fsdp"),
        P("fsdp", None),
    )
    return jax.shard_map(body, mesh=mesh, in_specs=in_specs, out_specs=out_specs, check_vma=False)
```

time: 1610 us -> 1430 us (0.89)
  Pallas kernels: 0 us -> 270 us
  matrix products: 404 us -> 195 us
  other arithmetic: 231 us -> 75.6 us
  local copies, waits for them, and re-layouts: 339 us -> 277 us
    pallas_call x0 -> x25, Pallas kernels: none -> 270 us  [the longest x13 229 us: call(): pl.pallas_call(kernel, out_shape=tuple((jax.ShapeDtypeStruct(s, d) for s,...]
    dot_general x133 -> x43, matrix products: 403 us -> 194 us  [the longest x20 70.9 us: dot_nt(): lax.dot_general(a, b, (((1,), (1,)), ((), ())), preferred_element_type=F32)]
    another operation x64 -> x1, other arithmetic: 57.5 us -> 0.08 us  [body(): jnp.stack([first_sums[:, 1:4].sum(axis=0), second_sums[:, 1:4].sum(axis=0)])]
    unnamed x758 -> x344, local copies, waits for them, and re-layouts: 118 us -> 66.2 us
    dynamic_slice x65 -> x6, local copies, waits for them, and re-layouts: 50.4 us -> 8.9 us  [the longest x4 8.22 us: unspread(): others = lax.dynamic_slice_in_dim(blocks[3], (1 - odd) * half, half, 0)]
    slice x57 -> x87, local copies, waits for them, and re-layouts: 30.6 us -> 60.6 us  [the longest x20 12.6 us: gather_parts(): from_y[:cut]]
    dynamic_update_slice x2 -> x0, local copies, waits for them, and re-layouts: 30 us -> none  [unspread(): lax.dynamic_update_slice_in_dim(to_send, add_bf16(part, passed), odd * ha...]
    ppermute x1 -> x8, local copies, waits for them, and re-layouts: 3.95 us -> 29.9 us  [swap_by_core(): return lax.ppermute(block, ('seq', 'fsdp'), pairs)]
  transfers between devices with their start and end apart: 171 -> 187, of which waited for: 64 -> 62; matrix products, arithmetic and copies ran while one was open for 50% -> 36% of each run, Pallas kernels for 0% -> 19%
where the time goes in v2:
time: 1430 us; the launch traced here: 1420 us
  waiting for transfers between devices  408 us (29%)
  local copies, waits for them, and re-layouts  277 us (19%)
  Pallas kernels  270 us (19%)
  matrix products  195 us (14%)
  starting transfers between devices  169 us (12%)
  other arithmetic  75.6 us (5%)
  between operations  23.8 us (2%)
    ppermute x132, waiting for transfers between devices, swap_seq(): return lax.ppermute(block, 'seq', [(i, i ^ bits) for i in range(seq_count)])  321 us
    pallas_call x13, Pallas kernels, call(): pl.pallas_call(kernel, out_shape=tuple((jax.ShapeDtypeStruct(s, d) for s,...  229 us
    ppermute x132, starting transfers between devices, swap_seq(): return lax.ppermute(block, 'seq', [(i, i ^ bits) for i in range(seq_count)])  135 us
    dot_general x20, matrix products, dot_nt(): lax.dot_general(a, b, (((1,), (1,)), ((), ())), preferred_element_type=F32)  70.9 us
    dot_general x14, matrix products, dot_nn(): lax.dot_general(a, b, (((1,), (0,)), ((), ())), preferred_element_type=F32)  70.5 us
    unnamed x344, local copies, waits for them, and re-layouts  66.2 us
    ppermute x12, waiting for transfers between devices, swap_by_core(): return lax.ppermute(block, ('seq', 'fsdp'), pairs)  49.7 us
    dot_general x8, matrix products, dot_tn(): lax.dot_general(a, b, (((0,), (0,)), ((), ())), preferred_element_type=F32)  49.2 us
  transfers between devices with their start and end apart: 187, of which 62 were waited for; matrix products, arithmetic and copies ran while one was open for 36% of the time, Pallas kernels for 19%

profile of v2, /device:TPU:0, one launch (start us, length us, event | category | flops | bytes accessed | tf_op | source)
XLA Modules:
  0.0 1417.9 jit_solution(4965854001155607879)
XLA Ops:
  35.6 20.2 %all-gather.18.cloned.1.call-done.refs_4_.refs_0_ = bf16[1408,1056]{1,0:T(8,128)(2,1)} async-done(((bf16[176,1056]{1,0:T(8,128)(2,1)}), bf16[1408,1056]{1,0:T(8,128)(2,1)}) %all-gather.18.cloned.1.call-update) | async-done | bytes 2973712 | tf_op jit(solution)/shard_map/all_gather | solution.py:697
  92.3 20.1 %collective-permute-done.4 = bf16[256,1408]{1,0:T(8,128)(2,1)S(1)} collective-permute-done((bf16[256,1408]{1,0:T(8,128)(2,1)S(1)}, bf16[256,1408]{1,0:T(8,128)(2,1)S(1)}, u32[]{:S(2)}, u32[]{:S(2)}) %collective-permute-start.4) | collective-permute-done | bytes 720928 | tf_op jit(solution)/shard_map/ppermute | solution.py:583
  142.6 19.8 %collective-permute-done.16.refs_11_.refs_7_ = bf16[352,704]{1,0:T(8,128)(2,1)S(1)} collective-permute-done((bf16[352,704]{1,0:T(8,128)(2,1)S(1)}, bf16[352,704]{1,0:T(8,128)(2,1)S(1)}, u32[]{:S(2)}, u32[]{:S(2)}) %collective-permute-start.16) | collective-permute-done | bytes 495648 | tf_op jit(solution)/shard_map/ppermute | solution.py:583
  164.7 15.1 %collective-permute-done.15.refs_10_.refs_6_ = bf16[352,704]{1,0:T(8,128)(2,1)S(1)} collective-permute-done((bf16[352,704]{1,0:T(8,128)(2,1)S(1)}, bf16[352,704]{1,0:T(8,128)(2,1)S(1)}, u32[]{:S(2)}, u32[]{:S(2)}) %collective-permute-start.15) | collective-permute-done | bytes 495648 | tf_op jit(solution)/shard_map/ppermute | solution.py:583
  189.9 15.1 %shard_map.288 = bf16[1024,352]{1,0:T(8,128)(2,1)} custom-call(bf16[1024,1056]{1,0:T(8,128)(2,1)} %convolution_convert_fusion.7.triples_ref), custom_call_target="tpu_custom_call" | custom-call | flops 1476395008 | bytes 2883584 | tf_op jit(solution)/shard_map/pallas_call | solution.py:40
  222.9 23.3 %shard_map.289 = (bf16[256,1408]{1,0:T(8,128)(2,1)}, f32[256,1408]{1,0:T(8,128)}, bf16[256,1408]{1,0:T(8,128)(2,1)}, bf16[4,256,352]{2,1,0:T(8,128)(2,1)}, bf16[...) custom-call(s32[10]{0:T(128)} %stack.87.scalars_ref, ...), custom_call_target="tpu_custom_call" | custom-call | flops 3045064704 | bytes 20545536 | tf_op jit(solution)/shard_map/pallas_call | solution.py:40
  273.8 30.5 %collective-permute-done.21 = bf16[128,1408]{1,0:T(8,128)(2,1)S(1)} collective-permute-done((bf16[128,1408]{1,0:T(8,128)(2,1)S(1)}, bf16[128,1408]{1,0:T(8,128)(2,1)S(1)}, u32[]{:S(2)}, u32[]{:S(2)}) %collective-permute-start.21) | collective-permute-done | bytes 360480 | tf_op jit(solution)/shard_map/ppermute | solution.py:583
  396.8 17.2 %collective-permute-done.38.refs_10_.refs_6_ = bf16[352,704]{1,0:T(8,128)(2,1)S(1)} collective-permute-done((bf16[352,704]{1,0:T(8,128)(2,1)}, bf16[352,704]{1,0:T(8,128)(2,1)S(1)}, u32[]{:S(2)}, u32[]{:S(2)}) %collective-permute-start.38) | collective-permute-done | bytes 495648 | tf_op jit(solution)/shard_map/ppermute | solution.py:583
  440.2 15.1 %shard_map.291 = bf16[1024,352]{1,0:T(8,128)(2,1)} custom-call(bf16[1024,1056]{1,0:T(8,128)(2,1)} %convolution_convert_fusion.6.triples_ref), custom_call_target="tpu_custom_call" | custom-call | flops 1476395008 | bytes 2883584 | tf_op jit(solution)/shard_map/pallas_call | solution.py:40
  470.2 23.4 %shard_map.292 = (bf16[256,1408]{1,0:T(8,128)(2,1)}, f32[256,1408]{1,0:T(8,128)}, bf16[256,1408]{1,0:T(8,128)(2,1)}, bf16[4,256,352]{2,1,0:T(8,128)(2,1)}, bf16[...) custom-call(s32[10]{0:T(128)} %stack.87.scalars_ref, ...), custom_call_target="tpu_custom_call" | custom-call | flops 3045064704 | bytes 20545536 | tf_op jit(solution)/shard_map/pallas_call | solution.py:40
  500.1 11.8 collective-permute-done.43
  541.0 11.6 fusion.15
  585.0 26.8 %shard_map.293 = (f32[256,1408]{1,0:T(8,128)}, bf16[4,256,352]{2,1,0:T(8,128)(2,1)}, bf16[4,256,352]{2,1,0:T(8,128)(2,1)}, bf16[4,256,352]{2,1,0:T(8,128)(2,1)},...) custom-call(s32[10]{0:T(128)} %stack.87.scalars_ref, ...), custom_call_target="tpu_custom_call" | custom-call | flops 5075107840 | bytes 24870912 | tf_op jit(solution)/shard_map/pallas_call | solution.py:40
  655.5 12.5 collective-permute-done.79
  683.8 24.9 %shard_map.294 = bf16[1024,1056]{1,0:T(8,128)(2,1)} custom-call(bf16[1024,1056]{1,0:T(8,128)(2,1)} %convolution_convert_fusion.6.triples_ref, bf16[256,352]{1,0:T(8,128)(2,1)} %get-tuple-element.87.refs_0_, bf16[256,352]{1,0:T(8,128)(2,1)} %collective-permute-done.58.refs_1_, bf16[256,352]{1,0:T(8,128)(2,1)} %collective-permute-done.59.refs_2_, ...), custom_call_target="tpu_custom_call" | custom-call | flops 3690987520 | bytes 5767168 | tf_op jit(solution)/shard_map/pallas_call | solution.py:40
  708.7 11.5 collective-permute-done.74
  770.5 11.2 shard_map.295
  831.4 24.2 %collective-permute-done.91 = bf16[2816,352]{0,1:T(8,128)(2,1)} collective-permute-done((bf16[2816,352]{0,1:T(8,128)(2,1)}, bf16[2816,352]{0,1:T(8,128)(2,1)}, u32[]{:S(2)}, u32[]{:S(2)}) %collective-permute-start.91) | collective-permute-done | bytes 1982496 | tf_op jit(solution)/shard_map/ppermute | solution.py:602
  865.4 14.4 %collective-permute-done.66 = bf16[256,1408]{1,0:T(8,128)(2,1)S(1)} collective-permute-done((bf16[256,1408]{1,0:T(8,128)(2,1)S(1)}, bf16[256,1408]{1,0:T(8,128)(2,1)S(1)}, u32[]{:S(2)}, u32[]{:S(2)}) %collective-permute-start.66) | collective-permute-done | bytes 720928 | tf_op jit(solution)/shard_map/ppermute | solution.py:583
  898.6 11.4 fusion.8
  950.5 26.6 %shard_map.297 = (f32[256,1408]{1,0:T(8,128)}, bf16[4,256,352]{2,1,0:T(8,128)(2,1)}, bf16[4,256,352]{2,1,0:T(8,128)(2,1)}, bf16[4,256,352]{2,1,0:T(8,128)(2,1)},...) custom-call(s32[10]{0:T(128)} %stack.87.scalars_ref, ...), custom_call_target="tpu_custom_call" | custom-call | flops 5075107840 | bytes 24870912 | tf_op jit(solution)/shard_map/pallas_call | solution.py:40
  1119.3 25.1 %shard_map.298 = bf16[1024,1056]{1,0:T(8,128)(2,1)} custom-call(bf16[1024,1056]{1,0:T(8,128)(2,1)} %convolution_convert_fusion.7.triples_ref, bf16[256,352]{1,0:T(8,128)(2,1)} %get-tuple-element.109.refs_0_, bf16[256,352]{1,0:T(8,128)(2,1)} %copy-done.137, bf16[256,352]{1,0:T(8,128)(2,1)} %copy-done.138, bf16[256,352]{1,0:T(8,128)(2,1)} %copy-done.139), custom_call_target="tpu_custom_call" | custom-call | flops 3690987520 | bytes 5767168 | tf_op jit(solution)/shard_map/pallas_call | solution.py:40
  1216.7 14.1 collective-permute-done.86
  1248.2 13.2 collective-permute-done.108
  (1065 shorter events, 954.9 us)
Async XLA Ops:
  13.9 117.7 %all-gather.14.cloned.1.call-start = ((), (), s32[]{:S(2)}) async-start(), calls=%async_computation.14 | async-start | bytes 2433024 | tf_op jit(solution)/shard_map/all_gather | solution.py:697
  14.9 121.6 %all-gather.20.cloned.1.call-start = ((), (), s32[]{:S(2)}) async-start(), calls=%async_computation.17 | async-start | bytes 1769472 | tf_op jit(solution)/shard_map/all_gather | solution.py:697
  18.2 163.9 %all-gather.16.cloned.1.call-start = ((), (), s32[]{:S(2)}) async-start(), calls=%async_computation.15 | async-start | bytes 3649536 | tf_op jit(solution)/shard_map/all_gather | solution.py:697
  19.8 228.4 %all-gather.26.cloned.1.call-start = ((), (), s32[]{:S(2)}) async-start(), calls=%async_computation.20 | async-start | bytes 3649536 | tf_op jit(solution)/shard_map/all_gather | solution.py:697
  23.0 282.9 %all-gather.22.cloned.1.call-start = ((), (), s32[]{:S(2)}) async-start(), calls=%async_computation.18 | async-start | bytes 4866048 | tf_op jit(solution)/shard_map/all_gather | solution.py:697
  28.7 288.0 %all-gather.32.cloned.1.call-start = ((), (), s32[]{:S(2)}) async-start(), calls=%async_computation.34 | async-start | bytes 4866048 | tf_op jit(solution)/shard_map/all_gather | solution.py:697
  33.6 303.3 %all-gather.28.cloned.1.call-start = ((), (), s32[]{:S(2)}) async-start(), calls=%async_computation.21 | async-start | bytes 1769472 | tf_op jit(solution)/shard_map/all_gather | solution.py:697
  34.5 397.1 %all-gather.24.cloned.1.call-start = ((), (), s32[]{:S(2)}) async-start(), calls=%async_computation.19 | async-start | bytes 3649536 | tf_op jit(solution)/shard_map/all_gather | solution.py:697
  69.9 452.5 %all-gather.30.cloned.1.call-start = ((), (), s32[]{:S(2)}) async-start(), calls=%async_computation.22 | async-start | bytes 4866048 | tf_op jit(solution)/shard_map/all_gather | solution.py:697
  83.9 457.2 %all-gather.34.cloned.1.call-start = ((), (), s32[]{:S(2)}) async-start(), calls=%async_computation.35 | async-start | bytes 4866048 | tf_op jit(solution)/shard_map/all_gather | solution.py:697
  252.6 103.0 %collective-permute-start.34 = (bf16[1408,1056]{0,1:T(8,128)(2,1)S(1)}, bf16[1408,1056]{0,1:T(8,128)(2,1)}, u32[]{:S(2)}, u32[]{:S(2)}) collective-permute-start(bf16[1408,1056]{0,1:T(8,128)(2,1)S(1)} %copy.185), channel_id=1, source_target_pairs={{0,8},{1,17},{2,10},{3,19},{4,12},{5,21},{6,14},{7,23},{8,0},{9,25... | collective-permute-start | bytes 8921096 | tf_op jit(solution)/shard_map/ppermute | solution.py:602
  253.1 96.4 %collective-permute-start.1 = (bf16[2816,352]{0,1:T(8,128)(2,1)}, bf16[2816,352]{0,1:T(8,128)(2,1)}, u32[]{:S(2)}, u32[]{:S(2)}) collective-permute-start(bf16[2816,352]{0,1:T(8,128)(2,1)} %collective-permute-done), channel_id=1, source_target_pairs={{0,1},{1,0},{2,3},{3,2},{4,5},{5,4},{6,7},{7,6},{8,9},{9,8},{10,11... | collective-permute-start | bytes 5947400 | tf_op jit(solution)/shard_map/ppermute | solution.py:588
  336.1 413.7 %reduce-scatter.14.cloned.1.call-start = ((), (), s32[]{:S(2)}) async-start(), calls=%async_computation.24 | async-start | bytes 4866048 | tf_op jit(solution)/shard_map/reduce_scatter | solution.py:701
  363.6 97.3 %collective-permute-start.35 = (bf16[1408,1056]{0,1:T(8,128)(2,1)}, bf16[1408,1056]{0,1:T(8,128)(2,1)}, u32[]{:S(2)}, u32[]{:S(2)}) collective-permute-start(bf16[1408,1056]{0,1:T(8,128)(2,1)} %collective-permute-done.34), channel_id=1, source_target_pairs={{0,1},{1,0},{2,3},{3,2},{4,5},{5,4},{6,7},{7,6},{8,9},{9,8},{10,11... | collective-permute-start | bytes 8921096 | tf_op jit(solution)/shard_map/ppermute | solution.py:588
  540.9 211.5 %reduce-scatter.12.cloned.1.call-start = ((), (), s32[]{:S(2)}) async-start(), calls=%async_computation.23 | async-start | bytes 4866048 | tf_op jit(solution)/shard_map/reduce_scatter | solution.py:701
  576.4 356.5 %reduce-scatter.16.cloned.1.call-start = ((), (), s32[]{:S(2)}) async-start(), calls=%async_computation.25 | async-start | bytes 1769472 | tf_op jit(solution)/shard_map/reduce_scatter | solution.py:701
  723.7 224.4 %reduce-scatter.18.cloned.1.call-start = ((), (), s32[]{:S(2)}) async-start(), calls=%async_computation.26 | async-start | bytes 3649536 | tf_op jit(solution)/shard_map/reduce_scatter | solution.py:701
  743.9 293.1 %reduce-scatter.22.cloned.1.call-start = ((), (), s32[]{:S(2)}) async-start(), calls=%async_computation.28 | async-start | bytes 3649536 | tf_op jit(solution)/shard_map/reduce_scatter | solution.py:701
  802.8 462.0 %reduce-scatter.20.cloned.1.call-start = ((), (), s32[]{:S(2)}) async-start(), calls=%async_computation.27 | async-start | bytes 2433024 | tf_op jit(solution)/shard_map/reduce_scatter | solution.py:701
  861.9 404.8 %reduce-scatter.24.cloned.1.call-start = ((), (), s32[]{:S(2)}) async-start(), calls=%async_computation.29 | async-start | bytes 4866048 | tf_op jit(solution)/shard_map/reduce_scatter | solution.py:701
  896.9 386.1 %reduce-scatter.30.cloned.1.call-start = ((), (), s32[]{:S(2)}) async-start(), calls=%async_computation.32 | async-start | bytes 1769472 | tf_op jit(solution)/shard_map/reduce_scatter | solution.py:701
  1003.0 324.2 %reduce-scatter.32.cloned.1.call-start = ((), (), s32[]{:S(2)}) async-start(), calls=%async_computation.33 | async-start | bytes 4866048 | tf_op jit(solution)/shard_map/reduce_scatter | solution.py:701
  1012.7 323.9 %reduce-scatter.26.cloned.1.call-start = ((), (), s32[]{:S(2)}) async-start(), calls=%async_computation.30 | async-start | bytes 3649536 | tf_op jit(solution)/shard_map/reduce_scatter | solution.py:701
  1155.3 188.3 %reduce-scatter.28.cloned.1.call-start = ((), (), s32[]{:S(2)}) async-start(), calls=%async_computation.31 | async-start | bytes 3649536 | tf_op jit(solution)/shard_map/reduce_scatter | solution.py:701
  (318 other events, 5810.8 us)
Sparse Core Ops, SparseCore 0:
  14.0 41.7 all-gather.17
  58.1 30.1 all-gather.13
  90.5 23.8 all-gather.19
  116.5 38.6 all-gather.15
  156.7 37.9 all-gather.25
  196.7 47.2 all-gather.21
  246.3 47.1 all-gather.31
  295.1 23.7 all-gather.27
  320.6 38.6 all-gather.23
  360.7 47.3 all-gather.29
  409.7 47.0 all-gather.33
  541.1 49.1 reduce-scatter.13
  593.3 49.4 reduce-scatter.11
  723.8 32.0 reduce-scatter.15
  758.6 39.3 reduce-scatter.17
  803.0 39.5 reduce-scatter.21
  862.0 34.1 reduce-scatter.19
  898.4 50.1 reduce-scatter.23
  1003.1 32.2 reduce-scatter.29
  1037.7 49.3 reduce-scatter.31
  1155.4 43.5 reduce-scatter.25
  1241.9 39.3 reduce-scatter.27

commit v3 on v2

v3 whole, which is shorter than its diff:
```python
import functools
import math

import jax
import jax.numpy as jnp
from jax import lax
from jax.experimental import pallas as pl
from jax.experimental.pallas import tpu as pltpu
from jax.sharding import PartitionSpec as P

H = 16
NORM_EPSILON = 1e-06
EXACT = lax.Precision.HIGHEST
BF16 = jnp.bfloat16
F32 = jnp.float32
LOG2_E = 1.4426950408889634
GELU_SCALE = math.sqrt(2.0 / math.pi)
VMEM_LIMIT = 56 * 1024 * 1024


def dot_nn(a, b):
    return lax.dot_general(a, b, (((1,), (0,)), ((), ())), preferred_element_type=F32)


def dot_nt(a, b):
    return lax.dot_general(a, b, (((1,), (1,)), ((), ())), preferred_element_type=F32)


def dot_tn(a, b):
    return lax.dot_general(a, b, (((0,), (0,)), ((), ())), preferred_element_type=F32)


def padded_width(width):
    return -(-width // 128) * 128


def call(kernel, outs, scratch, micros, *operands, scalars=None, deps=()):
    specs = [pl.BlockSpec(memory_space=pltpu.VMEM)] * len(operands)
    if scalars is not None:
        specs = [pl.BlockSpec(memory_space=pltpu.SMEM)] + specs
        operands = (scalars,) + tuple(operands)
    used, held = len(operands), len(deps)

    def run(*refs):
        kernel(*refs[:used], *refs[used + held :])

    return pl.pallas_call(
        run,
        out_shape=tuple(jax.ShapeDtypeStruct(s, d) for s, d in outs),
        in_specs=specs + [pl.BlockSpec(memory_space=pl.ANY)] * held,
        out_specs=tuple([pl.BlockSpec(memory_space=pltpu.VMEM)] * len(outs)),
        scratch_shapes=scratch,
        compiler_params=pltpu.CompilerParams(vmem_limit_bytes=VMEM_LIMIT),
        cost_estimate=pl.CostEstimate(
            flops=int(micros * 1.0e9), bytes_accessed=1000, transcendentals=0
        ),
    )(*operands, *deps)


def cut_of(rows):
    return rows // 32 * 16


def cuts(count, rows):
    return [(0, cut_of(rows)), (cut_of(rows), rows)] if count == 4 else [(0, rows)]


def pieces_of(count, rows):
    return [(j, low, high) for j in range(1, count) for low, high in cuts(count, rows)]


def put_pieces(refs, count, block, values):
    for ref, (j, low, high) in zip(refs, pieces_of(count, values.shape[0])):
        if j == block:
            ref[...] = values[low:high].astype(BF16)


def piece_shapes(count, rows, columns):
    return [((high - low, columns), BF16) for _, low, high in pieces_of(count, rows)]


def add_terms(count, refs):
    total = refs[0][...].astype(F32)
    if count != 4:
        for ref in refs[1:]:
            total = total + ref[...].astype(F32)
        return total
    for low, high in ((1, 2), (3, 4)):
        total = total + jnp.concatenate([refs[low][...], refs[high][...]], axis=0).astype(F32)
    return total


def norm_stats(values):
    mean = jnp.mean(values, axis=1, keepdims=True)
    centered = values - mean
    var = jnp.mean(centered * centered, axis=1, keepdims=True)
    scale = lax.rsqrt(var + NORM_EPSILON)
    return centered * scale, scale


def norm_back(values, gain, grad):
    unit, scale = norm_stats(values)
    grad_unit = grad * gain
    inner = jnp.mean(grad_unit * unit, axis=1, keepdims=True)
    grad_values = scale * (grad_unit - jnp.mean(grad_unit, axis=1, keepdims=True) - unit * inner)
    return grad_values, jnp.sum(grad * unit, axis=0, keepdims=True)


def self_forward_kernel(count, parts, head_size, normed, *refs):
    part_refs, refs = refs[:parts], refs[parts:]
    weight_ref, gains_ref, shift_ref = refs[:3]
    rows_ref, triples_ref = refs[3:5]
    mixed_refs = refs[5:]
    stride = weight_ref.shape[1] // 3
    rows, width = mixed_refs[0].shape
    factor = LOG2_E / math.sqrt(head_size)
    start = 0
    for ref in part_refs:
        values = ref[...]
        if not normed:
            unit, _ = norm_stats(values.astype(F32))
            values = (unit * gains_ref[0:1, :] + shift_ref[...]).astype(BF16)
        rows_ref[start : start + ref.shape[0], :] = values
        start += ref.shape[0]
    for j in range(count):
        at = slice(j * rows, (j + 1) * rows)
        triples_ref[at, :] = dot_nn(rows_ref[at, :], weight_ref[...]).astype(BF16)
    for j in range(count):
        at = slice(j * rows, (j + 1) * rows)
        for h in range(width // head_size):
            low = h * head_size
            q = triples_ref[at, low : low + head_size]
            k = triples_ref[:, stride + low : stride + low + head_size]
            v = triples_ref[:, 2 * stride + low : 2 * stride + low + head_size]
            scores = dot_nt(q, k)
            top = jnp.max(scores, axis=1, keepdims=True)
            weights = jnp.exp2((scores - top) * factor)
            total = jnp.sum(weights, axis=1, keepdims=True)
            mixed = dot_nn(weights.astype(BF16), v) * (1.0 / total)
            mixed_refs[j][:, low : low + head_size] = mixed.astype(BF16)


def self_forward(parts, weight, gains, shift, head_size, count, width, normed, deps=()):
    total = sum(m.shape[0] for m in parts)
    columns = parts[0].shape[1]
    found = call(
        functools.partial(self_forward_kernel, count, len(parts), head_size, normed),
        [((total, columns), BF16), ((total, weight.shape[1]), BF16)]
        + [((total // count, width), BF16)] * count,
        [],
        24,
        *parts,
        weight,
        gains,
        shift[None],
        deps=deps,
    )
    return found[0], found[1], list(found[2:])


def attention_back(q, k, v, grad, valid, head_size):
    factor = LOG2_E / math.sqrt(head_size)
    scores = dot_nt(k, q)
    if valid is not None:
        scores = jnp.where(valid, scores, -1e30)
    top = jnp.max(scores, axis=0, keepdims=True)
    weights = jnp.exp2((scores - top) * factor)
    weights = weights * (1.0 / jnp.sum(weights, axis=0, keepdims=True))
    grad_weights = dot_nt(v, grad)
    delta = jnp.sum(grad_weights * weights, axis=0, keepdims=True)
    grad_scores = (weights * (grad_weights - delta)).astype(BF16)
    scale = 1.0 / math.sqrt(head_size)
    return (
        dot_tn(grad_scores, k) * scale,
        dot_nn(grad_scores, q) * scale,
        dot_nn(weights.astype(BF16), grad),
    )


def self_backward_kernel(count, head_size, step, triples_ref, *refs):
    grad_refs, (weight_ref, out_ref, own_ref) = refs[:count], refs[count : count + 3]
    piece_refs, (keys_ref, values_ref) = refs[count + 3 : -2], refs[-2:]
    total = triples_ref.shape[0]
    rows, width = grad_refs[0].shape
    stride = weight_ref.shape[1] // 3
    for h in range(width // head_size):
        low = h * head_size
        k = triples_ref[:, stride + low : stride + low + head_size]
        v = triples_ref[:, 2 * stride + low : 2 * stride + low + head_size]
        for i in range(total // step):
            at = slice(i * step, (i + 1) * step)
            inside = (i * step) % rows
            q = triples_ref[at, low : low + head_size]
            grad = grad_refs[i * step // rows][inside : inside + step, low : low + head_size]
            grad_q, grad_k, grad_v = attention_back(q, k, v, grad, None, head_size)
            out_ref[at, low : low + head_size] = grad_q.astype(BF16)
            if i == 0:
                keys_ref[...] = grad_k
                values_ref[...] = grad_v
            else:
                keys_ref[...] += grad_k
                values_ref[...] += grad_v
        out_ref[:, stride + low : stride + low + head_size] = keys_ref[...].astype(BF16)
        out_ref[:, 2 * stride + low : 2 * stride + low + head_size] = values_ref[...].astype(BF16)
    if stride > width:
        for g in range(3):
            out_ref[:, g * stride + width : (g + 1) * stride] = jnp.zeros((total, stride - width), BF16)
    for j in range(count):
        found = dot_nt(out_ref[j * rows : (j + 1) * rows, :], weight_ref[...])
        if j == 0:
            own_ref[...] = found
        else:
            put_pieces(piece_refs, count, j, found)


def self_backward(triples, grads, weight, head_size, deps=()):
    count = len(grads)
    total, rows, columns = triples.shape[0], grads[0].shape[0], weight.shape[0]
    step = min(256, rows)
    found = call(
        functools.partial(self_backward_kernel, count, head_size, step),
        [(triples.shape, BF16), ((rows, columns), F32)] + piece_shapes(count, rows, columns),
        [pltpu.VMEM((total, head_size), F32), pltpu.VMEM((total, head_size), F32)],
        32,
        triples,
        *grads,
        weight,
        deps=deps,
    )
    return found[0], found[1], list(found[2:])


def fill_corner(count, matrix_refs, scalars_ref, corner_ref):
    if len(matrix_refs) == count:
        return list(matrix_refs)
    odd = scalars_ref[2 * count]
    half = matrix_refs[-1].shape[0]
    corner_ref[pl.ds(pl.multiple_of(odd * half, half), half), :] = matrix_refs[-2][...]
    corner_ref[pl.ds(pl.multiple_of((1 - odd) * half, half), half), :] = matrix_refs[-1][...]
    return list(matrix_refs[:-2]) + [corner_ref]


def corner_scratch(count, matrices):
    rows, columns = matrices[0].shape
    return pltpu.VMEM((rows, columns) if len(matrices) > count else (16, 128), BF16)


def fill_pairs(count, pair_refs, pairs_ref):
    padded = pairs_ref.shape[1]
    place = 0
    for ref in pair_refs:
        j, low = divmod(place, padded)
        pairs_ref[j, low : low + ref.shape[0], :] = ref[...]
        place += ref.shape[0]


def middle_forward_kernel(count, matrix_parts, pair_parts, head_size, scalars_ref, *refs):
    mixed_refs, refs = refs[:count], refs[count:]
    matrix_refs, refs = refs[:matrix_parts], refs[matrix_parts:]
    pair_refs, refs = refs[:pair_parts], refs[pair_parts:]
    hidden_ref, gains_ref = refs[:2]
    (self_ref, after_self_ref, norm_ref, queries_ref, cross_ref, after_cross_ref) = refs[2:8]
    mlp_refs = refs[8:-4]
    wide_ref, narrow_ref, corner_ref, pairs_ref = refs[-4:]
    width = mixed_refs[0].shape[1]
    stride = matrix_refs[0].shape[1] // 3
    matrices = fill_corner(count, matrix_refs, scalars_ref, corner_ref)
    fill_pairs(count, pair_refs, pairs_ref)
    order = [scalars_ref[i] for i in range(count)]
    relative = [scalars_ref[count + j] for j in range(count)]
    length = scalars_ref[2 * count + 1]
    spans = [slice(a * width, (a + 1) * width) for a in range(count)]

    for j in range(count):
        narrow_ref[relative[j]] = mixed_refs[j][...]
    for a in range(count):
        self_ref[:, spans[a]] = narrow_ref[a]
    tokens = self_ref[...]
    for i in range(count):
        wide_ref[order[i]] = dot_nn(tokens, matrices[i][:, :width])
    for a in range(count):
        after_self_ref[:, spans[a]] = hidden_ref[:, spans[a]].astype(F32) + wide_ref[a]
    normed = (norm_stats(after_self_ref[...])[0] * gains_ref[1:2, :]).astype(BF16)
    norm_ref[...] = normed
    for i in range(count):
        found = dot_nn(normed, matrices[i][:, stride : stride + width])
        queries_ref[order[i] ^ relative[0]] = found.astype(BF16)

    factor = LOG2_E / math.sqrt(head_size)
    keys_rows = pairs_ref.shape[1]
    valid = lax.broadcasted_iota(jnp.int32, (1, keys_rows), 1) < length
    pair_stride = pairs_ref.shape[2] // 2
    for j in range(count):
        for h in range(width // head_size):
            at = slice(h * head_size, (h + 1) * head_size)
            values_at = slice(pair_stride + h * head_size, pair_stride + (h + 1) * head_size)
            scores = dot_nt(queries_ref[j, :, at], pairs_ref[j, :, at])
            scores = jnp.where(valid, scores, -1e30)
            top = jnp.max(scores, axis=1, keepdims=True)
            weights = jnp.exp2((scores - top) * factor)
            total = jnp.sum(weights, axis=1, keepdims=True)
            mixed = dot_nn(weights.astype(BF16), pairs_ref[j, :, values_at]) * (1.0 / total)
            narrow_ref[relative[j], :, at] = mixed.astype(BF16)
    for a in range(count):
        cross_ref[:, spans[a]] = narrow_ref[a]
    tokens = cross_ref[...]
    for i in range(count):
        wide_ref[order[i]] = dot_nn(tokens, matrices[i][:, 2 * stride : 2 * stride + width])
    for a in range(count):
        after_cross_ref[:, spans[a]] = after_self_ref[:, spans[a]] + wide_ref[a]
    mlp_norm = norm_stats(after_cross_ref[...])[0] * gains_ref[2:3, :]
    for ref, (low, high) in zip(mlp_refs, cuts(count, mlp_norm.shape[0])):
        ref[...] = mlp_norm[low:high].astype(BF16)


def pairs_scratch(count, pairs):
    return pltpu.VMEM((count, sum(m.shape[0] for m in pairs) // count, pairs[0].shape[1]), BF16)


def middle_forward(scalars, mixed, matrices, pairs, hidden, gains, head_size, deps=()):
    count = len(mixed)
    rows, columns = hidden.shape
    width = columns // count
    found = call(
        functools.partial(
            middle_forward_kernel, count, len(matrices), len(pairs), head_size
        ),
        [
            ((rows, columns), BF16),
            ((rows, columns), F32),
            ((rows, columns), BF16),
            ((count, rows, width), BF16),
            ((rows, columns), BF16),
            ((rows, columns), F32),
        ]
        + [((high - low, columns), BF16) for low, high in cuts(count, rows)],
        [
            pltpu.VMEM((count, rows, width), F32),
            pltpu.VMEM((count, rows, width), BF16),
            corner_scratch(count, matrices),
            pairs_scratch(count, pairs),
        ],
        23,
        *mixed,
        *matrices,
        *pairs,
        hidden,
        gains,
        scalars=scalars,
        deps=deps,
    )
    return list(found[:6]) + [list(found[6:])]


def middle_backward_kernel(count, matrix_parts, pair_parts, terms, head_size, scalars_ref, *refs):
    matrix_refs, refs = refs[:matrix_parts], refs[matrix_parts:]
    pair_refs, refs = refs[:pair_parts], refs[pair_parts:]
    term_refs, refs = refs[:terms], refs[terms:]
    grad_out_ref, after_cross_ref, after_self_ref, queries_ref, gains_ref = refs[:5]
    out_ref, self_branch_ref, query_branch_ref, cross_branch_ref, gain_ref = refs[5:10]
    mixed_grad_refs, refs = refs[10 : 10 + count], refs[10 + count :]
    own_pairs_ref, pair_grad_refs = refs[0], refs[1:-6]
    wide_ref, narrow_ref, query_ref, corner_ref, pairs_ref, pair_total_ref = refs[-6:]
    width = queries_ref.shape[2]
    stride = matrix_refs[0].shape[1] // 3
    matrices = fill_corner(count, matrix_refs, scalars_ref, corner_ref)
    fill_pairs(count, pair_refs, pairs_ref)
    order = [scalars_ref[i] for i in range(count)]
    relative = [scalars_ref[count + j] for j in range(count)]
    length = scalars_ref[2 * count + 1]
    spans = [slice(a * width, (a + 1) * width) for a in range(count)]

    def back(branch_ref, group):
        columns = slice(group * stride, group * stride + width)
        total = dot_nt(branch_ref[0], matrices[0][:, columns])
        for i in range(1, count):
            total = total + dot_nt(branch_ref[i], matrices[i][:, columns])
        return total

    def divide(values):
        for a in range(count):
            narrow_ref[a] = values[:, spans[a]].astype(BF16)

    grad, grad_gain = norm_back(
        after_cross_ref[...], gains_ref[2:3, :], add_terms(count, term_refs)
    )
    gain_ref[1:2, :] = grad_gain
    wide_ref[...] = grad + grad_out_ref[...].astype(F32)
    divide(wide_ref[...])
    for i in range(count):
        cross_branch_ref[i] = narrow_ref[order[i]]
    divide(back(cross_branch_ref, 2))

    keys_rows = pairs_ref.shape[1]
    valid = lax.broadcasted_iota(jnp.int32, (keys_rows, 1), 0) < length
    pair_stride = pairs_ref.shape[2] // 2
    if pair_stride > width:
        for g in range(2):
            pair_total_ref[:, g * pair_stride + width : (g + 1) * pair_stride] = jnp.zeros(
                (keys_rows, pair_stride - width), F32
            )
    for j in range(count):
        for h in range(width // head_size):
            at = slice(h * head_size, (h + 1) * head_size)
            values_at = slice(pair_stride + h * head_size, pair_stride + (h + 1) * head_size)
            grad_q, grad_k, grad_v = attention_back(
                queries_ref[j, :, at],
                pairs_ref[j, :, at],
                pairs_ref[j, :, values_at],
                narrow_ref[relative[j], :, at],
                valid,
                head_size,
            )
            query_ref[j, :, at] = grad_q.astype(BF16)
            pair_total_ref[:, at] = grad_k
            pair_total_ref[:, values_at] = grad_v
        if j == 0:
            own_pairs_ref[...] = pair_total_ref[...]
        else:
            put_pieces(pair_grad_refs, count, j, pair_total_ref[...])
    for i in range(count):
        query_branch_ref[i] = query_ref[order[i] ^ relative[0]]
    grad, grad_gain = norm_back(after_self_ref[...], gains_ref[1:2, :], back(query_branch_ref, 1))
    gain_ref[0:1, :] = grad_gain
    out_ref[...] = grad + wide_ref[...]
    divide(out_ref[...])
    for i in range(count):
        self_branch_ref[i] = narrow_ref[order[i]]
    divide(back(self_branch_ref, 0))
    for j in range(count):
        mixed_grad_refs[j][...] = narrow_ref[relative[j]]


def middle_backward(
    scalars, matrices, pairs, terms, grad_out, after_cross, after_self, queries, gains, head_size, deps=()
):
    count, rows, width = queries.shape
    columns = count * width
    branch = ((count, rows, width), BF16)
    text = pairs_scratch(count, pairs)
    keys_rows, pair_columns = text.shape[1:]
    found = call(
        functools.partial(
            middle_backward_kernel, count, len(matrices), len(pairs), len(terms), head_size
        ),
        [((rows, columns), F32), branch, branch, branch, ((2, columns), F32)]
        + [((rows, width), BF16)] * count
        + [((keys_rows, pair_columns), F32)]
        + piece_shapes(count, keys_rows, pair_columns),
        [
            pltpu.VMEM((rows, columns), F32),
            pltpu.VMEM((count, rows, width), BF16),
            pltpu.VMEM((count, rows, width), BF16),
            corner_scratch(count, matrices),
            text,
            pltpu.VMEM((keys_rows, pair_columns), F32),
        ],
        37,
        *matrices,
        *pairs,
        *terms,
        grad_out,
        after_cross,
        after_self,
        queries,
        gains,
        scalars=scalars,
        deps=deps,
    )
    found = list(found)
    return found[:5] + [found[5 : 5 + count], found[5 + count], found[6 + count :]]


def mlp_forward_kernel(count, parts, *refs):
    part_refs, refs = refs[:parts], refs[parts:]
    up_ref, down_ref, rows_ref, up_rows_ref, activated_ref, own_ref = refs[:6]
    piece_refs = refs[6:]
    start = 0
    for ref in part_refs:
        rows_ref[start : start + ref.shape[0], :] = ref[...]
        start += ref.shape[0]
    rows = start // count
    for j in range(count - 1, -1, -1):
        at = slice(j * rows, (j + 1) * rows)
        values = dot_nn(rows_ref[at, :], up_ref[...])
        up_rows_ref[at, :] = values
        inner = GELU_SCALE * (values + 0.044715 * (values * values * values))
        activated_ref[at, :] = (0.5 * values * (1.0 + jnp.tanh(inner))).astype(BF16)
        found = dot_nn(activated_ref[at, :], down_ref[...])
        if j == 0:
            own_ref[...] = found
        else:
            put_pieces(piece_refs, count, j, found)


def mlp_forward(parts, up, down, count, deps=()):
    total, columns, hidden = sum(m.shape[0] for m in parts), up.shape[0], up.shape[1]
    rows = total // count
    found = call(
        functools.partial(mlp_forward_kernel, count, len(parts)),
        [
            ((total, columns), BF16),
            ((total, hidden), F32),
            ((total, hidden), BF16),
            ((rows, columns), F32),
        ]
        + piece_shapes(count, rows, columns),
        [],
        22,
        *parts,
        up,
        down,
        deps=deps,
    )
    return list(found[:4]) + [list(found[4:])]


def mlp_backward_kernel(count, parts, *refs):
    part_refs, refs = refs[:parts], refs[parts:]
    up_rows_ref, up_ref, down_ref, rows_ref, grad_up_ref, own_ref = refs[:6]
    piece_refs = refs[6:]
    start = 0
    for ref in part_refs:
        rows_ref[start : start + ref.shape[0], :] = ref[...]
        start += ref.shape[0]
    rows = start // count
    for j in range(count - 1, -1, -1):
        at = slice(j * rows, (j + 1) * rows)
        grad = dot_nt(rows_ref[at, :], down_ref[...])
        values = up_rows_ref[at, :]
        square = values * values
        bent = jnp.tanh(GELU_SCALE * (values + 0.044715 * (values * square)))
        slope = 0.5 * (1.0 + bent) + 0.5 * values * (1.0 - bent * bent) * (
            GELU_SCALE * (1.0 + 3.0 * 0.044715 * square)
        )
        grad_up_ref[at, :] = (grad * slope).astype(BF16)
        found = dot_nt(grad_up_ref[at, :], up_ref[...])
        if j == 0:
            own_ref[...] = found
        else:
            put_pieces(piece_refs, count, j, found)


def mlp_backward(parts, up_rows, up, down, count, deps=()):
    total, columns, hidden = sum(m.shape[0] for m in parts), up.shape[0], up.shape[1]
    rows = total // count
    found = call(
        functools.partial(mlp_backward_kernel, count, len(parts)),
        [((total, columns), BF16), ((total, hidden), BF16), ((rows, columns), F32)]
        + piece_shapes(count, rows, columns),
        [],
        22,
        *parts,
        up_rows,
        up,
        down,
        deps=deps,
    )
    return list(found[:3]) + [list(found[3:])]


def outer_kernel(count, groups, half, scalars_ref, *refs):
    rows_refs, branch_refs, refs = refs[:groups], refs[groups : 2 * groups], refs[2 * groups :]
    out_refs, turned_ref = refs[:-1], refs[-1]
    width = branch_refs[0].shape[2]
    stride = padded_width(width)
    odd = scalars_ref[2 * count]
    for g in range(groups):
        at = slice(g * stride, g * stride + width)
        turned_ref[...] = rows_refs[g][...].T
        out_refs[0][:, at] = dot_nn(turned_ref[...], branch_refs[g][0]).astype(BF16)
        for i in range(1, count):
            if not half:
                out_refs[i][:, at] = dot_nn(turned_ref[...], branch_refs[g][i]).astype(BF16)
                continue
            for k in range(2):
                low = pl.multiple_of((odd if k == 0 else 1 - odd) * half, half)
                found = dot_nn(turned_ref[pl.ds(low, half), :], branch_refs[g][i])
                out_refs[2 * i - 1 + k][:, at] = found.astype(BF16)
    if stride > width:
        for ref in out_refs:
            for g in range(groups):
                ref[:, g * stride + width : (g + 1) * stride] = jnp.zeros(
                    (ref.shape[0], stride - width), BF16
                )


def outer(scalars, rows, branches, deps=()):
    count, tokens, width = branches[0].shape
    groups, columns = len(rows), rows[0].shape[1]
    stride = padded_width(width)
    half = columns // 2 if count == 4 else 0
    shapes = [((columns, groups * stride), BF16)]
    if half:
        shapes += [((half, groups * stride), BF16)] * (2 * (count - 1))
    else:
        shapes = shapes * count
    return list(
        call(
            functools.partial(outer_kernel, count, groups, half),
            shapes,
            [pltpu.VMEM((columns, tokens), BF16)],
            3.5 * groups,
            *rows,
            *branches,
            scalars=scalars,
            deps=deps,
        )
    )


def join_kernel(count, scalars_ref, own_ref, mine_ref, other_ref, out_ref):
    odd = scalars_ref[2 * count]
    half = mine_ref.shape[0]
    for ref, place in ((mine_ref, odd), (other_ref, 1 - odd)):
        at = pl.ds(pl.multiple_of(place * half, half), half)
        out_ref[at, :] = (own_ref[at, :].astype(F32) + ref[...].astype(F32)).astype(BF16)


def join_halves(scalars, own, mine, other):
    count = lax.axis_size("seq")
    (found,) = call(
        functools.partial(join_kernel, count),
        [(own.shape, BF16)],
        [],
        4,
        own,
        mine,
        other,
        scalars=scalars,
    )
    return found


def joined_stats(first, second):
    count = first.shape[1] + second.shape[1]
    mean = (jnp.sum(first, axis=1, keepdims=True) + jnp.sum(second, axis=1, keepdims=True)) / count
    first, second = first - mean, second - mean
    var = (
        jnp.sum(first * first, axis=1, keepdims=True)
        + jnp.sum(second * second, axis=1, keepdims=True)
    ) / count
    scale = lax.rsqrt(var + NORM_EPSILON)
    return first * scale, second * scale, scale


def skip_forward_kernel(count, matrix_parts, terms, scalars_ref, *refs):
    matrix_refs, refs = refs[:matrix_parts], refs[matrix_parts:]
    term_refs, refs = refs[:terms], refs[terms:]
    residual_ref, second_ref, gains_ref, next_ref, shift_ref = refs[:5]
    first_ref, joined_ref, out_ref = refs[5:8]
    norm_refs, (wide_ref, corner_ref) = refs[8:-2], refs[-2:]
    rows, columns = first_ref.shape
    width = columns // count
    matrices = fill_corner(count, matrix_refs, scalars_ref, corner_ref)
    first_ref[...] = residual_ref[...] + add_terms(count, term_refs)
    first, second, _ = joined_stats(first_ref[...], second_ref[...].astype(F32))
    joined_ref[:, :columns] = (first * gains_ref[0:1, :]).astype(BF16)
    joined_ref[:, columns:] = (second * gains_ref[1:2, :]).astype(BF16)
    joined = joined_ref[...]
    for i in range(count):
        wide_ref[scalars_ref[i]] = dot_nn(joined, matrices[i][:, :width])
    for a in range(count):
        out_ref[:, a * width : (a + 1) * width] = wide_ref[a]
    normed = norm_stats(out_ref[...])[0] * next_ref[0:1, :] + shift_ref[...]
    for ref, (low, high) in zip(norm_refs, cuts(count, rows)):
        ref[...] = normed[low:high].astype(BF16)


def skip_forward(scalars, matrices, terms, residual, second, gains, next_gains, shift, deps=()):
    rows, columns = residual.shape
    count = lax.axis_size("seq")
    found = call(
        functools.partial(skip_forward_kernel, count, len(matrices), len(terms)),
        [((rows, columns), F32), ((rows, 2 * columns), BF16), ((rows, columns), F32)]
        + [((high - low, columns), BF16) for low, high in cuts(count, rows)],
        [pltpu.VMEM((count, rows, columns // count), F32), corner_scratch(count, matrices)],
        11,
        *matrices,
        *terms,
        residual,
        second,
        gains,
        next_gains,
        shift[None],
        scalars=scalars,
        deps=deps,
    )
    return list(found[:3]) + [list(found[3:])]


def skip_backward_kernel(count, matrix_parts, terms, scalars_ref, *refs):
    matrix_refs, refs = refs[:matrix_parts], refs[matrix_parts:]
    term_refs, refs = refs[:terms], refs[terms:]
    hidden_ref, next_ref, residual_ref, first_ref, second_ref, gains_ref = refs[:6]
    branch_ref, grad_first_ref, grad_second_ref, vectors_ref = refs[6:10]
    half_refs, (narrow_ref, corner_ref) = refs[10:-2], refs[-2:]
    rows, columns = first_ref.shape
    width = columns // count
    matrices = fill_corner(count, matrix_refs, scalars_ref, corner_ref)
    grad_norm = add_terms(count, term_refs)
    vectors_ref[0:1, :] = jnp.sum(grad_norm, axis=0, keepdims=True)
    grad, grad_gain = norm_back(hidden_ref[...], next_ref[0:1, :], grad_norm)
    vectors_ref[1:2, :] = grad_gain
    grad = grad + residual_ref[...]
    for a in range(count):
        narrow_ref[a] = grad[:, a * width : (a + 1) * width].astype(BF16)
    for i in range(count):
        branch_ref[i] = narrow_ref[scalars_ref[i]]

    def back(at):
        total = dot_nt(branch_ref[0], matrices[0][at, :width])
        for i in range(1, count):
            total = total + dot_nt(branch_ref[i], matrices[i][at, :width])
        return total

    grad_first_ref[...] = back(slice(0, columns))
    grad_second_ref[...] = back(slice(columns, 2 * columns))
    first, second, scale = joined_stats(first_ref[...], second_ref[...].astype(F32))
    vectors_ref[2:3, :] = jnp.sum(grad_first_ref[...] * first, axis=0, keepdims=True)
    vectors_ref[3:4, :] = jnp.sum(grad_second_ref[...] * second, axis=0, keepdims=True)
    grad_first = grad_first_ref[...] * gains_ref[0:1, :]
    grad_second = grad_second_ref[...] * gains_ref[1:2, :]
    mean = (
        jnp.sum(grad_first, axis=1, keepdims=True) + jnp.sum(grad_second, axis=1, keepdims=True)
    ) / (2 * columns)
    inner = (
        jnp.sum(grad_first * first, axis=1, keepdims=True)
        + jnp.sum(grad_second * second, axis=1, keepdims=True)
    ) / (2 * columns)
    grad_first_ref[...] = scale * (grad_first - mean - first * inner)
    grad_second_ref[...] = scale * (grad_second - mean - second * inner)
    for ref, (low, high) in zip(half_refs, cuts(count, rows)):
        ref[...] = grad_first_ref[low:high, :].astype(BF16)


def skip_backward(
    scalars, matrices, terms, hidden, next_gains, residual, first, second, gains, deps=()
):
    rows, columns = first.shape
    count = lax.axis_size("seq")
    narrow = (count, rows, columns // count)
    found = call(
        functools.partial(skip_backward_kernel, count, len(matrices), len(terms)),
        [
            (narrow, BF16),
            ((rows, columns), F32),
            ((rows, columns), F32),
            ((4, columns), F32),
        ]
        + [((high - low, columns), BF16) for low, high in cuts(count, rows)],
        [pltpu.VMEM(narrow, BF16), corner_scratch(count, matrices)],
        15,
        *matrices,
        *terms,
        hidden,
        next_gains,
        residual,
        first,
        second,
        gains,
        scalars=scalars,
        deps=deps,
    )
    return list(found[:4]) + [list(found[4:])]


def open_backward_kernel(count, terms, *refs):
    term_refs, refs = refs[:terms], refs[terms:]
    hidden_ref, gains_ref, residual_ref, out_ref, vectors_ref = refs
    grad_norm = add_terms(count, term_refs)
    vectors_ref[0:1, :] = jnp.sum(grad_norm, axis=0, keepdims=True)
    grad, grad_gain = norm_back(hidden_ref[...].astype(F32), gains_ref[0:1, :], grad_norm)
    vectors_ref[1:2, :] = grad_gain
    out_ref[...] = grad + residual_ref[...]


def open_backward(terms, hidden, gains, residual, deps=()):
    count = lax.axis_size("seq")
    return call(
        functools.partial(open_backward_kernel, count, len(terms)),
        [(residual.shape, F32), ((2, residual.shape[1]), F32)],
        [],
        5,
        *terms,
        hidden,
        gains,
        residual,
        deps=deps,
    )


def close_kernel(count, terms, *refs):
    refs[terms + 1][...] = (refs[terms][...] + add_terms(count, refs[:terms])).astype(BF16)


def close_forward(terms, residual, deps=()):
    count = lax.axis_size("seq")
    (found,) = call(
        functools.partial(close_kernel, count, len(terms)),
        [(residual.shape, BF16)],
        [],
        3,
        *terms,
        residual,
        deps=deps,
    )
    return found


def settle_kernel(count, parts, groups, pieces, width, scalars_ref, *refs):
    block_refs, refs = refs[:parts], refs[parts:]
    out_refs, stack_ref = refs[-pieces - 1 : -1], refs[-1]
    stride = stack_ref.shape[2] // (pieces * groups)
    for j in range(count):
        owner = scalars_ref[count + j]
        if j == count - 1 and parts > count:
            cut = block_refs[j].shape[0]
            stack_ref[owner, :cut] = block_refs[j][...]
            stack_ref[owner, cut:] = block_refs[j + 1][...]
        else:
            stack_ref[owner] = block_refs[j][...]
    for p in range(pieces):
        for g in range(groups):
            for a in range(count):
                low = (p * groups + g) * stride
                at = (g * count + a) * width
                out_refs[p][0, :, at : at + width] = stack_ref[a, :, low : low + width].astype(F32)


def settle_rows_kernel(count, parts, scalars_ref, *refs):
    block_refs, out_ref = refs[:parts], refs[-1]
    rows = block_refs[0].shape[0]
    for j in range(count):
        low = pl.multiple_of(scalars_ref[count + j] * rows, rows)
        if j == count - 1 and parts > count:
            cut = block_refs[j].shape[0]
            out_ref[0, pl.ds(low, cut), :] = block_refs[j][...].astype(F32)
            out_ref[0, pl.ds(low + cut, rows - cut), :] = block_refs[j + 1][...].astype(F32)
        else:
            out_ref[0, pl.ds(low, rows), :] = block_refs[j][...].astype(F32)


def settle_call(kernel, scalars, blocks, shape, pieces, layer, layer_count, before, scratch):
    held = [] if before is None else list(before)
    inputs = [pl.BlockSpec(memory_space=pltpu.VMEM)] * len(blocks)
    inputs += [pl.BlockSpec(memory_space=pl.ANY)] * len(held)
    found = pl.pallas_call(
        kernel,
        grid=(1,),
        out_shape=[jax.ShapeDtypeStruct((layer_count,) + shape, F32)] * pieces,
        in_specs=[pl.BlockSpec(memory_space=pltpu.SMEM)] + inputs,
        out_specs=[pl.BlockSpec((1,) + shape, lambda i: (layer, 0, 0))] * pieces,
        scratch_shapes=scratch,
        input_output_aliases={1 + len(blocks) + i: i for i in range(len(held))},
        compiler_params=pltpu.CompilerParams(vmem_limit_bytes=VMEM_LIMIT),
        cost_estimate=pl.CostEstimate(flops=4_000_000_000, bytes_accessed=1000, transcendentals=0),
    )(scalars, *blocks, *held)
    return list(found)


def settle(scalars, blocks, groups, pieces, width, layer, layer_count, before=None):
    count = lax.axis_size("seq")
    rows, columns = blocks[0].shape
    return settle_call(
        functools.partial(settle_kernel, count, len(blocks), groups, pieces, width),
        scalars,
        blocks,
        (rows, count * groups * width),
        pieces,
        layer,
        layer_count,
        before,
        [pltpu.VMEM((count, rows, columns), BF16)],
    )


def settle_rows(scalars, blocks, layer, layer_count, before=None):
    count = lax.axis_size("seq")
    rows, columns = blocks[0].shape
    return settle_call(
        functools.partial(settle_rows_kernel, count, len(blocks)),
        scalars,
        blocks,
        (count * rows, columns),
        1,
        layer,
        layer_count,
        before,
        [],
    )


def swap_seq(block, bits):
    seq_count = lax.axis_size("seq")
    return lax.ppermute(block, "seq", [(i, i ^ bits) for i in range(seq_count)])


def swap_fsdp(block, bits):
    fsdp_count = lax.axis_size("fsdp")
    return lax.ppermute(block, "fsdp", [(i, i ^ bits) for i in range(fsdp_count)])


def swap_core(block):
    return swap_fsdp(block, 1)


def swap_by_core(block, even_bits, odd_bits):
    seq_count, fsdp_count = lax.axis_size("seq"), lax.axis_size("fsdp")
    pairs = []
    for s in range(seq_count):
        for f in range(fsdp_count):
            other = s ^ (odd_bits if f % 2 else even_bits)
            pairs.append((s * fsdp_count + f, other * fsdp_count + f))
    return lax.ppermute(block, ("seq", "fsdp"), pairs)


def add_bf16(*terms):
    total = terms[0].astype(F32)
    for term in terms[1:]:
        total = total + term.astype(F32)
    return total.astype(BF16)


def halves_of(block):
    return [block[low:high] for low, high in cuts(lax.axis_size("seq"), block.shape[0])]


def gather_halves(halves):
    seq_count = lax.axis_size("seq")
    if seq_count != 4:
        return [halves[0]] + [swap_seq(halves[0], j) for j in range(1, seq_count)]
    top, bottom = halves
    y_top, x_bottom = swap_seq(top, 2), swap_seq(bottom, 1)
    x_top, y_bottom = swap_seq(top, 1), swap_seq(bottom, 2)
    return [top, bottom, x_top, x_bottom, y_top, y_bottom, swap_seq(y_top, 1), swap_seq(x_bottom, 2)]


def scatter_parts(own, pieces):
    seq_count = lax.axis_size("seq")
    if seq_count != 4:
        return [own] + [swap_seq(m, j + 1) for j, m in enumerate(pieces)]
    x_top, x_bottom, y_top, y_bottom, corner_top, corner_bottom = pieces
    by_x, by_y = swap_seq(corner_top, 1), swap_seq(corner_bottom, 2)
    from_x_top, from_y_bottom = swap_seq(x_top, 1), swap_seq(y_bottom, 2)
    from_y_top = swap_seq(add_bf16(y_top, by_x), 2)
    from_x_bottom = swap_seq(add_bf16(x_bottom, by_y), 1)
    return [own, from_x_top, from_x_bottom, from_y_top, from_y_bottom]


def exchange_rel(blocks):
    return [blocks[0]] + [swap_seq(blocks[j], j) for j in range(1, len(blocks))]


def gather_parts(block):
    seq_count = lax.axis_size("seq")
    if seq_count != 4:
        return [block] + [swap_seq(block, j) for j in range(1, seq_count)]
    cut = cut_of(block.shape[0])
    from_x, from_y = swap_seq(block, 1), swap_seq(block, 2)
    return [block, from_x, from_y, swap_seq(from_y[:cut], 1), swap_seq(from_x[cut:], 2)]


def list_order():
    s, seq_count = lax.axis_index("seq"), lax.axis_size("seq")
    if seq_count != 4:
        return [s ^ j for j in range(seq_count)]
    odd = lax.axis_index("fsdp") % 2
    return [s, s ^ (1 + odd), s ^ (2 - odd), s ^ 3]


def spread(block):
    seq_count = lax.axis_size("seq")
    if seq_count != 4:
        return [block] + [swap_seq(block, j) for j in range(1, seq_count)]
    odd = lax.axis_index("fsdp") % 2
    half = block.shape[0] // 2
    first = swap_by_core(block, 1, 2)
    part = swap_by_core(lax.dynamic_slice_in_dim(first, odd * half, half, 0), 2, 1)
    return [block, first, swap_core(first), part, swap_core(part)]


def unspread(scalars, blocks):
    seq_count = lax.axis_size("seq")
    if seq_count != 4:
        return add_bf16(blocks[0], *[swap_seq(blocks[j], j) for j in range(1, seq_count)])
    own, first_mine, first_other, second_mine, second_other, corner_mine, corner_other = blocks
    passed = swap_by_core(add_bf16(corner_mine, swap_core(corner_other)), 2, 1)
    other = swap_by_core(add_bf16(first_other, swap_core(second_mine)), 1, 2)
    mine = swap_by_core(add_bf16(first_mine, swap_core(second_other), passed), 1, 2)
    return join_halves(scalars, own, mine, other)


def own_part(matrix, groups, padded):
    s, seq_count = lax.axis_index("seq"), lax.axis_size("seq")
    width = matrix.shape[1] // (groups * seq_count)
    parts = [
        jnp.pad(
            lax.dynamic_slice_in_dim(matrix, (g * seq_count + s) * width, width, 1),
            ((0, 0), (0, padded - width)),
        )
        for g in range(groups)
    ]
    return jnp.concatenate(parts, axis=1)


def gather_fsdp(shard):
    return lax.all_gather(shard, "fsdp", axis=0, tiled=True)


def scatter_fsdp(full):
    return lax.psum_scatter(full.astype(BF16), "fsdp", scatter_dimension=0, tiled=True)


def text_pairs(text_rows, kv_part):
    return gather_halves([dot_nn(m, kv_part).astype(BF16) for m in halves_of(text_rows)])


def layer_forward(parts, hidden, scalars, gains, shift, pairs, weights, normed, deps):
    qkv_part, square_parts, _, up_part, down_part = weights
    seq_count = lax.axis_size("seq")
    tok_rows, model_width = hidden.shape
    head_size, width = model_width // H, model_width // seq_count
    first_all, triples, mixed = self_forward(
        parts, qkv_part, gains, shift, head_size, seq_count, width, normed, deps[0]
    )
    self_tokens, after_self, cross_norm, queries, cross_tokens, after_cross, mlp_halves = (
        middle_forward(
            scalars, exchange_rel(mixed), square_parts, pairs, hidden, gains, head_size, deps[1]
        )
    )
    mlp_all, up_rows, activated, own, pieces = mlp_forward(
        gather_halves(mlp_halves), up_part, down_part, seq_count, deps[2]
    )
    saved = (
        first_all,
        triples,
        self_tokens,
        after_self,
        cross_norm,
        queries,
        cross_tokens,
        after_cross,
        mlp_all,
        up_rows,
        activated,
    )
    return (scatter_parts(own, pieces), saved)


def layer_backward(out_parts, grad_out, saved, scalars, gains, text_rows, pairs, weights, deps):
    qkv_part, square_parts, kv_part, up_part, down_part = weights
    (
        first_all,
        triples,
        self_tokens,
        after_self,
        cross_norm,
        queries,
        cross_tokens,
        after_cross,
        mlp_all,
        up_rows,
        activated,
    ) = saved
    seq_count = lax.axis_size("seq")
    head_size = after_self.shape[1] // H

    out_all, grad_up_rows, own, pieces = mlp_backward(
        out_parts, up_rows, up_part, down_part, seq_count, deps[0]
    )
    terms = scatter_parts(own, pieces)
    grad_down = dot_tn(activated, out_all).astype(BF16)
    grad_up = dot_tn(mlp_all, grad_up_rows).astype(BF16)
    (
        grad_after_self,
        self_branch,
        query_branch,
        cross_branch,
        gain_grads,
        mixed_grads,
        own_pairs,
        pair_pieces,
    ) = middle_backward(
        scalars,
        square_parts,
        pairs,
        terms,
        grad_out,
        after_cross,
        after_self,
        queries,
        gains,
        head_size,
        (grad_down, grad_up) + deps[1],
    )
    squares = outer(
        scalars,
        [self_tokens, cross_norm, cross_tokens],
        [self_branch, query_branch, cross_branch],
    )
    grad_triples, own, pieces = self_backward(
        triples, exchange_rel(mixed_grads), qkv_part, head_size, (squares[0],) + deps[2]
    )
    terms = scatter_parts(own, pieces)
    grad_qkv = dot_tn(first_all, grad_triples).astype(BF16)
    pair_terms = scatter_parts(own_pairs, pair_pieces)
    if seq_count == 4:
        grad_pairs = jnp.concatenate(
            [
                add_bf16(pair_terms[0][low:high], pair_terms[1 + k], pair_terms[3 + k])
                for k, (low, high) in enumerate(cuts(seq_count, text_rows.shape[0]))
            ]
        )
    else:
        grad_pairs = add_bf16(*pair_terms)
    grad_text = dot_nt(grad_pairs, kv_part)
    shards = (
        scatter_fsdp(grad_qkv),
        scatter_fsdp(unspread(scalars, squares)),
        scatter_fsdp(dot_tn(text_rows, grad_pairs)),
        scatter_fsdp(grad_up),
        scatter_fsdp(grad_down),
    )
    return (terms, grad_after_self, gain_grads, grad_text, shards, grad_qkv)


def gather_block(layer, qkv, query, text_kv, self_out, cross_out, up, down):
    s, seq_count = lax.axis_index("seq"), lax.axis_size("seq")
    fsdp_count = lax.axis_size("fsdp")
    padded = padded_width(query.shape[2] // seq_count)
    squares = jnp.concatenate(
        [own_part(m[layer], 1, padded) for m in (self_out, query, cross_out)], axis=1
    )
    rows = down.shape[1] // seq_count
    return (
        gather_fsdp(own_part(qkv[layer], 3, padded)),
        spread(gather_fsdp(squares)),
        gather_fsdp(own_part(text_kv[layer], 2, padded)),
        gather_fsdp(own_part(up[layer], fsdp_count, up.shape[2] // (fsdp_count * seq_count))),
        gather_fsdp(lax.dynamic_slice_in_dim(down[layer], s * rows, rows, 0)),
    )


def finish_block(scalars, shards, width, layer, before):
    qkv_shard, square_shard, kv_shard, up_shard, down_shard = shards
    fsdp_count = lax.axis_size("fsdp")
    if before is None:
        before = [None] * 5
    up_width = up_shard.shape[1] // fsdp_count
    return [
        settle(scalars, gather_parts(qkv_shard), 3, 1, width, layer, 2, before[0]),
        settle(scalars, gather_parts(square_shard), 1, 3, width, layer, 2, before[1]),
        settle(scalars, gather_parts(kv_shard), 2, 1, width, layer, 2, before[2]),
        settle(scalars, gather_parts(up_shard), fsdp_count, 1, up_width, layer, 2, before[3]),
        settle_rows(scalars, gather_parts(down_shard), layer, 2, before[4]),
    ]


def sum_vectors(vectors):
    bits = 1
    while bits < lax.axis_size("seq"):
        vectors = vectors + swap_seq(vectors, bits)
        bits *= 2
    found, bits = vectors[None], 1
    while bits < lax.axis_size("fsdp"):
        found = jnp.concatenate([found, swap_fsdp(found, bits)], axis=0)
        bits *= 2
    return found


def body(
    latents,
    skip_input,
    text_tokens,
    text_lengths,
    condition,
    cotangent,
    mod_weight,
    norm_gains,
    qkv_weight,
    query_weight,
    text_kv_weight,
    self_out_weight,
    cross_out_weight,
    up_weight,
    down_weight,
    skip_gain,
    skip_weight,
):
    seq_count, fsdp_count = lax.axis_size("seq"), lax.axis_size("fsdp")
    s, f = lax.axis_index("seq"), lax.axis_index("fsdp")
    _, tok_rows, model_width = latents.shape
    width = model_width // seq_count
    shard_rows = mod_weight.shape[1]
    text_count = text_tokens.shape[1]
    padded = -(-text_count // 32) * 32
    text_rows = jnp.pad(text_tokens[0], ((0, padded - text_count), (0, 0)))
    scalars = jnp.stack(
        [*list_order(), *[s ^ j for j in range(seq_count)], f % 2, text_lengths[0]]
    ).astype(jnp.int32)

    gain_rows = jnp.concatenate(
        [norm_gains.reshape(-1, shard_rows), skip_gain.reshape(-1, shard_rows)], axis=0
    )
    small = jnp.concatenate(
        [
            condition.reshape(fsdp_count, 1, shard_rows),
            jnp.broadcast_to(gain_rows[None], (fsdp_count,) + gain_rows.shape),
        ],
        axis=1,
    ).astype(F32)
    small = lax.all_to_all(small, "fsdp", 0, 0, tiled=True)
    cond_part = small[:, 0]
    gains = jnp.swapaxes(small[:, 1:7], 0, 1).reshape(2, 3, model_width)
    skip_gains = small[:, 7:].reshape(2, model_width)
    silu_part = jax.nn.silu(cond_part)
    shift_terms = jnp.einsum("br,lrd->bld", silu_part, mod_weight.astype(F32), precision=EXACT)
    shifts = jnp.sum(lax.all_to_all(shift_terms, "fsdp", 0, 0, tiled=True), axis=0)

    stacks = (
        qkv_weight,
        query_weight,
        text_kv_weight,
        self_out_weight,
        cross_out_weight,
        up_weight,
        down_weight,
    )
    first_weights = gather_block(0, *stacks)
    first_pairs = text_pairs(text_rows, first_weights[2])
    first_terms, first_saved = layer_forward(
        gather_halves(halves_of(latents[0])),
        latents[0],
        scalars,
        gains[0],
        shifts[0],
        first_pairs,
        first_weights,
        False,
        ((), (), ()),
    )
    out_parts = gather_halves(halves_of(cotangent[0]))
    skip_parts = spread(
        gather_fsdp(own_part(skip_weight, 1, padded_width(width)))
    )
    first_out, joined_norm, skip_out, second_halves = skip_forward(
        scalars,
        skip_parts,
        first_terms,
        first_saved[7],
        skip_input[0],
        skip_gains,
        gains[1],
        shifts[1],
        (out_parts[-1], out_parts[-2]),
    )
    second_weights = gather_block(1, *stacks)
    second_pairs = text_pairs(text_rows, second_weights[2])
    second_terms, second_saved = layer_forward(
        gather_halves(second_halves),
        skip_out,
        scalars,
        gains[1],
        shifts[1],
        second_pairs,
        second_weights,
        True,
        ((), (), ()),
    )
    output = close_forward(second_terms, second_saved[7])

    terms, grad_after_self, gain_grads, text_second, shards_second, grad_qkv = layer_backward(
        out_parts,
        cotangent[0],
        second_saved,
        scalars,
        gains[1],
        text_rows,
        second_pairs,
        second_weights,
        ((), (), ()),
    )
    skip_branch, grad_first_out, grad_skip, vectors, first_halves = skip_backward(
        scalars,
        skip_parts,
        terms,
        skip_out,
        gains[1],
        grad_after_self,
        first_out,
        skip_input[0],
        skip_gains,
        (grad_qkv,),
    )
    vectors_second = jnp.concatenate([vectors[:2], gain_grads, vectors[2:]], axis=0)
    skip_shard = scatter_fsdp(
        unspread(scalars, outer(scalars, [joined_norm], [skip_branch]))
    )
    second_done = finish_block(scalars, shards_second, width, 1, None)
    terms, grad_after_self, gain_grads, text_first, shards_first, grad_qkv = layer_backward(
        gather_halves(first_halves),
        grad_first_out,
        first_saved,
        scalars,
        gains[0],
        text_rows,
        first_pairs,
        first_weights,
        (
            (shards_second[4], shards_second[3]),
            (shards_second[2], shards_second[1]),
            (shards_second[0], second_done[4][0], second_done[3][0]),
        ),
    )
    grad_latents, vectors = open_backward(
        terms, latents[0], gains[0], grad_after_self, (grad_qkv, skip_shard, second_done[0][0])
    )
    vectors_first = jnp.concatenate([vectors, gain_grads], axis=0)
    first_done = finish_block(scalars, shards_first, width, 0, second_done)
    (grad_qkv,), (grad_self_out, grad_query, grad_cross_out), (grad_kv,), (grad_up,), (grad_down,) = (
        first_done
    )
    (grad_skip_weight,) = settle(scalars, gather_parts(skip_shard), 1, 1, width, 0, 1)

    second_sums = sum_vectors(vectors_second)
    first_sums = sum_vectors(vectors_first)
    shift_grads = jnp.stack([first_sums[:, 0], second_sums[:, 0]], axis=1)
    gain_sums = jnp.stack([first_sums[:, 1:4].sum(axis=0), second_sums[:, 1:4].sum(axis=0)])
    grad_norm_gains = lax.dynamic_slice_in_dim(gain_sums, f * shard_rows, shard_rows, 2)
    grad_skip_gain = lax.dynamic_slice_in_dim(
        second_sums[:, 4:].sum(axis=0).reshape(-1), f * skip_gain.shape[0], skip_gain.shape[0], 0
    )
    turned = jnp.stack(
        [lax.dynamic_index_in_dim(silu_part, f ^ j, 0, False) for j in range(fsdp_count)]
    )
    grad_mod = jnp.einsum("br,bld->lrd", turned, shift_grads, precision=EXACT)
    grad_silu = jnp.einsum("bld,lrd->br", shift_grads, mod_weight.astype(F32), precision=EXACT)
    grad_silu = jnp.stack(
        [lax.dynamic_index_in_dim(grad_silu, f ^ j, 0, False) for j in range(fsdp_count)]
    )
    _, silu_pull = jax.vjp(jax.nn.silu, cond_part)
    grad_cond_part = silu_pull(grad_silu)[0]
    grad_condition = lax.all_to_all(grad_cond_part, "fsdp", 0, 0, tiled=True).reshape(1, -1)

    text_sum, bits = text_first + text_second, 1
    while bits < seq_count:
        text_sum = text_sum + swap_seq(text_sum.astype(BF16), bits).astype(F32)
        bits *= 2
    return (
        output[None],
        grad_latents[None],
        grad_skip[None],
        text_sum[None, :text_count],
        grad_condition,
        grad_mod,
        grad_norm_gains,
        grad_qkv,
        grad_query,
        grad_kv,
        grad_self_out,
        grad_cross_out,
        grad_up,
        grad_down,
        grad_skip_gain,
        grad_skip_weight[0],
    )


def solution(mesh):
    in_specs = (
        P("fsdp", "seq", None),
        P("fsdp", "seq", None),
        P("fsdp", None, None),
        P("fsdp"),
        P("fsdp", None),
        P("fsdp", "seq", None),
        P(None, "fsdp", None),
        P(None, None, "fsdp"),
        P(None, "fsdp", None),
        P(None, "fsdp", None),
        P(None, "fsdp", None),
        P(None, "fsdp", None),
        P(None, "fsdp", None),
        P(None, "fsdp", None),
        P(None, "fsdp", None),
        P("fsdp"),
        P("fsdp", None),
    )
    out_specs = (
        P("fsdp", "seq", None),
        P("fsdp", "seq", None),
        P("fsdp", "seq", None),
        P("fsdp", None, None),
        P("fsdp", None),
        P(None, "fsdp", None),
        P(None, None, "fsdp"),
        P(None, "fsdp", None),
        P(None, "fsdp", None),
        P(None, "fsdp", None),
        P(None, "fsdp", None),
        P(None, "fsdp", None),
        P(None, "fsdp", None),
        P(None, "fsdp", None),
        P("fsdp"),
        P("fsdp", None),
    )
    return jax.shard_map(body, mesh=mesh, in_specs=in_specs, out_specs=out_specs, check_vma=False)
```

time: 1430 us -> 1350 us (0.944)
  local copies, waits for them, and re-layouts: 277 us -> 70.9 us
  waiting for transfers between devices: 408 us -> 549 us
  matrix products: 195 us -> 67.5 us
  Pallas kernels: 270 us -> 383 us
  starting transfers between devices: 169 us -> 226 us
  other arithmetic: 75.6 us -> 32.4 us
    pallas_call x13 -> x22, Pallas kernels: 229 us -> 345 us  [call(): pl.pallas_call(run, out_shape=tuple((jax.ShapeDtypeStruct(s, d) for s, d...]
    all_gather x11, waiting for transfers between devices: 20.3 us -> 91.5 us  [gather_fsdp(): return lax.all_gather(shard, 'fsdp', axis=0, tiled=True)]
    dot_general x20 -> x2, matrix products: 70.9 us -> 1.51 us  [dot_nt(): lax.dot_general(a, b, (((1,), (1,)), ((), ())), preferred_element_type=F32)]
    dot_general x14 -> x4, matrix products: 70.5 us -> 4.76 us  [dot_nn(): lax.dot_general(a, b, (((1,), (0,)), ((), ())), preferred_element_type=F32)]
    ppermute x12 -> x15, waiting for transfers between devices: 49.7 us -> 111 us  [swap_by_core(): return lax.ppermute(block, ('seq', 'fsdp'), pairs)]
    ppermute x13 -> x0, local copies, waits for them, and re-layouts: 50 us -> none  [the longest x8 29.9 us: swap_by_core(): return lax.ppermute(block, ('seq', 'fsdp'), pairs)]
    unnamed x344 -> x397, local copies, waits for them, and re-layouts: 66.2 us -> 26.4 us
    slice x47 -> x8, local copies, waits for them, and re-layouts: 40.1 us -> 6.54 us  [the longest x3 4.05 us: gather_block(): m[layer]]
  transfers between devices with their start and end apart: 187 -> 219, of which waited for: 62 -> 82; matrix products, arithmetic and copies ran while one was open for 36% -> 10% of each run, Pallas kernels for 19% -> 27%
where the time goes in v3:
time: 1350 us
  waiting for transfers between devices  549 us (41%)
  Pallas kernels  383 us (28%)
  starting transfers between devices  226 us (17%)
  local copies, waits for them, and re-layouts  70.9 us (5%)
  matrix products  67.5 us (5%)
  other arithmetic  32.4 us (2%)
  between operations  17.5 us (1%)
    pallas_call x22, Pallas kernels, call(): pl.pallas_call(run, out_shape=tuple((jax.ShapeDtypeStruct(s, d) for s, d...  345 us
    ppermute x158, waiting for transfers between devices, swap_seq(): return lax.ppermute(block, 'seq', [(i, i ^ bits) for i in range(seq_count)])  326 us
    ppermute x158, starting transfers between devices, swap_seq(): return lax.ppermute(block, 'seq', [(i, i ^ bits) for i in range(seq_count)])  166 us
    ppermute x15, waiting for transfers between devices, swap_by_core(): return lax.ppermute(block, ('seq', 'fsdp'), pairs)  111 us
    all_gather x11, waiting for transfers between devices, gather_fsdp(): return lax.all_gather(shard, 'fsdp', axis=0, tiled=True)  91.5 us
    dot_general x8, matrix products, dot_tn(): lax.dot_general(a, b, (((0,), (0,)), ((), ())), preferred_element_type=F32)  56 us
    pallas_call x11, Pallas kernels, settle_call(): pl.pallas_call(kernel, grid=(1,), out_shape=[jax.ShapeDtypeStruct((layer_...  38.5 us
    ppermute x21, starting transfers between devices, swap_fsdp(): lax.ppermute(block, 'fsdp', [(i, i ^ bits) for i in range(fsdp_count)])  31 us
  transfers between devices with their start and end apart: 219, of which 82 were waited for; matrix products, arithmetic and copies ran while one was open for 10% of the time, Pallas kernels for 27%

profile of v3, /device:TPU:0, one launch (start us, length us, event | category | flops | bytes accessed | tf_op | source)
XLA Modules:
  0.0 1346.7 jit_solution(2405524547768938645)
XLA Ops:
  34.2 22.1 %all-gather.18.cloned.1.call-done.refs_5_.refs_1_ = bf16[1408,1152]{1,0:T(8,128)(2,1)} async-done(((bf16[176,1152]{1,0:T(8,128)(2,1)}), bf16[1408,1152]{1,0:T(8,128)(2,1)}) %all-gather.18.cloned.1.call-update) | async-done | bytes 3244048 | tf_op jit(solution)/shard_map/all_gather | solution.py:1008
  70.7 31.9 %collective-permute-done.13.refs_6_.refs_2_ = bf16[1408,1152]{1,0:T(8,128)(2,1)} collective-permute-done((bf16[1408,1152]{1,0:T(8,128)(2,1)}, bf16[1408,1152]{1,0:T(8,128)(2,1)}, u32[]{:S(2)}, u32[]{:S(2)}) %collective-permute-start.13) | collective-permute-done | bytes 3244064 | tf_op jit(solution)/shard_map/ppermute | solution.py:915
  151.1 18.4 %shard_map.288 = (bf16[1024,1408]{1,0:T(8,128)(2,1)}, bf16[1024,1152]{1,0:T(8,128)(2,1)}, bf16[256,352]{1,0:T(8,128)(2,1)}, bf16[256,352]{1,0:T(8,128)(2,1)}, bf...) custom-call(bf16[128,1408]{1,0:T(8,128)(2,1)} %get-tuple-element.437.refs_0_, ...), custom_call_target="tpu_custom_call" | custom-call | flops 24000000000 | bytes 1000 | tf_op jit(solution)/shard_map/pallas_call | solution.py:47
  183.3 21.1 %shard_map.289 = (bf16[256,1408]{1,0:T(8,128)(2,1)}, f32[256,1408]{1,0:T(8,128)}, bf16[256,1408]{1,0:T(8,128)(2,1)}, bf16[4,256,352]{2,1,0:T(8,128)(2,1)}, bf16[...) custom-call(s32[10]{0:T(128)} %stack.83.refs_0_.scalars_ref, ...), custom_call_target="tpu_custom_call" | custom-call | flops 23000000512 | bytes 1000 | tf_op jit(solution)/shard_map/pallas_call | solution.py:47
  231.7 16.8 %all-gather.22.cloned.1.call-done.refs_8_.refs_9_ = bf16[1408,1536]{1,0:T(8,128)(2,1)} async-done(((bf16[176,1536]{1,0:T(8,128)(2,1)}), bf16[1408,1536]{1,0:T(8,128)(2,1)}) %all-gather.22.cloned.1.call-update) | async-done | bytes 4325392 | tf_op jit(solution)/shard_map/all_gather | solution.py:1008
  248.4 49.4 %all-gather.32.cloned.1.call-done = bf16[1,1536,1408]{2,1,0:T(8,128)(2,1)} async-done(((bf16[1,192,1408]{2,1,0:T(8,128)(2,1)}), bf16[1,1536,1408]{2,1,0:T(8,128)(2,1)}) %all-gather.32.cloned.1.call-update) | async-done | bytes 4325392 | tf_op jit(solution)/shard_map/all_gather | solution.py:1008
  297.9 18.4 %shard_map.290 = (bf16[1024,1408]{1,0:T(8,128)(2,1)}, f32[1024,1536]{1,0:T(8,128)}, bf16[1024,1536]{1,0:T(8,128)(2,1)}, f32[256,1408]{1,0:T(8,128)}, bf16[128,14...) custom-call(bf16[128,1408]{1,0:T(8,128)(2,1)} %get-tuple-element.174, ...), custom_call_target="tpu_custom_call" | custom-call | flops 22000001024 | bytes 1000 | tf_op jit(solution)/shard_map/pallas_call | solution.py:47
  421.5 18.0 %shard_map.292 = (bf16[1024,1408]{1,0:T(8,128)(2,1)}, bf16[1024,1152]{1,0:T(8,128)(2,1)}, bf16[256,352]{1,0:T(8,128)(2,1)}, bf16[256,352]{1,0:T(8,128)(2,1)}, bf...) custom-call(bf16[128,1408]{1,0:T(8,128)(2,1)} %get-tuple-element.184.refs_0_, ...), custom_call_target="tpu_custom_call" | custom-call | flops 24000000000 | bytes 1000 | tf_op jit(solution)/shard_map/pallas_call | solution.py:47
  452.7 21.0 %shard_map.293 = (bf16[256,1408]{1,0:T(8,128)(2,1)}, f32[256,1408]{1,0:T(8,128)}, bf16[256,1408]{1,0:T(8,128)(2,1)}, bf16[4,256,352]{2,1,0:T(8,128)(2,1)}, bf16[...) custom-call(s32[10]{0:T(128)} %stack.83.refs_0_.scalars_ref, ...), custom_call_target="tpu_custom_call" | custom-call | flops 23000000512 | bytes 1000 | tf_op jit(solution)/shard_map/pallas_call | solution.py:47
  502.4 18.4 %shard_map.294 = (bf16[1024,1408]{1,0:T(8,128)(2,1)}, f32[1024,1536]{1,0:T(8,128)}, bf16[1024,1536]{1,0:T(8,128)(2,1)}, f32[256,1408]{1,0:T(8,128)}, bf16[128,14...) custom-call(bf16[128,1408]{1,0:T(8,128)(2,1)} %get-tuple-element.191, ...), custom_call_target="tpu_custom_call" | custom-call | flops 22000001024 | bytes 1000 | tf_op jit(solution)/shard_map/pallas_call | solution.py:47
  521.7 19.7 %shard_map.296 = (bf16[1024,1408]{1,0:T(8,128)(2,1)}, bf16[1024,1536]{1,0:T(8,128)(2,1)}, f32[256,1408]{1,0:T(8,128)}, bf16[128,1408]{1,0:T(8,128)(2,1)}, bf16[1...) custom-call(bf16[128,1408]{1,0:T(8,128)(2,1)} %get-tuple-element.432, ...), custom_call_target="tpu_custom_call" | custom-call | flops 22000001024 | bytes 1000 | tf_op jit(solution)/shard_map/pallas_call | solution.py:47
  576.5 27.9 %shard_map.297 = (f32[256,1408]{1,0:T(8,128)}, bf16[4,256,352]{2,1,0:T(8,128)(2,1)}, bf16[4,256,352]{2,1,0:T(8,128)(2,1)}, bf16[4,256,352]{2,1,0:T(8,128)(2,1)},...) custom-call(s32[10]{0:T(128)} %stack.83.refs_0_.scalars_ref, ...), custom_call_target="tpu_custom_call" | custom-call | flops 36999999488 | bytes 1000 | tf_op jit(solution)/shard_map/pallas_call | solution.py:47
  635.1 22.6 %collective-permute-done.101 = bf16[176,768]{1,0:T(8,128)(2,1)S(1)} collective-permute-done((bf16[176,768]{1,0:T(8,128)(2,1)S(1)}, bf16[176,768]{1,0:T(8,128)(2,1)S(1)}, u32[]{:S(2)}, u32[]{:S(2)}) %collective-permute-start.101) | collective-permute-done | bytes 270368 | tf_op jit(solution)/shard_map/ppermute | solution.py:896
  667.7 16.2 %collective-permute-done.110.refs_3_ = bf16[704,1152]{1,0:T(8,128)(2,1)S(1)} collective-permute-done((bf16[704,1152]{1,0:T(8,128)(2,1)S(1)}, bf16[704,1152]{1,0:T(8,128)(2,1)S(1)}, u32[]{:S(2)}, u32[]{:S(2)}) %collective-permute-start.110) | collective-permute-done | bytes 1622048 | tf_op jit(solution)/shard_map/ppermute | solution.py:915
  683.9 17.4 %collective-permute-done.108.refs_2_ = bf16[704,1152]{1,0:T(8,128)(2,1)S(1)} collective-permute-done((bf16[704,1152]{1,0:T(8,128)(2,1)S(1)}, bf16[704,1152]{1,0:T(8,128)(2,1)S(1)}, u32[]{:S(2)}, u32[]{:S(2)}) %collective-permute-start.108) | collective-permute-done | bytes 1622048 | tf_op jit(solution)/shard_map/ppermute | solution.py:915
  719.9 29.0 %shard_map.299 = (bf16[1024,1152]{1,0:T(8,128)(2,1)}, f32[256,1408]{1,0:T(8,128)}, bf16[128,1408]{1,0:T(8,128)(2,1)}, bf16[128,1408]{1,0:T(8,128)(2,1)}, bf16[12...) custom-call(bf16[1024,1152]{1,0:T(8,128)(2,1)} %get-tuple-element.202.ref, ...), custom_call_target="tpu_custom_call" | custom-call | flops 32000000000 | bytes 1000 | tf_op jit(solution)/shard_map/pallas_call | solution.py:47
  806.6 23.9 %collective-permute-done.130 = bf16[1408,384]{1,0:T(8,128)(2,1)S(1)} collective-permute-done((bf16[1408,384]{1,0:T(8,128)(2,1)S(1)}, bf16[1408,384]{1,0:T(8,128)(2,1)S(1)}, u32[]{:S(2)}, u32[]{:S(2)}) %collective-permute-start.130) | collective-permute-done | bytes 1081376 | tf_op jit(solution)/shard_map/ppermute | solution.py:915
  835.2 21.4 %collective-permute-done.88.refs_3_ = bf16[128,1408]{1,0:T(8,128)(2,1)S(1)} collective-permute-done((bf16[128,1408]{1,0:T(8,128)(2,1)S(1)}, bf16[128,1408]{1,0:T(8,128)(2,1)S(1)}, u32[]{:S(2)}, u32[]{:S(2)}) %collective-permute-start.88) | collective-permute-done | bytes 360480 | tf_op jit(solution)/shard_map/ppermute | solution.py:896
  868.7 19.5 %shard_map.301 = (bf16[1024,1408]{1,0:T(8,128)(2,1)}, bf16[1024,1536]{1,0:T(8,128)(2,1)}, f32[256,1408]{1,0:T(8,128)}, bf16[128,1408]{1,0:T(8,128)(2,1)}, bf16[1...) custom-call(bf16[128,1408]{1,0:T(8,128)(2,1)} %get-tuple-element.239, ...), custom_call_target="tpu_custom_call" | custom-call | flops 22000001024 | bytes 1000 | tf_op jit(solution)/shard_map/pallas_call | solution.py:47
  916.3 27.7 %shard_map.303 = (f32[256,1408]{1,0:T(8,128)}, bf16[4,256,352]{2,1,0:T(8,128)(2,1)}, bf16[4,256,352]{2,1,0:T(8,128)(2,1)}, bf16[4,256,352]{2,1,0:T(8,128)(2,1)},...) custom-call(s32[10]{0:T(128)} %stack.83.refs_0_.scalars_ref, ...), custom_call_target="tpu_custom_call" | custom-call | flops 36999999488 | bytes 1000 | tf_op jit(solution)/shard_map/pallas_call | solution.py:47
  1027.6 29.1 %shard_map.307 = (bf16[1024,1152]{1,0:T(8,128)(2,1)}, f32[256,1408]{1,0:T(8,128)}, bf16[128,1408]{1,0:T(8,128)(2,1)}, bf16[128,1408]{1,0:T(8,128)(2,1)}, bf16[12...) custom-call(bf16[1024,1152]{1,0:T(8,128)(2,1)} %get-tuple-element.201.ref, ...), custom_call_target="tpu_custom_call" | custom-call | flops 32000000000 | bytes 1000 | tf_op jit(solution)/shard_map/pallas_call | solution.py:47
  1080.3 21.7 %collective-permute-done.162 = bf16[704,1152]{1,0:T(8,128)(2,1)S(1)} collective-permute-done((bf16[704,1152]{1,0:T(8,128)(2,1)S(1)}, bf16[704,1152]{1,0:T(8,128)(2,1)S(1)}, u32[]{:S(2)}, u32[]{:S(2)}) %collective-permute-start.162) | collective-permute-done | bytes 1622048 | tf_op jit(solution)/shard_map/ppermute | solution.py:915
  1122.8 28.2 %collective-permute-done.178.refs_1_ = bf16[128,768]{1,0:T(8,128)(2,1)S(1)} collective-permute-done((bf16[128,768]{1,0:T(8,128)(2,1)S(1)}, bf16[128,768]{1,0:T(8,128)(2,1)S(1)}, u32[]{:S(2)}, u32[]{:S(2)}) %collective-permute-start.178) | collective-permute-done | bytes 196640 | tf_op jit(solution)/shard_map/ppermute | solution.py:896
  1257.2 14.6 %collective-permute-done.175.refs_2_ = bf16[128,768]{1,0:T(8,128)(2,1)} collective-permute-done((bf16[128,768]{1,0:T(8,128)(2,1)}, bf16[128,768]{1,0:T(8,128)(2,1)}, u32[]{:S(2)}, u32[]{:S(2)}) %collective-permute-start.175) | collective-permute-done | bytes 196640 | tf_op jit(solution)/shard_map/ppermute | solution.py:896
  (1014 shorter events, 774.7 us)
Async XLA Ops:
  14.3 108.0 %all-gather.20.cloned.1.call-start = ((), (), s32[]{:S(2)}) async-start(), calls=%async_computation.17 | async-start | bytes 1769472 | tf_op jit(solution)/shard_map/all_gather | solution.py:1008
  16.1 135.1 %all-gather.16.cloned.1.call-start = ((), (), s32[]{:S(2)}) async-start(), calls=%async_computation.15 | async-start | bytes 3649536 | tf_op jit(solution)/shard_map/all_gather | solution.py:1008
  20.1 154.3 %all-gather.14.cloned.1.call-start = ((), (), s32[]{:S(2)}) async-start(), calls=%async_computation.14 | async-start | bytes 2433024 | tf_op jit(solution)/shard_map/all_gather | solution.py:1008
  21.1 200.4 %all-gather.26.cloned.1.call-start = ((), (), s32[]{:S(2)}) async-start(), calls=%async_computation.20 | async-start | bytes 3649536 | tf_op jit(solution)/shard_map/all_gather | solution.py:1008
  23.2 225.3 %all-gather.22.cloned.1.call-start = ((), (), s32[]{:S(2)}) async-start(), calls=%async_computation.18 | async-start | bytes 4866048 | tf_op jit(solution)/shard_map/all_gather | solution.py:1008
  28.8 269.1 %all-gather.32.cloned.1.call-start = ((), (), s32[]{:S(2)}) async-start(), calls=%async_computation.34 | async-start | bytes 4866048 | tf_op jit(solution)/shard_map/all_gather | solution.py:1008
  32.4 290.9 %all-gather.28.cloned.1.call-start = ((), (), s32[]{:S(2)}) async-start(), calls=%async_computation.21 | async-start | bytes 1769472 | tf_op jit(solution)/shard_map/all_gather | solution.py:1008
  33.3 388.2 %all-gather.24.cloned.1.call-start = ((), (), s32[]{:S(2)}) async-start(), calls=%async_computation.19 | async-start | bytes 3649536 | tf_op jit(solution)/shard_map/all_gather | solution.py:1008
  62.3 432.7 %all-gather.30.cloned.1.call-start = ((), (), s32[]{:S(2)}) async-start(), calls=%async_computation.22 | async-start | bytes 4866048 | tf_op jit(solution)/shard_map/all_gather | solution.py:1008
  111.4 383.6 %all-gather.34.cloned.1.call-start = ((), (), s32[]{:S(2)}) async-start(), calls=%async_computation.35 | async-start | bytes 4866048 | tf_op jit(solution)/shard_map/all_gather | solution.py:1008
  224.0 125.5 %collective-permute-start.48 = (bf16[1408,1152]{1,0:T(8,128)(2,1)}, bf16[1408,1152]{1,0:T(8,128)(2,1)}, u32[]{:S(2)}, u32[]{:S(2)}) collective-permute-start(bf16[1408,1152]{1,0:T(8,128)(2,1)} %all-gather.26.cloned.1.call-done.refs_5_.refs_1_), channel_id=1, source_target_pairs={{0,8},{1,17},{2,10},{3,19},{4,12},{5,21},{6,14},{7,23},{8,0},{9,25... | collective-permute-start | bytes 9732104 | tf_op jit(solution)/shard_map/ppermute | solution.py:915
  231.7 117.2 %collective-permute-start.1 = (bf16[2816,384]{1,0:T(8,128)(2,1)}, bf16[2816,384]{1,0:T(8,128)(2,1)}, u32[]{:S(2)}, u32[]{:S(2)}) collective-permute-start(bf16[2816,384]{1,0:T(8,128)(2,1)} %collective-permute-done.refs_2_), channel_id=1, source_target_pairs={{0,1},{1,0},{2,3},{3,2},{4,5},{5,4},{6,7},{7,6},{8,9},{9,8},{10,11... | collective-permute-start | bytes 6488072 | tf_op jit(solution)/shard_map/ppermute | solution.py:901
  318.6 549.3 %reduce-scatter.12.cloned.1.call-start = ((), (), s32[]{:S(2)}) async-start(), calls=%async_computation.23 | async-start | bytes 4866048 | tf_op jit(solution)/shard_map/reduce_scatter | solution.py:1012
  550.0 318.0 %reduce-scatter.14.cloned.1.call-start = ((), (), s32[]{:S(2)}) async-start(), calls=%async_computation.24 | async-start | bytes 4866048 | tf_op jit(solution)/shard_map/reduce_scatter | solution.py:1012
  564.9 350.3 %reduce-scatter.16.cloned.1.call-start = ((), (), s32[]{:S(2)}) async-start(), calls=%async_computation.25 | async-start | bytes 1769472 | tf_op jit(solution)/shard_map/reduce_scatter | solution.py:1012
  660.8 254.5 %reduce-scatter.18.cloned.1.call-start = ((), (), s32[]{:S(2)}) async-start(), calls=%async_computation.26 | async-start | bytes 3649536 | tf_op jit(solution)/shard_map/reduce_scatter | solution.py:1012
  708.0 318.9 %reduce-scatter.20.cloned.1.call-start = ((), (), s32[]{:S(2)}) async-start(), calls=%async_computation.27 | async-start | bytes 3649536 | tf_op jit(solution)/shard_map/reduce_scatter | solution.py:1012
  778.4 414.4 %reduce-scatter.22.cloned.1.call-start = ((), (), s32[]{:S(2)}) async-start(), calls=%async_computation.28 | async-start | bytes 2433024 | tf_op jit(solution)/shard_map/reduce_scatter | solution.py:1012
  866.5 382.6 %reduce-scatter.28.cloned.1.call-start = ((), (), s32[]{:S(2)}) async-start(), calls=%async_computation.31 | async-start | bytes 1769472 | tf_op jit(solution)/shard_map/reduce_scatter | solution.py:1012
  965.8 284.7 %reduce-scatter.32.cloned.1.call-start = ((), (), s32[]{:S(2)}) async-start(), calls=%async_computation.33 | async-start | bytes 4866048 | tf_op jit(solution)/shard_map/reduce_scatter | solution.py:1012
  966.6 305.2 %reduce-scatter.30.cloned.1.call-start = ((), (), s32[]{:S(2)}) async-start(), calls=%async_computation.32 | async-start | bytes 4866048 | tf_op jit(solution)/shard_map/reduce_scatter | solution.py:1012
  967.2 316.7 %reduce-scatter.24.cloned.1.call-start = ((), (), s32[]{:S(2)}) async-start(), calls=%async_computation.29 | async-start | bytes 3649536 | tf_op jit(solution)/shard_map/reduce_scatter | solution.py:1012
  986.0 120.2 %collective-permute-start.64 = (bf16[128,1408]{1,0:T(8,128)(2,1)}, bf16[128,1408]{1,0:T(8,128)(2,1)}, u32[]{:S(2)}, u32[]{:S(2)}) collective-permute-start(bf16[128,1408]{1,0:T(8,128)(2,1)} %get-tuple-element.194), channel_id=1, source_target_pairs={{0,8},{8,0},{16,24},{24,16},{1,9},{9,1},{17,25},{25,17},{2,10},{10... | collective-permute-start | bytes 1081352 | tf_op jit(solution)/shard_map/ppermute | solution.py:896
  1064.4 247.1 %reduce-scatter.26.cloned.1.call-start = ((), (), s32[]{:S(2)}) async-start(), calls=%async_computation.30 | async-start | bytes 3649536 | tf_op jit(solution)/shard_map/reduce_scatter | solution.py:1012
  (391 other events, 6123.4 us)
Sparse Core Ops, SparseCore 0:
  14.5 41.7 all-gather.17
  58.5 23.8 all-gather.19
  84.6 43.6 all-gather.15
  130.4 27.9 all-gather.13
  160.4 38.5 all-gather.25
  201.1 47.3 all-gather.21
  250.7 47.1 all-gather.31
  299.5 23.7 all-gather.27
  325.5 38.6 all-gather.23
  366.3 47.2 all-gather.29
  415.8 47.1 all-gather.33
  550.1 50.9 reduce-scatter.11
  604.1 49.3 reduce-scatter.13
  660.9 33.1 reduce-scatter.15
  708.2 40.3 reduce-scatter.17
  778.5 41.0 reduce-scatter.19
  866.6 35.0 reduce-scatter.21
  965.9 33.3 reduce-scatter.27
  1001.7 49.3 reduce-scatter.31
  1053.4 49.3 reduce-scatter.29
  1105.1 42.1 reduce-scatter.23
  1176.8 40.4 reduce-scatter.25

commit v4 on v3

--- a/solution.py
+++ b/solution.py
@@ -34,8 +34,11 @@
     return -(-width // 128) * 128
 
 
-def call(kernel, outs, scratch, micros, *operands, scalars=None, deps=()):
-    specs = [pl.BlockSpec(memory_space=pltpu.VMEM)] * len(operands)
+def call(kernel, outs, scratch, micros, *operands, scalars=None, deps=(), outside=()):
+    specs = [
+        pl.BlockSpec(memory_space=pl.ANY if i in outside else pltpu.VMEM)
+        for i in range(len(operands))
+    ]
     if scalars is not None:
         specs = [pl.BlockSpec(memory_space=pltpu.SMEM)] + specs
         operands = (scalars,) + tuple(operands)
@@ -57,6 +60,24 @@
     )(*operands, *deps)
 
 
+def gate_kernel(*refs):
+    del refs
+
+
+def gate(values, deps):
+    values, deps = list(values), list(deps)
+    return list(
+        pl.pallas_call(
+            gate_kernel,
+            out_shape=tuple(jax.ShapeDtypeStruct(m.shape, m.dtype) for m in values),
+            in_specs=[pl.BlockSpec(memory_space=pl.ANY)] * (len(values) + len(deps)),
+            out_specs=tuple([pl.BlockSpec(memory_space=pl.ANY)] * len(values)),
+            input_output_aliases={i: i for i in range(len(values))},
+            cost_estimate=pl.CostEstimate(flops=1000, bytes_accessed=1000, transcendentals=0),
+        )(*values, *deps)
+    )
+
+
 def cut_of(rows):
     return rows // 32 * 16
 
@@ -110,8 +131,10 @@
     part_refs, refs = refs[:parts], refs[parts:]
     weight_ref, gains_ref, shift_ref = refs[:3]
     rows_ref, triples_ref = refs[3:5]
-    mixed_refs = refs[5:]
-    stride = weight_ref.shape[1] // 3
+    mixed_refs, (held_ref, done) = refs[5:-2], refs[-2:]
+    copy = pltpu.make_async_copy(weight_ref.at[:, : held_ref.shape[1]], held_ref, done)
+    copy.start()
+    stride = held_ref.shape[1] // 3
     rows, width = mixed_refs[0].shape
     factor = LOG2_E / math.sqrt(head_size)
     start = 0
@@ -122,9 +145,10 @@
             values = (unit * gains_ref[0:1, :] + shift_ref[...]).astype(BF16)
         rows_ref[start : start + ref.shape[0], :] = values
         start += ref.shape[0]
+    copy.wait()
     for j in range(count):
         at = slice(j * rows, (j + 1) * rows)
-        triples_ref[at, :] = dot_nn(rows_ref[at, :], weight_ref[...]).astype(BF16)
+        triples_ref[at, :] = dot_nn(rows_ref[at, :], held_ref[...]).astype(BF16)
     for j in range(count):
         at = slice(j * rows, (j + 1) * rows)
         for h in range(width // head_size):
@@ -143,17 +167,19 @@
 def self_forward(parts, weight, gains, shift, head_size, count, width, normed, deps=()):
     total = sum(m.shape[0] for m in parts)
     columns = parts[0].shape[1]
+    held = (columns, 3 * padded_width(width))
     found = call(
         functools.partial(self_forward_kernel, count, len(parts), head_size, normed),
-        [((total, columns), BF16), ((total, weight.shape[1]), BF16)]
+        [((total, columns), BF16), ((total, held[1]), BF16)]
         + [((total // count, width), BF16)] * count,
-        [],
+        [pltpu.VMEM(held, BF16), pltpu.SemaphoreType.DMA],
         24,
         *parts,
         weight,
         gains,
         shift[None],
         deps=deps,
+        outside=(len(parts),),
     )
     return found[0], found[1], list(found[2:])
 
@@ -179,10 +205,12 @@
 
 def self_backward_kernel(count, head_size, step, triples_ref, *refs):
     grad_refs, (weight_ref, out_ref, own_ref) = refs[:count], refs[count : count + 3]
-    piece_refs, (keys_ref, values_ref) = refs[count + 3 : -2], refs[-2:]
+    piece_refs, (keys_ref, values_ref, held_ref, done) = refs[count + 3 : -4], refs[-4:]
+    copy = pltpu.make_async_copy(weight_ref.at[:, : held_ref.shape[1]], held_ref, done)
+    copy.start()
     total = triples_ref.shape[0]
     rows, width = grad_refs[0].shape
-    stride = weight_ref.shape[1] // 3
+    stride = held_ref.shape[1] // 3
     for h in range(width // head_size):
         low = h * head_size
         k = triples_ref[:, stride + low : stride + low + head_size]
@@ -205,8 +233,9 @@
     if stride > width:
         for g in range(3):
             out_ref[:, g * stride + width : (g + 1) * stride] = jnp.zeros((total, stride - width), BF16)
+    copy.wait()
     for j in range(count):
-        found = dot_nt(out_ref[j * rows : (j + 1) * rows, :], weight_ref[...])
+        found = dot_nt(out_ref[j * rows : (j + 1) * rows, :], held_ref[...])
         if j == 0:
             own_ref[...] = found
         else:
@@ -220,12 +249,18 @@
     found = call(
         functools.partial(self_backward_kernel, count, head_size, step),
         [(triples.shape, BF16), ((rows, columns), F32)] + piece_shapes(count, rows, columns),
-        [pltpu.VMEM((total, head_size), F32), pltpu.VMEM((total, head_size), F32)],
+        [
+            pltpu.VMEM((total, head_size), F32),
+            pltpu.VMEM((total, head_size), F32),
+            pltpu.VMEM((columns, triples.shape[1]), BF16),
+            pltpu.SemaphoreType.DMA,
+        ],
         32,
         triples,
         *grads,
         weight,
         deps=deps,
+        outside=(1 + count,),
     )
     return found[0], found[1], list(found[2:])
 
@@ -471,48 +506,68 @@
     return found[:5] + [found[5 : 5 + count], found[5 + count], found[6 + count :]]
 
 
-def mlp_forward_kernel(count, parts, *refs):
-    part_refs, refs = refs[:parts], refs[parts:]
-    up_ref, down_ref, rows_ref, up_rows_ref, activated_ref, own_ref = refs[:6]
-    piece_refs = refs[6:]
+def mlp_up_kernel(count, parts, *refs):
+    part_refs, (up_ref, rows_ref, up_rows_ref, activated_ref) = refs[:parts], refs[parts:]
     start = 0
     for ref in part_refs:
         rows_ref[start : start + ref.shape[0], :] = ref[...]
         start += ref.shape[0]
     rows = start // count
-    for j in range(count - 1, -1, -1):
+    for j in range(count):
         at = slice(j * rows, (j + 1) * rows)
         values = dot_nn(rows_ref[at, :], up_ref[...])
         up_rows_ref[at, :] = values
         inner = GELU_SCALE * (values + 0.044715 * (values * values * values))
         activated_ref[at, :] = (0.5 * values * (1.0 + jnp.tanh(inner))).astype(BF16)
-        found = dot_nn(activated_ref[at, :], down_ref[...])
+
+
+def mlp_up(parts, up, count, deps=()):
+    total, columns, hidden = sum(m.shape[0] for m in parts), up.shape[0], up.shape[1]
+    return call(
+        functools.partial(mlp_up_kernel, count, len(parts)),
+        [((total, columns), BF16), ((total, hidden), F32), ((total, hidden), BF16)],
+        [],
+        15,
+        *parts,
+        up,
+        deps=deps,
+    )
+
+
+def mlp_down_kernel(count, activated_ref, down_ref, own_ref, *piece_refs):
+    rows = own_ref.shape[0]
+    for j in range(count - 1, -1, -1):
+        found = dot_nn(activated_ref[j * rows : (j + 1) * rows, :], down_ref[...])
         if j == 0:
             own_ref[...] = found
         else:
             put_pieces(piece_refs, count, j, found)
 
 
-def mlp_forward(parts, up, down, count, deps=()):
-    total, columns, hidden = sum(m.shape[0] for m in parts), up.shape[0], up.shape[1]
-    rows = total // count
+def mlp_down(activated, down, count, deps=()):
+    rows, columns = activated.shape[0] // count, down.shape[1]
     found = call(
-        functools.partial(mlp_forward_kernel, count, len(parts)),
-        [
-            ((total, columns), BF16),
-            ((total, hidden), F32),
-            ((total, hidden), BF16),
-            ((rows, columns), F32),
-        ]
-        + piece_shapes(count, rows, columns),
+        functools.partial(mlp_down_kernel, count),
+        [((rows, columns), F32)] + piece_shapes(count, rows, columns),
         [],
-        22,
-        *parts,
-        up,
+        11,
+        activated,
         down,
         deps=deps,
     )
-    return list(found[:4]) + [list(found[4:])]
+    return found[0], list(found[1:])
+
+
+def stack_kernel(*refs):
+    start = 0
+    for ref in refs[:-1]:
+        refs[-1][start : start + ref.shape[0], :] = ref[...]
+        start += ref.shape[0]
+
+
+def stack_rows(parts, deps=()):
+    shape = (sum(m.shape[0] for m in parts), parts[0].shape[1])
+    return call(stack_kernel, [(shape, parts[0].dtype)], [], 3, *parts, deps=deps)[0]
 
 
 def mlp_backward_kernel(count, parts, *refs):
@@ -808,10 +863,23 @@
     return found
 
 
-def settle_kernel(count, parts, groups, pieces, width, scalars_ref, *refs):
+def pack_kernel(count, *refs):
+    start = 0
+    for ref in refs[:count]:
+        refs[count][: ref.shape[0], start : start + ref.shape[1]] = ref[...]
+        start += ref.shape[1]
+
+
+def pack(shards):
+    rows = -(-max(m.shape[0] for m in shards) // 32) * 32
+    shape = (rows, sum(m.shape[1] for m in shards))
+    return call(functools.partial(pack_kernel, len(shards)), [(shape, BF16)], [], 3, *shards)[0]
+
+
+def settle_kernel(count, parts, plan, scalars_ref, *refs):
     block_refs, refs = refs[:parts], refs[parts:]
-    out_refs, stack_ref = refs[-pieces - 1 : -1], refs[-1]
-    stride = stack_ref.shape[2] // (pieces * groups)
+    outs = sum(entry[3] for entry in plan)
+    out_refs, stack_ref = refs[-outs - 1 : -1], refs[-1]
     for j in range(count):
         owner = scalars_ref[count + j]
         if j == count - 1 and parts > count:
@@ -820,75 +888,53 @@
             stack_ref[owner, cut:] = block_refs[j + 1][...]
         else:
             stack_ref[owner] = block_refs[j][...]
-    for p in range(pieces):
-        for g in range(groups):
+    place = 0
+    for first, rows, groups, pieces, width, stride in plan:
+        if not groups:
             for a in range(count):
-                low = (p * groups + g) * stride
-                at = (g * count + a) * width
-                out_refs[p][0, :, at : at + width] = stack_ref[a, :, low : low + width].astype(F32)
-
-
-def settle_rows_kernel(count, parts, scalars_ref, *refs):
-    block_refs, out_ref = refs[:parts], refs[-1]
-    rows = block_refs[0].shape[0]
-    for j in range(count):
-        low = pl.multiple_of(scalars_ref[count + j] * rows, rows)
-        if j == count - 1 and parts > count:
-            cut = block_refs[j].shape[0]
-            out_ref[0, pl.ds(low, cut), :] = block_refs[j][...].astype(F32)
-            out_ref[0, pl.ds(low + cut, rows - cut), :] = block_refs[j + 1][...].astype(F32)
-        else:
-            out_ref[0, pl.ds(low, rows), :] = block_refs[j][...].astype(F32)
-
-
-def settle_call(kernel, scalars, blocks, shape, pieces, layer, layer_count, before, scratch):
+                found = stack_ref[a, :rows, first : first + width]
+                out_refs[place][0, a * rows : (a + 1) * rows, :] = found.astype(F32)
+        for p in range(pieces):
+            for g in range(groups):
+                for a in range(count):
+                    low = first + (p * groups + g) * stride
+                    at = (g * count + a) * width
+                    found = stack_ref[a, :rows, low : low + width]
+                    out_refs[place + p][0, :, at : at + width] = found.astype(F32)
+        place += pieces
+
+
+def settle(scalars, blocks, plan, layer, layer_count, before):
+    count = lax.axis_size("seq")
+    shapes = []
+    for _, rows, groups, pieces, width, _ in plan:
+        shapes += [(rows, groups * count * width) if groups else (count * rows, width)] * pieces
     held = [] if before is None else list(before)
     inputs = [pl.BlockSpec(memory_space=pltpu.VMEM)] * len(blocks)
     inputs += [pl.BlockSpec(memory_space=pl.ANY)] * len(held)
     found = pl.pallas_call(
-        kernel,
+        functools.partial(settle_kernel, count, len(blocks), plan),
         grid=(1,),
-        out_shape=[jax.ShapeDtypeStruct((layer_count,) + shape, F32)] * pieces,
+        out_shape=[jax.ShapeDtypeStruct((layer_count,) + shape, F32) for shape in shapes],
         in_specs=[pl.BlockSpec(memory_space=pltpu.SMEM)] + inputs,
-        out_specs=[pl.BlockSpec((1,) + shape, lambda i: (layer, 0, 0))] * pieces,
-        scratch_shapes=scratch,
+        out_specs=[pl.BlockSpec((1,) + shape, lambda i: (layer, 0, 0)) for shape in shapes],
+        scratch_shapes=[pltpu.VMEM((count,) + blocks[0].shape, BF16)],
         input_output_aliases={1 + len(blocks) + i: i for i in range(len(held))},
         compiler_params=pltpu.CompilerParams(vmem_limit_bytes=VMEM_LIMIT),
-        cost_estimate=pl.CostEstimate(flops=4_000_000_000, bytes_accessed=1000, transcendentals=0),
+        cost_estimate=pl.CostEstimate(flops=8_000_000_000, bytes_accessed=1000, transcendentals=0),
     )(scalars, *blocks, *held)
     return list(found)
 
 
-def settle(scalars, blocks, groups, pieces, width, layer, layer_count, before=None):
-    count = lax.axis_size("seq")
-    rows, columns = blocks[0].shape
-    return settle_call(
-        functools.partial(settle_kernel, count, len(blocks), groups, pieces, width),
-        scalars,
-        blocks,
-        (rows, count * groups * width),
-        pieces,
-        layer,
-        layer_count,
-        before,
-        [pltpu.VMEM((count, rows, columns), BF16)],
-    )
-
-
-def settle_rows(scalars, blocks, layer, layer_count, before=None):
-    count = lax.axis_size("seq")
-    rows, columns = blocks[0].shape
-    return settle_call(
-        functools.partial(settle_rows_kernel, count, len(blocks)),
-        scalars,
-        blocks,
-        (count * rows, columns),
-        1,
-        layer,
-        layer_count,
-        before,
-        [],
-    )
+def finish(scalars, entries, layer, layer_count, before=None):
+    plan, first = [], 0
+    for shard, groups, pieces, width in entries:
+        rows, columns = shard.shape
+        stride = columns // (groups * pieces) if groups else columns
+        plan.append((first, rows, groups, pieces, width, stride))
+        first += columns
+    blocks = gather_parts(pack([entry[0] for entry in entries]))
+    return settle(scalars, blocks, tuple(plan), layer, layer_count, before)
 
 
 def swap_seq(block, bits):
@@ -1016,22 +1062,23 @@
     return gather_halves([dot_nn(m, kv_part).astype(BF16) for m in halves_of(text_rows)])
 
 
-def layer_forward(parts, hidden, scalars, gains, shift, pairs, weights, normed, deps):
-    qkv_part, square_parts, _, up_part, down_part = weights
+def layer_forward(parts, hidden, scalars, gains, shift, kv_part, text_rows, weights, normed, cross_deps):
+    lead_part, square_parts, up_part = weights
     seq_count = lax.axis_size("seq")
     tok_rows, model_width = hidden.shape
     head_size, width = model_width // H, model_width // seq_count
     first_all, triples, mixed = self_forward(
-        parts, qkv_part, gains, shift, head_size, seq_count, width, normed, deps[0]
-    )
+        parts, lead_part, gains, shift, head_size, seq_count, width, normed
+    )
+    (kv_part,) = gate([kv_part], [mixed[0]])
+    pairs = text_pairs(text_rows, kv_part)
     self_tokens, after_self, cross_norm, queries, cross_tokens, after_cross, mlp_halves = (
         middle_forward(
-            scalars, exchange_rel(mixed), square_parts, pairs, hidden, gains, head_size, deps[1]
+            scalars, exchange_rel(mixed), square_parts, pairs, hidden, gains, head_size, cross_deps
         )
     )
-    mlp_all, up_rows, activated, own, pieces = mlp_forward(
-        gather_halves(mlp_halves), up_part, down_part, seq_count, deps[2]
-    )
+    mlp_parts = gather_halves(mlp_halves)
+    mlp_all, up_rows, activated = mlp_up(mlp_parts, up_part, seq_count)
     saved = (
         first_all,
         triples,
@@ -1045,116 +1092,49 @@
         up_rows,
         activated,
     )
-    return (scatter_parts(own, pieces), saved)
-
-
-def layer_backward(out_parts, grad_out, saved, scalars, gains, text_rows, pairs, weights, deps):
-    qkv_part, square_parts, kv_part, up_part, down_part = weights
-    (
-        first_all,
-        triples,
-        self_tokens,
-        after_self,
-        cross_norm,
-        queries,
-        cross_tokens,
-        after_cross,
-        mlp_all,
-        up_rows,
-        activated,
-    ) = saved
-    seq_count = lax.axis_size("seq")
-    head_size = after_self.shape[1] // H
-
-    out_all, grad_up_rows, own, pieces = mlp_backward(
-        out_parts, up_rows, up_part, down_part, seq_count, deps[0]
-    )
-    terms = scatter_parts(own, pieces)
-    grad_down = dot_tn(activated, out_all).astype(BF16)
-    grad_up = dot_tn(mlp_all, grad_up_rows).astype(BF16)
-    (
-        grad_after_self,
-        self_branch,
-        query_branch,
-        cross_branch,
-        gain_grads,
-        mixed_grads,
-        own_pairs,
-        pair_pieces,
-    ) = middle_backward(
-        scalars,
-        square_parts,
-        pairs,
-        terms,
-        grad_out,
-        after_cross,
-        after_self,
-        queries,
-        gains,
-        head_size,
-        (grad_down, grad_up) + deps[1],
-    )
-    squares = outer(
-        scalars,
-        [self_tokens, cross_norm, cross_tokens],
-        [self_branch, query_branch, cross_branch],
-    )
-    grad_triples, own, pieces = self_backward(
-        triples, exchange_rel(mixed_grads), qkv_part, head_size, (squares[0],) + deps[2]
-    )
-    terms = scatter_parts(own, pieces)
-    grad_qkv = dot_tn(first_all, grad_triples).astype(BF16)
-    pair_terms = scatter_parts(own_pairs, pair_pieces)
-    if seq_count == 4:
-        grad_pairs = jnp.concatenate(
-            [
-                add_bf16(pair_terms[0][low:high], pair_terms[1 + k], pair_terms[3 + k])
-                for k, (low, high) in enumerate(cuts(seq_count, text_rows.shape[0]))
-            ]
+    return (saved, kv_part, pairs, mlp_parts)
+
+
+def unspread_first(blocks, ready):
+    own, first_mine, first_other, second_mine, second_other, corner_mine, corner_other = blocks
+    swapped = [swap_core(corner_other), swap_core(second_mine), swap_core(second_other)]
+    from_corner, to_other, to_mine = gate(swapped, ready)
+    passed = swap_by_core(add_bf16(corner_mine, from_corner), 2, 1)
+    other = swap_by_core(add_bf16(first_other, to_other), 1, 2)
+    return own, other, passed, [first_mine, to_mine]
+
+
+def unspread_last(scalars, first, ready):
+    own, other, passed, terms = first
+    (passed,) = gate([passed], ready)
+    mine = swap_by_core(add_bf16(*terms, passed), 1, 2)
+    return join_halves(scalars, own, mine, other)
+
+
+def unspread_any(blocks):
+    return add_bf16(blocks[0], *[swap_seq(m, j + 1) for j, m in enumerate(blocks[1:])])
+
+
+def gather_lead(layer, qkv, query, self_out, cross_out):
+    padded = padded_width(query.shape[2] // lax.axis_size("seq"))
+    return gather_fsdp(
+        jnp.concatenate(
+            [own_part(qkv[layer], 3, padded)]
+            + [own_part(m[layer], 1, padded) for m in (self_out, query, cross_out)],
+            axis=1,
         )
-    else:
-        grad_pairs = add_bf16(*pair_terms)
-    grad_text = dot_nt(grad_pairs, kv_part)
-    shards = (
-        scatter_fsdp(grad_qkv),
-        scatter_fsdp(unspread(scalars, squares)),
-        scatter_fsdp(dot_tn(text_rows, grad_pairs)),
-        scatter_fsdp(grad_up),
-        scatter_fsdp(grad_down),
-    )
-    return (terms, grad_after_self, gain_grads, grad_text, shards, grad_qkv)
-
-
-def gather_block(layer, qkv, query, text_kv, self_out, cross_out, up, down):
-    s, seq_count = lax.axis_index("seq"), lax.axis_size("seq")
-    fsdp_count = lax.axis_size("fsdp")
-    padded = padded_width(query.shape[2] // seq_count)
-    squares = jnp.concatenate(
-        [own_part(m[layer], 1, padded) for m in (self_out, query, cross_out)], axis=1
-    )
+    )
+
+
+def gather_rest(layer, text_kv, up, down):
+    s, seq_count, fsdp_count = lax.axis_index("seq"), lax.axis_size("seq"), lax.axis_size("fsdp")
+    padded = padded_width(text_kv.shape[2] // (2 * seq_count))
     rows = down.shape[1] // seq_count
     return (
-        gather_fsdp(own_part(qkv[layer], 3, padded)),
-        spread(gather_fsdp(squares)),
         gather_fsdp(own_part(text_kv[layer], 2, padded)),
         gather_fsdp(own_part(up[layer], fsdp_count, up.shape[2] // (fsdp_count * seq_count))),
         gather_fsdp(lax.dynamic_slice_in_dim(down[layer], s * rows, rows, 0)),
     )
-
-
-def finish_block(scalars, shards, width, layer, before):
-    qkv_shard, square_shard, kv_shard, up_shard, down_shard = shards
-    fsdp_count = lax.axis_size("fsdp")
-    if before is None:
-        before = [None] * 5
-    up_width = up_shard.shape[1] // fsdp_count
-    return [
-        settle(scalars, gather_parts(qkv_shard), 3, 1, width, layer, 2, before[0]),
-        settle(scalars, gather_parts(square_shard), 1, 3, width, layer, 2, before[1]),
-        settle(scalars, gather_parts(kv_shard), 2, 1, width, layer, 2, before[2]),
-        settle(scalars, gather_parts(up_shard), fsdp_count, 1, up_width, layer, 2, before[3]),
-        settle_rows(scalars, gather_parts(down_shard), layer, 2, before[4]),
-    ]
 
 
 def sum_vectors(vectors):
@@ -1218,68 +1198,173 @@
     shift_terms = jnp.einsum("br,lrd->bld", silu_part, mod_weight.astype(F32), precision=EXACT)
     shifts = jnp.sum(lax.all_to_all(shift_terms, "fsdp", 0, 0, tiled=True), axis=0)
 
-    stacks = (
-        qkv_weight,
-        query_weight,
-        text_kv_weight,
-        self_out_weight,
-        cross_out_weight,
-        up_weight,
-        down_weight,
-    )
-    first_weights = gather_block(0, *stacks)
-    first_pairs = text_pairs(text_rows, first_weights[2])
-    first_terms, first_saved = layer_forward(
+    lead_stacks = (qkv_weight, query_weight, self_out_weight, cross_out_weight)
+    rest_stacks = (text_kv_weight, up_weight, down_weight)
+    lead_columns = 3 * padded_width(width)
+    head_size = model_width // H
+    fours = seq_count == 4
+
+    lead_first = gather_lead(0, *lead_stacks)
+    kv_first, up_first, down_first = gather_rest(0, *rest_stacks)
+    (square_first,) = gate([lead_first[:, lead_columns:]], [shifts])
+    squares_first = spread(square_first)
+    saved_first, kv_first, pairs_first, mlp_parts = layer_forward(
         gather_halves(halves_of(latents[0])),
         latents[0],
         scalars,
         gains[0],
         shifts[0],
-        first_pairs,
-        first_weights,
+        kv_first,
+        text_rows,
+        (lead_first, squares_first, up_first),
         False,
-        ((), (), ()),
-    )
-    out_parts = gather_halves(halves_of(cotangent[0]))
-    skip_parts = spread(
-        gather_fsdp(own_part(skip_weight, 1, padded_width(width)))
-    )
+        (),
+    )
+    out_halves = gate(halves_of(cotangent[0]), mlp_parts[-2:])
+    out_parts = gather_halves(out_halves)
+    own, pieces = mlp_down(saved_first[10], down_first, seq_count)
+    terms = scatter_parts(own, pieces)
+
+    (skip_matrix,) = gate(
+        [gather_fsdp(own_part(skip_weight, 1, padded_width(width)))], [own]
+    )
+    skip_parts = spread(skip_matrix)
     first_out, joined_norm, skip_out, second_halves = skip_forward(
         scalars,
         skip_parts,
-        first_terms,
-        first_saved[7],
+        terms,
+        saved_first[7],
         skip_input[0],
         skip_gains,
         gains[1],
         shifts[1],
-        (out_parts[-1], out_parts[-2]),
-    )
-    second_weights = gather_block(1, *stacks)
-    second_pairs = text_pairs(text_rows, second_weights[2])
-    second_terms, second_saved = layer_forward(
-        gather_halves(second_halves),
+        out_parts[-2:],
+    )
+
+    lead_second = gather_lead(1, *lead_stacks)
+    kv_second, up_second, down_second = gather_rest(1, *rest_stacks)
+    second_parts = gather_halves(second_halves)
+    (square_second,) = gate([lead_second[:, lead_columns:]], second_parts[-2:])
+    squares_second = spread(square_second)
+    saved_second, kv_second, pairs_second, _ = layer_forward(
+        second_parts,
         skip_out,
         scalars,
         gains[1],
         shifts[1],
-        second_pairs,
-        second_weights,
+        kv_second,
+        text_rows,
+        (lead_second, squares_second, up_second),
         True,
-        ((), (), ()),
-    )
-    output = close_forward(second_terms, second_saved[7])
-
-    terms, grad_after_self, gain_grads, text_second, shards_second, grad_qkv = layer_backward(
-        out_parts,
+        (),
+    )
+    out_all = stack_rows(out_parts, (saved_second[7],))
+
+    def block_backward(rows, grad_out, saved, block, weights, early, mlp_deps, middle_deps, self_deps):
+        lead_part, square_parts, kv_part, up_part, down_part = weights
+        grad_down = dot_tn(saved[10], early).astype(BF16) if early is not None else None
+        found_all, grad_up_rows, own, pieces = mlp_backward(
+            rows,
+            saved[9],
+            up_part,
+            down_part,
+            seq_count,
+            mlp_deps + ((grad_down,) if early is not None else ()),
+        )
+        terms = scatter_parts(own, pieces)
+        if early is None:
+            grad_down = dot_tn(saved[10], found_all).astype(BF16)
+        grad_up = dot_tn(saved[8], grad_up_rows).astype(BF16)
+        down_shard, up_shard = scatter_fsdp(grad_down), scatter_fsdp(grad_up)
+        (
+            grad_after_self,
+            self_branch,
+            query_branch,
+            cross_branch,
+            gain_grads,
+            mixed_grads,
+            own_pairs,
+            pair_pieces,
+        ) = middle_backward(
+            scalars,
+            square_parts,
+            pairs_first if block == 0 else pairs_second,
+            terms,
+            grad_out,
+            saved[7],
+            saved[3],
+            saved[5],
+            gains[block],
+            head_size,
+            (grad_down, grad_up) + middle_deps(grad_up_rows),
+        )
+        squares = outer(
+            scalars,
+            [saved[2], saved[4], saved[6]],
+            [self_branch, query_branch, cross_branch],
+        )
+        grad_triples, own, pieces = self_backward(
+            saved[1],
+            exchange_rel(mixed_grads),
+            lead_part,
+            head_size,
+            (squares[0], down_shard) + self_deps(grad_after_self),
+        )
+        terms = scatter_parts(own, pieces)
+        grad_qkv = dot_tn(saved[0], grad_triples).astype(BF16)
+        pair_pieces = gate(pair_pieces, [grad_triples])
+        pair_terms = scatter_parts(own_pairs, pair_pieces)
+        if fours:
+            grad_pairs = jnp.concatenate(
+                [
+                    add_bf16(pair_terms[0][low:high], pair_terms[1 + k], pair_terms[3 + k])
+                    for k, (low, high) in enumerate(cuts(seq_count, text_rows.shape[0]))
+                ]
+            )
+        else:
+            grad_pairs = add_bf16(*pair_terms)
+        grad_text = dot_nt(grad_pairs, kv_part)
+        kv_shard = scatter_fsdp(dot_tn(text_rows, grad_pairs))
+        if fours:
+            squares = unspread_first(squares, [grad_triples])
+        return (
+            terms,
+            grad_after_self,
+            gain_grads,
+            grad_text,
+            squares,
+            grad_qkv,
+            scatter_fsdp(grad_qkv),
+            kv_shard,
+            up_shard,
+            down_shard,
+        )
+
+    def squares_done(squares, ready):
+        joined = unspread_last(scalars, squares, ready) if fours else unspread_any(squares)
+        return joined, scatter_fsdp(joined)
+
+    (
+        terms,
+        grad_after_self,
+        gain_grads,
+        text_second,
+        squares,
+        grad_qkv,
+        qkv_shard,
+        kv_shard,
+        up_shard,
+        down_shard,
+    ) = block_backward(
+        [out_all],
         cotangent[0],
-        second_saved,
-        scalars,
-        gains[1],
-        text_rows,
-        second_pairs,
-        second_weights,
-        ((), (), ()),
+        saved_second,
+        1,
+        (lead_second, squares_second, kv_second, up_second, down_second),
+        out_all,
+        (),
+        lambda done: (),
+        lambda done: (),
     )
     skip_branch, grad_first_out, grad_skip, vectors, first_halves = skip_backward(
         scalars,
@@ -1291,40 +1376,80 @@
         first_out,
         skip_input[0],
         skip_gains,
-        (grad_qkv,),
+        (grad_qkv, up_shard),
     )
     vectors_second = jnp.concatenate([vectors[:2], gain_grads, vectors[2:]], axis=0)
-    skip_shard = scatter_fsdp(
-        unspread(scalars, outer(scalars, [joined_norm], [skip_branch]))
-    )
-    second_done = finish_block(scalars, shards_second, width, 1, None)
-    terms, grad_after_self, gain_grads, text_first, shards_first, grad_qkv = layer_backward(
+    square_joined, square_shard = squares_done(squares, [grad_first_out])
+    skip_outer = outer(scalars, [joined_norm], [skip_branch])
+    held = {}
+
+    def skip_first(done):
+        if fours:
+            held["first"] = unspread_first(skip_outer, [done])
+        else:
+            held["joined"] = unspread_any(skip_outer)
+        return (kv_shard,)
+
+    def skip_last(done):
+        if fours:
+            held["joined"] = unspread_last(scalars, held["first"], [done])
+        held["shard"] = scatter_fsdp(held["joined"])
+        return (qkv_shard,)
+
+    second_layer = (qkv_shard, square_shard, kv_shard, up_shard, down_shard)
+    (
+        terms,
+        grad_after_self,
+        gain_grads,
+        text_first,
+        squares,
+        grad_qkv,
+        qkv_shard,
+        kv_shard,
+        up_shard,
+        down_shard,
+    ) = block_backward(
         gather_halves(first_halves),
         grad_first_out,
-        first_saved,
-        scalars,
-        gains[0],
-        text_rows,
-        first_pairs,
-        first_weights,
-        (
-            (shards_second[4], shards_second[3]),
-            (shards_second[2], shards_second[1]),
-            (shards_second[0], second_done[4][0], second_done[3][0]),
-        ),
-    )
+        saved_first,
+        0,
+        (lead_first, squares_first, kv_first, up_first, down_first),
+        None,
+        (skip_outer[0], square_joined),
+        skip_first,
+        skip_last,
+    )
+    skip_shard = held["shard"]
     grad_latents, vectors = open_backward(
-        terms, latents[0], gains[0], grad_after_self, (grad_qkv, skip_shard, second_done[0][0])
+        terms, latents[0], gains[0], grad_after_self, (grad_qkv, skip_shard, square_shard)
     )
     vectors_first = jnp.concatenate([vectors, gain_grads], axis=0)
-    first_done = finish_block(scalars, shards_first, width, 0, second_done)
-    (grad_qkv,), (grad_self_out, grad_query, grad_cross_out), (grad_kv,), (grad_up,), (grad_down,) = (
-        first_done
-    )
-    (grad_skip_weight,) = settle(scalars, gather_parts(skip_shard), 1, 1, width, 0, 1)
-
-    second_sums = sum_vectors(vectors_second)
-    first_sums = sum_vectors(vectors_first)
+    _, square_shard = squares_done(squares, [grad_latents])
+    first_layer = (qkv_shard, square_shard, kv_shard, up_shard, down_shard)
+
+    own, pieces = mlp_down(saved_second[10], down_second, seq_count, (grad_latents,))
+    output = close_forward(scatter_parts(own, pieces), saved_second[7])
+
+    def entries(layer):
+        qkv, square, kv, up, down = layer
+        return (
+            [
+                (up, fsdp_count, 1, up.shape[1] // fsdp_count),
+                (kv, 2, 1, width),
+                (down, 0, 1, down.shape[1]),
+            ],
+            [(qkv, 3, 1, width), (square, 1, 3, width)],
+        )
+
+    early, late = entries(second_layer)
+    early_done, late_done = finish(scalars, early, 1, 2), finish(scalars, late, 1, 2)
+    early, late = entries(first_layer)
+    grad_up, grad_kv, grad_down = finish(scalars, early, 0, 2, early_done)
+    grad_qkv, grad_self_out, grad_query, grad_cross_out = finish(scalars, late, 0, 2, late_done)
+    (grad_skip_weight,) = finish(scalars, [(skip_shard, 1, 1, width)], 0, 1)
+
+    sums = sum_vectors(jnp.concatenate([vectors_first, vectors_second], axis=0))
+    first_sums, second_sums = sums[:, :4], sums[:, 4:]
     shift_grads = jnp.stack([first_sums[:, 0], second_sums[:, 0]], axis=1)
     gain_sums = jnp.stack([first_sums[:, 1:4].sum(axis=0), second_sums[:, 1:4].sum(axis=0)])
     grad_norm_gains = lax.dynamic_slice_in_dim(gain_sums, f * shard_rows, shard_rows, 2)

time: 1350 us -> 1410 us (1.044)
  starting transfers between devices: 226 us -> 189 us
  blocking collectives: 0 us -> 25.2 us
  local copies, waits for them, and re-layouts: 70.9 us -> 92.4 us
  waiting for transfers between devices: 549 us -> 567 us
  other arithmetic: 32.4 us -> 47.2 us
    ppermute x158 -> x132, waiting for transfers between devices: 326 us -> 392 us  [swap_seq(): return lax.ppermute(block, 'seq', [(i, i ^ bits) for i in range(seq_count)])]
    all_gather x11 -> x9, waiting for transfers between devices: 91.5 us -> 28.5 us  [gather_fsdp(): return lax.all_gather(shard, 'fsdp', axis=0, tiled=True)]
    all_to_all x0 -> x2, blocking collectives: none -> 25.2 us  [the longest x1 13 us: body(): small = lax.all_to_all(small, 'fsdp', 0, 0, tiled=True)]
    ppermute x158 -> x132, starting transfers between devices: 166 us -> 143 us  [swap_seq(): return lax.ppermute(block, 'seq', [(i, i ^ bits) for i in range(seq_count)])]
    ppermute x15, waiting for transfers between devices: 111 us -> 134 us  [swap_by_core(): return lax.ppermute(block, ('seq', 'fsdp'), pairs)]
    pallas_call x22 -> x30, Pallas kernels: 345 us -> 366 us  [call(): pl.pallas_call(run, out_shape=tuple((jax.ShapeDtypeStruct(s, d) for s, d...]
    convert_element_type x27, other arithmetic: 22.6 us -> 39.3 us  [add_bf16(): return total.astype(BF16)]
    unnamed x397 -> x341, local copies, waits for them, and re-layouts: 26.4 us -> 36.9 us
  transfers between devices with their start and end apart: 219 -> 186, of which waited for: 82 -> 82; matrix products, arithmetic and copies ran while one was open for 10% -> 12% of each run, Pallas kernels for 27% -> 28%
where the time goes in v4:
time: 1410 us; the launch traced here: 1400 us
  waiting for transfers between devices  567 us (40%)
  Pallas kernels  395 us (28%)
  starting transfers between devices  189 us (13%)
  local copies, waits for them, and re-layouts  92.4 us (7%)
  matrix products  66.4 us (5%)
  other arithmetic  47.2 us (3%)
  blocking collectives  25.2 us (2%)
  between operations  17.4 us (1%)
    ppermute x132, waiting for transfers between devices, swap_seq(): return lax.ppermute(block, 'seq', [(i, i ^ bits) for i in range(seq_count)])  392 us
    pallas_call x30, Pallas kernels, call(): pl.pallas_call(run, out_shape=tuple((jax.ShapeDtypeStruct(s, d) for s, d...  366 us
    ppermute x132, starting transfers between devices, swap_seq(): return lax.ppermute(block, 'seq', [(i, i ^ bits) for i in range(seq_count)])  143 us
    ppermute x15, waiting for transfers between devices, swap_by_core(): return lax.ppermute(block, ('seq', 'fsdp'), pairs)  134 us
    dot_general x8, matrix products, dot_tn(): lax.dot_general(a, b, (((0,), (0,)), ((), ())), preferred_element_type=F32)  53.7 us
    convert_element_type x27, other arithmetic, add_bf16(): return total.astype(BF16)  39.3 us
    unnamed x341, local copies, waits for them, and re-layouts  36.9 us
    pallas_call x5, Pallas kernels, settle(): pl.pallas_call(functools.partial(settle_kernel, count, len(blocks), plan)...  28.7 us
  transfers between devices with their start and end apart: 186, of which 82 were waited for; matrix products, arithmetic and copies ran while one was open for 12% of the time, Pallas kernels for 28%

profile of v4, /device:TPU:0, one launch (start us, length us, event | category | flops | bytes accessed | tf_op | source)
XLA Modules:
  0.0 1399.3 jit_solution(6035021021431764919)
XLA Ops:
  61.3 28.5 %all-gather.14.cloned.1.call-done.refs_8_.refs_5_ = bf16[1408,2304]{1,0:T(8,128)(2,1)} async-done(((bf16[176,2304]{1,0:T(8,128)(2,1)}), bf16[1408,2304]{1,0:T(8,128)(2,1)}) %all-gather.14.cloned.1.call-update) | async-done | bytes 6488080 | tf_op jit(solution)/shard_map/all_gather | solution.py:1054
  97.9 34.4 %collective-permute-done.9.refs_6_.refs_2_ = bf16[1408,1152]{1,0:T(8,128)(2,1)} collective-permute-done((bf16[1408,1152]{1,0:T(8,128)(2,1)}, bf16[1408,1152]{1,0:T(8,128)(2,1)}, u32[]{:S(2)}, u32[]{:S(2)}) %collective-permute-start.9) | collective-permute-done | bytes 3244064 | tf_op jit(solution)/shard_map/ppermute | solution.py:961
  141.0 25.5 %collective-permute-done.2.refs_4_ = bf16[128,1408]{1,0:T(8,128)(2,1)S(1)} collective-permute-done((bf16[128,1408]{1,0:T(8,128)(2,1)}, bf16[128,1408]{1,0:T(8,128)(2,1)S(1)}, u32[]{:S(2)}, u32[]{:S(2)}) %collective-permute-start.2) | collective-permute-done | bytes 360480 | tf_op jit(solution)/shard_map/ppermute | solution.py:942
  179.7 18.6 %shard_map.288 = (bf16[1024,1408]{1,0:T(8,128)(2,1)}, bf16[1024,1152]{1,0:T(8,128)(2,1)}, bf16[256,352]{1,0:T(8,128)(2,1)}, bf16[256,352]{1,0:T(8,128)(2,1)}, bf...) custom-call(bf16[128,1408]{1,0:T(8,128)(2,1)} %get-tuple-element.501.refs_0_, bf16[128,1408]{1,0:T(8,128)(2,1)} %copy-done.71, ...), custom_call_target="tpu_custom_call" | custom-call | flops 24000000000 | bytes 1000 | tf_op jit(solution)/shard_map/pallas_call | solution.py:50
  234.2 21.1 %shard_map.291 = (bf16[256,1408]{1,0:T(8,128)(2,1)}, f32[256,1408]{1,0:T(8,128)}, bf16[256,1408]{1,0:T(8,128)(2,1)}, bf16[4,256,352]{2,1,0:T(8,128)(2,1)}, bf16[...) custom-call(s32[10]{0:T(128)} %stack.83.refs_0_.scalars_ref, ...), custom_call_target="tpu_custom_call" | custom-call | flops 23000000512 | bytes 1000 | tf_op jit(solution)/shard_map/pallas_call | solution.py:50
  305.5 26.1 %collective-permute-done.25.refs_2_ = bf16[2816,384]{1,0:T(8,128)(2,1)} collective-permute-done((bf16[2816,384]{1,0:T(8,128)(2,1)}, bf16[2816,384]{1,0:T(8,128)(2,1)}, u32[]{:S(2)}, u32[]{:S(2)}) %collective-permute-start.25) | collective-permute-done | bytes 2162720 | tf_op jit(solution)/shard_map/ppermute | solution.py:961
  422.0 37.5 %collective-permute-done.48.refs_6_.refs_2_ = bf16[1408,1152]{1,0:T(8,128)(2,1)S(1)} collective-permute-done((bf16[1408,1152]{1,0:T(8,128)(2,1)}, bf16[1408,1152]{1,0:T(8,128)(2,1)S(1)}, u32[]{:S(2)}, u32[]{:S(2)}) %collective-permute-start.48) | collective-permute-done | bytes 3244064 | tf_op jit(solution)/shard_map/ppermute | solution.py:961
  466.7 18.8 %collective-permute-done.50.refs_8_.refs_4_ = bf16[704,1152]{1,0:T(8,128)(2,1)} collective-permute-done((bf16[704,1152]{1,0:T(8,128)(2,1)S(1)}, bf16[704,1152]{1,0:T(8,128)(2,1)}, u32[]{:S(2)}, u32[]{:S(2)}) %collective-permute-start.50) | collective-permute-done | bytes 1622048 | tf_op jit(solution)/shard_map/ppermute | solution.py:961
  489.3 18.2 %shard_map.297 = (bf16[1024,1408]{1,0:T(8,128)(2,1)}, bf16[1024,1152]{1,0:T(8,128)(2,1)}, bf16[256,352]{1,0:T(8,128)(2,1)}, bf16[256,352]{1,0:T(8,128)(2,1)}, bf...) custom-call(bf16[128,1408]{1,0:T(8,128)(2,1)} %get-tuple-element.217.refs_0_, ...), custom_call_target="tpu_custom_call" | custom-call | flops 24000000000 | bytes 1000 | tf_op jit(solution)/shard_map/pallas_call | solution.py:50
  540.3 21.0 %shard_map.300 = (bf16[256,1408]{1,0:T(8,128)(2,1)}, f32[256,1408]{1,0:T(8,128)}, bf16[256,1408]{1,0:T(8,128)(2,1)}, bf16[4,256,352]{2,1,0:T(8,128)(2,1)}, bf16[...) custom-call(s32[10]{0:T(128)} %stack.83.refs_0_.scalars_ref, ...), custom_call_target="tpu_custom_call" | custom-call | flops 23000000512 | bytes 1000 | tf_op jit(solution)/shard_map/pallas_call | solution.py:50
  611.7 19.7 %shard_map.303 = (bf16[1024,1408]{1,0:T(8,128)(2,1)}, bf16[1024,1536]{1,0:T(8,128)(2,1)}, f32[256,1408]{1,0:T(8,128)}, bf16[128,1408]{1,0:T(8,128)(2,1)}, bf16[1...) custom-call(bf16[1024,1408]{1,0:T(8,128)(2,1)} %shard_map.302.refs_0, ...), custom_call_target="tpu_custom_call" | custom-call | flops 22000001024 | bytes 1000 | tf_op jit(solution)/shard_map/pallas_call | solution.py:50
  656.0 27.7 %shard_map.304 = (f32[256,1408]{1,0:T(8,128)}, bf16[4,256,352]{2,1,0:T(8,128)(2,1)}, bf16[4,256,352]{2,1,0:T(8,128)(2,1)}, bf16[4,256,352]{2,1,0:T(8,128)(2,1)},...) custom-call(s32[10]{0:T(128)} %stack.83.refs_0_.scalars_ref, ...), custom_call_target="tpu_custom_call" | custom-call | flops 36999999488 | bytes 1000 | tf_op jit(solution)/shard_map/pallas_call | solution.py:50
  699.4 28.4 %shard_map.306 = (bf16[1024,1152]{1,0:T(8,128)(2,1)}, f32[256,1408]{1,0:T(8,128)}, bf16[128,1408]{1,0:T(8,128)(2,1)}, bf16[128,1408]{1,0:T(8,128)(2,1)}, bf16[12...) custom-call(bf16[1024,1152]{1,0:T(8,128)(2,1)} %get-tuple-element.228.ref, ...), custom_call_target="tpu_custom_call" | custom-call | flops 32000000000 | bytes 1000 | tf_op jit(solution)/shard_map/pallas_call | solution.py:50
  775.6 19.4 %collective-permute-done.76 = bf16[128,1408]{1,0:T(8,128)(2,1)S(1)} collective-permute-done((bf16[128,1408]{1,0:T(8,128)(2,1)}, bf16[128,1408]{1,0:T(8,128)(2,1)S(1)}, u32[]{:S(2)}, u32[]{:S(2)}) %collective-permute-start.76) | collective-permute-done | bytes 360480 | tf_op jit(solution)/shard_map/ppermute | solution.py:942
  811.3 13.8 shard_map.307
  866.6 19.5 %shard_map.312 = (bf16[1024,1408]{1,0:T(8,128)(2,1)}, bf16[1024,1536]{1,0:T(8,128)(2,1)}, f32[256,1408]{1,0:T(8,128)}, bf16[128,1408]{1,0:T(8,128)(2,1)}, bf16[1...) custom-call(bf16[128,1408]{1,0:T(8,128)(2,1)} %get-tuple-element.264, ...), custom_call_target="tpu_custom_call" | custom-call | flops 22000001024 | bytes 1000 | tf_op jit(solution)/shard_map/pallas_call | solution.py:50
  942.7 27.9 %shard_map.314 = (f32[256,1408]{1,0:T(8,128)}, bf16[4,256,352]{2,1,0:T(8,128)(2,1)}, bf16[4,256,352]{2,1,0:T(8,128)(2,1)}, bf16[4,256,352]{2,1,0:T(8,128)(2,1)},...) custom-call(s32[10]{0:T(128)} %stack.83.refs_0_.scalars_ref, ...), custom_call_target="tpu_custom_call" | custom-call | flops 36999999488 | bytes 1000 | tf_op jit(solution)/shard_map/pallas_call | solution.py:50
  1012.7 28.6 %shard_map.316 = (bf16[1024,1152]{1,0:T(8,128)(2,1)}, f32[256,1408]{1,0:T(8,128)}, bf16[128,1408]{1,0:T(8,128)(2,1)}, bf16[128,1408]{1,0:T(8,128)(2,1)}, bf16[12...) custom-call(bf16[1024,1152]{1,0:T(8,128)(2,1)} %get-tuple-element.227.ref, ...), custom_call_target="tpu_custom_call" | custom-call | flops 32000000000 | bytes 1000 | tf_op jit(solution)/shard_map/pallas_call | solution.py:50
  1084.5 30.7 %collective-permute-done.109 = bf16[128,1408]{1,0:T(8,128)(2,1)S(1)} collective-permute-done((bf16[128,1408]{1,0:T(8,128)(2,1)S(1)}, bf16[128,1408]{1,0:T(8,128)(2,1)S(1)}, u32[]{:S(2)}, u32[]{:S(2)}) %collective-permute-start.109) | collective-permute-done | bytes 360480 | tf_op jit(solution)/shard_map/ppermute | solution.py:942
  1146.0 15.3 %collective-permute-done.158.refs_2_ = bf16[192,3712]{1,0:T(8,128)(2,1)} collective-permute-done((bf16[192,3712]{1,0:T(8,128)(2,1)}, bf16[192,3712]{1,0:T(8,128)(2,1)}, u32[]{:S(2)}, u32[]{:S(2)}) %collective-permute-start.158) | collective-permute-done | bytes 1425440 | tf_op jit(solution)/shard_map/ppermute | solution.py:942
  1169.5 21.0 %collective-permute-done.162.refs_2_ = bf16[352,384]{1,0:T(8,128)(2,1)S(1)} collective-permute-done((bf16[352,384]{1,0:T(8,128)(2,1)}, bf16[352,384]{1,0:T(8,128)(2,1)S(1)}, u32[]{:S(2)}, u32[]{:S(2)}) %collective-permute-start.162) | collective-permute-done | bytes 270368 | tf_op jit(solution)/shard_map/ppermute | solution.py:942
  1239.5 13.9 collective-permute-start.136
  1302.5 18.3 %collective-permute-done.125.refs_4_ = bf16[128,1408]{1,0:T(8,128)(2,1)} collective-permute-done((bf16[128,1408]{1,0:T(8,128)(2,1)}, bf16[128,1408]{1,0:T(8,128)(2,1)}, u32[]{:S(2)}, u32[]{:S(2)}) %collective-permute-start.125) | collective-permute-done | bytes 360480 | tf_op jit(solution)/shard_map/ppermute | solution.py:942
  1347.7 15.2 %collective-permute-done.146.refs_2_ = bf16[192,2304]{1,0:T(8,128)(2,1)} collective-permute-done((bf16[192,2304]{1,0:T(8,128)(2,1)}, bf16[192,2304]{1,0:T(8,128)(2,1)}, u32[]{:S(2)}, u32[]{:S(2)}) %collective-permute-start.146) | collective-permute-done | bytes 884768 | tf_op jit(solution)/shard_map/ppermute | solution.py:942
  (889 shorter events, 832.9 us)
Async XLA Ops:
  7.2 82.6 %all-gather.14.cloned.1.call-start = ((), (), s32[]{:S(2)}) async-start(), calls=%async_computation.15 | async-start | bytes 7299072 | tf_op jit(solution)/shard_map/all_gather | solution.py:1054
  17.6 184.2 %all-gather.16.cloned.1.call-start = ((), (), s32[]{:S(2)}) async-start(), calls=%async_computation.16 | async-start | bytes 1769472 | tf_op jit(solution)/shard_map/all_gather | solution.py:1054
  20.7 249.7 %all-gather.18.cloned.1.call-start = ((), (), s32[]{:S(2)}) async-start(), calls=%async_computation.17 | async-start | bytes 4866048 | tf_op jit(solution)/shard_map/all_gather | solution.py:1054
  26.2 267.9 %all-gather.26.cloned.1.call-start = ((), (), s32[]{:S(2)}) async-start(), calls=%async_computation.32 | async-start | bytes 4866048 | tf_op jit(solution)/shard_map/all_gather | solution.py:1054
  31.4 272.3 %all-gather.12.cloned.1.call-start = ((), (), s32[]{:S(2)}) async-start(), calls=%async_computation.14 | async-start | bytes 2433024 | tf_op jit(solution)/shard_map/all_gather | solution.py:1054
  32.4 378.7 %all-gather.20.cloned.1.call-start = ((), (), s32[]{:S(2)}) async-start(), calls=%async_computation.18 | async-start | bytes 7299072 | tf_op jit(solution)/shard_map/all_gather | solution.py:1054
  97.6 413.5 %all-gather.22.cloned.1.call-start = ((), (), s32[]{:S(2)}) async-start(), calls=%async_computation.19 | async-start | bytes 1769472 | tf_op jit(solution)/shard_map/all_gather | solution.py:1054
  305.4 279.5 %all-gather.24.cloned.1.call-start = ((), (), s32[]{:S(2)}) async-start(), calls=%async_computation.20 | async-start | bytes 4866048 | tf_op jit(solution)/shard_map/all_gather | solution.py:1054
  334.6 277.1 %all-gather.28.cloned.1.call-start = ((), (), s32[]{:S(2)}) async-start(), calls=%async_computation.33 | async-start | bytes 4866048 | tf_op jit(solution)/shard_map/all_gather | solution.py:1054
  466.1 232.5 %reduce-scatter.12.cloned.1.call-start = ((), (), s32[]{:S(2)}) async-start(), calls=%async_computation.21 | async-start | bytes 4866048 | tf_op jit(solution)/shard_map/reduce_scatter | solution.py:1058
  466.6 72.4 %collective-permute-start.49 = (bf16[1408,1152]{1,0:T(8,128)(2,1)}, bf16[1408,1152]{1,0:T(8,128)(2,1)}, u32[]{:S(2)}, u32[]{:S(2)}) collective-permute-start(bf16[1408,1152]{1,0:T(8,128)(2,1)} %copy-done.41), channel_id=1, source_target_pairs={{0,1},{1,0},{2,3},{3,2},{4,5},{5,4},{6,7},{7,6},{8,9},{9,8},{10,11... | collective-permute-start | bytes 9732104 | tf_op jit(solution)/shard_map/ppermute | solution.py:947
  611.2 189.9 %reduce-scatter.14.cloned.1.call-start = ((), (), s32[]{:S(2)}) async-start(), calls=%async_computation.22 | async-start | bytes 4866048 | tf_op jit(solution)/shard_map/reduce_scatter | solution.py:1058
  654.6 281.8 %reduce-scatter.16.cloned.1.call-start = ((), (), s32[]{:S(2)}) async-start(), calls=%async_computation.23 | async-start | bytes 1769472 | tf_op jit(solution)/shard_map/reduce_scatter | solution.py:1058
  756.9 254.9 %reduce-scatter.20.cloned.1.call-start = ((), (), s32[]{:S(2)}) async-start(), calls=%async_computation.25 | async-start | bytes 3649536 | tf_op jit(solution)/shard_map/reduce_scatter | solution.py:1058
  761.8 63.3 %collective-permute-start.90 = (bf16[704,1152]{1,0:T(8,128)(2,1)}, bf16[704,1152]{1,0:T(8,128)(2,1)S(1)}, u32[]{:S(2)}, u32[]{:S(2)}) collective-permute-start(bf16[704,1152]{1,0:T(8,128)(2,1)} %add_convert_fusion.5), channel_id=1, source_target_pairs={{0,16},{1,9},{2,18},{3,11},{4,20},{5,13},{6,22},{7,15},{8,24},{9,1... | collective-permute-start | bytes 4866056 | tf_op jit(solution)/shard_map/ppermute | solution.py:961
  798.7 213.2 %reduce-scatter.18.cloned.1.call-start = ((), (), s32[]{:S(2)}) async-start(), calls=%async_computation.24 | async-start | bytes 4866048 | tf_op jit(solution)/shard_map/reduce_scatter | solution.py:1058
  894.6 238.1 %reduce-scatter.22.cloned.1.call-start = ((), (), s32[]{:S(2)}) async-start(), calls=%async_computation.26 | async-start | bytes 2433024 | tf_op jit(solution)/shard_map/reduce_scatter | solution.py:1058
  899.0 77.9 %collective-permute-start.119 = (bf16[1408,384]{1,0:T(8,128)(2,1)}, bf16[1408,384]{1,0:T(8,128)(2,1)}, u32[]{:S(2)}, u32[]{:S(2)}) collective-permute-start(bf16[1408,384]{1,0:T(8,128)(2,1)} %add_convert_fusion.6), channel_id=1, source_target_pairs={{0,8},{1,17},{2,10},{3,19},{4,12},{5,21},{6,14},{7,23},{8,0},{9,25... | collective-permute-start | bytes 3244040 | tf_op jit(solution)/shard_map/ppermute | solution.py:961
  995.4 137.4 %reduce-scatter.24.cloned.1.call-start = ((), (), s32[]{:S(2)}) async-start(), calls=%async_computation.27 | async-start | bytes 3649536 | tf_op jit(solution)/shard_map/reduce_scatter | solution.py:1058
  996.0 280.0 %reduce-scatter.30.cloned.1.call-start = ((), (), s32[]{:S(2)}) async-start(), calls=%async_computation.30 | async-start | bytes 4866048 | tf_op jit(solution)/shard_map/reduce_scatter | solution.py:1058
  996.6 279.4 %reduce-scatter.32.cloned.1.call-start = ((), (), s32[]{:S(2)}) async-start(), calls=%async_computation.31 | async-start | bytes 1769472 | tf_op jit(solution)/shard_map/reduce_scatter | solution.py:1058
  1061.7 260.3 %reduce-scatter.26.cloned.1.call-start = ((), (), s32[]{:S(2)}) async-start(), calls=%async_computation.28 | async-start | bytes 3649536 | tf_op jit(solution)/shard_map/reduce_scatter | solution.py:1058
  1070.0 252.0 %reduce-scatter.28.cloned.1.call-start = ((), (), s32[]{:S(2)}) async-start(), calls=%async_computation.29 | async-start | bytes 3649536 | tf_op jit(solution)/shard_map/reduce_scatter | solution.py:1058
  1130.7 70.8 %collective-permute-start.144 = (bf16[704,1152]{1,0:T(8,128)(2,1)}, bf16[704,1152]{1,0:T(8,128)(2,1)}, u32[]{:S(2)}, u32[]{:S(2)}) collective-permute-start(bf16[704,1152]{1,0:T(8,128)(2,1)} %add_convert_fusion), channel_id=1, source_target_pairs={{0,8},{1,17},{2,10},{3,19},{4,12},{5,21},{6,14},{7,23},{8,0},{9,25... | collective-permute-start | bytes 4866056 | tf_op jit(solution)/shard_map/ppermute | solution.py:961
  (325 other events, 5262.2 us)
Sparse Core Ops, SparseCore 0:
  17.7 72.0 all-gather.13
  91.4 23.5 all-gather.15
  117.3 47.9 all-gather.17
  167.4 47.1 all-gather.25
  216.1 28.3 all-gather.11
  246.5 65.8 all-gather.19
  314.1 23.8 all-gather.21
  340.2 47.7 all-gather.23
  466.3 45.7 all-gather.27
  611.3 48.8 reduce-scatter.11
  663.3 49.3 reduce-scatter.13
  757.1 31.8 reduce-scatter.15
  798.8 39.8 reduce-scatter.19
  894.7 49.4 reduce-scatter.17
  995.5 37.6 reduce-scatter.21
  1036.0 40.2 reduce-scatter.23
  1078.6 50.0 reduce-scatter.29
  1130.8 32.0 reduce-scatter.31
  1165.2 39.4 reduce-scatter.25
  1209.2 60.5 reduce-scatter.27

commit v5 on v4

--- a/solution.py
+++ b/solution.py
@@ -49,13 +49,14 @@
 
     return pl.pallas_call(
         run,
+        name=getattr(kernel, "func", kernel).__name__,
         out_shape=tuple(jax.ShapeDtypeStruct(s, d) for s, d in outs),
         in_specs=specs + [pl.BlockSpec(memory_space=pl.ANY)] * held,
         out_specs=tuple([pl.BlockSpec(memory_space=pltpu.VMEM)] * len(outs)),
         scratch_shapes=scratch,
         compiler_params=pltpu.CompilerParams(vmem_limit_bytes=VMEM_LIMIT),
         cost_estimate=pl.CostEstimate(
-            flops=int(micros * 1.0e9), bytes_accessed=1000, transcendentals=0
+            flops=int(micros * 1000), bytes_accessed=1000, transcendentals=0
         ),
     )(*operands, *deps)
 
@@ -82,22 +83,30 @@
     return rows // 32 * 16
 
 
-def cuts(count, rows):
-    return [(0, cut_of(rows)), (cut_of(rows), rows)] if count == 4 else [(0, rows)]
-
-
-def pieces_of(count, rows):
-    return [(j, low, high) for j in range(1, count) for low, high in cuts(count, rows)]
+def piece_shapes(count, rows, columns):
+    if count != 4:
+        return [((rows, columns), BF16)] * (count - 1)
+    cut = cut_of(rows)
+    return [((m, columns), BF16) for m in (2 * cut, 2 * (rows - cut), rows - cut, cut)]
 
 
 def put_pieces(refs, count, block, values):
-    for ref, (j, low, high) in zip(refs, pieces_of(count, values.shape[0])):
-        if j == block:
-            ref[...] = values[low:high].astype(BF16)
-
-
-def piece_shapes(count, rows, columns):
-    return [((high - low, columns), BF16) for _, low, high in pieces_of(count, rows)]
+    if count != 4:
+        refs[block - 1][...] = values.astype(BF16)
+        return
+    to_x, to_y, x_bottom, y_top = refs
+    rows = values.shape[0]
+    cut = cut_of(rows)
+    top, bottom = values[:cut].astype(BF16), values[cut:].astype(BF16)
+    if block == 1:
+        to_x[cut:, :] = top
+        x_bottom[...] = bottom
+    elif block == 2:
+        y_top[...] = top
+        to_y[rows - cut :, :] = bottom
+    else:
+        to_x[:cut, :] = top
+        to_y[: rows - cut, :] = bottom
 
 
 def add_terms(count, refs):
@@ -106,9 +115,11 @@
         for ref in refs[1:]:
             total = total + ref[...].astype(F32)
         return total
-    for low, high in ((1, 2), (3, 4)):
-        total = total + jnp.concatenate([refs[low][...], refs[high][...]], axis=0).astype(F32)
-    return total
+    from_x, from_y, x_bottom, y_top = [ref[...] for ref in refs[1:]]
+    cut, rest = y_top.shape[0], x_bottom.shape[0]
+    by_x = jnp.concatenate([from_x[cut:], x_bottom], axis=0)
+    by_y = jnp.concatenate([y_top, from_y[rest:]], axis=0)
+    return total + by_x.astype(F32) + by_y.astype(F32)
 
 
 def norm_stats(values):
@@ -280,27 +291,27 @@
     return pltpu.VMEM((rows, columns) if len(matrices) > count else (16, 128), BF16)
 
 
-def fill_pairs(count, pair_refs, pairs_ref):
-    padded = pairs_ref.shape[1]
+def fill_pairs(count, block, pair_refs, pairs_ref):
+    padded, columns = pairs_ref.shape[1:]
     place = 0
     for ref in pair_refs:
         j, low = divmod(place, padded)
-        pairs_ref[j, low : low + ref.shape[0], :] = ref[...]
+        pairs_ref[j, low : low + ref.shape[0], :] = ref[:, block * columns : (block + 1) * columns]
         place += ref.shape[0]
 
 
-def middle_forward_kernel(count, matrix_parts, pair_parts, head_size, scalars_ref, *refs):
+def middle_forward_kernel(block, count, matrix_parts, pair_parts, head_size, scalars_ref, *refs):
     mixed_refs, refs = refs[:count], refs[count:]
     matrix_refs, refs = refs[:matrix_parts], refs[matrix_parts:]
     pair_refs, refs = refs[:pair_parts], refs[pair_parts:]
     hidden_ref, gains_ref = refs[:2]
     (self_ref, after_self_ref, norm_ref, queries_ref, cross_ref, after_cross_ref) = refs[2:8]
-    mlp_refs = refs[8:-4]
+    mlp_ref = refs[8]
     wide_ref, narrow_ref, corner_ref, pairs_ref = refs[-4:]
     width = mixed_refs[0].shape[1]
     stride = matrix_refs[0].shape[1] // 3
     matrices = fill_corner(count, matrix_refs, scalars_ref, corner_ref)
-    fill_pairs(count, pair_refs, pairs_ref)
+    fill_pairs(count, block, pair_refs, pairs_ref)
     order = [scalars_ref[i] for i in range(count)]
     relative = [scalars_ref[count + j] for j in range(count)]
     length = scalars_ref[2 * count + 1]
@@ -343,22 +354,22 @@
         wide_ref[order[i]] = dot_nn(tokens, matrices[i][:, 2 * stride : 2 * stride + width])
     for a in range(count):
         after_cross_ref[:, spans[a]] = after_self_ref[:, spans[a]] + wide_ref[a]
-    mlp_norm = norm_stats(after_cross_ref[...])[0] * gains_ref[2:3, :]
-    for ref, (low, high) in zip(mlp_refs, cuts(count, mlp_norm.shape[0])):
-        ref[...] = mlp_norm[low:high].astype(BF16)
+    mlp_ref[...] = (norm_stats(after_cross_ref[...])[0] * gains_ref[2:3, :]).astype(BF16)
 
 
 def pairs_scratch(count, pairs):
-    return pltpu.VMEM((count, sum(m.shape[0] for m in pairs) // count, pairs[0].shape[1]), BF16)
-
-
-def middle_forward(scalars, mixed, matrices, pairs, hidden, gains, head_size, deps=()):
+    return pltpu.VMEM(
+        (count, sum(m.shape[0] for m in pairs) // count, pairs[0].shape[1] // 2), BF16
+    )
+
+
+def middle_forward(block, scalars, mixed, matrices, pairs, hidden, gains, head_size, deps=()):
     count = len(mixed)
     rows, columns = hidden.shape
     width = columns // count
-    found = call(
+    return call(
         functools.partial(
-            middle_forward_kernel, count, len(matrices), len(pairs), head_size
+            middle_forward_kernel, block, count, len(matrices), len(pairs), head_size
         ),
         [
             ((rows, columns), BF16),
@@ -367,8 +378,8 @@
             ((count, rows, width), BF16),
             ((rows, columns), BF16),
             ((rows, columns), F32),
-        ]
-        + [((high - low, columns), BF16) for low, high in cuts(count, rows)],
+            ((rows, columns), BF16),
+        ],
         [
             pltpu.VMEM((count, rows, width), F32),
             pltpu.VMEM((count, rows, width), BF16),
@@ -384,10 +395,9 @@
         scalars=scalars,
         deps=deps,
     )
-    return list(found[:6]) + [list(found[6:])]
-
-
-def middle_backward_kernel(count, matrix_parts, pair_parts, terms, head_size, scalars_ref, *refs):
+
+
+def middle_backward_kernel(block, count, matrix_parts, pair_parts, terms, head_size, scalars_ref, *refs):
     matrix_refs, refs = refs[:matrix_parts], refs[matrix_parts:]
     pair_refs, refs = refs[:pair_parts], refs[pair_parts:]
     term_refs, refs = refs[:terms], refs[terms:]
@@ -399,7 +409,7 @@
     width = queries_ref.shape[2]
     stride = matrix_refs[0].shape[1] // 3
     matrices = fill_corner(count, matrix_refs, scalars_ref, corner_ref)
-    fill_pairs(count, pair_refs, pairs_ref)
+    fill_pairs(count, block, pair_refs, pairs_ref)
     order = [scalars_ref[i] for i in range(count)]
     relative = [scalars_ref[count + j] for j in range(count)]
     length = scalars_ref[2 * count + 1]
@@ -452,7 +462,7 @@
         if j == 0:
             own_pairs_ref[...] = pair_total_ref[...]
         else:
-            put_pieces(pair_grad_refs, count, j, pair_total_ref[...])
+            pair_grad_refs[j - 1][...] = pair_total_ref[...].astype(BF16)
     for i in range(count):
         query_branch_ref[i] = query_ref[order[i] ^ relative[0]]
     grad, grad_gain = norm_back(after_self_ref[...], gains_ref[1:2, :], back(query_branch_ref, 1))
@@ -467,7 +477,7 @@
 
 
 def middle_backward(
-    scalars, matrices, pairs, terms, grad_out, after_cross, after_self, queries, gains, head_size, deps=()
+    block, scalars, matrices, pairs, terms, grad_out, after_cross, after_self, queries, gains, head_size, deps=()
 ):
     count, rows, width = queries.shape
     columns = count * width
@@ -476,12 +486,12 @@
     keys_rows, pair_columns = text.shape[1:]
     found = call(
         functools.partial(
-            middle_backward_kernel, count, len(matrices), len(pairs), len(terms), head_size
+            middle_backward_kernel, block, count, len(matrices), len(pairs), len(terms), head_size
         ),
         [((rows, columns), F32), branch, branch, branch, ((2, columns), F32)]
         + [((rows, width), BF16)] * count
         + [((keys_rows, pair_columns), F32)]
-        + piece_shapes(count, keys_rows, pair_columns),
+        + [((keys_rows, pair_columns), BF16)] * (count - 1),
         [
             pltpu.VMEM((rows, columns), F32),
             pltpu.VMEM((count, rows, width), BF16),
@@ -703,8 +713,7 @@
     matrix_refs, refs = refs[:matrix_parts], refs[matrix_parts:]
     term_refs, refs = refs[:terms], refs[terms:]
     residual_ref, second_ref, gains_ref, next_ref, shift_ref = refs[:5]
-    first_ref, joined_ref, out_ref = refs[5:8]
-    norm_refs, (wide_ref, corner_ref) = refs[8:-2], refs[-2:]
+    first_ref, joined_ref, out_ref, norm_ref, wide_ref, corner_ref = refs[5:]
     rows, columns = first_ref.shape
     width = columns // count
     matrices = fill_corner(count, matrix_refs, scalars_ref, corner_ref)
@@ -718,17 +727,20 @@
     for a in range(count):
         out_ref[:, a * width : (a + 1) * width] = wide_ref[a]
     normed = norm_stats(out_ref[...])[0] * next_ref[0:1, :] + shift_ref[...]
-    for ref, (low, high) in zip(norm_refs, cuts(count, rows)):
-        ref[...] = normed[low:high].astype(BF16)
+    norm_ref[...] = normed.astype(BF16)
 
 
 def skip_forward(scalars, matrices, terms, residual, second, gains, next_gains, shift, deps=()):
     rows, columns = residual.shape
     count = lax.axis_size("seq")
-    found = call(
+    return call(
         functools.partial(skip_forward_kernel, count, len(matrices), len(terms)),
-        [((rows, columns), F32), ((rows, 2 * columns), BF16), ((rows, columns), F32)]
-        + [((high - low, columns), BF16) for low, high in cuts(count, rows)],
+        [
+            ((rows, columns), F32),
+            ((rows, 2 * columns), BF16),
+            ((rows, columns), F32),
+            ((rows, columns), BF16),
+        ],
         [pltpu.VMEM((count, rows, columns // count), F32), corner_scratch(count, matrices)],
         11,
         *matrices,
@@ -741,15 +753,14 @@
         scalars=scalars,
         deps=deps,
     )
-    return list(found[:3]) + [list(found[3:])]
 
 
 def skip_backward_kernel(count, matrix_parts, terms, scalars_ref, *refs):
     matrix_refs, refs = refs[:matrix_parts], refs[matrix_parts:]
     term_refs, refs = refs[:terms], refs[terms:]
     hidden_ref, next_ref, residual_ref, first_ref, second_ref, gains_ref = refs[:6]
-    branch_ref, grad_first_ref, grad_second_ref, vectors_ref = refs[6:10]
-    half_refs, (narrow_ref, corner_ref) = refs[10:-2], refs[-2:]
+    branch_ref, grad_first_ref, grad_second_ref, vectors_ref, round_ref = refs[6:11]
+    narrow_ref, corner_ref = refs[11:]
     rows, columns = first_ref.shape
     width = columns // count
     matrices = fill_corner(count, matrix_refs, scalars_ref, corner_ref)
@@ -785,8 +796,7 @@
     ) / (2 * columns)
     grad_first_ref[...] = scale * (grad_first - mean - first * inner)
     grad_second_ref[...] = scale * (grad_second - mean - second * inner)
-    for ref, (low, high) in zip(half_refs, cuts(count, rows)):
-        ref[...] = grad_first_ref[low:high, :].astype(BF16)
+    round_ref[...] = grad_first_ref[...].astype(BF16)
 
 
 def skip_backward(
@@ -795,15 +805,15 @@
     rows, columns = first.shape
     count = lax.axis_size("seq")
     narrow = (count, rows, columns // count)
-    found = call(
+    return call(
         functools.partial(skip_backward_kernel, count, len(matrices), len(terms)),
         [
             (narrow, BF16),
             ((rows, columns), F32),
             ((rows, columns), F32),
             ((4, columns), F32),
-        ]
-        + [((high - low, columns), BF16) for low, high in cuts(count, rows)],
+            ((rows, columns), BF16),
+        ],
         [pltpu.VMEM(narrow, BF16), corner_scratch(count, matrices)],
         15,
         *matrices,
@@ -817,7 +827,6 @@
         scalars=scalars,
         deps=deps,
     )
-    return list(found[:4]) + [list(found[4:])]
 
 
 def open_backward_kernel(count, terms, *refs):
@@ -870,10 +879,10 @@
         start += ref.shape[1]
 
 
-def pack(shards):
+def pack(shards, deps=()):
     rows = -(-max(m.shape[0] for m in shards) // 32) * 32
     shape = (rows, sum(m.shape[1] for m in shards))
-    return call(functools.partial(pack_kernel, len(shards)), [(shape, BF16)], [], 3, *shards)[0]
+    return call(functools.partial(pack_kernel, len(shards)), [(shape, BF16)], [], 3, *shards, deps=deps)[0]
 
 
 def settle_kernel(count, parts, plan, scalars_ref, *refs):
@@ -926,15 +935,19 @@
     return list(found)
 
 
-def finish(scalars, entries, layer, layer_count, before=None):
+def plan_of(entries):
     plan, first = [], 0
     for shard, groups, pieces, width in entries:
         rows, columns = shard.shape
         stride = columns // (groups * pieces) if groups else columns
         plan.append((first, rows, groups, pieces, width, stride))
         first += columns
-    blocks = gather_parts(pack([entry[0] for entry in entries]))
-    return settle(scalars, blocks, tuple(plan), layer, layer_count, before)
+    return tuple(plan)
+
+
+def finish(scalars, entries, layer, layer_count, before=None, deps=()):
+    blocks = gather_parts(pack([entry[0] for entry in entries], deps))
+    return settle(scalars, blocks, plan_of(entries), layer, layer_count, before)
 
 
 def swap_seq(block, bits):
@@ -968,43 +981,49 @@
     return total.astype(BF16)
 
 
-def halves_of(block):
-    return [block[low:high] for low, high in cuts(lax.axis_size("seq"), block.shape[0])]
-
-
-def gather_halves(halves):
+def scatter_first(pieces):
     seq_count = lax.axis_size("seq")
     if seq_count != 4:
-        return [halves[0]] + [swap_seq(halves[0], j) for j in range(1, seq_count)]
-    top, bottom = halves
-    y_top, x_bottom = swap_seq(top, 2), swap_seq(bottom, 1)
-    x_top, y_bottom = swap_seq(top, 1), swap_seq(bottom, 2)
-    return [top, bottom, x_top, x_bottom, y_top, y_bottom, swap_seq(y_top, 1), swap_seq(x_bottom, 2)]
-
-
-def scatter_parts(own, pieces):
+        return [swap_seq(m, j + 1) for j, m in enumerate(pieces)]
+    return [swap_seq(pieces[0], 1), swap_seq(pieces[1], 2), pieces[2], pieces[3]]
+
+
+def scatter_last(own, first, ready=None):
     seq_count = lax.axis_size("seq")
     if seq_count != 4:
-        return [own] + [swap_seq(m, j + 1) for j, m in enumerate(pieces)]
-    x_top, x_bottom, y_top, y_bottom, corner_top, corner_bottom = pieces
-    by_x, by_y = swap_seq(corner_top, 1), swap_seq(corner_bottom, 2)
-    from_x_top, from_y_bottom = swap_seq(x_top, 1), swap_seq(y_bottom, 2)
-    from_y_top = swap_seq(add_bf16(y_top, by_x), 2)
-    from_x_bottom = swap_seq(add_bf16(x_bottom, by_y), 1)
-    return [own, from_x_top, from_x_bottom, from_y_top, from_y_bottom]
+        return [own] + first
+    from_x, from_y, x_bottom, y_top = first
+    if ready is not None:
+        from_x, from_y = gate([from_x, from_y], ready)
+    cut, rest = y_top.shape[0], x_bottom.shape[0]
+    to_y, to_x = add_bf16(y_top, from_x[:cut]), add_bf16(x_bottom, from_y[:rest])
+    return [own, from_x, from_y, swap_seq(to_x, 1), swap_seq(to_y, 2)]
 
 
 def exchange_rel(blocks):
     return [blocks[0]] + [swap_seq(blocks[j], j) for j in range(1, len(blocks))]
 
 
-def gather_parts(block):
+def gather_first(block):
     seq_count = lax.axis_size("seq")
     if seq_count != 4:
         return [block] + [swap_seq(block, j) for j in range(1, seq_count)]
+    return [block, swap_seq(block, 1), swap_seq(block, 2)]
+
+
+def gather_last(first, ready=None):
+    seq_count = lax.axis_size("seq")
+    if seq_count != 4:
+        return first
+    block, from_x, from_y = first
+    if ready is not None:
+        from_x, from_y = gate([from_x, from_y], ready)
     cut = cut_of(block.shape[0])
-    from_x, from_y = swap_seq(block, 1), swap_seq(block, 2)
     return [block, from_x, from_y, swap_seq(from_y[:cut], 1), swap_seq(from_x[cut:], 2)]
+
+
+def gather_parts(block):
+    return gather_last(gather_first(block))
 
 
 def list_order():
@@ -1015,15 +1034,27 @@
     return [s, s ^ (1 + odd), s ^ (2 - odd), s ^ 3]
 
 
-def spread(block):
+def spread_first(block):
     seq_count = lax.axis_size("seq")
     if seq_count != 4:
         return [block] + [swap_seq(block, j) for j in range(1, seq_count)]
+    return [block, swap_by_core(block, 1, 2)]
+
+
+def spread_last(blocks, ready, part_ready=None):
+    seq_count = lax.axis_size("seq")
+    if seq_count != 4:
+        return blocks
     odd = lax.axis_index("fsdp") % 2
+    block, first = blocks
     half = block.shape[0] // 2
-    first = swap_by_core(block, 1, 2)
+    if ready is not None:
+        (first,) = gate([first], ready)
     part = swap_by_core(lax.dynamic_slice_in_dim(first, odd * half, half, 0), 2, 1)
-    return [block, first, swap_core(first), part, swap_core(part)]
+    other = swap_core(first)
+    if part_ready is not None:
+        (part,) = gate([part], part_ready)
+    return [block, first, other, part, swap_core(part)]
 
 
 def unspread(scalars, blocks):
@@ -1058,26 +1089,30 @@
     return lax.psum_scatter(full.astype(BF16), "fsdp", scatter_dimension=0, tiled=True)
 
 
-def text_pairs(text_rows, kv_part):
-    return gather_halves([dot_nn(m, kv_part).astype(BF16) for m in halves_of(text_rows)])
-
-
-def layer_forward(parts, hidden, scalars, gains, shift, kv_part, text_rows, weights, normed, cross_deps):
+def layer_forward(parts, hidden, scalars, gains, shift, pairs, weights, normed, deps):
     lead_part, square_parts, up_part = weights
     seq_count = lax.axis_size("seq")
     tok_rows, model_width = hidden.shape
     head_size, width = model_width // H, model_width // seq_count
     first_all, triples, mixed = self_forward(
-        parts, lead_part, gains, shift, head_size, seq_count, width, normed
-    )
-    (kv_part,) = gate([kv_part], [mixed[0]])
-    pairs = text_pairs(text_rows, kv_part)
-    self_tokens, after_self, cross_norm, queries, cross_tokens, after_cross, mlp_halves = (
+        parts,
+        lead_part,
+        gains,
+        shift,
+        head_size,
+        seq_count,
+        width,
+        normed,
+        (square_parts[0],) + deps,
+    )
+    mixed_rel = exchange_rel(mixed)
+    square_parts = spread_last(square_parts, [mixed[0]], mixed_rel[1:])
+    self_tokens, after_self, cross_norm, queries, cross_tokens, after_cross, mlp_norm = (
         middle_forward(
-            scalars, exchange_rel(mixed), square_parts, pairs, hidden, gains, head_size, cross_deps
+            int(normed), scalars, mixed_rel, square_parts, pairs, hidden, gains, head_size
         )
     )
-    mlp_parts = gather_halves(mlp_halves)
+    mlp_parts = gather_parts(mlp_norm)
     mlp_all, up_rows, activated = mlp_up(mlp_parts, up_part, seq_count)
     saved = (
         first_all,
@@ -1092,22 +1127,24 @@
         up_rows,
         activated,
     )
-    return (saved, kv_part, pairs, mlp_parts)
+    return (saved, square_parts, mlp_parts)
 
 
 def unspread_first(blocks, ready):
     own, first_mine, first_other, second_mine, second_other, corner_mine, corner_other = blocks
-    swapped = [swap_core(corner_other), swap_core(second_mine), swap_core(second_other)]
-    from_corner, to_other, to_mine = gate(swapped, ready)
-    passed = swap_by_core(add_bf16(corner_mine, from_corner), 2, 1)
-    other = swap_by_core(add_bf16(first_other, to_other), 1, 2)
-    return own, other, passed, [first_mine, to_mine]
-
-
-def unspread_last(scalars, first, ready):
-    own, other, passed, terms = first
-    (passed,) = gate([passed], ready)
+    from_corner, to_other = swap_core(corner_other), swap_core(second_mine)
+    to_mine = swap_core(second_other)
+    sums = [add_bf16(corner_mine, from_corner), add_bf16(first_other, to_other)]
+    sums = gate(sums, ready)
+    hops = [swap_by_core(sums[0], 2, 1), swap_by_core(sums[1], 1, 2)]
+    return own, hops, [first_mine, to_mine], sums
+
+
+def unspread_last(scalars, first, hops_ready, joined_ready):
+    own, hops, terms, _ = first
+    passed, other = gate(hops, hops_ready)
     mine = swap_by_core(add_bf16(*terms, passed), 1, 2)
+    (mine,) = gate([mine], joined_ready)
     return join_halves(scalars, own, mine, other)
 
 
@@ -1115,23 +1152,19 @@
     return add_bf16(blocks[0], *[swap_seq(m, j + 1) for j, m in enumerate(blocks[1:])])
 
 
-def gather_lead(layer, qkv, query, self_out, cross_out):
+def lead_part(layer, qkv, query, self_out, cross_out):
     padded = padded_width(query.shape[2] // lax.axis_size("seq"))
-    return gather_fsdp(
-        jnp.concatenate(
-            [own_part(qkv[layer], 3, padded)]
-            + [own_part(m[layer], 1, padded) for m in (self_out, query, cross_out)],
-            axis=1,
-        )
-    )
-
-
-def gather_rest(layer, text_kv, up, down):
+    return jnp.concatenate(
+        [own_part(qkv[layer], 3, padded)]
+        + [own_part(m[layer], 1, padded) for m in (self_out, query, cross_out)],
+        axis=1,
+    )
+
+
+def gather_rest(layer, up, down):
     s, seq_count, fsdp_count = lax.axis_index("seq"), lax.axis_size("seq"), lax.axis_size("fsdp")
-    padded = padded_width(text_kv.shape[2] // (2 * seq_count))
     rows = down.shape[1] // seq_count
     return (
-        gather_fsdp(own_part(text_kv[layer], 2, padded)),
         gather_fsdp(own_part(up[layer], fsdp_count, up.shape[2] // (fsdp_count * seq_count))),
         gather_fsdp(lax.dynamic_slice_in_dim(down[layer], s * rows, rows, 0)),
     )
@@ -1190,46 +1223,59 @@
         ],
         axis=1,
     ).astype(F32)
+    latent_hops = gather_first(latents[0])
+    (small,) = gate([small], latent_hops[1:])
     small = lax.all_to_all(small, "fsdp", 0, 0, tiled=True)
     cond_part = small[:, 0]
     gains = jnp.swapaxes(small[:, 1:7], 0, 1).reshape(2, 3, model_width)
     skip_gains = small[:, 7:].reshape(2, model_width)
     silu_part = jax.nn.silu(cond_part)
     shift_terms = jnp.einsum("br,lrd->bld", silu_part, mod_weight.astype(F32), precision=EXACT)
+    latent_parts = gather_last(latent_hops)
+    (shift_terms,) = gate([shift_terms], latent_parts[-2:])
+    out_hops = gather_first(gate([cotangent[0]], latent_parts[-2:])[0])
     shifts = jnp.sum(lax.all_to_all(shift_terms, "fsdp", 0, 0, tiled=True), axis=0)
 
     lead_stacks = (qkv_weight, query_weight, self_out_weight, cross_out_weight)
-    rest_stacks = (text_kv_weight, up_weight, down_weight)
+    rest_stacks = (up_weight, down_weight)
     lead_columns = 3 * padded_width(width)
     head_size = model_width // H
     fours = seq_count == 4
 
-    lead_first = gather_lead(0, *lead_stacks)
-    kv_first, up_first, down_first = gather_rest(0, *rest_stacks)
-    (square_first,) = gate([lead_first[:, lead_columns:]], [shifts])
-    squares_first = spread(square_first)
-    saved_first, kv_first, pairs_first, mlp_parts = layer_forward(
-        gather_halves(halves_of(latents[0])),
+    padded_columns = padded_width(width)
+    kv_both = gather_fsdp(
+        jnp.concatenate([own_part(text_kv_weight[l], 2, padded_columns) for l in range(2)], axis=1)
+    )
+    lead_first = gather_fsdp(
+        gate([lead_part(0, *lead_stacks)], [kv_both] + latent_hops[1:])[0]
+    )
+    up_first, down_first = gather_rest(0, *rest_stacks)
+    pairs_all = gather_parts(dot_nn(text_rows, kv_both).astype(BF16))
+    (lead_first,) = gate([lead_first], [shifts] + pairs_all[-2:])
+    square_first = lead_first[:, lead_columns:]
+    pairs_first, pairs_second = pairs_all, pairs_all
+    saved_first, squares_first, mlp_parts = layer_forward(
+        latent_parts,
         latents[0],
         scalars,
         gains[0],
         shifts[0],
-        kv_first,
-        text_rows,
-        (lead_first, squares_first, up_first),
+        pairs_first,
+        (lead_first, spread_first(square_first), up_first),
         False,
         (),
     )
-    out_halves = gate(halves_of(cotangent[0]), mlp_parts[-2:])
-    out_parts = gather_halves(out_halves)
     own, pieces = mlp_down(saved_first[10], down_first, seq_count)
-    terms = scatter_parts(own, pieces)
+    terms = scatter_last(own, scatter_first(pieces))
 
     (skip_matrix,) = gate(
-        [gather_fsdp(own_part(skip_weight, 1, padded_width(width)))], [own]
-    )
-    skip_parts = spread(skip_matrix)
-    first_out, joined_norm, skip_out, second_halves = skip_forward(
+        [gather_fsdp(own_part(skip_weight, 1, padded_width(width)))], mlp_parts[-2:]
+    )
+    skip_parts = spread_last(spread_first(skip_matrix), [own], terms[-2:])
+    lead_second = gather_fsdp(lead_part(1, *lead_stacks))
+    (square_second,) = gate([lead_second[:, lead_columns:]], terms[-2:])
+    squares_second = spread_first(square_second)
+    first_out, joined_norm, skip_out, second_norm = skip_forward(
         scalars,
         skip_parts,
         terms,
@@ -1238,30 +1284,28 @@
         skip_gains,
         gains[1],
         shifts[1],
-        out_parts[-2:],
-    )
-
-    lead_second = gather_lead(1, *lead_stacks)
-    kv_second, up_second, down_second = gather_rest(1, *rest_stacks)
-    second_parts = gather_halves(second_halves)
-    (square_second,) = gate([lead_second[:, lead_columns:]], second_parts[-2:])
-    squares_second = spread(square_second)
-    saved_second, kv_second, pairs_second, _ = layer_forward(
-        second_parts,
+        (square_second,),
+    )
+
+    up_second, down_second = gather_rest(1, *rest_stacks)
+    saved_second, squares_second, mlp_parts = layer_forward(
+        gather_parts(second_norm),
         skip_out,
         scalars,
         gains[1],
         shifts[1],
-        kv_second,
-        text_rows,
+        pairs_second,
         (lead_second, squares_second, up_second),
         True,
         (),
     )
-    out_all = stack_rows(out_parts, (saved_second[7],))
-
-    def block_backward(rows, grad_out, saved, block, weights, early, mlp_deps, middle_deps, self_deps):
-        lead_part, square_parts, kv_part, up_part, down_part = weights
+    out_parts = gather_last(out_hops, [squares_second[-1]])
+    out_all = stack_rows(out_parts, (mlp_parts[1],))
+
+    held = {}
+
+    def block_backward(rows, grad_out, saved, block, weights, early, hooks):
+        lead_matrix, square_parts, pairs, up_part, down_part = weights
         grad_down = dot_tn(saved[10], early).astype(BF16) if early is not None else None
         found_all, grad_up_rows, own, pieces = mlp_backward(
             rows,
@@ -1269,12 +1313,16 @@
             up_part,
             down_part,
             seq_count,
-            mlp_deps + ((grad_down,) if early is not None else ()),
+            hooks[0] + ((grad_down,) if early is not None else ()),
         )
-        terms = scatter_parts(own, pieces)
+        first = scatter_first(gate(pieces, hooks[3]) if hooks[3] else pieces)
+        terms = scatter_last(own, first)
+        held["hops"] = first[:2]
         if early is None:
             grad_down = dot_tn(saved[10], found_all).astype(BF16)
+            (grad_down,) = gate([grad_down], first[:2])
         grad_up = dot_tn(saved[8], grad_up_rows).astype(BF16)
+        (grad_up,) = gate([grad_up], first[:2])
         down_shard, up_shard = scatter_fsdp(grad_down), scatter_fsdp(grad_up)
         (
             grad_after_self,
@@ -1284,11 +1332,12 @@
             gain_grads,
             mixed_grads,
             own_pairs,
-            pair_pieces,
+            pair_blocks,
         ) = middle_backward(
+            block,
             scalars,
             square_parts,
-            pairs_first if block == 0 else pairs_second,
+            pairs,
             terms,
             grad_out,
             saved[7],
@@ -1296,37 +1345,36 @@
             saved[5],
             gains[block],
             head_size,
-            (grad_down, grad_up) + middle_deps(grad_up_rows),
+            (grad_down, grad_up) + hooks[1](grad_up_rows, terms),
         )
+        mixed_rel = exchange_rel(mixed_grads)
+        pair_blocks = gate(pair_blocks, mixed_rel[1:])
+        pair_terms = [swap_seq(m, j + 1) for j, m in enumerate(pair_blocks)]
+        grad_triples, own, pieces = self_backward(
+            saved[1],
+            mixed_rel,
+            lead_matrix,
+            head_size,
+            (down_shard,) + hooks[2](mixed_grads[0]),
+        )
+        pair_terms = gate(pair_terms, [grad_triples])
+        first = scatter_first(gate(pieces, pair_terms))
+        terms = scatter_last(own, first)
+        grad_qkv = dot_tn(saved[0], grad_triples).astype(BF16)
+        (grad_qkv,) = gate([grad_qkv], first[:2])
+        held["last"] = first[:2]
         squares = outer(
             scalars,
             [saved[2], saved[4], saved[6]],
             [self_branch, query_branch, cross_branch],
+            (grad_triples,),
         )
-        grad_triples, own, pieces = self_backward(
-            saved[1],
-            exchange_rel(mixed_grads),
-            lead_part,
-            head_size,
-            (squares[0], down_shard) + self_deps(grad_after_self),
-        )
-        terms = scatter_parts(own, pieces)
-        grad_qkv = dot_tn(saved[0], grad_triples).astype(BF16)
-        pair_pieces = gate(pair_pieces, [grad_triples])
-        pair_terms = scatter_parts(own_pairs, pair_pieces)
-        if fours:
-            grad_pairs = jnp.concatenate(
-                [
-                    add_bf16(pair_terms[0][low:high], pair_terms[1 + k], pair_terms[3 + k])
-                    for k, (low, high) in enumerate(cuts(seq_count, text_rows.shape[0]))
-                ]
-            )
-        else:
-            grad_pairs = add_bf16(*pair_terms)
+        squares = gate(squares, first[:2])
+        pair_terms = gate(pair_terms, first[:2])
+        grad_pairs = add_bf16(own_pairs, *pair_terms)
+        kv_part = kv_both[:, 2 * block * padded_columns : 2 * (block + 1) * padded_columns]
         grad_text = dot_nt(grad_pairs, kv_part)
         kv_shard = scatter_fsdp(dot_tn(text_rows, grad_pairs))
-        if fours:
-            squares = unspread_first(squares, [grad_triples])
         return (
             terms,
             grad_after_self,
@@ -1334,15 +1382,19 @@
             grad_text,
             squares,
             grad_qkv,
-            scatter_fsdp(grad_qkv),
-            kv_shard,
-            up_shard,
-            down_shard,
+            grad_triples,
+            (scatter_fsdp(grad_qkv), kv_shard, up_shard, down_shard),
         )
 
-    def squares_done(squares, ready):
-        joined = unspread_last(scalars, squares, ready) if fours else unspread_any(squares)
-        return joined, scatter_fsdp(joined)
+    def second_own(grad_up_rows, terms):
+        own, pieces = mlp_down(saved_second[10], down_second, seq_count, (grad_up_rows,))
+        pieces = gate(pieces, terms[-2:])
+        held["own"], held["own_hops"] = own, scatter_first(pieces)
+        return tuple(pieces)
+
+    def second_sum(ready):
+        held["ready"] = ready
+        return tuple(held["own_hops"][:2])
 
     (
         terms,
@@ -1351,22 +1403,18 @@
         text_second,
         squares,
         grad_qkv,
-        qkv_shard,
-        kv_shard,
-        up_shard,
-        down_shard,
+        grad_triples,
+        (qkv_shard, kv_shard, up_shard, down_shard),
     ) = block_backward(
         [out_all],
         cotangent[0],
         saved_second,
         1,
-        (lead_second, squares_second, kv_second, up_second, down_second),
+        (lead_second, squares_second, pairs_second, up_second, down_second),
         out_all,
-        (),
-        lambda done: (),
-        lambda done: (),
-    )
-    skip_branch, grad_first_out, grad_skip, vectors, first_halves = skip_backward(
+        ((), second_own, second_sum, ()),
+    )
+    skip_branch, grad_first_out, grad_skip, vectors, first_round = skip_backward(
         scalars,
         skip_parts,
         terms,
@@ -1379,56 +1427,14 @@
         (grad_qkv, up_shard),
     )
     vectors_second = jnp.concatenate([vectors[:2], gain_grads, vectors[2:]], axis=0)
-    square_joined, square_shard = squares_done(squares, [grad_first_out])
-    skip_outer = outer(scalars, [joined_norm], [skip_branch])
-    held = {}
-
-    def skip_first(done):
-        if fours:
-            held["first"] = unspread_first(skip_outer, [done])
-        else:
-            held["joined"] = unspread_any(skip_outer)
-        return (kv_shard,)
-
-    def skip_last(done):
-        if fours:
-            held["joined"] = unspread_last(scalars, held["first"], [done])
-        held["shard"] = scatter_fsdp(held["joined"])
-        return (qkv_shard,)
-
-    second_layer = (qkv_shard, square_shard, kv_shard, up_shard, down_shard)
-    (
-        terms,
-        grad_after_self,
-        gain_grads,
-        text_first,
-        squares,
-        grad_qkv,
-        qkv_shard,
-        kv_shard,
-        up_shard,
-        down_shard,
-    ) = block_backward(
-        gather_halves(first_halves),
-        grad_first_out,
-        saved_first,
-        0,
-        (lead_first, squares_first, kv_first, up_first, down_first),
-        None,
-        (skip_outer[0], square_joined),
-        skip_first,
-        skip_last,
-    )
-    skip_shard = held["shard"]
-    grad_latents, vectors = open_backward(
-        terms, latents[0], gains[0], grad_after_self, (grad_qkv, skip_shard, square_shard)
-    )
-    vectors_first = jnp.concatenate([vectors, gain_grads], axis=0)
-    _, square_shard = squares_done(squares, [grad_latents])
-    first_layer = (qkv_shard, square_shard, kv_shard, up_shard, down_shard)
-
-    own, pieces = mlp_down(saved_second[10], down_second, seq_count, (grad_latents,))
-    output = close_forward(scatter_parts(own, pieces), saved_second[7])
+    first_hops = gather_first(first_round)
+    first_parts = gather_last(first_hops)
+    if fours:
+        squares = unspread_first(squares, first_parts[-2:])
+    output = close_forward(
+        scatter_last(held["own"], held["own_hops"], first_hops[1:]), saved_second[7]
+    )
+    skip_outer = outer(scalars, [joined_norm], [skip_branch], tuple(first_hops[1:]))
 
     def entries(layer):
         qkv, square, kv, up, down = layer
@@ -1441,8 +1447,71 @@
             [(qkv, 3, 1, width), (square, 1, 3, width)],
         )
 
-    early, late = entries(second_layer)
-    early_done, late_done = finish(scalars, early, 1, 2), finish(scalars, late, 1, 2)
+    early, _ = entries((qkv_shard, qkv_shard, kv_shard, up_shard, down_shard))
+
+    def first_middle(grad_up_rows, terms):
+        if fours:
+            held["skip"] = unspread_first(skip_outer, terms[-2:])
+        held["up"], held["terms"] = grad_up_rows, terms
+        held["packed"] = pack([entry[0] for entry in early], (grad_up_rows,))
+        return (held["packed"],)
+
+    def first_self(ready):
+        held["blocks"] = gather_first(gate([held["packed"]], [ready])[0])
+        held["middle"] = ready
+        return (qkv_shard,)
+
+    (
+        terms,
+        grad_after_self,
+        gain_grads,
+        text_first,
+        first_squares,
+        grad_qkv,
+        grad_triples,
+        (first_qkv_shard, first_kv_shard, first_up_shard, first_down_shard),
+    ) = block_backward(
+        first_parts,
+        grad_first_out,
+        saved_first,
+        0,
+        (lead_first, squares_first, pairs_first, up_first, down_first),
+        None,
+        (
+            (skip_outer[0],) + (tuple(squares[3]) if fours else ()),
+            first_middle,
+            first_self,
+            squares[1] if fours else (),
+        ),
+    )
+    if fours:
+        joined = unspread_last(scalars, squares, held["hops"], held["last"])
+        skip_joined = unspread_last(scalars, held["skip"], held["last"], terms[-2:])
+        first_squares = unspread_first(first_squares, terms[-2:])
+    else:
+        joined, skip_joined = unspread_any(squares), unspread_any(skip_outer)
+    square_shard, skip_shard = scatter_fsdp(joined), scatter_fsdp(skip_joined)
+    grad_latents, vectors = open_backward(
+        terms, latents[0], gains[0], grad_after_self, (grad_qkv,)
+    )
+    vectors_first = jnp.concatenate([vectors, gain_grads], axis=0)
+    if fours:
+        first_joined = unspread_last(scalars, first_squares, [grad_latents], [grad_latents])
+    else:
+        first_joined = unspread_any(first_squares)
+    first_layer = (
+        first_qkv_shard,
+        scatter_fsdp(first_joined),
+        first_kv_shard,
+        first_up_shard,
+        first_down_shard,
+    )
+
+    early_done = settle(
+        scalars, gather_last(held["blocks"], terms[-2:]), plan_of(early), 1, 2, None
+    )
+    _, late = entries((qkv_shard, square_shard, kv_shard, up_shard, down_shard))
+    late_done = finish(scalars, late, 1, 2, None, (terms[-1],))
     early, late = entries(first_layer)
     grad_up, grad_kv, grad_down = finish(scalars, early, 0, 2, early_done)
     grad_qkv, grad_self_out, grad_query, grad_cross_out = finish(scalars, late, 0, 2, late_done)

time: 1410 us -> 1350 us (0.957)
  starting transfers between devices: 189 us -> 130 us
  waiting for transfers between devices: 567 us -> 535 us
  local copies, waits for them, and re-layouts: 92.4 us -> 122 us
    ppermute x132 -> x94, starting transfers between devices: 143 us -> 104 us  [swap_seq(): return lax.ppermute(block, 'seq', [(i, i ^ bits) for i in range(seq_count)])]
    unnamed x341 -> x355, local copies, waits for them, and re-layouts: 36.9 us -> 59.9 us
    ppermute x132 -> x94, waiting for transfers between devices: 392 us -> 371 us  [swap_seq(): return lax.ppermute(block, 'seq', [(i, i ^ bits) for i in range(seq_count)])]
    ppermute x18, starting transfers between devices: 21.8 us -> 5.58 us  [swap_fsdp(): lax.ppermute(block, 'fsdp', [(i, i ^ bits) for i in range(fsdp_count)])]
    all_gather x9 -> x8, waiting for transfers between devices: 28.5 us -> 20.9 us  [gather_fsdp(): return lax.all_gather(shard, 'fsdp', axis=0, tiled=True)]
    slice x19 -> x31, local copies, waits for them, and re-layouts: 25.6 us -> 29.2 us  [the longest x12 8.01 us: gather_last(): from_y[:cut]]
    convert_element_type x27 -> x23, other arithmetic: 39.3 us -> 37.3 us  [add_bf16(): return total.astype(BF16)]
  transfers between devices with their start and end apart: 186 -> 147, of which waited for: 82 -> 62; matrix products, arithmetic and copies ran while one was open for 12% -> 14% of each run, Pallas kernels for 28% -> 29%
where the time goes in v5:
time: 1350 us; the launch traced here: 1340 us
  waiting for transfers between devices  535 us (40%)
  Pallas kernels  397 us (29%)
  starting transfers between devices  130 us (10%)
  local copies, waits for them, and re-layouts  122 us (9%)
  matrix products  70.8 us (5%)
  other arithmetic  45.5 us (3%)
  blocking collectives  21.1 us (2%)
  between operations  16.6 us (1%)
    ppermute x94, waiting for transfers between devices, swap_seq(): return lax.ppermute(block, 'seq', [(i, i ^ bits) for i in range(seq_count)])  371 us
    pallas_call x30, Pallas kernels, call(): pl.pallas_call(run, name=getattr(kernel, 'func', kernel).__name__, out_sh...  369 us
    ppermute x15, waiting for transfers between devices, swap_by_core(): return lax.ppermute(block, ('seq', 'fsdp'), pairs)  128 us
    ppermute x94, starting transfers between devices, swap_seq(): return lax.ppermute(block, 'seq', [(i, i ^ bits) for i in range(seq_count)])  104 us
    unnamed x355, local copies, waits for them, and re-layouts  59.9 us
    dot_general x8, matrix products, dot_tn(): lax.dot_general(a, b, (((0,), (0,)), ((), ())), preferred_element_type=F32)  55.1 us
    convert_element_type x23, other arithmetic, add_bf16(): return total.astype(BF16)  37.3 us
    pallas_call x5, Pallas kernels, settle(): pl.pallas_call(functools.partial(settle_kernel, count, len(blocks), plan)...  28.6 us
  transfers between devices with their start and end apart: 147, of which 62 were waited for; matrix products, arithmetic and copies ran while one was open for 14% of the time, Pallas kernels for 29%

profile of v5, /device:TPU:0, one launch (start us, length us, event | category | flops | bytes accessed | tf_op | source)
XLA Modules:
  0.0 1338.7 jit_solution(378383199661917760)
XLA Ops:
  30.5 20.8 %all-gather.13.cloned.1.call-done.refs_1_ = bf16[1024,1536]{1,0:T(8,128)(2,1)} async-done(((bf16[128,1536]{1,0:T(8,128)(2,1)}), bf16[1024,1536]{1,0:T(8,128)(2,1)}) %all-gather.13.cloned.1.call-update) | async-done | bytes 3145744 | tf_op jit(solution)/shard_map/all_gather | solution.py:1085
  77.9 20.1 %collective-permute-done.4.refs_12_.refs_8_ = bf16[352,1536]{1,0:T(8,128)(2,1)S(1)} collective-permute-done((bf16[352,1536]{1,0:T(8,128)(2,1)}, bf16[352,1536]{1,0:T(8,128)(2,1)S(1)}, u32[]{:S(2)}, u32[]{:S(2)}) %collective-permute-start.4) | collective-permute-done | bytes 1081376 | tf_op jit(solution)/shard_map/ppermute | solution.py:955
  138.1 18.6 %self_forward_kernel.2 = (bf16[1024,1408]{1,0:T(8,128)(2,1)}, bf16[1024,1152]{1,0:T(8,128)(2,1)}, bf16[256,352]{1,0:T(8,128)(2,1)}, bf16[256,352]{1,0:T(8,128)(2...) custom-call(bf16[256,1408]{1,0:T(8,128)(2,1)} %bitcast.168, bf16[256,1408]{1,0:T(8,128)(2,1)} %copy-done.30, ...), custom_call_target="tpu_custom_call" | custom-call | flops 24000 | bytes 1000 | tf_op jit(solution)/shard_map/self_forward_kernel/pallas_call | solution.py:50
  156.6 18.7 %collective-permute-done.11.refs_0_ = bf16[1408,1152]{1,0:T(8,128)(2,1)} collective-permute-done((bf16[1408,1152]{1,0:T(8,128)(2,1)}, bf16[1408,1152]{1,0:T(8,128)(2,1)}, u32[]{:S(2)}, u32[]{:S(2)}) %collective-permute-start.11) | collective-permute-done | bytes 3244064 | tf_op jit(solution)/shard_map/ppermute | solution.py:974
  214.5 20.4 %middle_forward_kernel.2 = (bf16[256,1408]{1,0:T(8,128)(2,1)}, f32[256,1408]{1,0:T(8,128)}, bf16[256,1408]{1,0:T(8,128)(2,1)}, bf16[4,256,352]{2,1,0:T(8,128)(2,...) custom-call(s32[10]{0:T(128)} %stack.83.refs_0_.scalars_ref, ...), custom_call_target="tpu_custom_call" | custom-call | flops 23000 | bytes 1000 | tf_op jit(solution)/shard_map/middle_forward_kernel/pallas_call | solution.py:50
  235.8 17.6 %collective-permute-done.15.refs_2_ = bf16[256,1408]{1,0:T(8,128)(2,1)S(1)} collective-permute-done((bf16[256,1408]{1,0:T(8,128)(2,1)}, bf16[256,1408]{1,0:T(8,128)(2,1)S(1)}, u32[]{:S(2)}, u32[]{:S(2)}) %collective-permute-start.15) | collective-permute-done | bytes 720928 | tf_op jit(solution)/shard_map/ppermute | solution.py:955
  290.2 17.2 %collective-permute-done.24.refs_7_ = bf16[256,1408]{1,0:T(8,128)(2,1)S(1)} collective-permute-done((bf16[256,1408]{1,0:T(8,128)(2,1)}, bf16[256,1408]{1,0:T(8,128)(2,1)S(1)}, u32[]{:S(2)}, u32[]{:S(2)}) %collective-permute-start.24) | collective-permute-done | bytes 720928 | tf_op jit(solution)/shard_map/ppermute | solution.py:955
  356.7 17.6 %collective-permute-done.28.refs_2_ = bf16[256,1408]{1,0:T(8,128)(2,1)S(1)} collective-permute-done((bf16[256,1408]{1,0:T(8,128)(2,1)}, bf16[256,1408]{1,0:T(8,128)(2,1)S(1)}, u32[]{:S(2)}, u32[]{:S(2)}) %collective-permute-start.28) | collective-permute-done | bytes 720928 | tf_op jit(solution)/shard_map/ppermute | solution.py:955
  393.7 18.5 %self_forward_kernel.3 = (bf16[1024,1408]{1,0:T(8,128)(2,1)}, bf16[1024,1152]{1,0:T(8,128)(2,1)}, bf16[256,352]{1,0:T(8,128)(2,1)}, bf16[256,352]{1,0:T(8,128)(2...) custom-call(bf16[256,1408]{1,0:T(8,128)(2,1)} %get-tuple-element.233.refs_0_, bf16[256,1408]{1,0:T(8,128)(2,1)} %copy-done.80, ...), custom_call_target="tpu_custom_call" | custom-call | flops 24000 | bytes 1000 | tf_op jit(solution)/shard_map/self_forward_kernel/pallas_call | solution.py:50
  424.2 17.1 %collective-permute-done.32.refs_2_.refs_3_ = bf16[256,352]{1,0:T(8,128)(2,1)S(1)} collective-permute-done((bf16[256,352]{1,0:T(8,128)(2,1)S(1)}, bf16[256,352]{1,0:T(8,128)(2,1)S(1)}, u32[]{:S(2)}, u32[]{:S(2)}) %collective-permute-start.32) | collective-permute-done | bytes 180256 | tf_op jit(solution)/shard_map/ppermute | solution.py:955
  450.2 21.3 %middle_forward_kernel.3 = (bf16[256,1408]{1,0:T(8,128)(2,1)}, f32[256,1408]{1,0:T(8,128)}, bf16[256,1408]{1,0:T(8,128)(2,1)}, bf16[4,256,352]{2,1,0:T(8,128)(2,...) custom-call(s32[10]{0:T(128)} %stack.83.refs_0_.scalars_ref, ...), custom_call_target="tpu_custom_call" | custom-call | flops 23000 | bytes 1000 | tf_op jit(solution)/shard_map/middle_forward_kernel/pallas_call | solution.py:50
  529.7 20.5 %mlp_backward_kernel.2 = (bf16[1024,1408]{1,0:T(8,128)(2,1)}, bf16[1024,1536]{1,0:T(8,128)(2,1)}, f32[256,1408]{1,0:T(8,128)}, bf16[256,1408]{1,0:T(8,128)(2,1)}...) custom-call(bf16[1024,1408]{1,0:T(8,128)(2,1)} %stack_kernel.1.refs_0_, ...), custom_call_target="tpu_custom_call" | custom-call | flops 22000 | bytes 1000 | tf_op jit(solution)/shard_map/mlp_backward_kernel/pallas_call | solution.py:50
  583.3 27.9 %middle_backward_kernel.2 = (f32[256,1408]{1,0:T(8,128)}, bf16[4,256,352]{2,1,0:T(8,128)(2,1)}, bf16[4,256,352]{2,1,0:T(8,128)(2,1)}, bf16[4,256,352]{2,1,0:T(8,...) custom-call(s32[10]{0:T(128)} %stack.83.refs_0_.scalars_ref, ...), custom_call_target="tpu_custom_call" | custom-call | flops 37000 | bytes 1000 | tf_op jit(solution)/shard_map/middle_backward_kernel/pallas_call | solution.py:50
  640.2 28.8 %self_backward_kernel.2 = (bf16[1024,1152]{1,0:T(8,128)(2,1)}, f32[256,1408]{1,0:T(8,128)}, bf16[256,1408]{1,0:T(8,128)(2,1)}, bf16[256,1408]{1,0:T(8,128)(2,1)}...) custom-call(bf16[1024,1152]{1,0:T(8,128)(2,1)} %get-tuple-element.256.refs_0_, ...), custom_call_target="tpu_custom_call" | custom-call | flops 32000 | bytes 1000 | tf_op jit(solution)/shard_map/self_backward_kernel/pallas_call | solution.py:50
  739.1 15.2 %collective-permute-done.63.refs_3_.refs_4_.refs_2_ = bf16[256,1408]{1,0:T(8,128)(2,1)S(1)} collective-permute-done((bf16[256,1408]{1,0:T(8,128)(2,1)}, bf16[256,1408]{1,0:T(8,128)(2,1)S(1)}, u32[]{:S(2)}, u32[]{:S(2)}) %collective-permute-start.63) | collective-permute-done | bytes 720928 | tf_op jit(solution)/shard_map/ppermute | solution.py:955
  771.7 20.2 %mlp_backward_kernel.3 = (bf16[1024,1408]{1,0:T(8,128)(2,1)}, bf16[1024,1536]{1,0:T(8,128)(2,1)}, f32[256,1408]{1,0:T(8,128)}, bf16[256,1408]{1,0:T(8,128)(2,1)}...) custom-call(bf16[256,1408]{1,0:T(8,128)(2,1)} %get-tuple-element.290.refs_0_, ...), custom_call_target="tpu_custom_call" | custom-call | flops 22000 | bytes 1000 | tf_op jit(solution)/shard_map/mlp_backward_kernel/pallas_call | solution.py:50
  837.5 27.9 %middle_backward_kernel.3 = (f32[256,1408]{1,0:T(8,128)}, bf16[4,256,352]{2,1,0:T(8,128)(2,1)}, bf16[4,256,352]{2,1,0:T(8,128)(2,1)}, bf16[4,256,352]{2,1,0:T(8,...) custom-call(s32[10]{0:T(128)} %stack.83.refs_0_.scalars_ref, ...), custom_call_target="tpu_custom_call" | custom-call | flops 37000 | bytes 1000 | tf_op jit(solution)/shard_map/middle_backward_kernel/pallas_call | solution.py:50
  878.6 28.8 %self_backward_kernel.3 = (bf16[1024,1152]{1,0:T(8,128)(2,1)}, f32[256,1408]{1,0:T(8,128)}, bf16[256,1408]{1,0:T(8,128)(2,1)}, bf16[256,1408]{1,0:T(8,128)(2,1)}...) custom-call(bf16[1024,1152]{1,0:T(8,128)(2,1)} %get-tuple-element.293.refs_0_, ...), custom_call_target="tpu_custom_call" | custom-call | flops 32000 | bytes 1000 | tf_op jit(solution)/shard_map/self_backward_kernel/pallas_call | solution.py:50
  932.1 18.9 %collective-permute-done.120.refs_0_ = bf16[1408,384]{1,0:T(8,128)(2,1)S(1)} collective-permute-done((bf16[1408,384]{1,0:T(8,128)(2,1)}, bf16[1408,384]{1,0:T(8,128)(2,1)S(1)}, u32[]{:S(2)}, u32[]{:S(2)}) %collective-permute-start.120) | collective-permute-done | bytes 1081376 | tf_op jit(solution)/shard_map/ppermute | solution.py:974
  988.5 19.7 %collective-permute-done.104.refs_0_ = bf16[704,1152]{1,0:T(8,128)(2,1)S(1)} collective-permute-done((bf16[704,1152]{1,0:T(8,128)(2,1)S(1)}, bf16[704,1152]{1,0:T(8,128)(2,1)S(1)}, u32[]{:S(2)}, u32[]{:S(2)}) %collective-permute-start.104) | collective-permute-done | bytes 1622048 | tf_op jit(solution)/shard_map/ppermute | solution.py:974
  1048.2 31.3 %collective-permute-done.96.refs_0_ = bf16[704,1152]{1,0:T(8,128)(2,1)S(1)} collective-permute-done((bf16[704,1152]{1,0:T(8,128)(2,1)}, bf16[704,1152]{1,0:T(8,128)(2,1)S(1)}, u32[]{:S(2)}, u32[]{:S(2)}) %collective-permute-start.96) | collective-permute-done | bytes 1622048 | tf_op jit(solution)/shard_map/ppermute | solution.py:974
  1086.8 20.4 %collective-permute-done.98.refs_0_ = bf16[704,1152]{1,0:T(8,128)(2,1)S(1)} collective-permute-done((bf16[704,1152]{1,0:T(8,128)(2,1)}, bf16[704,1152]{1,0:T(8,128)(2,1)S(1)}, u32[]{:S(2)}, u32[]{:S(2)}) %collective-permute-start.98) | collective-permute-done | bytes 1622048 | tf_op jit(solution)/shard_map/ppermute | solution.py:974
  1127.0 33.9 %collective-permute-done.89 = f32[10,1408]{1,0:T(8,128)S(1)} collective-permute-done((f32[10,1408]{1,0:T(8,128)S(1)}, f32[10,1408]{1,0:T(8,128)S(1)}, u32[]{:S(2)}, u32[]{:S(2)}) %collective-permute-start.89) | collective-permute-done | bytes 56352 | tf_op jit(solution)/shard_map/ppermute | solution.py:955
  1211.6 28.0 %collective-permute-done.110.refs_2_ = bf16[192,3712]{1,0:T(8,128)(2,1)} collective-permute-done((bf16[192,3712]{1,0:T(8,128)(2,1)}, bf16[192,3712]{1,0:T(8,128)(2,1)}, u32[]{:S(2)}, u32[]{:S(2)}) %collective-permute-start.110) | collective-permute-done | bytes 1425440 | tf_op jit(solution)/shard_map/ppermute | solution.py:955
  (857 shorter events, 792.6 us)
Async XLA Ops:
  9.8 122.2 %all-gather.15.cloned.1.call-start = ((), (), s32[]{:S(2)}) async-start(), calls=%async_computation.16 | async-start | bytes 7299072 | tf_op jit(solution)/shard_map/all_gather | solution.py:1085
  51.3 204.9 %all-gather.11.cloned.1.call-start = ((), (), s32[]{:S(2)}) async-start(), calls=%async_computation.14 | async-start | bytes 2433024 | tf_op jit(solution)/shard_map/all_gather | solution.py:1085
  52.3 214.4 %all-gather.17.cloned.1.call-start = ((), (), s32[]{:S(2)}) async-start(), calls=%async_computation.17 | async-start | bytes 4866048 | tf_op jit(solution)/shard_map/all_gather | solution.py:1085
  57.8 221.6 %all-gather.23.cloned.1.call-start = ((), (), s32[]{:S(2)}) async-start(), calls=%async_computation.31 | async-start | bytes 4866048 | tf_op jit(solution)/shard_map/all_gather | solution.py:1085
  63.0 256.7 %all-gather.19.cloned.1.call-start = ((), (), s32[]{:S(2)}) async-start(), calls=%async_computation.18 | async-start | bytes 7299072 | tf_op jit(solution)/shard_map/all_gather | solution.py:1085
  66.7 438.0 %all-gather.21.cloned.1.call-start = ((), (), s32[]{:S(2)}) async-start(), calls=%async_computation.19 | async-start | bytes 4866048 | tf_op jit(solution)/shard_map/all_gather | solution.py:1085
  179.6 350.1 %all-gather.25.cloned.1.call-start = ((), (), s32[]{:S(2)}) async-start(), calls=%async_computation.32 | async-start | bytes 4866048 | tf_op jit(solution)/shard_map/all_gather | solution.py:1085
  265.0 49.5 %collective-permute-start.19 = (bf16[2816,384]{1,0:T(8,128)(2,1)}, bf16[2816,384]{1,0:T(8,128)(2,1)S(1)}, u32[]{:S(2)}, u32[]{:S(2)}) collective-permute-start(bf16[2816,384]{1,0:T(8,128)(2,1)} %shard_map.294.refs_1_), channel_id=1, source_target_pairs={{0,8},{1,17},{2,10},{3,19},{4,12},{5,21},{6,14},{7,23},{8,0},{9,25... | collective-permute-start | bytes 6488072 | tf_op jit(solution)/shard_map/ppermute | solution.py:974
  325.0 87.3 %collective-permute-start.34 = (bf16[1408,1152]{1,0:T(8,128)(2,1)}, bf16[1408,1152]{1,0:T(8,128)(2,1)}, u32[]{:S(2)}, u32[]{:S(2)}) collective-permute-start(bf16[1408,1152]{1,0:T(8,128)(2,1)} %shard_map.297.refs_16_.refs_8_.refs_5_.refs_1_), channel_id=1, source_target_pairs={{0,8},{1,17},{2,10},{3,19},{4,12},{5,21},{6,14},{7,23},{8,0},{9,25... | collective-permute-start | bytes 9732104 | tf_op jit(solution)/shard_map/ppermute | solution.py:974
  341.1 297.9 %reduce-scatter.12.cloned.1.call-start = ((), (), s32[]{:S(2)}) async-start(), calls=%async_computation.20 | async-start | bytes 4866048 | tf_op jit(solution)/shard_map/reduce_scatter | solution.py:1089
  529.2 185.3 %reduce-scatter.14.cloned.1.call-start = ((), (), s32[]{:S(2)}) async-start(), calls=%async_computation.21 | async-start | bytes 4866048 | tf_op jit(solution)/shard_map/reduce_scatter | solution.py:1089
  569.5 260.7 %reduce-scatter.16.cloned.1.call-start = ((), (), s32[]{:S(2)}) async-start(), calls=%async_computation.22 | async-start | bytes 1769472 | tf_op jit(solution)/shard_map/reduce_scatter | solution.py:1089
  688.9 189.7 %reduce-scatter.20.cloned.1.call-start = ((), (), s32[]{:S(2)}) async-start(), calls=%async_computation.24 | async-start | bytes 3649536 | tf_op jit(solution)/shard_map/reduce_scatter | solution.py:1089
  696.5 182.1 %reduce-scatter.18.cloned.1.call-start = ((), (), s32[]{:S(2)}) async-start(), calls=%async_computation.23 | async-start | bytes 4866048 | tf_op jit(solution)/shard_map/reduce_scatter | solution.py:1089
  815.9 379.9 %reduce-scatter.28.cloned.1.call-start = ((), (), s32[]{:S(2)}) async-start(), calls=%async_computation.28 | async-start | bytes 4866048 | tf_op jit(solution)/shard_map/reduce_scatter | solution.py:1089
  825.5 370.3 %reduce-scatter.30.cloned.1.call-start = ((), (), s32[]{:S(2)}) async-start(), calls=%async_computation.29 | async-start | bytes 1769472 | tf_op jit(solution)/shard_map/reduce_scatter | solution.py:1089
  830.2 80.5 %collective-permute-start.119 = (bf16[1408,384]{1,0:T(8,128)(2,1)}, bf16[1408,384]{1,0:T(8,128)(2,1)}, u32[]{:S(2)}, u32[]{:S(2)}) collective-permute-start(bf16[1408,384]{1,0:T(8,128)(2,1)} %get-tuple-element.421), channel_id=1, source_target_pairs={{0,1},{1,0},{2,3},{3,2},{4,5},{5,4},{6,7},{7,6},{8,9},{9,8},{10,11... | collective-permute-start | bytes 3244040 | tf_op jit(solution)/shard_map/ppermute | solution.py:960
  927.6 315.5 %reduce-scatter.32.cloned.1.call-start = ((), (), s32[]{:S(2)}) async-start(), calls=%async_computation.30 | async-start | bytes 2433024 | tf_op jit(solution)/shard_map/reduce_scatter | solution.py:1089
  980.6 264.2 %reduce-scatter.26.cloned.1.call-start = ((), (), s32[]{:S(2)}) async-start(), calls=%async_computation.27 | async-start | bytes 3649536 | tf_op jit(solution)/shard_map/reduce_scatter | solution.py:1089
  1015.0 258.1 %reduce-scatter.22.cloned.1.call-start = ((), (), s32[]{:S(2)}) async-start(), calls=%async_computation.25 | async-start | bytes 3649536 | tf_op jit(solution)/shard_map/reduce_scatter | solution.py:1089
  1035.2 237.9 %reduce-scatter.24.cloned.1.call-start = ((), (), s32[]{:S(2)}) async-start(), calls=%async_computation.26 | async-start | bytes 3649536 | tf_op jit(solution)/shard_map/reduce_scatter | solution.py:1089
  1172.1 74.9 %collective-permute-start.115 = (bf16[96,3712]{1,0:T(8,128)(2,1)}, bf16[96,3712]{1,0:T(8,128)(2,1)}, u32[]{:S(2)}, u32[]{:S(2)}) collective-permute-start(bf16[96,3712]{1,0:T(8,128)(2,1)} %slice.286), channel_id=1, source_target_pairs={{0,8},{8,0},{16,24},{24,16},{1,9},{9,1},{17,25},{25,17},{2,10},{10... | collective-permute-start | bytes 2138120 | tf_op jit(solution)/shard_map/ppermute | solution.py:955
  1175.7 72.7 %collective-permute-start.116 = (bf16[96,3712]{1,0:T(8,128)(2,1)}, bf16[96,3712]{1,0:T(8,128)(2,1)}, u32[]{:S(2)}, u32[]{:S(2)}) collective-permute-start(bf16[96,3712]{1,0:T(8,128)(2,1)} %slice.287), channel_id=1, source_target_pairs={{0,16},{8,24},{16,0},{24,8},{1,17},{9,25},{17,1},{25,9},{2,18},{10... | collective-permute-start | bytes 2138120 | tf_op jit(solution)/shard_map/ppermute | solution.py:955
  1185.5 71.0 %collective-permute-start.87 = (bf16[352,1024]{1,0:T(8,128)(2,1)}, bf16[352,1024]{1,0:T(8,128)(2,1)}, u32[]{:S(2)}, u32[]{:S(2)}) collective-permute-start(bf16[352,1024]{1,0:T(8,128)(2,1)} %get-tuple-element.476), channel_id=1, source_target_pairs={{0,16},{8,24},{16,0},{24,8},{1,17},{9,25},{17,1},{25,9},{2,18},{10... | collective-permute-start | bytes 2162696 | tf_op jit(solution)/shard_map/ppermute | solution.py:955
  (289 other events, 3516.7 us)
Sparse Core Ops, SparseCore 0:
  10.2 40.9 all-gather.12
  53.5 66.3 all-gather.14
  121.5 28.8 all-gather.10
  152.5 47.1 all-gather.16
  201.8 47.1 all-gather.22
  251.1 65.0 all-gather.18
  317.9 47.0 all-gather.20
  366.6 47.1 all-gather.24
  529.3 49.9 reduce-scatter.11
  582.2 49.3 reduce-scatter.13
  689.0 32.5 reduce-scatter.15
  723.8 39.9 reduce-scatter.19
  816.0 50.1 reduce-scatter.17
  869.0 49.3 reduce-scatter.27
  927.8 32.0 reduce-scatter.29
  980.8 33.9 reduce-scatter.31
  1017.0 40.3 reduce-scatter.25
  1060.2 39.9 reduce-scatter.21
  1113.9 39.0 reduce-scatter.23

commit v6 on v5

--- a/solution.py
+++ b/solution.py
@@ -880,7 +880,7 @@
 
 
 def pack(shards, deps=()):
-    rows = -(-max(m.shape[0] for m in shards) // 32) * 32
+    rows = -(-max(m.shape[0] for m in shards) // 16) * 16
     shape = (rows, sum(m.shape[1] for m in shards))
     return call(functools.partial(pack_kernel, len(shards)), [(shape, BF16)], [], 3, *shards, deps=deps)[0]
 
@@ -1127,7 +1127,7 @@
         up_rows,
         activated,
     )
-    return (saved, square_parts, mlp_parts)
+    return (saved, square_parts, mlp_parts, mixed_rel)
 
 
 def unspread_first(blocks, ready):
@@ -1140,11 +1140,15 @@
     return own, hops, [first_mine, to_mine], sums
 
 
-def unspread_last(scalars, first, hops_ready, joined_ready):
+def unspread_next(first, ready):
     own, hops, terms, _ = first
-    passed, other = gate(hops, hops_ready)
-    mine = swap_by_core(add_bf16(*terms, passed), 1, 2)
-    (mine,) = gate([mine], joined_ready)
+    passed, other = gate(hops, ready)
+    return own, swap_by_core(add_bf16(*terms, passed), 1, 2), other
+
+
+def unspread_last(scalars, second, ready):
+    own, mine, other = second
+    (mine,) = gate([mine], ready)
     return join_halves(scalars, own, mine, other)
 
 
@@ -1152,13 +1156,13 @@
     return add_bf16(blocks[0], *[swap_seq(m, j + 1) for j, m in enumerate(blocks[1:])])
 
 
-def lead_part(layer, qkv, query, self_out, cross_out):
-    padded = padded_width(query.shape[2] // lax.axis_size("seq"))
-    return jnp.concatenate(
-        [own_part(qkv[layer], 3, padded)]
-        + [own_part(m[layer], 1, padded) for m in (self_out, query, cross_out)],
-        axis=1,
-    )
+def qkv_own(layer, qkv):
+    return own_part(qkv[layer], 3, padded_width(qkv.shape[2] // (3 * lax.axis_size("seq"))))
+
+
+def squares_own(layer, *stacks):
+    padded = padded_width(stacks[0].shape[2] // lax.axis_size("seq"))
+    return jnp.concatenate([own_part(m[layer], 1, padded) for m in stacks], axis=1)
 
 
 def gather_rest(layer, up, down):
@@ -1236,9 +1240,8 @@
     out_hops = gather_first(gate([cotangent[0]], latent_parts[-2:])[0])
     shifts = jnp.sum(lax.all_to_all(shift_terms, "fsdp", 0, 0, tiled=True), axis=0)
 
-    lead_stacks = (qkv_weight, query_weight, self_out_weight, cross_out_weight)
+    square_stacks = (self_out_weight, query_weight, cross_out_weight)
     rest_stacks = (up_weight, down_weight)
-    lead_columns = 3 * padded_width(width)
     head_size = model_width // H
     fours = seq_count == 4
 
@@ -1246,22 +1249,23 @@
     kv_both = gather_fsdp(
         jnp.concatenate([own_part(text_kv_weight[l], 2, padded_columns) for l in range(2)], axis=1)
     )
-    lead_first = gather_fsdp(
-        gate([lead_part(0, *lead_stacks)], [kv_both] + latent_hops[1:])[0]
-    )
+    square_shard, qkv_shard = gate(
+        [squares_own(0, *square_stacks), qkv_own(0, qkv_weight)], [kv_both] + latent_hops[1:]
+    )
+    square_first, lead_first = gather_fsdp(square_shard), gather_fsdp(qkv_shard)
     up_first, down_first = gather_rest(0, *rest_stacks)
     pairs_all = gather_parts(dot_nn(text_rows, kv_both).astype(BF16))
-    (lead_first,) = gate([lead_first], [shifts] + pairs_all[-2:])
-    square_first = lead_first[:, lead_columns:]
+    spread_squares = spread_first(gate([square_first], pairs_all[-2:])[0])
+    (lead_first,) = gate([lead_first], [shifts])
     pairs_first, pairs_second = pairs_all, pairs_all
-    saved_first, squares_first, mlp_parts = layer_forward(
+    saved_first, squares_first, mlp_parts, mixed_rel = layer_forward(
         latent_parts,
         latents[0],
         scalars,
         gains[0],
         shifts[0],
         pairs_first,
-        (lead_first, spread_first(square_first), up_first),
+        (lead_first, spread_squares, up_first),
         False,
         (),
     )
@@ -1269,11 +1273,12 @@
     terms = scatter_last(own, scatter_first(pieces))
 
     (skip_matrix,) = gate(
-        [gather_fsdp(own_part(skip_weight, 1, padded_width(width)))], mlp_parts[-2:]
-    )
-    skip_parts = spread_last(spread_first(skip_matrix), [own], terms[-2:])
-    lead_second = gather_fsdp(lead_part(1, *lead_stacks))
-    (square_second,) = gate([lead_second[:, lead_columns:]], terms[-2:])
+        [gather_fsdp(own_part(skip_weight, 1, padded_width(width)))], mixed_rel[1:]
+    )
+    skip_parts = spread_last(spread_first(skip_matrix), mlp_parts[-2:], [own])
+    square_second = gather_fsdp(squares_own(1, *square_stacks))
+    lead_second = gather_fsdp(qkv_own(1, qkv_weight))
+    (square_second,) = gate([square_second], terms[-2:])
     squares_second = spread_first(square_second)
     first_out, joined_norm, skip_out, second_norm = skip_forward(
         scalars,
@@ -1288,7 +1293,7 @@
     )
 
     up_second, down_second = gather_rest(1, *rest_stacks)
-    saved_second, squares_second, mlp_parts = layer_forward(
+    saved_second, squares_second, mlp_parts, _ = layer_forward(
         gather_parts(second_norm),
         skip_out,
         scalars,
@@ -1432,7 +1437,7 @@
     if fours:
         squares = unspread_first(squares, first_parts[-2:])
     output = close_forward(
-        scatter_last(held["own"], held["own_hops"], first_hops[1:]), saved_second[7]
+        scatter_last(held["own"], held["own_hops"], terms[-2:]), saved_second[7]
     )
     skip_outer = outer(scalars, [joined_norm], [skip_branch], tuple(first_hops[1:]))
 
@@ -1454,12 +1459,13 @@
             held["skip"] = unspread_first(skip_outer, terms[-2:])
         held["up"], held["terms"] = grad_up_rows, terms
         held["packed"] = pack([entry[0] for entry in early], (grad_up_rows,))
-        return (held["packed"],)
+        return (held["packed"],) + (tuple(held["skip"][3]) if fours else ())
 
     def first_self(ready):
-        held["blocks"] = gather_first(gate([held["packed"]], [ready])[0])
-        held["middle"] = ready
-        return (qkv_shard,)
+        if not fours:
+            return (qkv_shard,)
+        held["squares"] = unspread_next(squares, held["hops"])
+        return (qkv_shard, held["squares"][1], *held["skip"][1])
 
     (
         terms,
@@ -1485,18 +1491,22 @@
         ),
     )
     if fours:
-        joined = unspread_last(scalars, squares, held["hops"], held["last"])
-        skip_joined = unspread_last(scalars, held["skip"], held["last"], terms[-2:])
-        first_squares = unspread_first(first_squares, terms[-2:])
+        outer_done = [first_squares[1]]
+        joined = unspread_last(scalars, held["squares"], outer_done)
+        skip_second = unspread_next(held["skip"], outer_done)
+        skip_joined = unspread_last(scalars, skip_second, [joined])
+        first_squares = unspread_next(unspread_first(first_squares, terms[3:4]), terms[-2:])
     else:
         joined, skip_joined = unspread_any(squares), unspread_any(skip_outer)
+        outer_done = [joined]
     square_shard, skip_shard = scatter_fsdp(joined), scatter_fsdp(skip_joined)
+    early_hops = gather_first(gate([held["packed"]], outer_done)[0])
     grad_latents, vectors = open_backward(
-        terms, latents[0], gains[0], grad_after_self, (grad_qkv,)
+        terms, latents[0], gains[0], grad_after_self, (grad_qkv, *early_hops[1:])
     )
     vectors_first = jnp.concatenate([vectors, gain_grads], axis=0)
     if fours:
-        first_joined = unspread_last(scalars, first_squares, [grad_latents], [grad_latents])
+        first_joined = unspread_last(scalars, first_squares, [grad_latents])
     else:
         first_joined = unspread_any(first_squares)
     first_layer = (
@@ -1508,10 +1518,15 @@
     )
 
     early_done = settle(
-        scalars, gather_last(held["blocks"], terms[-2:]), plan_of(early), 1, 2, None
+        scalars,
+        gather_last(early_hops),
+        plan_of(early),
+        1,
+        2,
+        None,
     )
     _, late = entries((qkv_shard, square_shard, kv_shard, up_shard, down_shard))
-    late_done = finish(scalars, late, 1, 2, None, (terms[-1],))
+    late_done = finish(scalars, late, 1, 2, None)
     early, late = entries(first_layer)
     grad_up, grad_kv, grad_down = finish(scalars, early, 0, 2, early_done)
     grad_qkv, grad_self_out, grad_query, grad_cross_out = finish(scalars, late, 0, 2, late_done)

time: 1350 us -> 1380 us (1.022)
  waiting for transfers between devices: 535 us -> 609 us
  blocking collectives: 21.1 us -> 0 us
  local copies, waits for them, and re-layouts: 122 us -> 102 us
    ppermute x94, waiting for transfers between devices: 371 us -> 520 us  [swap_seq(): return lax.ppermute(block, 'seq', [(i, i ^ bits) for i in range(seq_count)])]
    ppermute x15, waiting for transfers between devices: 128 us -> 33.9 us  [swap_by_core(): return lax.ppermute(block, ('seq', 'fsdp'), pairs)]
    all_to_all x2 -> x0, blocking collectives: 21.1 us -> none  [the longest x1 11.6 us: body(): small = lax.all_to_all(small, 'fsdp', 0, 0, tiled=True)]
    unnamed x355 -> x341, local copies, waits for them, and re-layouts: 59.9 us -> 52 us
  transfers between devices with their start and end apart: 147 -> 151, of which waited for: 62 -> 67; matrix products, arithmetic and copies ran while one was open for 14% -> 12% of each run, Pallas kernels for 29% -> 29%
where the time goes in v6:
time: 1380 us; the launch traced here: 1370 us
  waiting for transfers between devices  609 us (44%)
  Pallas kernels  397 us (29%)
  starting transfers between devices  132 us (10%)
  local copies, waits for them, and re-layouts  102 us (7%)
  matrix products  69.2 us (5%)
  other arithmetic  44.9 us (3%)
  between operations  17.1 us (1%)
    ppermute x94, waiting for transfers between devices, swap_seq(): return lax.ppermute(block, 'seq', [(i, i ^ bits) for i in range(seq_count)])  520 us
    pallas_call x30, Pallas kernels, call(): pl.pallas_call(run, name=getattr(kernel, 'func', kernel).__name__, out_sh...  369 us
    ppermute x94, starting transfers between devices, swap_seq(): return lax.ppermute(block, 'seq', [(i, i ^ bits) for i in range(seq_count)])  102 us
    dot_general x8, matrix products, dot_tn(): lax.dot_general(a, b, (((0,), (0,)), ((), ())), preferred_element_type=F32)  54.9 us
    unnamed x341, local copies, waits for them, and re-layouts  52 us
    convert_element_type x23, other arithmetic, add_bf16(): return total.astype(BF16)  35.5 us
    ppermute x15, waiting for transfers between devices, swap_by_core(): return lax.ppermute(block, ('seq', 'fsdp'), pairs)  33.9 us
    pallas_call x5, Pallas kernels, settle(): pl.pallas_call(functools.partial(settle_kernel, count, len(blocks), plan)...  28.4 us
  transfers between devices with their start and end apart: 151, of which 67 were waited for; matrix products, arithmetic and copies ran while one was open for 12% of the time, Pallas kernels for 29%

profile of v6, /device:TPU:0, one launch (start us, length us, event | category | flops | bytes accessed | tf_op | source)
XLA Modules:
  0.0 1371.8 jit_solution(3928468348713017501)
XLA Ops:
  30.5 20.8 %all-gather.15.cloned.1.call-done.refs_2_ = bf16[1024,1536]{1,0:T(8,128)(2,1)} async-done(((bf16[128,1536]{1,0:T(8,128)(2,1)}), bf16[1024,1536]{1,0:T(8,128)(2,1)}) %all-gather.15.cloned.1.call-update) | async-done | bytes 3145744 | tf_op jit(solution)/shard_map/all_gather | solution.py:1085
  73.8 23.1 %collective-permute-done.4.refs_12_.refs_8_ = bf16[352,1536]{1,0:T(8,128)(2,1)S(1)} collective-permute-done((bf16[352,1536]{1,0:T(8,128)(2,1)S(1)}, bf16[352,1536]{1,0:T(8,128)(2,1)S(1)}, u32[]{:S(2)}, u32[]{:S(2)}) %collective-permute-start.4) | collective-permute-done | bytes 1081376 | tf_op jit(solution)/shard_map/ppermute | solution.py:955
  129.2 29.3 %collective-permute-done.2.refs_1_.refs_3_ = bf16[128,1408]{1,0:T(8,128)(2,1)S(1)} collective-permute-done((bf16[128,1408]{1,0:T(8,128)(2,1)S(1)}, bf16[128,1408]{1,0:T(8,128)(2,1)S(1)}, u32[]{:S(2)}, u32[]{:S(2)}) %collective-permute-start.2) | collective-permute-done | bytes 360480 | tf_op jit(solution)/shard_map/ppermute | solution.py:955
  170.2 19.1 %self_forward_kernel.2 = (bf16[1024,1408]{1,0:T(8,128)(2,1)}, bf16[1024,1152]{1,0:T(8,128)(2,1)}, bf16[256,352]{1,0:T(8,128)(2,1)}, bf16[256,352]{1,0:T(8,128)(2...) custom-call(bf16[256,1408]{1,0:T(8,128)(2,1)} %bitcast.168, bf16[256,1408]{1,0:T(8,128)(2,1)} %copy-done.33, ...), custom_call_target="tpu_custom_call" | custom-call | flops 24000 | bytes 1000 | tf_op jit(solution)/shard_map/self_forward_kernel/pallas_call | solution.py:50
  228.5 20.4 %middle_forward_kernel.2 = (bf16[256,1408]{1,0:T(8,128)(2,1)}, f32[256,1408]{1,0:T(8,128)}, bf16[256,1408]{1,0:T(8,128)(2,1)}, bf16[4,256,352]{2,1,0:T(8,128)(2,...) custom-call(s32[10]{0:T(128)} %stack.83.refs_0_.scalars_ref, ...), custom_call_target="tpu_custom_call" | custom-call | flops 23000 | bytes 1000 | tf_op jit(solution)/shard_map/middle_forward_kernel/pallas_call | solution.py:50
  252.2 16.0 %collective-permute-done.16.refs_2_ = bf16[256,1408]{1,0:T(8,128)(2,1)S(1)} collective-permute-done((bf16[256,1408]{1,0:T(8,128)(2,1)}, bf16[256,1408]{1,0:T(8,128)(2,1)S(1)}, u32[]{:S(2)}, u32[]{:S(2)}) %collective-permute-start.16) | collective-permute-done | bytes 720928 | tf_op jit(solution)/shard_map/ppermute | solution.py:955
  272.9 26.2 %collective-permute-done.17.refs_1_.refs_3_ = bf16[128,1408]{1,0:T(8,128)(2,1)S(1)} collective-permute-done((bf16[128,1408]{1,0:T(8,128)(2,1)}, bf16[128,1408]{1,0:T(8,128)(2,1)S(1)}, u32[]{:S(2)}, u32[]{:S(2)}) %collective-permute-start.17) | collective-permute-done | bytes 360480 | tf_op jit(solution)/shard_map/ppermute | solution.py:955
  357.9 18.4 %collective-permute-done.21.refs_0_ = bf16[1408,384]{1,0:T(8,128)(2,1)} collective-permute-done((bf16[1408,384]{1,0:T(8,128)(2,1)}, bf16[1408,384]{1,0:T(8,128)(2,1)}, u32[]{:S(2)}, u32[]{:S(2)}) %collective-permute-start.21) | collective-permute-done | bytes 1081376 | tf_op jit(solution)/shard_map/ppermute | solution.py:974
  392.0 18.3 %collective-permute-done.28.refs_2_ = bf16[256,1408]{1,0:T(8,128)(2,1)S(1)} collective-permute-done((bf16[256,1408]{1,0:T(8,128)(2,1)}, bf16[256,1408]{1,0:T(8,128)(2,1)S(1)}, u32[]{:S(2)}, u32[]{:S(2)}) %collective-permute-start.28) | collective-permute-done | bytes 720928 | tf_op jit(solution)/shard_map/ppermute | solution.py:955
  427.3 18.5 %self_forward_kernel.3 = (bf16[1024,1408]{1,0:T(8,128)(2,1)}, bf16[1024,1152]{1,0:T(8,128)(2,1)}, bf16[256,352]{1,0:T(8,128)(2,1)}, bf16[256,352]{1,0:T(8,128)(2...) custom-call(bf16[256,1408]{1,0:T(8,128)(2,1)} %get-tuple-element.235.refs_0_, bf16[256,1408]{1,0:T(8,128)(2,1)} %copy-done.77, ...), custom_call_target="tpu_custom_call" | custom-call | flops 24000 | bytes 1000 | tf_op jit(solution)/shard_map/self_forward_kernel/pallas_call | solution.py:50
  456.8 20.2 %collective-permute-done.32.refs_2_.refs_3_ = bf16[256,352]{1,0:T(8,128)(2,1)S(1)} collective-permute-done((bf16[256,352]{1,0:T(8,128)(2,1)S(1)}, bf16[256,352]{1,0:T(8,128)(2,1)S(1)}, u32[]{:S(2)}, u32[]{:S(2)}) %collective-permute-start.32) | collective-permute-done | bytes 180256 | tf_op jit(solution)/shard_map/ppermute | solution.py:955
  483.8 21.3 %middle_forward_kernel.3 = (bf16[256,1408]{1,0:T(8,128)(2,1)}, f32[256,1408]{1,0:T(8,128)}, bf16[256,1408]{1,0:T(8,128)(2,1)}, bf16[4,256,352]{2,1,0:T(8,128)(2,...) custom-call(s32[10]{0:T(128)} %stack.83.refs_0_.scalars_ref, ...), custom_call_target="tpu_custom_call" | custom-call | flops 23000 | bytes 1000 | tf_op jit(solution)/shard_map/middle_forward_kernel/pallas_call | solution.py:50
  562.3 20.5 %mlp_backward_kernel.2 = (bf16[1024,1408]{1,0:T(8,128)(2,1)}, bf16[1024,1536]{1,0:T(8,128)(2,1)}, f32[256,1408]{1,0:T(8,128)}, bf16[256,1408]{1,0:T(8,128)(2,1)}...) custom-call(bf16[1024,1408]{1,0:T(8,128)(2,1)} %stack_kernel.1.refs_0_, ...), custom_call_target="tpu_custom_call" | custom-call | flops 22000 | bytes 1000 | tf_op jit(solution)/shard_map/mlp_backward_kernel/pallas_call | solution.py:50
  616.6 27.9 %middle_backward_kernel.2 = (f32[256,1408]{1,0:T(8,128)}, bf16[4,256,352]{2,1,0:T(8,128)(2,1)}, bf16[4,256,352]{2,1,0:T(8,128)(2,1)}, bf16[4,256,352]{2,1,0:T(8,...) custom-call(s32[10]{0:T(128)} %stack.83.refs_0_.scalars_ref, ...), custom_call_target="tpu_custom_call" | custom-call | flops 37000 | bytes 1000 | tf_op jit(solution)/shard_map/middle_backward_kernel/pallas_call | solution.py:50
  673.5 28.8 %self_backward_kernel.2 = (bf16[1024,1152]{1,0:T(8,128)(2,1)}, f32[256,1408]{1,0:T(8,128)}, bf16[256,1408]{1,0:T(8,128)(2,1)}, bf16[256,1408]{1,0:T(8,128)(2,1)}...) custom-call(bf16[1024,1152]{1,0:T(8,128)(2,1)} %get-tuple-element.258.refs_0_, ...), custom_call_target="tpu_custom_call" | custom-call | flops 32000 | bytes 1000 | tf_op jit(solution)/shard_map/self_backward_kernel/pallas_call | solution.py:50
  802.2 20.2 %mlp_backward_kernel.3 = (bf16[1024,1408]{1,0:T(8,128)(2,1)}, bf16[1024,1536]{1,0:T(8,128)(2,1)}, f32[256,1408]{1,0:T(8,128)}, bf16[256,1408]{1,0:T(8,128)(2,1)}...) custom-call(bf16[256,1408]{1,0:T(8,128)(2,1)} %get-tuple-element.295.refs_0_, ...), custom_call_target="tpu_custom_call" | custom-call | flops 22000 | bytes 1000 | tf_op jit(solution)/shard_map/mlp_backward_kernel/pallas_call | solution.py:50
  880.9 16.4 %collective-permute-done.74.refs_2_.refs_14_ = bf16[128,1408]{1,0:T(8,128)(2,1)S(1)} collective-permute-done((bf16[128,1408]{1,0:T(8,128)(2,1)S(1)}, bf16[128,1408]{1,0:T(8,128)(2,1)S(1)}, u32[]{:S(2)}, u32[]{:S(2)}) %collective-permute-start.74) | collective-permute-done | bytes 360480 | tf_op jit(solution)/shard_map/ppermute | solution.py:955
  903.1 27.9 %middle_backward_kernel.3 = (f32[256,1408]{1,0:T(8,128)}, bf16[4,256,352]{2,1,0:T(8,128)(2,1)}, bf16[4,256,352]{2,1,0:T(8,128)(2,1)}, bf16[4,256,352]{2,1,0:T(8,...) custom-call(s32[10]{0:T(128)} %stack.83.refs_0_.scalars_ref, ...), custom_call_target="tpu_custom_call" | custom-call | flops 37000 | bytes 1000 | tf_op jit(solution)/shard_map/middle_backward_kernel/pallas_call | solution.py:50
  950.2 28.9 %self_backward_kernel.3 = (bf16[1024,1152]{1,0:T(8,128)(2,1)}, f32[256,1408]{1,0:T(8,128)}, bf16[256,1408]{1,0:T(8,128)(2,1)}, bf16[256,1408]{1,0:T(8,128)(2,1)}...) custom-call(bf16[1024,1152]{1,0:T(8,128)(2,1)} %get-tuple-element.290.refs_0_, ...), custom_call_target="tpu_custom_call" | custom-call | flops 32000 | bytes 1000 | tf_op jit(solution)/shard_map/self_backward_kernel/pallas_call | solution.py:50
  1061.5 41.7 %collective-permute-done.91.refs_4_.refs_3_ = bf16[128,1408]{1,0:T(8,128)(2,1)S(1)} collective-permute-done((bf16[128,1408]{1,0:T(8,128)(2,1)S(1)}, bf16[128,1408]{1,0:T(8,128)(2,1)S(1)}, u32[]{:S(2)}, u32[]{:S(2)}) %collective-permute-start.91) | collective-permute-done | bytes 360480 | tf_op jit(solution)/shard_map/ppermute | solution.py:955
  1110.2 33.2 %collective-permute-done.93.refs_10_.refs_2_ = bf16[192,3712]{1,0:T(8,128)(2,1)} collective-permute-done((bf16[192,3712]{1,0:T(8,128)(2,1)}, bf16[192,3712]{1,0:T(8,128)(2,1)}, u32[]{:S(2)}, u32[]{:S(2)}) %collective-permute-start.93) | collective-permute-done | bytes 1425440 | tf_op jit(solution)/shard_map/ppermute | solution.py:955
  1185.9 17.0 %collective-permute-done.96 = f32[10,1408]{1,0:T(8,128)S(1)} collective-permute-done((f32[10,1408]{1,0:T(8,128)S(1)}, f32[10,1408]{1,0:T(8,128)S(1)}, u32[]{:S(2)}, u32[]{:S(2)}) %collective-permute-start.96) | collective-permute-done | bytes 56352 | tf_op jit(solution)/shard_map/ppermute | solution.py:955
  1256.9 19.6 %collective-permute-done.116.refs_2_ = bf16[192,3712]{1,0:T(8,128)(2,1)} collective-permute-done((bf16[192,3712]{1,0:T(8,128)(2,1)}, bf16[192,3712]{1,0:T(8,128)(2,1)}, u32[]{:S(2)}, u32[]{:S(2)}) %collective-permute-start.116) | collective-permute-done | bytes 1425440 | tf_op jit(solution)/shard_map/ppermute | solution.py:955
  1294.9 21.0 %collective-permute-done.123.refs_1_ = bf16[352,384]{1,0:T(8,128)(2,1)S(1)} collective-permute-done((bf16[352,384]{1,0:T(8,128)(2,1)S(1)}, bf16[352,384]{1,0:T(8,128)(2,1)S(1)}, u32[]{:S(2)}, u32[]{:S(2)}) %collective-permute-start.123) | collective-permute-done | bytes 270368 | tf_op jit(solution)/shard_map/ppermute | solution.py:955
  (850 shorter events, 799.8 us)
Async XLA Ops:
  9.8 102.4 %all-gather.19.cloned.1.call-start = ((), (), s32[]{:S(2)}) async-start(), calls=%async_computation.17 | async-start | bytes 3649536 | tf_op jit(solution)/shard_map/all_gather | solution.py:1085
  51.3 118.9 %all-gather.17.cloned.1.call-start = ((), (), s32[]{:S(2)}) async-start(), calls=%async_computation.16 | async-start | bytes 3649536 | tf_op jit(solution)/shard_map/all_gather | solution.py:1085
  52.0 199.1 %all-gather.13.cloned.1.call-start = ((), (), s32[]{:S(2)}) async-start(), calls=%async_computation.14 | async-start | bytes 2433024 | tf_op jit(solution)/shard_map/all_gather | solution.py:1085
  53.0 219.9 %all-gather.21.cloned.1.call-start = ((), (), s32[]{:S(2)}) async-start(), calls=%async_computation.18 | async-start | bytes 4866048 | tf_op jit(solution)/shard_map/all_gather | solution.py:1085
  58.5 254.1 %all-gather.29.cloned.1.call-start = ((), (), s32[]{:S(2)}) async-start(), calls=%async_computation.33 | async-start | bytes 4866048 | tf_op jit(solution)/shard_map/all_gather | solution.py:1085
  63.6 287.0 %all-gather.23.cloned.1.call-start = ((), (), s32[]{:S(2)}) async-start(), calls=%async_computation.19 | async-start | bytes 3649536 | tf_op jit(solution)/shard_map/all_gather | solution.py:1085
  66.7 349.3 %all-gather.25.cloned.1.call-start = ((), (), s32[]{:S(2)}) async-start(), calls=%async_computation.20 | async-start | bytes 3649536 | tf_op jit(solution)/shard_map/all_gather | solution.py:1085
  112.2 77.1 %collective-permute-start.12 = (bf16[1408,1152]{1,0:T(8,128)(2,1)}, bf16[1408,1152]{1,0:T(8,128)(2,1)}, u32[]{:S(2)}, u32[]{:S(2)}) collective-permute-start(bf16[1408,1152]{1,0:T(8,128)(2,1)} %shard_map.292.refs_8_.refs_5_.refs_1_), channel_id=1, source_target_pairs={{0,8},{1,17},{2,10},{3,19},{4,12},{5,21},{6,14},{7,23},{8,0},{9,25... | collective-permute-start | bytes 9732104 | tf_op jit(solution)/shard_map/ppermute | solution.py:974
  163.4 374.4 %all-gather.27.cloned.1.call-start = ((), (), s32[]{:S(2)}) async-start(), calls=%async_computation.21 | async-start | bytes 4866048 | tf_op jit(solution)/shard_map/all_gather | solution.py:1085
  194.5 367.7 %all-gather.31.cloned.1.call-start = ((), (), s32[]{:S(2)}) async-start(), calls=%async_computation.34 | async-start | bytes 4866048 | tf_op jit(solution)/shard_map/all_gather | solution.py:1085
  251.1 95.0 %collective-permute-start.11 = (bf16[2816,384]{1,0:T(8,128)(2,1)}, bf16[2816,384]{1,0:T(8,128)(2,1)S(1)}, u32[]{:S(2)}, u32[]{:S(2)}) collective-permute-start(bf16[2816,384]{1,0:T(8,128)(2,1)} %shard_map.293.refs_1_), channel_id=1, source_target_pairs={{0,8},{1,17},{2,10},{3,19},{4,12},{5,21},{6,14},{7,23},{8,0},{9,25... | collective-permute-start | bytes 6488072 | tf_op jit(solution)/shard_map/ppermute | solution.py:974
  356.3 89.6 %collective-permute-start.34 = (bf16[1408,1152]{1,0:T(8,128)(2,1)}, bf16[1408,1152]{1,0:T(8,128)(2,1)}, u32[]{:S(2)}, u32[]{:S(2)}) collective-permute-start(bf16[1408,1152]{1,0:T(8,128)(2,1)} %shard_map.298.refs_16_.refs_8_.refs_5_.refs_1_), channel_id=1, source_target_pairs={{0,8},{1,17},{2,10},{3,19},{4,12},{5,21},{6,14},{7,23},{8,0},{9,25... | collective-permute-start | bytes 9732104 | tf_op jit(solution)/shard_map/ppermute | solution.py:974
  378.2 294.1 %reduce-scatter.12.cloned.1.call-start = ((), (), s32[]{:S(2)}) async-start(), calls=%async_computation.22 | async-start | bytes 4866048 | tf_op jit(solution)/shard_map/reduce_scatter | solution.py:1089
  561.8 183.5 %reduce-scatter.14.cloned.1.call-start = ((), (), s32[]{:S(2)}) async-start(), calls=%async_computation.23 | async-start | bytes 4866048 | tf_op jit(solution)/shard_map/reduce_scatter | solution.py:1089
  602.2 298.4 %reduce-scatter.16.cloned.1.call-start = ((), (), s32[]{:S(2)}) async-start(), calls=%async_computation.24 | async-start | bytes 1769472 | tf_op jit(solution)/shard_map/reduce_scatter | solution.py:1089
  722.0 227.0 %reduce-scatter.20.cloned.1.call-start = ((), (), s32[]{:S(2)}) async-start(), calls=%async_computation.26 | async-start | bytes 3649536 | tf_op jit(solution)/shard_map/reduce_scatter | solution.py:1089
  729.5 219.5 %reduce-scatter.18.cloned.1.call-start = ((), (), s32[]{:S(2)}) async-start(), calls=%async_computation.25 | async-start | bytes 4866048 | tf_op jit(solution)/shard_map/reduce_scatter | solution.py:1089
  846.7 392.7 %reduce-scatter.28.cloned.1.call-start = ((), (), s32[]{:S(2)}) async-start(), calls=%async_computation.30 | async-start | bytes 4866048 | tf_op jit(solution)/shard_map/reduce_scatter | solution.py:1089
  856.3 383.2 %reduce-scatter.30.cloned.1.call-start = ((), (), s32[]{:S(2)}) async-start(), calls=%async_computation.31 | async-start | bytes 1769472 | tf_op jit(solution)/shard_map/reduce_scatter | solution.py:1089
  868.5 80.5 %collective-permute-start.82 = (bf16[704,1152]{1,0:T(8,128)(2,1)}, bf16[704,1152]{1,0:T(8,128)(2,1)S(1)}, u32[]{:S(2)}, u32[]{:S(2)}) collective-permute-start(bf16[704,1152]{1,0:T(8,128)(2,1)} %add_convert_fusion.3), channel_id=1, source_target_pairs={{0,8},{1,17},{2,10},{3,19},{4,12},{5,21},{6,14},{7,23},{8,0},{9,25... | collective-permute-start | bytes 4866056 | tf_op jit(solution)/shard_map/ppermute | solution.py:974
  1001.5 247.9 %reduce-scatter.32.cloned.1.call-start = ((), (), s32[]{:S(2)}) async-start(), calls=%async_computation.32 | async-start | bytes 2433024 | tf_op jit(solution)/shard_map/reduce_scatter | solution.py:1089
  1037.1 217.7 %reduce-scatter.26.cloned.1.call-start = ((), (), s32[]{:S(2)}) async-start(), calls=%async_computation.29 | async-start | bytes 3649536 | tf_op jit(solution)/shard_map/reduce_scatter | solution.py:1089
  1037.8 278.6 %reduce-scatter.22.cloned.1.call-start = ((), (), s32[]{:S(2)}) async-start(), calls=%async_computation.27 | async-start | bytes 3649536 | tf_op jit(solution)/shard_map/reduce_scatter | solution.py:1089
  1046.4 270.1 %reduce-scatter.24.cloned.1.call-start = ((), (), s32[]{:S(2)}) async-start(), calls=%async_computation.28 | async-start | bytes 3649536 | tf_op jit(solution)/shard_map/reduce_scatter | solution.py:1089
  (291 other events, 4198.4 us)
Sparse Core Ops, SparseCore 0:
  10.2 40.9 all-gather.14
  53.5 37.9 all-gather.18
  93.7 39.0 all-gather.16
  134.9 28.4 all-gather.12
  165.4 47.9 all-gather.20
  215.5 47.1 all-gather.28
  264.9 37.8 all-gather.22
  304.4 37.9 all-gather.24
  344.0 47.2 all-gather.26
  392.8 47.1 all-gather.30
  561.9 49.8 reduce-scatter.11
  614.7 49.3 reduce-scatter.13
  722.1 31.7 reduce-scatter.15
  756.0 39.5 reduce-scatter.19
  846.8 49.5 reduce-scatter.17
  899.2 49.3 reduce-scatter.27
  1001.6 31.2 reduce-scatter.29
  1037.2 33.1 reduce-scatter.31
  1072.8 40.4 reduce-scatter.25
  1116.0 40.0 reduce-scatter.21
  1170.7 38.8 reduce-scatter.23

commit v7 on v6

--- a/solution.py
+++ b/solution.py
@@ -1227,17 +1227,21 @@
         ],
         axis=1,
     ).astype(F32)
-    latent_hops = gather_first(latents[0])
-    (small,) = gate([small], latent_hops[1:])
+    latent_parts = gather_parts(latents[0])
+    (small,) = gate([small], latent_parts[-2:])
     small = lax.all_to_all(small, "fsdp", 0, 0, tiled=True)
     cond_part = small[:, 0]
     gains = jnp.swapaxes(small[:, 1:7], 0, 1).reshape(2, 3, model_width)
     skip_gains = small[:, 7:].reshape(2, model_width)
     silu_part = jax.nn.silu(cond_part)
     shift_terms = jnp.einsum("br,lrd->bld", silu_part, mod_weight.astype(F32), precision=EXACT)
-    latent_parts = gather_last(latent_hops)
-    (shift_terms,) = gate([shift_terms], latent_parts[-2:])
-    out_hops = gather_first(gate([cotangent[0]], latent_parts[-2:])[0])
+    padded_columns = padded_width(width)
+    kv_both = gather_fsdp(
+        jnp.concatenate([own_part(text_kv_weight[l], 2, padded_columns) for l in range(2)], axis=1)
+    )
+    pair_hops = gather_first(dot_nn(text_rows, kv_both).astype(BF16))
+    pairs_all = gather_last(pair_hops)
+    (shift_terms,) = gate([shift_terms], pair_hops[1:])
     shifts = jnp.sum(lax.all_to_all(shift_terms, "fsdp", 0, 0, tiled=True), axis=0)
 
     square_stacks = (self_out_weight, query_weight, cross_out_weight)
@@ -1245,17 +1249,12 @@
     head_size = model_width // H
     fours = seq_count == 4
 
-    padded_columns = padded_width(width)
-    kv_both = gather_fsdp(
-        jnp.concatenate([own_part(text_kv_weight[l], 2, padded_columns) for l in range(2)], axis=1)
-    )
     square_shard, qkv_shard = gate(
-        [squares_own(0, *square_stacks), qkv_own(0, qkv_weight)], [kv_both] + latent_hops[1:]
+        [squares_own(0, *square_stacks), qkv_own(0, qkv_weight)], [kv_both] + latent_parts[-2:]
     )
     square_first, lead_first = gather_fsdp(square_shard), gather_fsdp(qkv_shard)
     up_first, down_first = gather_rest(0, *rest_stacks)
-    pairs_all = gather_parts(dot_nn(text_rows, kv_both).astype(BF16))
-    spread_squares = spread_first(gate([square_first], pairs_all[-2:])[0])
+    spread_squares = spread_first(gate([square_first], [shifts])[0])
     (lead_first,) = gate([lead_first], [shifts])
     pairs_first, pairs_second = pairs_all, pairs_all
     saved_first, squares_first, mlp_parts, mixed_rel = layer_forward(
@@ -1293,6 +1292,7 @@
     )
 
     up_second, down_second = gather_rest(1, *rest_stacks)
+    out_hops = gather_first(gate([cotangent[0]], [skip_out])[0])
     saved_second, squares_second, mlp_parts, _ = layer_forward(
         gather_parts(second_norm),
         skip_out,
@@ -1360,7 +1360,7 @@
             mixed_rel,
             lead_matrix,
             head_size,
-            (down_shard,) + hooks[2](mixed_grads[0]),
+            (down_shard,) + hooks[2](mixed_rel[1]),
         )
         pair_terms = gate(pair_terms, [grad_triples])
         first = scatter_first(gate(pieces, pair_terms))
@@ -1436,9 +1436,8 @@
     first_parts = gather_last(first_hops)
     if fours:
         squares = unspread_first(squares, first_parts[-2:])
-    output = close_forward(
-        scatter_last(held["own"], held["own_hops"], terms[-2:]), saved_second[7]
-    )
+    own_terms = scatter_last(held["own"], held["own_hops"], terms[-2:])
+    output = close_forward(own_terms, saved_second[7])
     skip_outer = outer(scalars, [joined_norm], [skip_branch], tuple(first_hops[1:]))
 
     def entries(layer):
@@ -1446,26 +1445,24 @@
         return (
             [
                 (up, fsdp_count, 1, up.shape[1] // fsdp_count),
-                (kv, 2, 1, width),
                 (down, 0, 1, down.shape[1]),
             ],
-            [(qkv, 3, 1, width), (square, 1, 3, width)],
+            [(qkv, 3, 1, width), (square, 1, 3, width), (kv, 2, 1, width)],
         )
 
     early, _ = entries((qkv_shard, qkv_shard, kv_shard, up_shard, down_shard))
 
     def first_middle(grad_up_rows, terms):
-        if fours:
-            held["skip"] = unspread_first(skip_outer, terms[-2:])
         held["up"], held["terms"] = grad_up_rows, terms
         held["packed"] = pack([entry[0] for entry in early], (grad_up_rows,))
-        return (held["packed"],) + (tuple(held["skip"][3]) if fours else ())
+        held["early"] = gather_first(gate([held["packed"]], terms[-2:])[0])
+        return (held["early"][0], kv_shard)
 
     def first_self(ready):
         if not fours:
             return (qkv_shard,)
-        held["squares"] = unspread_next(squares, held["hops"])
-        return (qkv_shard, held["squares"][1], *held["skip"][1])
+        held["joined"] = unspread_last(scalars, unspread_next(squares, held["hops"]), [ready])
+        return (qkv_shard, held["joined"], *held["early"][1:])
 
     (
         terms,
@@ -1484,7 +1481,7 @@
         (lead_first, squares_first, pairs_first, up_first, down_first),
         None,
         (
-            (skip_outer[0],) + (tuple(squares[3]) if fours else ()),
+            (skip_outer[0], *own_terms[-2:]) + (tuple(squares[3]) if fours else ()),
             first_middle,
             first_self,
             squares[1] if fours else (),
@@ -1492,23 +1489,27 @@
     )
     if fours:
         outer_done = [first_squares[1]]
-        joined = unspread_last(scalars, held["squares"], outer_done)
-        skip_second = unspread_next(held["skip"], outer_done)
-        skip_joined = unspread_last(scalars, skip_second, [joined])
-        first_squares = unspread_next(unspread_first(first_squares, terms[3:4]), terms[-2:])
+        joined = held["joined"]
+        first_squares = unspread_first(first_squares, outer_done)
+        skip_first = unspread_first(skip_outer, first_squares[3])
+        first_squares = unspread_next(first_squares, terms[-2:])
+        first_joined = unspread_last(scalars, first_squares, terms[-2:])
+        skip_joined = unspread_last(
+            scalars, unspread_next(skip_first, [first_squares[1]]), [first_joined]
+        )
     else:
         joined, skip_joined = unspread_any(squares), unspread_any(skip_outer)
+        first_joined = unspread_any(first_squares)
         outer_done = [joined]
     square_shard, skip_shard = scatter_fsdp(joined), scatter_fsdp(skip_joined)
-    early_hops = gather_first(gate([held["packed"]], outer_done)[0])
+    early, _ = entries(
+        (first_qkv_shard, first_qkv_shard, first_kv_shard, first_up_shard, first_down_shard)
+    )
+    first_hops = gather_first(pack([entry[0] for entry in early], outer_done))
     grad_latents, vectors = open_backward(
-        terms, latents[0], gains[0], grad_after_self, (grad_qkv, *early_hops[1:])
+        terms, latents[0], gains[0], grad_after_self, (grad_qkv, first_joined, *first_hops[1:])
     )
     vectors_first = jnp.concatenate([vectors, gain_grads], axis=0)
-    if fours:
-        first_joined = unspread_last(scalars, first_squares, [grad_latents])
-    else:
-        first_joined = unspread_any(first_squares)
     first_layer = (
         first_qkv_shard,
         scatter_fsdp(first_joined),
@@ -1519,7 +1520,7 @@
 
     early_done = settle(
         scalars,
-        gather_last(early_hops),
+        gather_last(held["early"], outer_done),
         plan_of(early),
         1,
         2,
@@ -1528,8 +1529,12 @@
     _, late = entries((qkv_shard, square_shard, kv_shard, up_shard, down_shard))
     late_done = finish(scalars, late, 1, 2, None)
     early, late = entries(first_layer)
-    grad_up, grad_kv, grad_down = finish(scalars, early, 0, 2, early_done)
-    grad_qkv, grad_self_out, grad_query, grad_cross_out = finish(scalars, late, 0, 2, late_done)
+    grad_up, grad_down = settle(
+        scalars, gather_last(first_hops), plan_of(early), 0, 2, early_done
+    )
+    grad_qkv, grad_self_out, grad_query, grad_cross_out, grad_kv = finish(
+        scalars, late, 0, 2, late_done
+    )
     (grad_skip_weight,) = finish(scalars, [(skip_shard, 1, 1, width)], 0, 1)
 
     sums = sum_vectors(jnp.concatenate([vectors_first, vectors_second], axis=0))

time: 1380 us -> 1400 us (1.014)
  blocking collectives: 0 us -> 22.3 us
    all_to_all x0 -> x2, blocking collectives: none -> 22.3 us  [the longest x1 12.7 us: body(): lax.all_to_all(shift_terms, 'fsdp', 0, 0, tiled=True)]
    ppermute x15, waiting for transfers between devices: 33.9 us -> 56 us  [swap_by_core(): return lax.ppermute(block, ('seq', 'fsdp'), pairs)]
    ppermute x94, waiting for transfers between devices: 520 us -> 501 us  [swap_seq(): return lax.ppermute(block, 'seq', [(i, i ^ bits) for i in range(seq_count)])]
    unnamed x341 -> x335, local copies, waits for them, and re-layouts: 52 us -> 46.4 us
  transfers between devices with their start and end apart: 151 -> 149, of which waited for: 67 -> 65; matrix products, arithmetic and copies ran while one was open for 12% -> 12% of each run, Pallas kernels for 29% -> 28%
where the time goes in v7:
time: 1400 us; the launch traced here: 1390 us
  waiting for transfers between devices  614 us (44%)
  Pallas kernels  398 us (28%)
  starting transfers between devices  126 us (9%)
  local copies, waits for them, and re-layouts  103 us (7%)
  matrix products  65.6 us (5%)
  other arithmetic  45.9 us (3%)
  blocking collectives  22.3 us (2%)
  between operations  17.1 us (1%)
    ppermute x94, waiting for transfers between devices, swap_seq(): return lax.ppermute(block, 'seq', [(i, i ^ bits) for i in range(seq_count)])  501 us
    pallas_call x30, Pallas kernels, call(): pl.pallas_call(run, name=getattr(kernel, 'func', kernel).__name__, out_sh...  368 us
    ppermute x94, starting transfers between devices, swap_seq(): return lax.ppermute(block, 'seq', [(i, i ^ bits) for i in range(seq_count)])  102 us
    ppermute x15, waiting for transfers between devices, swap_by_core(): return lax.ppermute(block, ('seq', 'fsdp'), pairs)  56 us
    dot_general x8, matrix products, dot_tn(): lax.dot_general(a, b, (((0,), (0,)), ((), ())), preferred_element_type=F32)  52.1 us
    unnamed x335, local copies, waits for them, and re-layouts  46.4 us
    convert_element_type x23, other arithmetic, add_bf16(): return total.astype(BF16)  36.4 us
    all_gather x10, waiting for transfers between devices, gather_fsdp(): return lax.all_gather(shard, 'fsdp', axis=0, tiled=True)  29.7 us
  transfers between devices with their start and end apart: 149, of which 65 were waited for; matrix products, arithmetic and copies ran while one was open for 12% of the time, Pallas kernels for 28%

profile of v7, /device:TPU:0, one launch (start us, length us, event | category | flops | bytes accessed | tf_op | source)
XLA Modules:
  0.0 1391.5 jit_solution(18445185736956439768)
XLA Ops:
  116.2 18.5 %all-gather.17.cloned.1.call-done.refs_0_ = bf16[1408,1152]{1,0:T(8,128)(2,1)} async-done(((bf16[176,1152]{1,0:T(8,128)(2,1)}), bf16[1408,1152]{1,0:T(8,128)(2,1)}) %all-gather.17.cloned.1.call-update) | async-done | bytes 3244048 | tf_op jit(solution)/shard_map/all_gather | solution.py:1085
  134.7 18.6 %self_forward_kernel.2 = (bf16[1024,1408]{1,0:T(8,128)(2,1)}, bf16[1024,1152]{1,0:T(8,128)(2,1)}, bf16[256,352]{1,0:T(8,128)(2,1)}, bf16[256,352]{1,0:T(8,128)(2...) custom-call(bf16[256,1408]{1,0:T(8,128)(2,1)} %bitcast.168, bf16[256,1408]{1,0:T(8,128)(2,1)} %copy-done.77, ...), custom_call_target="tpu_custom_call" | custom-call | flops 24000 | bytes 1000 | tf_op jit(solution)/shard_map/self_forward_kernel/pallas_call | solution.py:50
  167.0 17.9 %collective-permute-done.7.refs_2_.refs_3_ = bf16[256,352]{1,0:T(8,128)(2,1)S(1)} collective-permute-done((bf16[256,352]{1,0:T(8,128)(2,1)}, bf16[256,352]{1,0:T(8,128)(2,1)S(1)}, u32[]{:S(2)}, u32[]{:S(2)}) %collective-permute-start.7) | collective-permute-done | bytes 180256 | tf_op jit(solution)/shard_map/ppermute | solution.py:955
  204.0 20.3 %middle_forward_kernel.2 = (bf16[256,1408]{1,0:T(8,128)(2,1)}, f32[256,1408]{1,0:T(8,128)}, bf16[256,1408]{1,0:T(8,128)(2,1)}, bf16[4,256,352]{2,1,0:T(8,128)(2,...) custom-call(s32[10]{0:T(128)} %stack.83.refs_0_.scalars_ref, ...), custom_call_target="tpu_custom_call" | custom-call | flops 23000 | bytes 1000 | tf_op jit(solution)/shard_map/middle_forward_kernel/pallas_call | solution.py:50
  228.0 15.6 %collective-permute-done.16.refs_2_ = bf16[256,1408]{1,0:T(8,128)(2,1)S(1)} collective-permute-done((bf16[256,1408]{1,0:T(8,128)(2,1)}, bf16[256,1408]{1,0:T(8,128)(2,1)S(1)}, u32[]{:S(2)}, u32[]{:S(2)}) %collective-permute-start.16) | collective-permute-done | bytes 720928 | tf_op jit(solution)/shard_map/ppermute | solution.py:955
  248.3 26.1 %collective-permute-done.17.refs_1_.refs_3_ = bf16[128,1408]{1,0:T(8,128)(2,1)S(1)} collective-permute-done((bf16[128,1408]{1,0:T(8,128)(2,1)}, bf16[128,1408]{1,0:T(8,128)(2,1)S(1)}, u32[]{:S(2)}, u32[]{:S(2)}) %collective-permute-start.17) | collective-permute-done | bytes 360480 | tf_op jit(solution)/shard_map/ppermute | solution.py:955
  332.6 18.6 %collective-permute-done.21.refs_0_ = bf16[1408,384]{1,0:T(8,128)(2,1)} collective-permute-done((bf16[1408,384]{1,0:T(8,128)(2,1)}, bf16[1408,384]{1,0:T(8,128)(2,1)}, u32[]{:S(2)}, u32[]{:S(2)}) %collective-permute-start.21) | collective-permute-done | bytes 1081376 | tf_op jit(solution)/shard_map/ppermute | solution.py:974
  367.9 18.3 %collective-permute-done.28.refs_2_ = bf16[256,1408]{1,0:T(8,128)(2,1)S(1)} collective-permute-done((bf16[256,1408]{1,0:T(8,128)(2,1)}, bf16[256,1408]{1,0:T(8,128)(2,1)S(1)}, u32[]{:S(2)}, u32[]{:S(2)}) %collective-permute-start.28) | collective-permute-done | bytes 720928 | tf_op jit(solution)/shard_map/ppermute | solution.py:955
  402.6 18.5 %self_forward_kernel.3 = (bf16[1024,1408]{1,0:T(8,128)(2,1)}, bf16[1024,1152]{1,0:T(8,128)(2,1)}, bf16[256,352]{1,0:T(8,128)(2,1)}, bf16[256,352]{1,0:T(8,128)(2...) custom-call(bf16[256,1408]{1,0:T(8,128)(2,1)} %get-tuple-element.237.refs_0_, bf16[256,1408]{1,0:T(8,128)(2,1)} %copy-done.79, ...), custom_call_target="tpu_custom_call" | custom-call | flops 24000 | bytes 1000 | tf_op jit(solution)/shard_map/self_forward_kernel/pallas_call | solution.py:50
  431.3 20.9 %collective-permute-done.32.refs_2_.refs_3_ = bf16[256,352]{1,0:T(8,128)(2,1)S(1)} collective-permute-done((bf16[256,352]{1,0:T(8,128)(2,1)S(1)}, bf16[256,352]{1,0:T(8,128)(2,1)S(1)}, u32[]{:S(2)}, u32[]{:S(2)}) %collective-permute-start.32) | collective-permute-done | bytes 180256 | tf_op jit(solution)/shard_map/ppermute | solution.py:955
  458.9 21.3 %middle_forward_kernel.3 = (bf16[256,1408]{1,0:T(8,128)(2,1)}, f32[256,1408]{1,0:T(8,128)}, bf16[256,1408]{1,0:T(8,128)(2,1)}, bf16[4,256,352]{2,1,0:T(8,128)(2,...) custom-call(s32[10]{0:T(128)} %stack.83.refs_0_.scalars_ref, ...), custom_call_target="tpu_custom_call" | custom-call | flops 23000 | bytes 1000 | tf_op jit(solution)/shard_map/middle_forward_kernel/pallas_call | solution.py:50
  537.3 20.5 %mlp_backward_kernel.2 = (bf16[1024,1408]{1,0:T(8,128)(2,1)}, bf16[1024,1536]{1,0:T(8,128)(2,1)}, f32[256,1408]{1,0:T(8,128)}, bf16[256,1408]{1,0:T(8,128)(2,1)}...) custom-call(bf16[1024,1408]{1,0:T(8,128)(2,1)} %stack_kernel.1.refs_0_, ...), custom_call_target="tpu_custom_call" | custom-call | flops 22000 | bytes 1000 | tf_op jit(solution)/shard_map/mlp_backward_kernel/pallas_call | solution.py:50
  591.0 27.9 %middle_backward_kernel.2 = (f32[256,1408]{1,0:T(8,128)}, bf16[4,256,352]{2,1,0:T(8,128)(2,1)}, bf16[4,256,352]{2,1,0:T(8,128)(2,1)}, bf16[4,256,352]{2,1,0:T(8,...) custom-call(s32[10]{0:T(128)} %stack.83.refs_0_.scalars_ref, ...), custom_call_target="tpu_custom_call" | custom-call | flops 37000 | bytes 1000 | tf_op jit(solution)/shard_map/middle_backward_kernel/pallas_call | solution.py:50
  647.7 28.8 %self_backward_kernel.2 = (bf16[1024,1152]{1,0:T(8,128)(2,1)}, f32[256,1408]{1,0:T(8,128)}, bf16[256,1408]{1,0:T(8,128)(2,1)}, bf16[256,1408]{1,0:T(8,128)(2,1)}...) custom-call(bf16[1024,1152]{1,0:T(8,128)(2,1)} %get-tuple-element.260.refs_0_, ...), custom_call_target="tpu_custom_call" | custom-call | flops 32000 | bytes 1000 | tf_op jit(solution)/shard_map/self_backward_kernel/pallas_call | solution.py:50
  782.0 29.9 %collective-permute-done.63.refs_4_.refs_10_ = bf16[128,1408]{1,0:T(8,128)(2,1)S(1)} collective-permute-done((bf16[128,1408]{1,0:T(8,128)(2,1)S(1)}, bf16[128,1408]{1,0:T(8,128)(2,1)S(1)}, u32[]{:S(2)}, u32[]{:S(2)}) %collective-permute-start.63) | collective-permute-done | bytes 360480 | tf_op jit(solution)/shard_map/ppermute | solution.py:955
  812.8 20.2 %mlp_backward_kernel.3 = (bf16[1024,1408]{1,0:T(8,128)(2,1)}, bf16[1024,1536]{1,0:T(8,128)(2,1)}, f32[256,1408]{1,0:T(8,128)}, bf16[256,1408]{1,0:T(8,128)(2,1)}...) custom-call(bf16[256,1408]{1,0:T(8,128)(2,1)} %get-tuple-element.297.refs_0_, ...), custom_call_target="tpu_custom_call" | custom-call | flops 22000 | bytes 1000 | tf_op jit(solution)/shard_map/mlp_backward_kernel/pallas_call | solution.py:50
  873.2 15.2 %collective-permute-done.74.refs_1_.refs_14_ = bf16[128,1408]{1,0:T(8,128)(2,1)S(1)} collective-permute-done((bf16[128,1408]{1,0:T(8,128)(2,1)}, bf16[128,1408]{1,0:T(8,128)(2,1)S(1)}, u32[]{:S(2)}, u32[]{:S(2)}) %collective-permute-start.74) | collective-permute-done | bytes 360480 | tf_op jit(solution)/shard_map/ppermute | solution.py:955
  889.2 27.8 %middle_backward_kernel.3 = (f32[256,1408]{1,0:T(8,128)}, bf16[4,256,352]{2,1,0:T(8,128)(2,1)}, bf16[4,256,352]{2,1,0:T(8,128)(2,1)}, bf16[4,256,352]{2,1,0:T(8,...) custom-call(s32[10]{0:T(128)} %stack.83.refs_0_.scalars_ref, ...), custom_call_target="tpu_custom_call" | custom-call | flops 37000 | bytes 1000 | tf_op jit(solution)/shard_map/middle_backward_kernel/pallas_call | solution.py:50
  937.0 31.4 %collective-permute-done.77.refs_3_.refs_4_ = bf16[256,352]{1,0:T(8,128)(2,1)S(1)} collective-permute-done((bf16[256,352]{1,0:T(8,128)(2,1)S(1)}, bf16[256,352]{1,0:T(8,128)(2,1)S(1)}, u32[]{:S(2)}, u32[]{:S(2)}) %collective-permute-start.77) | collective-permute-done | bytes 180256 | tf_op jit(solution)/shard_map/ppermute | solution.py:955
  972.7 28.8 %self_backward_kernel.3 = (bf16[1024,1152]{1,0:T(8,128)(2,1)}, f32[256,1408]{1,0:T(8,128)}, bf16[256,1408]{1,0:T(8,128)(2,1)}, bf16[256,1408]{1,0:T(8,128)(2,1)}...) custom-call(bf16[1024,1152]{1,0:T(8,128)(2,1)} %get-tuple-element.292.refs_0_, ...), custom_call_target="tpu_custom_call" | custom-call | flops 32000 | bytes 1000 | tf_op jit(solution)/shard_map/self_backward_kernel/pallas_call | solution.py:50
  1054.8 42.5 %collective-permute-done.89.refs_3_.refs_2_.refs_4_ = bf16[128,1408]{1,0:T(8,128)(2,1)S(1)} collective-permute-done((bf16[128,1408]{1,0:T(8,128)(2,1)S(1)}, bf16[128,1408]{1,0:T(8,128)(2,1)S(1)}, u32[]{:S(2)}, u32[]{:S(2)}) %collective-permute-start.89) | collective-permute-done | bytes 360480 | tf_op jit(solution)/shard_map/ppermute | solution.py:955
  1118.4 24.8 %collective-permute-done.120.refs_0_ = bf16[1408,384]{1,0:T(8,128)(2,1)S(1)} collective-permute-done((bf16[1408,384]{1,0:T(8,128)(2,1)}, bf16[1408,384]{1,0:T(8,128)(2,1)S(1)}, u32[]{:S(2)}, u32[]{:S(2)}) %collective-permute-start.120) | collective-permute-done | bytes 1081376 | tf_op jit(solution)/shard_map/ppermute | solution.py:974
  1238.4 30.0 %collective-permute-done.100 = f32[10,1408]{1,0:T(8,128)S(1)} collective-permute-done((f32[10,1408]{1,0:T(8,128)S(1)}, f32[10,1408]{1,0:T(8,128)S(1)}, u32[]{:S(2)}, u32[]{:S(2)}) %collective-permute-start.100) | collective-permute-done | bytes 56352 | tf_op jit(solution)/shard_map/ppermute | solution.py:955
  1339.6 19.1 %collective-permute-done.124.refs_2_ = bf16[352,384]{1,0:T(8,128)(2,1)S(1)} collective-permute-done((bf16[352,384]{1,0:T(8,128)(2,1)}, bf16[352,384]{1,0:T(8,128)(2,1)S(1)}, u32[]{:S(2)}, u32[]{:S(2)}) %collective-permute-start.124) | collective-permute-done | bytes 270368 | tf_op jit(solution)/shard_map/ppermute | solution.py:955
  (843 shorter events, 812.8 us)
Async XLA Ops:
  9.8 103.9 %all-gather.19.cloned.1.call-start = ((), (), s32[]{:S(2)}) async-start(), calls=%async_computation.17 | async-start | bytes 3649536 | tf_op jit(solution)/shard_map/all_gather | solution.py:1085
  51.3 83.4 %all-gather.17.cloned.1.call-start = ((), (), s32[]{:S(2)}) async-start(), calls=%async_computation.16 | async-start | bytes 3649536 | tf_op jit(solution)/shard_map/all_gather | solution.py:1085
  52.0 174.4 %all-gather.13.cloned.1.call-start = ((), (), s32[]{:S(2)}) async-start(), calls=%async_computation.14 | async-start | bytes 2433024 | tf_op jit(solution)/shard_map/all_gather | solution.py:1085
  53.0 195.3 %all-gather.21.cloned.1.call-start = ((), (), s32[]{:S(2)}) async-start(), calls=%async_computation.18 | async-start | bytes 4866048 | tf_op jit(solution)/shard_map/all_gather | solution.py:1085
  58.5 229.3 %all-gather.29.cloned.1.call-start = ((), (), s32[]{:S(2)}) async-start(), calls=%async_computation.33 | async-start | bytes 4866048 | tf_op jit(solution)/shard_map/all_gather | solution.py:1085
  63.5 261.6 %all-gather.23.cloned.1.call-start = ((), (), s32[]{:S(2)}) async-start(), calls=%async_computation.19 | async-start | bytes 3649536 | tf_op jit(solution)/shard_map/all_gather | solution.py:1085
  66.7 324.2 %all-gather.25.cloned.1.call-start = ((), (), s32[]{:S(2)}) async-start(), calls=%async_computation.20 | async-start | bytes 3649536 | tf_op jit(solution)/shard_map/all_gather | solution.py:1085
  67.5 444.9 %all-gather.27.cloned.1.call-start = ((), (), s32[]{:S(2)}) async-start(), calls=%async_computation.21 | async-start | bytes 4866048 | tf_op jit(solution)/shard_map/all_gather | solution.py:1085
  158.9 378.4 %all-gather.31.cloned.1.call-start = ((), (), s32[]{:S(2)}) async-start(), calls=%async_computation.34 | async-start | bytes 4866048 | tf_op jit(solution)/shard_map/all_gather | solution.py:1085
  226.5 94.5 %collective-permute-start.9 = (bf16[2816,384]{1,0:T(8,128)(2,1)}, bf16[2816,384]{1,0:T(8,128)(2,1)S(1)}, u32[]{:S(2)}, u32[]{:S(2)}) collective-permute-start(bf16[2816,384]{1,0:T(8,128)(2,1)} %shard_map.293.refs_1_), channel_id=1, source_target_pairs={{0,8},{1,17},{2,10},{3,19},{4,12},{5,21},{6,14},{7,23},{8,0},{9,25... | collective-permute-start | bytes 6488072 | tf_op jit(solution)/shard_map/ppermute | solution.py:974
  331.6 89.5 %collective-permute-start.34 = (bf16[1408,1152]{1,0:T(8,128)(2,1)}, bf16[1408,1152]{1,0:T(8,128)(2,1)}, u32[]{:S(2)}, u32[]{:S(2)}) collective-permute-start(bf16[1408,1152]{1,0:T(8,128)(2,1)} %shard_map.298.refs_16_.refs_8_.refs_5_.refs_1_), channel_id=1, source_target_pairs={{0,8},{1,17},{2,10},{3,19},{4,12},{5,21},{6,14},{7,23},{8,0},{9,25... | collective-permute-start | bytes 9732104 | tf_op jit(solution)/shard_map/ppermute | solution.py:974
  353.2 293.4 %reduce-scatter.12.cloned.1.call-start = ((), (), s32[]{:S(2)}) async-start(), calls=%async_computation.22 | async-start | bytes 4866048 | tf_op jit(solution)/shard_map/reduce_scatter | solution.py:1089
  536.8 182.9 %reduce-scatter.14.cloned.1.call-start = ((), (), s32[]{:S(2)}) async-start(), calls=%async_computation.23 | async-start | bytes 4866048 | tf_op jit(solution)/shard_map/reduce_scatter | solution.py:1089
  577.3 311.9 %reduce-scatter.16.cloned.1.call-start = ((), (), s32[]{:S(2)}) async-start(), calls=%async_computation.24 | async-start | bytes 1769472 | tf_op jit(solution)/shard_map/reduce_scatter | solution.py:1089
  697.3 275.4 %reduce-scatter.20.cloned.1.call-start = ((), (), s32[]{:S(2)}) async-start(), calls=%async_computation.26 | async-start | bytes 3649536 | tf_op jit(solution)/shard_map/reduce_scatter | solution.py:1089
  704.9 267.8 %reduce-scatter.18.cloned.1.call-start = ((), (), s32[]{:S(2)}) async-start(), calls=%async_computation.25 | async-start | bytes 4866048 | tf_op jit(solution)/shard_map/reduce_scatter | solution.py:1089
  851.6 312.3 %reduce-scatter.30.cloned.1.call-start = ((), (), s32[]{:S(2)}) async-start(), calls=%async_computation.31 | async-start | bytes 3649536 | tf_op jit(solution)/shard_map/reduce_scatter | solution.py:1089
  859.6 64.7 %collective-permute-start.80 = (bf16[704,1152]{1,0:T(8,128)(2,1)}, bf16[704,1152]{1,0:T(8,128)(2,1)S(1)}, u32[]{:S(2)}, u32[]{:S(2)}) collective-permute-start(bf16[704,1152]{1,0:T(8,128)(2,1)} %add_convert_fusion.3), channel_id=1, source_target_pairs={{0,8},{1,17},{2,10},{3,19},{4,12},{5,21},{6,14},{7,23},{8,0},{9,25... | collective-permute-start | bytes 4866056 | tf_op jit(solution)/shard_map/ppermute | solution.py:974
  931.7 240.8 %reduce-scatter.22.cloned.1.call-start = ((), (), s32[]{:S(2)}) async-start(), calls=%async_computation.27 | async-start | bytes 4866048 | tf_op jit(solution)/shard_map/reduce_scatter | solution.py:1089
  932.3 391.1 %reduce-scatter.28.cloned.1.call-start = ((), (), s32[]{:S(2)}) async-start(), calls=%async_computation.30 | async-start | bytes 1769472 | tf_op jit(solution)/shard_map/reduce_scatter | solution.py:1089
  1024.2 299.2 %reduce-scatter.24.cloned.1.call-start = ((), (), s32[]{:S(2)}) async-start(), calls=%async_computation.28 | async-start | bytes 3649536 | tf_op jit(solution)/shard_map/reduce_scatter | solution.py:1089
  1044.2 279.3 %reduce-scatter.26.cloned.1.call-start = ((), (), s32[]{:S(2)}) async-start(), calls=%async_computation.29 | async-start | bytes 3649536 | tf_op jit(solution)/shard_map/reduce_scatter | solution.py:1089
  1163.5 170.3 %reduce-scatter.32.cloned.1.call-start = ((), (), s32[]{:S(2)}) async-start(), calls=%async_computation.32 | async-start | bytes 2433024 | tf_op jit(solution)/shard_map/reduce_scatter | solution.py:1089
  1204.3 65.8 %collective-permute-start.122 = (bf16[1408,384]{1,0:T(8,128)(2,1)}, bf16[1408,384]{1,0:T(8,128)(2,1)S(1)}, u32[]{:S(2)}, u32[]{:S(2)}) collective-permute-start(bf16[1408,384]{1,0:T(8,128)(2,1)} %add_convert_fusion.6), channel_id=1, source_target_pairs={{0,8},{1,17},{2,10},{3,19},{4,12},{5,21},{6,14},{7,23},{8,0},{9,25... | collective-permute-start | bytes 3244040 | tf_op jit(solution)/shard_map/ppermute | solution.py:974
  (286 other events, 4010.5 us)
Sparse Core Ops, SparseCore 0:
  10.2 40.9 all-gather.14
  53.5 39.1 all-gather.18
  94.8 39.8 all-gather.16
  136.2 28.4 all-gather.12
  166.7 47.9 all-gather.20
  216.8 47.1 all-gather.28
  266.2 37.8 all-gather.22
  305.7 37.9 all-gather.24
  345.3 47.3 all-gather.26
  394.1 47.1 all-gather.30
  536.9 50.0 reduce-scatter.11
  589.9 49.3 reduce-scatter.13
  697.4 32.2 reduce-scatter.15
  731.9 39.4 reduce-scatter.19
  851.8 48.7 reduce-scatter.17
  931.8 38.8 reduce-scatter.29
  973.4 50.0 reduce-scatter.21
  1025.7 32.0 reduce-scatter.27
  1060.1 40.8 reduce-scatter.23
  1163.6 39.7 reduce-scatter.25
  1275.5 40.1 reduce-scatter.31

commit v8 on v7

--- a/solution.py
+++ b/solution.py
@@ -889,7 +889,12 @@
     block_refs, refs = refs[:parts], refs[parts:]
     outs = sum(entry[3] for entry in plan)
     out_refs, stack_ref = refs[-outs - 1 : -1], refs[-1]
+    ordered = parts == 1
     for j in range(count):
+        if ordered:
+            held = stack_ref.shape[1]
+            stack_ref[j] = block_refs[0][j * held : (j + 1) * held, :]
+            continue
         owner = scalars_ref[count + j]
         if j == count - 1 and parts > count:
             cut = block_refs[j].shape[0]
@@ -927,7 +932,12 @@
         out_shape=[jax.ShapeDtypeStruct((layer_count,) + shape, F32) for shape in shapes],
         in_specs=[pl.BlockSpec(memory_space=pltpu.SMEM)] + inputs,
         out_specs=[pl.BlockSpec((1,) + shape, lambda i: (layer, 0, 0)) for shape in shapes],
-        scratch_shapes=[pltpu.VMEM((count,) + blocks[0].shape, BF16)],
+        scratch_shapes=[
+            pltpu.VMEM(
+                (count, blocks[0].shape[0] // (count if len(blocks) == 1 else 1), blocks[0].shape[1]),
+                BF16,
+            )
+        ],
         input_output_aliases={1 + len(blocks) + i: i for i in range(len(held))},
         compiler_params=pltpu.CompilerParams(vmem_limit_bytes=VMEM_LIMIT),
         cost_estimate=pl.CostEstimate(flops=8_000_000_000, bytes_accessed=1000, transcendentals=0),
@@ -1041,16 +1051,23 @@
     return [block, swap_by_core(block, 1, 2)]
 
 
-def spread_last(blocks, ready, part_ready=None):
+def spread_slice(blocks, ready):
+    if lax.axis_size("seq") != 4:
+        return blocks
+    block, first = blocks
+    if ready is not None:
+        (first,) = gate([first], ready)
+    half = block.shape[0] // 2
+    odd = lax.axis_index("fsdp") % 2
+    return [block, first, lax.dynamic_slice_in_dim(first, odd * half, half, 0)]
+
+
+def spread_last(blocks, part_ready):
     seq_count = lax.axis_size("seq")
     if seq_count != 4:
         return blocks
-    odd = lax.axis_index("fsdp") % 2
-    block, first = blocks
-    half = block.shape[0] // 2
-    if ready is not None:
-        (first,) = gate([first], ready)
-    part = swap_by_core(lax.dynamic_slice_in_dim(first, odd * half, half, 0), 2, 1)
+    block, first, part = blocks
+    part = swap_by_core(part, 2, 1)
     other = swap_core(first)
     if part_ready is not None:
         (part,) = gate([part], part_ready)
@@ -1089,7 +1106,7 @@
     return lax.psum_scatter(full.astype(BF16), "fsdp", scatter_dimension=0, tiled=True)
 
 
-def layer_forward(parts, hidden, scalars, gains, shift, pairs, weights, normed, deps):
+def layer_forward(parts, hidden, scalars, gains, shift, pairs, weights, normed, deps, hold=None):
     lead_part, square_parts, up_part = weights
     seq_count = lax.axis_size("seq")
     tok_rows, model_width = hidden.shape
@@ -1103,13 +1120,16 @@
         seq_count,
         width,
         normed,
-        (square_parts[0],) + deps,
+        (square_parts[-1],) + deps,
     )
     mixed_rel = exchange_rel(mixed)
-    square_parts = spread_last(square_parts, [mixed[0]], mixed_rel[1:])
+    square_parts = spread_last(square_parts, mixed_rel[1:])
+    held = []
+    if hold is not None:
+        held = gate([hold], [square_parts[-1]])
     self_tokens, after_self, cross_norm, queries, cross_tokens, after_cross, mlp_norm = (
         middle_forward(
-            int(normed), scalars, mixed_rel, square_parts, pairs, hidden, gains, head_size
+            int(normed), scalars, mixed_rel, square_parts, pairs, hidden, gains, head_size, held
         )
     )
     mlp_parts = gather_parts(mlp_norm)
@@ -1127,7 +1147,7 @@
         up_rows,
         activated,
     )
-    return (saved, square_parts, mlp_parts, mixed_rel)
+    return (saved, square_parts, mlp_parts, held)
 
 
 def unspread_first(blocks, ready):
@@ -1254,10 +1274,11 @@
     )
     square_first, lead_first = gather_fsdp(square_shard), gather_fsdp(qkv_shard)
     up_first, down_first = gather_rest(0, *rest_stacks)
-    spread_squares = spread_first(gate([square_first], [shifts])[0])
+    spread_squares = spread_slice(spread_first(gate([square_first], [cond_part])[0]), [shifts])
     (lead_first,) = gate([lead_first], [shifts])
     pairs_first, pairs_second = pairs_all, pairs_all
-    saved_first, squares_first, mlp_parts, mixed_rel = layer_forward(
+    skip_matrix = gather_fsdp(own_part(skip_weight, 1, padded_width(width)))
+    saved_first, squares_first, mlp_parts, (skip_matrix,) = layer_forward(
         latent_parts,
         latents[0],
         scalars,
@@ -1266,18 +1287,17 @@
         pairs_first,
         (lead_first, spread_squares, up_first),
         False,
-        (),
+        tuple(pairs_all[-2:]),
+        skip_matrix,
     )
     own, pieces = mlp_down(saved_first[10], down_first, seq_count)
-    terms = scatter_last(own, scatter_first(pieces))
-
-    (skip_matrix,) = gate(
-        [gather_fsdp(own_part(skip_weight, 1, padded_width(width)))], mixed_rel[1:]
-    )
-    skip_parts = spread_last(spread_first(skip_matrix), mlp_parts[-2:], [own])
+    first = scatter_first(pieces)
+    terms = scatter_last(own, first)
+
+    skip_parts = spread_last(spread_slice(spread_first(skip_matrix), mlp_parts[-2:]), [own])
     square_second = gather_fsdp(squares_own(1, *square_stacks))
     lead_second = gather_fsdp(qkv_own(1, qkv_weight))
-    (square_second,) = gate([square_second], terms[-2:])
+    (square_second,) = gate([square_second], first[:2])
     squares_second = spread_first(square_second)
     first_out, joined_norm, skip_out, second_norm = skip_forward(
         scalars,
@@ -1293,8 +1313,10 @@
 
     up_second, down_second = gather_rest(1, *rest_stacks)
     out_hops = gather_first(gate([cotangent[0]], [skip_out])[0])
+    second_parts = gather_parts(second_norm)
+    squares_second = spread_slice(squares_second, second_parts[1:3])
     saved_second, squares_second, mlp_parts, _ = layer_forward(
-        gather_parts(second_norm),
+        second_parts,
         skip_out,
         scalars,
         gains[1],
@@ -1451,18 +1473,19 @@
         )
 
     early, _ = entries((qkv_shard, qkv_shard, kv_shard, up_shard, down_shard))
+    early_all = lax.all_gather(
+        pack([entry[0] for entry in early], first_hops[1:]), "seq", axis=0, tiled=True
+    )
 
     def first_middle(grad_up_rows, terms):
-        held["up"], held["terms"] = grad_up_rows, terms
-        held["packed"] = pack([entry[0] for entry in early], (grad_up_rows,))
-        held["early"] = gather_first(gate([held["packed"]], terms[-2:])[0])
-        return (held["early"][0], kv_shard)
+        del grad_up_rows, terms
+        return (kv_shard,)
 
     def first_self(ready):
         if not fours:
             return (qkv_shard,)
-        held["joined"] = unspread_last(scalars, unspread_next(squares, held["hops"]), [ready])
-        return (qkv_shard, held["joined"], *held["early"][1:])
+        held["squares"] = unspread_next(squares, held["hops"])
+        return (qkv_shard, held["squares"][1])
 
     (
         terms,
@@ -1481,7 +1504,7 @@
         (lead_first, squares_first, pairs_first, up_first, down_first),
         None,
         (
-            (skip_outer[0], *own_terms[-2:]) + (tuple(squares[3]) if fours else ()),
+            (skip_outer[0],) + (tuple(squares[3]) if fours else ()),
             first_middle,
             first_self,
             squares[1] if fours else (),
@@ -1489,7 +1512,7 @@
     )
     if fours:
         outer_done = [first_squares[1]]
-        joined = held["joined"]
+        joined = unspread_last(scalars, held["squares"], outer_done)
         first_squares = unspread_first(first_squares, outer_done)
         skip_first = unspread_first(skip_outer, first_squares[3])
         first_squares = unspread_next(first_squares, terms[-2:])
@@ -1507,7 +1530,7 @@
     )
     first_hops = gather_first(pack([entry[0] for entry in early], outer_done))
     grad_latents, vectors = open_backward(
-        terms, latents[0], gains[0], grad_after_self, (grad_qkv, first_joined, *first_hops[1:])
+        terms, latents[0], gains[0], grad_after_self, (grad_qkv, early_all)
     )
     vectors_first = jnp.concatenate([vectors, gain_grads], axis=0)
     first_layer = (
@@ -1520,7 +1543,7 @@
 
     early_done = settle(
         scalars,
-        gather_last(held["early"], outer_done),
+        [early_all],
         plan_of(early),
         1,
         2,

time: 1400 us -> 1380 us (0.986)
  waiting for transfers between devices: 614 us -> 591 us
    ppermute x94 -> x90, waiting for transfers between devices: 501 us -> 410 us  [swap_seq(): return lax.ppermute(block, 'seq', [(i, i ^ bits) for i in range(seq_count)])]
    reduce_scatter x11, waiting for transfers between devices: 0.14 us -> 44.4 us  [scatter_fsdp(): lax.psum_scatter(full.astype(BF16), 'fsdp', scatter_dimension=0, tiled=True)]
    ppermute x15, waiting for transfers between devices: 56 us -> 77 us  [swap_by_core(): return lax.ppermute(block, ('seq', 'fsdp'), pairs)]
    ppermute x94 -> x90, starting transfers between devices: 102 us -> 107 us  [swap_seq(): return lax.ppermute(block, 'seq', [(i, i ^ bits) for i in range(seq_count)])]
    unnamed x335 -> x317, local copies, waits for them, and re-layouts: 46.4 us -> 51.6 us
  transfers between devices with their start and end apart: 149 -> 147, of which waited for: 65 -> 71; matrix products, arithmetic and copies ran while one was open for 12% -> 13% of each run, Pallas kernels for 28% -> 29%
where the time goes in v8:
time: 1380 us; the launch traced here: 1370 us
  waiting for transfers between devices  591 us (43%)
  Pallas kernels  398 us (29%)
  starting transfers between devices  136 us (10%)
  local copies, waits for them, and re-layouts  107 us (8%)
  matrix products  68.4 us (5%)
  other arithmetic  46.7 us (3%)
  between operations  16.8 us (1%)
    ppermute x90, waiting for transfers between devices, swap_seq(): return lax.ppermute(block, 'seq', [(i, i ^ bits) for i in range(seq_count)])  410 us
    pallas_call x30, Pallas kernels, call(): pl.pallas_call(run, name=getattr(kernel, 'func', kernel).__name__, out_sh...  369 us
    ppermute x90, starting transfers between devices, swap_seq(): return lax.ppermute(block, 'seq', [(i, i ^ bits) for i in range(seq_count)])  107 us
    ppermute x15, waiting for transfers between devices, swap_by_core(): return lax.ppermute(block, ('seq', 'fsdp'), pairs)  77 us
    dot_general x8, matrix products, dot_tn(): lax.dot_general(a, b, (((0,), (0,)), ((), ())), preferred_element_type=F32)  55.4 us
    unnamed x317, local copies, waits for them, and re-layouts  51.6 us
    reduce_scatter x11, waiting for transfers between devices, scatter_fsdp(): lax.psum_scatter(full.astype(BF16), 'fsdp', scatter_dimension=0, tiled=True)  44.4 us
    convert_element_type x23, other arithmetic, add_bf16(): return total.astype(BF16)  37.9 us
  transfers between devices with their start and end apart: 147, of which 71 were waited for; matrix products, arithmetic and copies ran while one was open for 13% of the time, Pallas kernels for 29%

profile of v8, /device:TPU:0, one launch (start us, length us, event | category | flops | bytes accessed | tf_op | source)
XLA Modules:
  0.0 1373.2 jit_solution(1432642861397632106)
XLA Ops:
  104.7 49.7 %collective-permute-done.5.refs_1_.refs_11_.refs_7_ = bf16[352,1536]{1,0:T(8,128)(2,1)S(1)} collective-permute-done((bf16[352,1536]{1,0:T(8,128)(2,1)}, bf16[352,1536]{1,0:T(8,128)(2,1)S(1)}, u32[]{:S(2)}, u32[]{:S(2)}) %collective-permute-start.5) | collective-permute-done | bytes 1081376 | tf_op jit(solution)/shard_map/ppermute | solution.py:965
  187.2 15.0 %collective-permute-done.9.refs_10_.refs_14_ = bf16[176,1536]{1,0:T(8,128)(2,1)S(1)} collective-permute-done((bf16[176,1536]{1,0:T(8,128)(2,1)}, bf16[176,1536]{1,0:T(8,128)(2,1)S(1)}, u32[]{:S(2)}, u32[]{:S(2)}) %collective-permute-start.9) | collective-permute-done | bytes 540704 | tf_op jit(solution)/shard_map/ppermute | solution.py:965
  203.0 18.5 %self_forward_kernel.2 = (bf16[1024,1408]{1,0:T(8,128)(2,1)}, bf16[1024,1152]{1,0:T(8,128)(2,1)}, bf16[256,352]{1,0:T(8,128)(2,1)}, bf16[256,352]{1,0:T(8,128)(2...) custom-call(bf16[256,1408]{1,0:T(8,128)(2,1)} %bitcast.146, bf16[256,1408]{1,0:T(8,128)(2,1)} %copy-done.80, ...), custom_call_target="tpu_custom_call" | custom-call | flops 24000 | bytes 1000 | tf_op jit(solution)/shard_map/self_forward_kernel/pallas_call | solution.py:50
  242.2 20.9 %middle_forward_kernel.2 = (bf16[256,1408]{1,0:T(8,128)(2,1)}, f32[256,1408]{1,0:T(8,128)}, bf16[256,1408]{1,0:T(8,128)(2,1)}, bf16[4,256,352]{2,1,0:T(8,128)(2,...) custom-call(s32[10]{0:T(128)} %stack.83.refs_0_.scalars_ref, ...), custom_call_target="tpu_custom_call" | custom-call | flops 23000 | bytes 1000 | tf_op jit(solution)/shard_map/middle_forward_kernel/pallas_call | solution.py:50
  265.5 16.1 %collective-permute-done.16.refs_2_ = bf16[256,1408]{1,0:T(8,128)(2,1)S(1)} collective-permute-done((bf16[256,1408]{1,0:T(8,128)(2,1)}, bf16[256,1408]{1,0:T(8,128)(2,1)S(1)}, u32[]{:S(2)}, u32[]{:S(2)}) %collective-permute-start.16) | collective-permute-done | bytes 720928 | tf_op jit(solution)/shard_map/ppermute | solution.py:965
  319.6 13.5 collective-permute-done.23.refs_1_.refs_7_
  343.2 23.3 %collective-permute-done.21.refs_0_ = bf16[1408,384]{1,0:T(8,128)(2,1)} collective-permute-done((bf16[1408,384]{1,0:T(8,128)(2,1)}, bf16[1408,384]{1,0:T(8,128)(2,1)}, u32[]{:S(2)}, u32[]{:S(2)}) %collective-permute-start.21) | collective-permute-done | bytes 1081376 | tf_op jit(solution)/shard_map/ppermute | solution.py:984
  437.9 14.8 %collective-permute-done.30.refs_4_ = bf16[128,1408]{1,0:T(8,128)(2,1)S(1)} collective-permute-done((bf16[128,1408]{1,0:T(8,128)(2,1)S(1)}, bf16[128,1408]{1,0:T(8,128)(2,1)S(1)}, u32[]{:S(2)}, u32[]{:S(2)}) %collective-permute-start.30) | collective-permute-done | bytes 360480 | tf_op jit(solution)/shard_map/ppermute | solution.py:965
  453.5 18.4 %self_forward_kernel.3 = (bf16[1024,1408]{1,0:T(8,128)(2,1)}, bf16[1024,1152]{1,0:T(8,128)(2,1)}, bf16[256,352]{1,0:T(8,128)(2,1)}, bf16[256,352]{1,0:T(8,128)(2...) custom-call(bf16[256,1408]{1,0:T(8,128)(2,1)} %get-tuple-element.235.refs_0_, bf16[256,1408]{1,0:T(8,128)(2,1)} %copy-done.59, ...), custom_call_target="tpu_custom_call" | custom-call | flops 24000 | bytes 1000 | tf_op jit(solution)/shard_map/self_forward_kernel/pallas_call | solution.py:50
  487.9 21.3 %middle_forward_kernel.3 = (bf16[256,1408]{1,0:T(8,128)(2,1)}, f32[256,1408]{1,0:T(8,128)}, bf16[256,1408]{1,0:T(8,128)(2,1)}, bf16[4,256,352]{2,1,0:T(8,128)(2,...) custom-call(s32[10]{0:T(128)} %stack.83.refs_0_.scalars_ref, ...), custom_call_target="tpu_custom_call" | custom-call | flops 23000 | bytes 1000 | tf_op jit(solution)/shard_map/middle_forward_kernel/pallas_call | solution.py:50
  567.1 20.5 %mlp_backward_kernel.2 = (bf16[1024,1408]{1,0:T(8,128)(2,1)}, bf16[1024,1536]{1,0:T(8,128)(2,1)}, f32[256,1408]{1,0:T(8,128)}, bf16[256,1408]{1,0:T(8,128)(2,1)}...) custom-call(bf16[1024,1408]{1,0:T(8,128)(2,1)} %stack_kernel.1.refs_0_, ...), custom_call_target="tpu_custom_call" | custom-call | flops 22000 | bytes 1000 | tf_op jit(solution)/shard_map/mlp_backward_kernel/pallas_call | solution.py:50
  620.8 27.9 %middle_backward_kernel.2 = (f32[256,1408]{1,0:T(8,128)}, bf16[4,256,352]{2,1,0:T(8,128)(2,1)}, bf16[4,256,352]{2,1,0:T(8,128)(2,1)}, bf16[4,256,352]{2,1,0:T(8,...) custom-call(s32[10]{0:T(128)} %stack.83.refs_0_.scalars_ref, ...), custom_call_target="tpu_custom_call" | custom-call | flops 37000 | bytes 1000 | tf_op jit(solution)/shard_map/middle_backward_kernel/pallas_call | solution.py:50
  677.6 28.8 %self_backward_kernel.2 = (bf16[1024,1152]{1,0:T(8,128)(2,1)}, f32[256,1408]{1,0:T(8,128)}, bf16[256,1408]{1,0:T(8,128)(2,1)}, bf16[256,1408]{1,0:T(8,128)(2,1)}...) custom-call(bf16[1024,1152]{1,0:T(8,128)(2,1)} %get-tuple-element.258.refs_0_, ...), custom_call_target="tpu_custom_call" | custom-call | flops 32000 | bytes 1000 | tf_op jit(solution)/shard_map/self_backward_kernel/pallas_call | solution.py:50
  759.1 14.0 %skip_backward_kernel.1 = (bf16[4,256,352]{2,1,0:T(8,128)(2,1)}, f32[256,1408]{1,0:T(8,128)}, f32[256,1408]{1,0:T(8,128)}, f32[4,1408]{1,0:T(4,128)}, bf16[256,1408]{1,0:T(8,128)(2,1)}) custom-call(s32[10]{0:T(128)} %stack.83.refs_0_.scalars_ref, bf16[2816,384]{1,0:T(8,128)(2,1)} %shard_map.295.refs_17_.refs_1_, bf16[2816,384]{1,0:T(8,128)(2,1)} %shard_map.296.refs_2_, ...), custom_call_target="tpu_custom_call" | custom-call | flops 15000 | bytes 1000 | tf_op jit(solution)/shard_map/skip_backward_kernel/pallas_call | solution.py:50
  775.5 14.2 %collective-permute-done.65.refs_4_.refs_2_.refs_3_ = bf16[256,1408]{1,0:T(8,128)(2,1)S(1)} collective-permute-done((bf16[256,1408]{1,0:T(8,128)(2,1)}, bf16[256,1408]{1,0:T(8,128)(2,1)S(1)}, u32[]{:S(2)}, u32[]{:S(2)}) %collective-permute-start.65) | collective-permute-done | bytes 720928 | tf_op jit(solution)/shard_map/ppermute | solution.py:965
  807.1 20.2 %mlp_backward_kernel.3 = (bf16[1024,1408]{1,0:T(8,128)(2,1)}, bf16[1024,1536]{1,0:T(8,128)(2,1)}, f32[256,1408]{1,0:T(8,128)}, bf16[256,1408]{1,0:T(8,128)(2,1)}...) custom-call(bf16[256,1408]{1,0:T(8,128)(2,1)} %get-tuple-element.295.refs_0_, ...), custom_call_target="tpu_custom_call" | custom-call | flops 22000 | bytes 1000 | tf_op jit(solution)/shard_map/mlp_backward_kernel/pallas_call | solution.py:50
  885.6 15.4 %collective-permute-done.74.refs_14_ = bf16[128,1408]{1,0:T(8,128)(2,1)S(1)} collective-permute-done((bf16[128,1408]{1,0:T(8,128)(2,1)}, bf16[128,1408]{1,0:T(8,128)(2,1)S(1)}, u32[]{:S(2)}, u32[]{:S(2)}) %collective-permute-start.74) | collective-permute-done | bytes 360480 | tf_op jit(solution)/shard_map/ppermute | solution.py:965
  901.7 28.5 %middle_backward_kernel.3 = (f32[256,1408]{1,0:T(8,128)}, bf16[4,256,352]{2,1,0:T(8,128)(2,1)}, bf16[4,256,352]{2,1,0:T(8,128)(2,1)}, bf16[4,256,352]{2,1,0:T(8,...) custom-call(s32[10]{0:T(128)} %stack.83.refs_0_.scalars_ref, ...), custom_call_target="tpu_custom_call" | custom-call | flops 37000 | bytes 1000 | tf_op jit(solution)/shard_map/middle_backward_kernel/pallas_call | solution.py:50
  957.0 28.7 %self_backward_kernel.3 = (bf16[1024,1152]{1,0:T(8,128)(2,1)}, f32[256,1408]{1,0:T(8,128)}, bf16[256,1408]{1,0:T(8,128)(2,1)}, bf16[256,1408]{1,0:T(8,128)(2,1)}...) custom-call(bf16[1024,1152]{1,0:T(8,128)(2,1)} %get-tuple-element.290.refs_0_, ...), custom_call_target="tpu_custom_call" | custom-call | flops 32000 | bytes 1000 | tf_op jit(solution)/shard_map/self_backward_kernel/pallas_call | solution.py:50
  1025.6 41.4 %collective-permute-done.87.refs_4_.refs_3_.refs_2_ = bf16[128,1408]{1,0:T(8,128)(2,1)S(1)} collective-permute-done((bf16[128,1408]{1,0:T(8,128)(2,1)S(1)}, bf16[128,1408]{1,0:T(8,128)(2,1)S(1)}, u32[]{:S(2)}, u32[]{:S(2)}) %collective-permute-start.87) | collective-permute-done | bytes 360480 | tf_op jit(solution)/shard_map/ppermute | solution.py:965
  1088.0 25.5 %collective-permute-done.116.refs_0_ = bf16[1408,384]{1,0:T(8,128)(2,1)S(1)} collective-permute-done((bf16[1408,384]{1,0:T(8,128)(2,1)}, bf16[1408,384]{1,0:T(8,128)(2,1)S(1)}, u32[]{:S(2)}, u32[]{:S(2)}) %collective-permute-start.116) | collective-permute-done | bytes 1081376 | tf_op jit(solution)/shard_map/ppermute | solution.py:984
  1114.5 12.9 collective-permute-done.117.refs_1_
  1211.7 16.7 %collective-permute-done.94 = f32[4,10,1408]{2,1,0:T(8,128)S(1)} collective-permute-done((f32[4,10,1408]{2,1,0:T(8,128)S(1)}, f32[4,10,1408]{2,1,0:T(8,128)S(1)}, u32[]{:S(2)}, u32[]{:S(2)}) %collective-permute-start.94) | collective-permute-done | bytes 225312 | tf_op jit(solution)/shard_map/ppermute | solution.py:970
  1271.1 42.5 %reduce-scatter.24.cloned.1.call-done.refs_1_ = bf16[176,1152]{1,0:T(8,128)(2,1)} async-done(((bf16[1408,1152]{1,0:T(8,128)(2,1)}), bf16[176,1152]{1,0:T(8,128)(2,1)}) %reduce-scatter.24.cloned.1.call-update) | async-done | bytes 405520 | tf_op jit(solution)/shard_map/reduce_scatter | solution.py:1106
  (819 shorter events, 807.5 us)
Async XLA Ops:
  9.8 82.8 %all-gather.18.cloned.1.call-start = ((), (), s32[]{:S(2)}) async-start(), calls=%async_computation.16 | async-start | bytes 3649536 | tf_op jit(solution)/shard_map/all_gather | solution.py:1102
  51.3 124.7 %all-gather.20.cloned.1.call-start = ((), (), s32[]{:S(2)}) async-start(), calls=%async_computation.17 | async-start | bytes 3649536 | tf_op jit(solution)/shard_map/all_gather | solution.py:1102
  52.0 182.9 %all-gather.14.cloned.1.call-start = ((), (), s32[]{:S(2)}) async-start(), calls=%async_computation.14 | async-start | bytes 2433024 | tf_op jit(solution)/shard_map/all_gather | solution.py:1102
  53.0 232.8 %all-gather.22.cloned.1.call-start = ((), (), s32[]{:S(2)}) async-start(), calls=%async_computation.18 | async-start | bytes 4866048 | tf_op jit(solution)/shard_map/all_gather | solution.py:1102
  58.5 248.9 %all-gather.32.cloned.1.call-start = ((), (), s32[]{:S(2)}) async-start(), calls=%async_computation.34 | async-start | bytes 4866048 | tf_op jit(solution)/shard_map/all_gather | solution.py:1102
  63.5 256.1 %all-gather.24.cloned.1.call-start = ((), (), s32[]{:S(2)}) async-start(), calls=%async_computation.19 | async-start | bytes 3649536 | tf_op jit(solution)/shard_map/all_gather | solution.py:1102
  66.6 360.9 %all-gather.26.cloned.1.call-start = ((), (), s32[]{:S(2)}) async-start(), calls=%async_computation.20 | async-start | bytes 3649536 | tf_op jit(solution)/shard_map/all_gather | solution.py:1102
  67.5 474.9 %all-gather.28.cloned.1.call-start = ((), (), s32[]{:S(2)}) async-start(), calls=%async_computation.21 | async-start | bytes 4866048 | tf_op jit(solution)/shard_map/all_gather | solution.py:1102
  159.8 407.3 %all-gather.34.cloned.1.call-start = ((), (), s32[]{:S(2)}) async-start(), calls=%async_computation.35 | async-start | bytes 4866048 | tf_op jit(solution)/shard_map/all_gather | solution.py:1102
  239.8 95.7 %collective-permute-start.14 = (bf16[2816,384]{1,0:T(8,128)(2,1)}, bf16[2816,384]{1,0:T(8,128)(2,1)S(1)}, u32[]{:S(2)}, u32[]{:S(2)}) collective-permute-start(bf16[2816,384]{1,0:T(8,128)(2,1)} %shard_map.295.refs_17_.refs_1_), channel_id=1, source_target_pairs={{0,8},{1,17},{2,10},{3,19},{4,12},{5,21},{6,14},{7,23},{8,0},{9,25... | collective-permute-start | bytes 6488072 | tf_op jit(solution)/shard_map/ppermute | solution.py:984
  334.4 85.9 %collective-permute-start.31 = (bf16[1408,1152]{1,0:T(8,128)(2,1)}, bf16[1408,1152]{1,0:T(8,128)(2,1)}, u32[]{:S(2)}, u32[]{:S(2)}) collective-permute-start(bf16[1408,1152]{1,0:T(8,128)(2,1)} %shard_map.298.refs_16_.refs_5_.refs_1_), channel_id=1, source_target_pairs={{0,8},{1,17},{2,10},{3,19},{4,12},{5,21},{6,14},{7,23},{8,0},{9,25... | collective-permute-start | bytes 9732104 | tf_op jit(solution)/shard_map/ppermute | solution.py:984
  343.1 333.4 %reduce-scatter.12.cloned.1.call-start = ((), (), s32[]{:S(2)}) async-start(), calls=%async_computation.22 | async-start | bytes 4866048 | tf_op jit(solution)/shard_map/reduce_scatter | solution.py:1106
  566.6 183.6 %reduce-scatter.14.cloned.1.call-start = ((), (), s32[]{:S(2)}) async-start(), calls=%async_computation.23 | async-start | bytes 4866048 | tf_op jit(solution)/shard_map/reduce_scatter | solution.py:1106
  606.7 271.1 %reduce-scatter.16.cloned.1.call-start = ((), (), s32[]{:S(2)}) async-start(), calls=%async_computation.24 | async-start | bytes 1769472 | tf_op jit(solution)/shard_map/reduce_scatter | solution.py:1106
  726.6 229.2 %reduce-scatter.20.cloned.1.call-start = ((), (), s32[]{:S(2)}) async-start(), calls=%async_computation.26 | async-start | bytes 3649536 | tf_op jit(solution)/shard_map/reduce_scatter | solution.py:1106
  734.2 221.7 %reduce-scatter.18.cloned.1.call-start = ((), (), s32[]{:S(2)}) async-start(), calls=%async_computation.25 | async-start | bytes 4866048 | tf_op jit(solution)/shard_map/reduce_scatter | solution.py:1106
  851.4 318.4 %all-gather.30.cloned.1.call-start = ((), (), s32[]{:S(2)}) async-start(), calls=%async_computation.27 | async-start | bytes 5652480 | tf_op jit(solution)/shard_map/all_gather | solution.py:1476
  853.7 344.3 %reduce-scatter.30.cloned.1.call-start = ((), (), s32[]{:S(2)}) async-start(), calls=%async_computation.32 | async-start | bytes 4866048 | tf_op jit(solution)/shard_map/reduce_scatter | solution.py:1106
  863.8 364.9 %reduce-scatter.28.cloned.1.call-start = ((), (), s32[]{:S(2)}) async-start(), calls=%async_computation.31 | async-start | bytes 3649536 | tf_op jit(solution)/shard_map/reduce_scatter | solution.py:1106
  872.1 83.7 %collective-permute-start.80 = (bf16[704,1152]{1,0:T(8,128)(2,1)}, bf16[704,1152]{1,0:T(8,128)(2,1)S(1)}, u32[]{:S(2)}, u32[]{:S(2)}) collective-permute-start(bf16[704,1152]{1,0:T(8,128)(2,1)} %add_convert_fusion.3), channel_id=1, source_target_pairs={{0,8},{1,17},{2,10},{3,19},{4,12},{5,21},{6,14},{7,23},{8,0},{9,25... | collective-permute-start | bytes 4866056 | tf_op jit(solution)/shard_map/ppermute | solution.py:984
  1013.8 239.7 %reduce-scatter.32.cloned.1.call-start = ((), (), s32[]{:S(2)}) async-start(), calls=%async_computation.33 | async-start | bytes 2433024 | tf_op jit(solution)/shard_map/reduce_scatter | solution.py:1106
  1151.4 117.9 %reduce-scatter.26.cloned.1.call-start = ((), (), s32[]{:S(2)}) async-start(), calls=%async_computation.30 | async-start | bytes 1769472 | tf_op jit(solution)/shard_map/reduce_scatter | solution.py:1106
  1156.6 114.5 %reduce-scatter.22.cloned.1.call-start = ((), (), s32[]{:S(2)}) async-start(), calls=%async_computation.28 | async-start | bytes 3649536 | tf_op jit(solution)/shard_map/reduce_scatter | solution.py:1106
  1164.2 149.4 %reduce-scatter.24.cloned.1.call-start = ((), (), s32[]{:S(2)}) async-start(), calls=%async_computation.29 | async-start | bytes 3649536 | tf_op jit(solution)/shard_map/reduce_scatter | solution.py:1106
  (278 other events, 4029.2 us)
Sparse Core Ops, SparseCore 0:
  10.2 40.9 all-gather.15
  53.5 39.0 all-gather.17
  94.8 37.8 all-gather.19
  134.2 28.4 all-gather.13
  164.8 47.9 all-gather.21
  214.9 47.1 all-gather.31
  264.3 37.8 all-gather.23
  303.8 37.9 all-gather.25
  343.5 49.2 all-gather.27
  394.3 47.1 all-gather.33
  566.7 49.2 reduce-scatter.11
  618.9 49.3 reduce-scatter.13
  726.7 32.0 reduce-scatter.15
  761.0 39.6 reduce-scatter.19
  851.5 49.3 reduce-scatter.17
  903.1 72.8 all-gather.29
  978.1 61.2 reduce-scatter.29
  1041.7 39.4 reduce-scatter.27
  1151.5 32.6 reduce-scatter.31
  1186.9 37.2 reduce-scatter.25
  1227.0 44.0 reduce-scatter.21
  1273.5 40.0 reduce-scatter.23

commit v9 on v8

--- a/solution.py
+++ b/solution.py
@@ -417,9 +417,9 @@
 
     def back(branch_ref, group):
         columns = slice(group * stride, group * stride + width)
-        total = dot_nt(branch_ref[0], matrices[0][:, columns])
+        total = dot_nt(branch_ref[order[0]], matrices[0][:, columns])
         for i in range(1, count):
-            total = total + dot_nt(branch_ref[i], matrices[i][:, columns])
+            total = total + dot_nt(branch_ref[order[i]], matrices[i][:, columns])
         return total
 
     def divide(values):
@@ -431,10 +431,9 @@
     )
     gain_ref[1:2, :] = grad_gain
     wide_ref[...] = grad + grad_out_ref[...].astype(F32)
+    cross_branch_ref[...] = wide_ref[...].astype(BF16)
     divide(wide_ref[...])
-    for i in range(count):
-        cross_branch_ref[i] = narrow_ref[order[i]]
-    divide(back(cross_branch_ref, 2))
+    divide(back(narrow_ref, 2))
 
     keys_rows = pairs_ref.shape[1]
     valid = lax.broadcasted_iota(jnp.int32, (keys_rows, 1), 0) < length
@@ -456,22 +455,21 @@
                 valid,
                 head_size,
             )
-            query_ref[j, :, at] = grad_q.astype(BF16)
+            query_ref[relative[j], :, at] = grad_q.astype(BF16)
             pair_total_ref[:, at] = grad_k
             pair_total_ref[:, values_at] = grad_v
         if j == 0:
             own_pairs_ref[...] = pair_total_ref[...]
         else:
             pair_grad_refs[j - 1][...] = pair_total_ref[...].astype(BF16)
-    for i in range(count):
-        query_branch_ref[i] = query_ref[order[i] ^ relative[0]]
-    grad, grad_gain = norm_back(after_self_ref[...], gains_ref[1:2, :], back(query_branch_ref, 1))
+    for a in range(count):
+        query_branch_ref[:, spans[a]] = query_ref[a]
+    grad, grad_gain = norm_back(after_self_ref[...], gains_ref[1:2, :], back(query_ref, 1))
     gain_ref[0:1, :] = grad_gain
     out_ref[...] = grad + wide_ref[...]
+    self_branch_ref[...] = out_ref[...].astype(BF16)
     divide(out_ref[...])
-    for i in range(count):
-        self_branch_ref[i] = narrow_ref[order[i]]
-    divide(back(self_branch_ref, 0))
+    divide(back(narrow_ref, 0))
     for j in range(count):
         mixed_grad_refs[j][...] = narrow_ref[relative[j]]
 
@@ -481,7 +479,7 @@
 ):
     count, rows, width = queries.shape
     columns = count * width
-    branch = ((count, rows, width), BF16)
+    branch = ((rows, columns), BF16)
     text = pairs_scratch(count, pairs)
     keys_rows, pair_columns = text.shape[1:]
     found = call(
@@ -624,77 +622,71 @@
     return list(found[:3]) + [list(found[3:])]
 
 
-def outer_kernel(count, groups, half, scalars_ref, *refs):
-    rows_refs, branch_refs, refs = refs[:groups], refs[groups : 2 * groups], refs[2 * groups :]
-    out_refs, turned_ref = refs[:-1], refs[-1]
-    width = branch_refs[0].shape[2]
-    stride = padded_width(width)
-    odd = scalars_ref[2 * count]
+def outer_kernel(groups, *refs):
+    rows_refs, branch_refs, out_ref = refs[:groups], refs[groups : 2 * groups], refs[2 * groups]
+    width = branch_refs[0].shape[1]
     for g in range(groups):
-        at = slice(g * stride, g * stride + width)
-        turned_ref[...] = rows_refs[g][...].T
-        out_refs[0][:, at] = dot_nn(turned_ref[...], branch_refs[g][0]).astype(BF16)
-        for i in range(1, count):
-            if not half:
-                out_refs[i][:, at] = dot_nn(turned_ref[...], branch_refs[g][i]).astype(BF16)
-                continue
-            for k in range(2):
-                low = pl.multiple_of((odd if k == 0 else 1 - odd) * half, half)
-                found = dot_nn(turned_ref[pl.ds(low, half), :], branch_refs[g][i])
-                out_refs[2 * i - 1 + k][:, at] = found.astype(BF16)
-    if stride > width:
-        for ref in out_refs:
-            for g in range(groups):
-                ref[:, g * stride + width : (g + 1) * stride] = jnp.zeros(
-                    (ref.shape[0], stride - width), BF16
+        turned = rows_refs[g][...].T
+        out_ref[:, g * width : (g + 1) * width] = dot_nn(turned, branch_refs[g][...]).astype(BF16)
+
+
+def outer(rows, branches, deps=()):
+    groups, columns = len(rows), rows[0].shape[1]
+    shape = (columns, groups * branches[0].shape[1])
+    return call(
+        functools.partial(outer_kernel, groups),
+        [(shape, BF16)],
+        [],
+        3.5 * groups,
+        *rows,
+        *branches,
+        deps=deps,
+    )[0]
+
+
+def fold_kernel(count, groups, scalars_ref, shard_ref, own_ref, *refs):
+    piece_refs, stack_ref = refs[:-1], refs[-1]
+    stride = stack_ref.shape[2] // groups
+    width = shard_ref.shape[1] // (groups * count)
+    for a in range(count):
+        for g in range(groups):
+            low = (g * count + a) * width
+            stack_ref[a, :, g * stride : g * stride + width] = shard_ref[:, low : low + width]
+            if stride > width:
+                stack_ref[a, :, g * stride + width : (g + 1) * stride] = jnp.zeros(
+                    (shard_ref.shape[0], stride - width), BF16
                 )
-
-
-def outer(scalars, rows, branches, deps=()):
-    count, tokens, width = branches[0].shape
-    groups, columns = len(rows), rows[0].shape[1]
-    stride = padded_width(width)
-    half = columns // 2 if count == 4 else 0
-    shapes = [((columns, groups * stride), BF16)]
-    if half:
-        shapes += [((half, groups * stride), BF16)] * (2 * (count - 1))
-    else:
-        shapes = shapes * count
-    return list(
-        call(
-            functools.partial(outer_kernel, count, groups, half),
-            shapes,
-            [pltpu.VMEM((columns, tokens), BF16)],
-            3.5 * groups,
-            *rows,
-            *branches,
-            scalars=scalars,
-            deps=deps,
-        )
-    )
-
-
-def join_kernel(count, scalars_ref, own_ref, mine_ref, other_ref, out_ref):
-    odd = scalars_ref[2 * count]
-    half = mine_ref.shape[0]
-    for ref, place in ((mine_ref, odd), (other_ref, 1 - odd)):
-        at = pl.ds(pl.multiple_of(place * half, half), half)
-        out_ref[at, :] = (own_ref[at, :].astype(F32) + ref[...].astype(F32)).astype(BF16)
-
-
-def join_halves(scalars, own, mine, other):
+    for j in range(count):
+        values = stack_ref[scalars_ref[count + j]]
+        if j == 0:
+            own_ref[...] = values.astype(F32)
+        else:
+            put_pieces(piece_refs, count, j, values)
+
+
+def fold(scalars, shard, groups):
     count = lax.axis_size("seq")
-    (found,) = call(
-        functools.partial(join_kernel, count),
-        [(own.shape, BF16)],
-        [],
-        4,
-        own,
-        mine,
-        other,
+    rows = shard.shape[0]
+    columns = groups * padded_width(shard.shape[1] // (groups * count))
+    found = call(
+        functools.partial(fold_kernel, count, groups),
+        [((rows, columns), F32)] + piece_shapes(count, rows, columns),
+        [pltpu.VMEM((count, rows, columns), BF16)],
+        3,
+        shard,
         scalars=scalars,
     )
-    return found
+    return found[0], list(found[1:])
+
+
+def sum_kernel(count, terms, *refs):
+    refs[terms][...] = add_terms(count, refs[:terms]).astype(BF16)
+
+
+def sum_terms(terms):
+    count = lax.axis_size("seq")
+    shape = terms[0].shape
+    return call(functools.partial(sum_kernel, count, len(terms)), [(shape, BF16)], [], 2, *terms)[0]
 
 
 def joined_stats(first, second):
@@ -709,79 +701,55 @@
     return first * scale, second * scale, scale
 
 
-def skip_forward_kernel(count, matrix_parts, terms, scalars_ref, *refs):
-    matrix_refs, refs = refs[:matrix_parts], refs[matrix_parts:]
+def skip_forward_kernel(count, terms, matrix_ref, *refs):
     term_refs, refs = refs[:terms], refs[terms:]
     residual_ref, second_ref, gains_ref, next_ref, shift_ref = refs[:5]
-    first_ref, joined_ref, out_ref, norm_ref, wide_ref, corner_ref = refs[5:]
-    rows, columns = first_ref.shape
-    width = columns // count
-    matrices = fill_corner(count, matrix_refs, scalars_ref, corner_ref)
+    first_ref, joined_ref, out_ref, norm_ref = refs[5:]
+    columns = first_ref.shape[1]
     first_ref[...] = residual_ref[...] + add_terms(count, term_refs)
     first, second, _ = joined_stats(first_ref[...], second_ref[...].astype(F32))
     joined_ref[:, :columns] = (first * gains_ref[0:1, :]).astype(BF16)
     joined_ref[:, columns:] = (second * gains_ref[1:2, :]).astype(BF16)
-    joined = joined_ref[...]
-    for i in range(count):
-        wide_ref[scalars_ref[i]] = dot_nn(joined, matrices[i][:, :width])
-    for a in range(count):
-        out_ref[:, a * width : (a + 1) * width] = wide_ref[a]
+    out_ref[...] = dot_nn(joined_ref[...], matrix_ref[...])
     normed = norm_stats(out_ref[...])[0] * next_ref[0:1, :] + shift_ref[...]
     norm_ref[...] = normed.astype(BF16)
 
 
-def skip_forward(scalars, matrices, terms, residual, second, gains, next_gains, shift, deps=()):
+def skip_forward(matrix, terms, residual, second, gains, next_gains, shift, deps=()):
     rows, columns = residual.shape
-    count = lax.axis_size("seq")
     return call(
-        functools.partial(skip_forward_kernel, count, len(matrices), len(terms)),
+        functools.partial(skip_forward_kernel, lax.axis_size("seq"), len(terms)),
         [
             ((rows, columns), F32),
             ((rows, 2 * columns), BF16),
             ((rows, columns), F32),
             ((rows, columns), BF16),
         ],
-        [pltpu.VMEM((count, rows, columns // count), F32), corner_scratch(count, matrices)],
+        [],
         11,
-        *matrices,
+        matrix,
         *terms,
         residual,
         second,
         gains,
         next_gains,
         shift[None],
-        scalars=scalars,
         deps=deps,
     )
 
 
-def skip_backward_kernel(count, matrix_parts, terms, scalars_ref, *refs):
-    matrix_refs, refs = refs[:matrix_parts], refs[matrix_parts:]
+def skip_backward_kernel(count, terms, matrix_ref, *refs):
     term_refs, refs = refs[:terms], refs[terms:]
     hidden_ref, next_ref, residual_ref, first_ref, second_ref, gains_ref = refs[:6]
-    branch_ref, grad_first_ref, grad_second_ref, vectors_ref, round_ref = refs[6:11]
-    narrow_ref, corner_ref = refs[11:]
-    rows, columns = first_ref.shape
-    width = columns // count
-    matrices = fill_corner(count, matrix_refs, scalars_ref, corner_ref)
+    branch_ref, grad_first_ref, grad_second_ref, vectors_ref, round_ref = refs[6:]
+    columns = first_ref.shape[1]
     grad_norm = add_terms(count, term_refs)
     vectors_ref[0:1, :] = jnp.sum(grad_norm, axis=0, keepdims=True)
     grad, grad_gain = norm_back(hidden_ref[...], next_ref[0:1, :], grad_norm)
     vectors_ref[1:2, :] = grad_gain
-    grad = grad + residual_ref[...]
-    for a in range(count):
-        narrow_ref[a] = grad[:, a * width : (a + 1) * width].astype(BF16)
-    for i in range(count):
-        branch_ref[i] = narrow_ref[scalars_ref[i]]
-
-    def back(at):
-        total = dot_nt(branch_ref[0], matrices[0][at, :width])
-        for i in range(1, count):
-            total = total + dot_nt(branch_ref[i], matrices[i][at, :width])
-        return total
-
-    grad_first_ref[...] = back(slice(0, columns))
-    grad_second_ref[...] = back(slice(columns, 2 * columns))
+    branch_ref[...] = (grad + residual_ref[...]).astype(BF16)
+    grad_first_ref[...] = dot_nt(branch_ref[...], matrix_ref[:columns, :])
+    grad_second_ref[...] = dot_nt(branch_ref[...], matrix_ref[columns:, :])
     first, second, scale = joined_stats(first_ref[...], second_ref[...].astype(F32))
     vectors_ref[2:3, :] = jnp.sum(grad_first_ref[...] * first, axis=0, keepdims=True)
     vectors_ref[3:4, :] = jnp.sum(grad_second_ref[...] * second, axis=0, keepdims=True)
@@ -800,23 +768,21 @@
 
 
 def skip_backward(
-    scalars, matrices, terms, hidden, next_gains, residual, first, second, gains, deps=()
+    matrix, terms, hidden, next_gains, residual, first, second, gains, deps=()
 ):
     rows, columns = first.shape
-    count = lax.axis_size("seq")
-    narrow = (count, rows, columns // count)
     return call(
-        functools.partial(skip_backward_kernel, count, len(matrices), len(terms)),
+        functools.partial(skip_backward_kernel, lax.axis_size("seq"), len(terms)),
         [
-            (narrow, BF16),
+            ((rows, columns), BF16),
             ((rows, columns), F32),
             ((rows, columns), F32),
             ((4, columns), F32),
             ((rows, columns), BF16),
         ],
-        [pltpu.VMEM(narrow, BF16), corner_scratch(count, matrices)],
+        [],
         15,
-        *matrices,
+        matrix,
         *terms,
         hidden,
         next_gains,
@@ -824,7 +790,6 @@
         first,
         second,
         gains,
-        scalars=scalars,
         deps=deps,
     )
 
@@ -1074,17 +1039,6 @@
     return [block, first, other, part, swap_core(part)]
 
 
-def unspread(scalars, blocks):
-    seq_count = lax.axis_size("seq")
-    if seq_count != 4:
-        return add_bf16(blocks[0], *[swap_seq(blocks[j], j) for j in range(1, seq_count)])
-    own, first_mine, first_other, second_mine, second_other, corner_mine, corner_other = blocks
-    passed = swap_by_core(add_bf16(corner_mine, swap_core(corner_other)), 2, 1)
-    other = swap_by_core(add_bf16(first_other, swap_core(second_mine)), 1, 2)
-    mine = swap_by_core(add_bf16(first_mine, swap_core(second_other), passed), 1, 2)
-    return join_halves(scalars, own, mine, other)
-
-
 def own_part(matrix, groups, padded):
     s, seq_count = lax.axis_index("seq"), lax.axis_size("seq")
     width = matrix.shape[1] // (groups * seq_count)
@@ -1150,30 +1104,11 @@
     return (saved, square_parts, mlp_parts, held)
 
 
-def unspread_first(blocks, ready):
-    own, first_mine, first_other, second_mine, second_other, corner_mine, corner_other = blocks
-    from_corner, to_other = swap_core(corner_other), swap_core(second_mine)
-    to_mine = swap_core(second_other)
-    sums = [add_bf16(corner_mine, from_corner), add_bf16(first_other, to_other)]
-    sums = gate(sums, ready)
-    hops = [swap_by_core(sums[0], 2, 1), swap_by_core(sums[1], 1, 2)]
-    return own, hops, [first_mine, to_mine], sums
-
-
-def unspread_next(first, ready):
-    own, hops, terms, _ = first
-    passed, other = gate(hops, ready)
-    return own, swap_by_core(add_bf16(*terms, passed), 1, 2), other
-
-
-def unspread_last(scalars, second, ready):
-    own, mine, other = second
-    (mine,) = gate([mine], ready)
-    return join_halves(scalars, own, mine, other)
-
-
-def unspread_any(blocks):
-    return add_bf16(blocks[0], *[swap_seq(m, j + 1) for j, m in enumerate(blocks[1:])])
+def sum_shard(scalars, shard, groups, ready=None):
+    if ready is not None:
+        (shard,) = gate([shard], ready)
+    own, pieces = fold(scalars, shard, groups)
+    return sum_terms(scatter_last(own, scatter_first(pieces)))
 
 
 def qkv_own(layer, qkv):
@@ -1267,18 +1202,16 @@
     square_stacks = (self_out_weight, query_weight, cross_out_weight)
     rest_stacks = (up_weight, down_weight)
     head_size = model_width // H
-    fours = seq_count == 4
 
     square_shard, qkv_shard = gate(
         [squares_own(0, *square_stacks), qkv_own(0, qkv_weight)], [kv_both] + latent_parts[-2:]
     )
     square_first, lead_first = gather_fsdp(square_shard), gather_fsdp(qkv_shard)
     up_first, down_first = gather_rest(0, *rest_stacks)
-    spread_squares = spread_slice(spread_first(gate([square_first], [cond_part])[0]), [shifts])
+    spread_squares = spread_slice(spread_first(gate([square_first], pair_hops[1:])[0]), [shifts])
     (lead_first,) = gate([lead_first], [shifts])
     pairs_first, pairs_second = pairs_all, pairs_all
-    skip_matrix = gather_fsdp(own_part(skip_weight, 1, padded_width(width)))
-    saved_first, squares_first, mlp_parts, (skip_matrix,) = layer_forward(
+    saved_first, squares_first, mlp_parts, _ = layer_forward(
         latent_parts,
         latents[0],
         scalars,
@@ -1287,21 +1220,19 @@
         pairs_first,
         (lead_first, spread_squares, up_first),
         False,
-        tuple(pairs_all[-2:]),
-        skip_matrix,
+        (),
     )
     own, pieces = mlp_down(saved_first[10], down_first, seq_count)
     first = scatter_first(pieces)
     terms = scatter_last(own, first)
 
-    skip_parts = spread_last(spread_slice(spread_first(skip_matrix), mlp_parts[-2:]), [own])
-    square_second = gather_fsdp(squares_own(1, *square_stacks))
+    skip_matrix = gather_fsdp(skip_weight)
+    square_second = gather_fsdp(gate([squares_own(1, *square_stacks)], mlp_parts[-2:])[0])
     lead_second = gather_fsdp(qkv_own(1, qkv_weight))
     (square_second,) = gate([square_second], first[:2])
     squares_second = spread_first(square_second)
     first_out, joined_norm, skip_out, second_norm = skip_forward(
-        scalars,
-        skip_parts,
+        skip_matrix,
         terms,
         saved_first[7],
         skip_input[0],
@@ -1391,12 +1322,12 @@
         (grad_qkv,) = gate([grad_qkv], first[:2])
         held["last"] = first[:2]
         squares = outer(
-            scalars,
             [saved[2], saved[4], saved[6]],
             [self_branch, query_branch, cross_branch],
             (grad_triples,),
         )
-        squares = gate(squares, first[:2])
+        held["outer"] = squares
+        square_shard = scatter_fsdp(gate([squares], first[:2])[0])
         pair_terms = gate(pair_terms, first[:2])
         grad_pairs = add_bf16(own_pairs, *pair_terms)
         kv_part = kv_both[:, 2 * block * padded_columns : 2 * (block + 1) * padded_columns]
@@ -1407,7 +1338,7 @@
             grad_after_self,
             gain_grads,
             grad_text,
-            squares,
+            square_shard,
             grad_qkv,
             grad_triples,
             (scatter_fsdp(grad_qkv), kv_shard, up_shard, down_shard),
@@ -1428,7 +1359,7 @@
         grad_after_self,
         gain_grads,
         text_second,
-        squares,
+        square_shard,
         grad_qkv,
         grad_triples,
         (qkv_shard, kv_shard, up_shard, down_shard),
@@ -1442,8 +1373,7 @@
         ((), second_own, second_sum, ()),
     )
     skip_branch, grad_first_out, grad_skip, vectors, first_round = skip_backward(
-        scalars,
-        skip_parts,
+        skip_matrix,
         terms,
         skip_out,
         gains[1],
@@ -1451,16 +1381,15 @@
         first_out,
         skip_input[0],
         skip_gains,
-        (grad_qkv, up_shard),
+        (grad_qkv, up_shard, held["outer"]),
     )
     vectors_second = jnp.concatenate([vectors[:2], gain_grads, vectors[2:]], axis=0)
     first_hops = gather_first(first_round)
     first_parts = gather_last(first_hops)
-    if fours:
-        squares = unspread_first(squares, first_parts[-2:])
     own_terms = scatter_last(held["own"], held["own_hops"], terms[-2:])
     output = close_forward(own_terms, saved_second[7])
-    skip_outer = outer(scalars, [joined_norm], [skip_branch], tuple(first_hops[1:]))
+    skip_outer = outer([joined_norm], [skip_branch], tuple(first_hops[1:]))
+    skip_shard = scatter_fsdp(skip_outer)
 
     def entries(layer):
         qkv, square, kv, up, down = layer
@@ -1473,26 +1402,20 @@
         )
 
     early, _ = entries((qkv_shard, qkv_shard, kv_shard, up_shard, down_shard))
-    early_all = lax.all_gather(
-        pack([entry[0] for entry in early], first_hops[1:]), "seq", axis=0, tiled=True
-    )
-
     def first_middle(grad_up_rows, terms):
         del grad_up_rows, terms
         return (kv_shard,)
 
     def first_self(ready):
-        if not fours:
-            return (qkv_shard,)
-        held["squares"] = unspread_next(squares, held["hops"])
-        return (qkv_shard, held["squares"][1])
+        del ready
+        return (qkv_shard,)
 
     (
         terms,
         grad_after_self,
         gain_grads,
         text_first,
-        first_squares,
+        first_square_shard,
         grad_qkv,
         grad_triples,
         (first_qkv_shard, first_kv_shard, first_up_shard, first_down_shard),
@@ -1504,38 +1427,26 @@
         (lead_first, squares_first, pairs_first, up_first, down_first),
         None,
         (
-            (skip_outer[0],) + (tuple(squares[3]) if fours else ()),
+            (skip_outer,),
             first_middle,
             first_self,
-            squares[1] if fours else (),
+            (),
         ),
     )
-    if fours:
-        outer_done = [first_squares[1]]
-        joined = unspread_last(scalars, held["squares"], outer_done)
-        first_squares = unspread_first(first_squares, outer_done)
-        skip_first = unspread_first(skip_outer, first_squares[3])
-        first_squares = unspread_next(first_squares, terms[-2:])
-        first_joined = unspread_last(scalars, first_squares, terms[-2:])
-        skip_joined = unspread_last(
-            scalars, unspread_next(skip_first, [first_squares[1]]), [first_joined]
-        )
-    else:
-        joined, skip_joined = unspread_any(squares), unspread_any(skip_outer)
-        first_joined = unspread_any(first_squares)
-        outer_done = [joined]
-    square_shard, skip_shard = scatter_fsdp(joined), scatter_fsdp(skip_joined)
+    early_hops = gather_first(pack([entry[0] for entry in early], held["last"]))
+    square_sum = sum_shard(scalars, square_shard, 3, held["last"])
+    skip_sum = sum_shard(scalars, skip_shard, 1, held["last"])
     early, _ = entries(
         (first_qkv_shard, first_qkv_shard, first_kv_shard, first_up_shard, first_down_shard)
     )
-    first_hops = gather_first(pack([entry[0] for entry in early], outer_done))
+    first_hops = gather_first(pack([entry[0] for entry in early], terms[-2:]))
     grad_latents, vectors = open_backward(
-        terms, latents[0], gains[0], grad_after_self, (grad_qkv, early_all)
+        terms, latents[0], gains[0], grad_after_self, (grad_qkv,)
     )
     vectors_first = jnp.concatenate([vectors, gain_grads], axis=0)
     first_layer = (
         first_qkv_shard,
-        scatter_fsdp(first_joined),
+        sum_shard(scalars, first_square_shard, 3),
         first_kv_shard,
         first_up_shard,
         first_down_shard,
@@ -1543,13 +1454,13 @@
 
     early_done = settle(
         scalars,
-        [early_all],
+        gather_last(early_hops),
         plan_of(early),
         1,
         2,
         None,
     )
-    _, late = entries((qkv_shard, square_shard, kv_shard, up_shard, down_shard))
+    _, late = entries((qkv_shard, square_sum, kv_shard, up_shard, down_shard))
     late_done = finish(scalars, late, 1, 2, None)
     early, late = entries(first_layer)
     grad_up, grad_down = settle(
@@ -1558,7 +1469,7 @@
     grad_qkv, grad_self_out, grad_query, grad_cross_out, grad_kv = finish(
         scalars, late, 0, 2, late_done
     )
-    (grad_skip_weight,) = finish(scalars, [(skip_shard, 1, 1, width)], 0, 1)
+    (grad_skip_weight,) = finish(scalars, [(skip_sum, 1, 1, width)], 0, 1)
 
     sums = sum_vectors(jnp.concatenate([vectors_first, vectors_second], axis=0))
     first_sums, second_sums = sums[:, :4], sums[:, 4:]

time: 1380 us -> 1400 us (1.014)
  waiting for transfers between devices: 591 us -> 641 us
  other arithmetic: 46.7 us -> 25.5 us
    reduce_scatter x11, waiting for transfers between devices: 44.4 us -> 209 us  [scatter_fsdp(): lax.psum_scatter(full.astype(BF16), 'fsdp', scatter_dimension=0, tiled=True)]
    ppermute x90 -> x106, waiting for transfers between devices: 410 us -> 306 us  [swap_seq(): return lax.ppermute(block, 'seq', [(i, i ^ bits) for i in range(seq_count)])]
    ppermute x15 -> x4, waiting for transfers between devices: 77 us -> 5.01 us  [swap_by_core(): return lax.ppermute(block, ('seq', 'fsdp'), pairs)]
    all_gather x10, waiting for transfers between devices: 23.2 us -> 83 us  [gather_fsdp(): return lax.all_gather(shard, 'fsdp', axis=0, tiled=True)]
    convert_element_type x23 -> x20, other arithmetic: 37.9 us -> 13.1 us  [add_bf16(): return total.astype(BF16)]
    ppermute x90 -> x106, starting transfers between devices: 107 us -> 120 us  [swap_seq(): return lax.ppermute(block, 'seq', [(i, i ^ bits) for i in range(seq_count)])]
    unnamed x317 -> x335, local copies, waits for them, and re-layouts: 51.6 us -> 40.5 us
    pallas_call x30 -> x33, Pallas kernels: 369 us -> 366 us  [call(): pl.pallas_call(run, name=getattr(kernel, 'func', kernel).__name__, out_sh...]
  transfers between devices with their start and end apart: 147 -> 140, of which waited for: 71 -> 65; matrix products, arithmetic and copies ran while one was open for 13% -> 11% of each run, Pallas kernels for 29% -> 28%
where the time goes in v9:
time: 1400 us; the launch traced here: 1390 us
  waiting for transfers between devices  641 us (46%)
  Pallas kernels  394 us (28%)
  starting transfers between devices  136 us (10%)
  local copies, waits for them, and re-layouts  94 us (7%)
  matrix products  68.9 us (5%)
  other arithmetic  25.5 us (2%)
  between operations  16.8 us (1%)
    pallas_call x33, Pallas kernels, call(): pl.pallas_call(run, name=getattr(kernel, 'func', kernel).__name__, out_sh...  366 us
    ppermute x106, waiting for transfers between devices, swap_seq(): return lax.ppermute(block, 'seq', [(i, i ^ bits) for i in range(seq_count)])  306 us
    reduce_scatter x11, waiting for transfers between devices, scatter_fsdp(): lax.psum_scatter(full.astype(BF16), 'fsdp', scatter_dimension=0, tiled=True)  209 us
    ppermute x106, starting transfers between devices, swap_seq(): return lax.ppermute(block, 'seq', [(i, i ^ bits) for i in range(seq_count)])  120 us
    all_gather x10, waiting for transfers between devices, gather_fsdp(): return lax.all_gather(shard, 'fsdp', axis=0, tiled=True)  83 us
    dot_general x8, matrix products, dot_tn(): lax.dot_general(a, b, (((0,), (0,)), ((), ())), preferred_element_type=F32)  54.4 us
    unnamed x335, local copies, waits for them, and re-layouts  40.5 us
    pallas_call x5, Pallas kernels, settle(): pl.pallas_call(functools.partial(settle_kernel, count, len(blocks), plan)...  28.8 us
  transfers between devices with their start and end apart: 140, of which 65 were waited for; matrix products, arithmetic and copies ran while one was open for 11% of the time, Pallas kernels for 28%

profile of v9, /device:TPU:0, one launch (start us, length us, event | category | flops | bytes accessed | tf_op | source)
XLA Modules:
  0.0 1386.4 jit_solution(13576737286463160937)
XLA Ops:
  63.9 23.1 %collective-permute-done.4.refs_1_.refs_11_.refs_7_ = bf16[352,1536]{1,0:T(8,128)(2,1)S(1)} collective-permute-done((bf16[352,1536]{1,0:T(8,128)(2,1)S(1)}, bf16[352,1536]{1,0:T(8,128)(2,1)S(1)}, u32[]{:S(2)}, u32[]{:S(2)}) %collective-permute-start.4) | collective-permute-done | bytes 1081376 | tf_op jit(solution)/shard_map/ppermute | solution.py:930
  136.4 18.6 %self_forward_kernel.2 = (bf16[1024,1408]{1,0:T(8,128)(2,1)}, bf16[1024,1152]{1,0:T(8,128)(2,1)}, bf16[256,352]{1,0:T(8,128)(2,1)}, bf16[256,352]{1,0:T(8,128)(2...) custom-call(bf16[256,1408]{1,0:T(8,128)(2,1)} %bitcast.168, bf16[256,1408]{1,0:T(8,128)(2,1)} %copy-done.63, ...), custom_call_target="tpu_custom_call" | custom-call | flops 24000 | bytes 1000 | tf_op jit(solution)/shard_map/self_forward_kernel/pallas_call | solution.py:50
  186.0 20.5 %middle_forward_kernel.2 = (bf16[256,1408]{1,0:T(8,128)(2,1)}, f32[256,1408]{1,0:T(8,128)}, bf16[256,1408]{1,0:T(8,128)(2,1)}, bf16[4,256,352]{2,1,0:T(8,128)(2,...) custom-call(s32[10]{0:T(128)} %stack.83.refs_0_.scalars_ref, ...), custom_call_target="tpu_custom_call" | custom-call | flops 23000 | bytes 1000 | tf_op jit(solution)/shard_map/middle_forward_kernel/pallas_call | solution.py:50
  210.0 14.4 %collective-permute-done.16.refs_2_ = bf16[256,1408]{1,0:T(8,128)(2,1)S(1)} collective-permute-done((bf16[256,1408]{1,0:T(8,128)(2,1)}, bf16[256,1408]{1,0:T(8,128)(2,1)S(1)}, u32[]{:S(2)}, u32[]{:S(2)}) %collective-permute-start.16) | collective-permute-done | bytes 720928 | tf_op jit(solution)/shard_map/ppermute | solution.py:930
  239.5 12.8 mlp_up_kernel.2
  263.1 14.2 %collective-permute-done.19.refs_1_.refs_2_ = bf16[256,1408]{1,0:T(8,128)(2,1)S(1)} collective-permute-done((bf16[256,1408]{1,0:T(8,128)(2,1)}, bf16[256,1408]{1,0:T(8,128)(2,1)S(1)}, u32[]{:S(2)}, u32[]{:S(2)}) %collective-permute-start.19) | collective-permute-done | bytes 720928 | tf_op jit(solution)/shard_map/ppermute | solution.py:930
  287.8 64.9 %all-gather.13.cloned.1.call-done.refs_0_ = bf16[2816,1408]{1,0:T(8,128)(2,1)} async-done(((bf16[352,1408]{1,0:T(8,128)(2,1)}), bf16[2816,1408]{1,0:T(8,128)(2,1)}) %all-gather.13.cloned.1.call-update) | async-done | bytes 7929872 | tf_op jit(solution)/shard_map/all_gather | solution.py:1056
  366.1 15.5 %collective-permute-done.23.refs_1_ = bf16[256,1408]{1,0:T(8,128)(2,1)S(1)} collective-permute-done((bf16[256,1408]{1,0:T(8,128)(2,1)}, bf16[256,1408]{1,0:T(8,128)(2,1)S(1)}, u32[]{:S(2)}, u32[]{:S(2)}) %collective-permute-start.23) | collective-permute-done | bytes 720928 | tf_op jit(solution)/shard_map/ppermute | solution.py:930
  400.4 15.0 %collective-permute-done.26.refs_4_ = bf16[128,1408]{1,0:T(8,128)(2,1)S(1)} collective-permute-done((bf16[128,1408]{1,0:T(8,128)(2,1)}, bf16[128,1408]{1,0:T(8,128)(2,1)S(1)}, u32[]{:S(2)}, u32[]{:S(2)}) %collective-permute-start.26) | collective-permute-done | bytes 360480 | tf_op jit(solution)/shard_map/ppermute | solution.py:930
  416.1 18.2 %self_forward_kernel.3 = (bf16[1024,1408]{1,0:T(8,128)(2,1)}, bf16[1024,1152]{1,0:T(8,128)(2,1)}, bf16[256,352]{1,0:T(8,128)(2,1)}, bf16[256,352]{1,0:T(8,128)(2...) custom-call(bf16[256,1408]{1,0:T(8,128)(2,1)} %get-tuple-element.199.refs_0_, bf16[256,1408]{1,0:T(8,128)(2,1)} %copy-done.47, ...), custom_call_target="tpu_custom_call" | custom-call | flops 24000 | bytes 1000 | tf_op jit(solution)/shard_map/self_forward_kernel/pallas_call | solution.py:50
  452.0 21.7 %middle_forward_kernel.3 = (bf16[256,1408]{1,0:T(8,128)(2,1)}, f32[256,1408]{1,0:T(8,128)}, bf16[256,1408]{1,0:T(8,128)(2,1)}, bf16[4,256,352]{2,1,0:T(8,128)(2,...) custom-call(s32[10]{0:T(128)} %stack.83.refs_0_.scalars_ref, ...), custom_call_target="tpu_custom_call" | custom-call | flops 23000 | bytes 1000 | tf_op jit(solution)/shard_map/middle_forward_kernel/pallas_call | solution.py:50
  510.4 12.6 mlp_up_kernel.3
  531.8 20.5 %mlp_backward_kernel.2 = (bf16[1024,1408]{1,0:T(8,128)(2,1)}, bf16[1024,1536]{1,0:T(8,128)(2,1)}, f32[256,1408]{1,0:T(8,128)}, bf16[256,1408]{1,0:T(8,128)(2,1)}...) custom-call(bf16[1024,1408]{1,0:T(8,128)(2,1)} %stack_kernel.1.refs_0_, ...), custom_call_target="tpu_custom_call" | custom-call | flops 22000 | bytes 1000 | tf_op jit(solution)/shard_map/mlp_backward_kernel/pallas_call | solution.py:50
  585.3 27.5 %middle_backward_kernel.2 = (f32[256,1408]{1,0:T(8,128)}, bf16[256,1408]{1,0:T(8,128)(2,1)}, bf16[256,1408]{1,0:T(8,128)(2,1)}, bf16[256,1408]{1,0:T(8,128)(2,1)...) custom-call(s32[10]{0:T(128)} %stack.83.refs_0_.scalars_ref, ...), custom_call_target="tpu_custom_call" | custom-call | flops 37000 | bytes 1000 | tf_op jit(solution)/shard_map/middle_backward_kernel/pallas_call | solution.py:50
  641.6 28.7 %self_backward_kernel.2 = (bf16[1024,1152]{1,0:T(8,128)(2,1)}, f32[256,1408]{1,0:T(8,128)}, bf16[256,1408]{1,0:T(8,128)(2,1)}, bf16[256,1408]{1,0:T(8,128)(2,1)}...) custom-call(bf16[1024,1152]{1,0:T(8,128)(2,1)} %get-tuple-element.222.refs_0_, ...), custom_call_target="tpu_custom_call" | custom-call | flops 32000 | bytes 1000 | tf_op jit(solution)/shard_map/self_backward_kernel/pallas_call | solution.py:50
  714.3 12.5 skip_backward_kernel.1
  728.5 14.6 %collective-permute-done.61.refs_3_.refs_2_ = bf16[256,1408]{1,0:T(8,128)(2,1)S(1)} collective-permute-done((bf16[256,1408]{1,0:T(8,128)(2,1)}, bf16[256,1408]{1,0:T(8,128)(2,1)S(1)}, u32[]{:S(2)}, u32[]{:S(2)}) %collective-permute-start.61) | collective-permute-done | bytes 720928 | tf_op jit(solution)/shard_map/ppermute | solution.py:930
  753.0 20.5 %mlp_backward_kernel.3 = (bf16[1024,1408]{1,0:T(8,128)(2,1)}, bf16[1024,1536]{1,0:T(8,128)(2,1)}, f32[256,1408]{1,0:T(8,128)}, bf16[256,1408]{1,0:T(8,128)(2,1)}...) custom-call(bf16[256,1408]{1,0:T(8,128)(2,1)} %get-tuple-element.265.refs_0_, ...), custom_call_target="tpu_custom_call" | custom-call | flops 22000 | bytes 1000 | tf_op jit(solution)/shard_map/mlp_backward_kernel/pallas_call | solution.py:50
  808.2 27.5 %middle_backward_kernel.3 = (f32[256,1408]{1,0:T(8,128)}, bf16[256,1408]{1,0:T(8,128)(2,1)}, bf16[256,1408]{1,0:T(8,128)(2,1)}, bf16[256,1408]{1,0:T(8,128)(2,1)...) custom-call(s32[10]{0:T(128)} %stack.83.refs_0_.scalars_ref, ...), custom_call_target="tpu_custom_call" | custom-call | flops 37000 | bytes 1000 | tf_op jit(solution)/shard_map/middle_backward_kernel/pallas_call | solution.py:50
  855.3 28.8 %self_backward_kernel.3 = (bf16[1024,1152]{1,0:T(8,128)(2,1)}, f32[256,1408]{1,0:T(8,128)}, bf16[256,1408]{1,0:T(8,128)(2,1)}, bf16[256,1408]{1,0:T(8,128)(2,1)}...) custom-call(bf16[1024,1152]{1,0:T(8,128)(2,1)} %get-tuple-element.254.refs_0_, ...), custom_call_target="tpu_custom_call" | custom-call | flops 32000 | bytes 1000 | tf_op jit(solution)/shard_map/self_backward_kernel/pallas_call | solution.py:50
  963.4 24.6 %collective-permute-done.84 = f32[4,10,1408]{2,1,0:T(8,128)S(1)} collective-permute-done((f32[4,10,1408]{2,1,0:T(8,128)S(1)}, f32[4,10,1408]{2,1,0:T(8,128)S(1)}, u32[]{:S(2)}, u32[]{:S(2)}) %collective-permute-start.84) | collective-permute-done | bytes 225312 | tf_op jit(solution)/shard_map/ppermute | solution.py:935
  1007.7 102.5 %reduce-scatter.28.cloned.1.call-done.refs_0_ = bf16[176,4224]{1,0:T(8,128)(2,1)} async-done(((bf16[1408,4224]{1,0:T(8,128)(2,1)}), bf16[176,4224]{1,0:T(8,128)(2,1)}) %reduce-scatter.28.cloned.1.call-update) | async-done | bytes 1486864 | tf_op jit(solution)/shard_map/reduce_scatter | solution.py:1060
  1127.3 106.6 %reduce-scatter.24.cloned.1.call-done.refs_1_ = bf16[176,4224]{1,0:T(8,128)(2,1)} async-done(((bf16[1408,4224]{1,0:T(8,128)(2,1)}), bf16[176,4224]{1,0:T(8,128)(2,1)}) %reduce-scatter.24.cloned.1.call-update) | async-done | bytes 1486864 | tf_op jit(solution)/shard_map/reduce_scatter | solution.py:1060
  1297.4 17.5 %collective-permute-done.87.refs_3_ = bf16[96,1152]{1,0:T(8,128)(2,1)S(1)} collective-permute-done((bf16[96,1152]{1,0:T(8,128)(2,1)S(1)}, bf16[96,1152]{1,0:T(8,128)(2,1)S(1)}, u32[]{:S(2)}, u32[]{:S(2)}) %collective-permute-start.87) | collective-permute-done | bytes 221216 | tf_op jit(solution)/shard_map/ppermute | solution.py:930
  (809 shorter events, 686.4 us)
Async XLA Ops:
  52.0 187.4 %all-gather.21.cloned.1.call-start = ((), (), s32[]{:S(2)}) async-start(), calls=%async_computation.18 | async-start | bytes 4866048 | tf_op jit(solution)/shard_map/all_gather | solution.py:1056
  57.6 194.7 %all-gather.29.cloned.1.call-start = ((), (), s32[]{:S(2)}) async-start(), calls=%async_computation.33 | async-start | bytes 4866048 | tf_op jit(solution)/shard_map/all_gather | solution.py:1056
  116.1 162.0 %all-gather.23.cloned.1.call-start = ((), (), s32[]{:S(2)}) async-start(), calls=%async_computation.19 | async-start | bytes 3649536 | tf_op jit(solution)/shard_map/all_gather | solution.py:1056
  236.3 157.9 %all-gather.25.cloned.1.call-start = ((), (), s32[]{:S(2)}) async-start(), calls=%async_computation.20 | async-start | bytes 3649536 | tf_op jit(solution)/shard_map/all_gather | solution.py:1056
  238.1 269.2 %all-gather.27.cloned.1.call-start = ((), (), s32[]{:S(2)}) async-start(), calls=%async_computation.21 | async-start | bytes 4866048 | tf_op jit(solution)/shard_map/all_gather | solution.py:1056
  239.4 292.4 %all-gather.31.cloned.1.call-start = ((), (), s32[]{:S(2)}) async-start(), calls=%async_computation.34 | async-start | bytes 4866048 | tf_op jit(solution)/shard_map/all_gather | solution.py:1056
  281.9 358.7 %reduce-scatter.12.cloned.1.call-start = ((), (), s32[]{:S(2)}) async-start(), calls=%async_computation.22 | async-start | bytes 4866048 | tf_op jit(solution)/shard_map/reduce_scatter | solution.py:1060
  531.5 181.9 %reduce-scatter.14.cloned.1.call-start = ((), (), s32[]{:S(2)}) async-start(), calls=%async_computation.23 | async-start | bytes 4866048 | tf_op jit(solution)/shard_map/reduce_scatter | solution.py:1060
  571.3 236.1 %reduce-scatter.16.cloned.1.call-start = ((), (), s32[]{:S(2)}) async-start(), calls=%async_computation.24 | async-start | bytes 1769472 | tf_op jit(solution)/shard_map/reduce_scatter | solution.py:1060
  691.2 164.0 %reduce-scatter.20.cloned.1.call-start = ((), (), s32[]{:S(2)}) async-start(), calls=%async_computation.26 | async-start | bytes 3649536 | tf_op jit(solution)/shard_map/reduce_scatter | solution.py:1060
  698.8 156.5 %reduce-scatter.18.cloned.1.call-start = ((), (), s32[]{:S(2)}) async-start(), calls=%async_computation.25 | async-start | bytes 4866048 | tf_op jit(solution)/shard_map/reduce_scatter | solution.py:1060
  787.0 169.8 %reduce-scatter.30.cloned.1.call-start = ((), (), s32[]{:S(2)}) async-start(), calls=%async_computation.31 | async-start | bytes 4866048 | tf_op jit(solution)/shard_map/reduce_scatter | solution.py:1060
  796.6 197.7 %reduce-scatter.32.cloned.1.call-start = ((), (), s32[]{:S(2)}) async-start(), calls=%async_computation.32 | async-start | bytes 8921088 | tf_op jit(solution)/shard_map/reduce_scatter | solution.py:1060
  797.2 313.0 %reduce-scatter.28.cloned.1.call-start = ((), (), s32[]{:S(2)}) async-start(), calls=%async_computation.30 | async-start | bytes 13381632 | tf_op jit(solution)/shard_map/reduce_scatter | solution.py:1060
  797.8 436.1 %reduce-scatter.24.cloned.1.call-start = ((), (), s32[]{:S(2)}) async-start(), calls=%async_computation.28 | async-start | bytes 13381632 | tf_op jit(solution)/shard_map/reduce_scatter | solution.py:1060
  902.1 416.6 %reduce-scatter.26.cloned.1.call-start = ((), (), s32[]{:S(2)}) async-start(), calls=%async_computation.29 | async-start | bytes 1769472 | tf_op jit(solution)/shard_map/reduce_scatter | solution.py:1060
  912.3 406.4 %reduce-scatter.22.cloned.1.call-start = ((), (), s32[]{:S(2)}) async-start(), calls=%async_computation.27 | async-start | bytes 3649536 | tf_op jit(solution)/shard_map/reduce_scatter | solution.py:1060
  955.9 154.3 %collective-permute-start.105 = (bf16[192,2944]{1,0:T(8,128)(2,1)}, bf16[192,2944]{1,0:T(8,128)(2,1)}, u32[]{:S(2)}, u32[]{:S(2)}) collective-permute-start(bf16[192,2944]{1,0:T(8,128)(2,1)} %pack_kernel.8.refs_0_), channel_id=1, source_target_pairs={{0,8},{8,0},{16,24},{24,16},{1,9},{9,1},{17,25},{25,17},{2,10},{10... | collective-permute-start | bytes 3391496 | tf_op jit(solution)/shard_map/ppermute | solution.py:930
  959.1 281.0 %collective-permute-start.102 = (bf16[192,2944]{1,0:T(8,128)(2,1)}, bf16[192,2944]{1,0:T(8,128)(2,1)}, u32[]{:S(2)}, u32[]{:S(2)}) collective-permute-start(bf16[192,2944]{1,0:T(8,128)(2,1)} %pack_kernel.7.refs_0_), channel_id=1, source_target_pairs={{0,16},{8,24},{16,0},{24,8},{1,17},{9,25},{17,1},{25,9},{2,18},{10... | collective-permute-start | bytes 3391496 | tf_op jit(solution)/shard_map/ppermute | solution.py:930
  997.1 119.8 %collective-permute-start.109 = (bf16[352,384]{1,0:T(8,128)(2,1)}, bf16[352,384]{1,0:T(8,128)(2,1)S(1)}, u32[]{:S(2)}, u32[]{:S(2)}) collective-permute-start(bf16[352,384]{1,0:T(8,128)(2,1)} %get-tuple-element.350), channel_id=1, source_target_pairs={{0,8},{8,0},{16,24},{24,16},{1,9},{9,1},{17,25},{25,17},{2,10},{10... | collective-permute-start | bytes 811016 | tf_op jit(solution)/shard_map/ppermute | solution.py:930
  1001.6 117.5 %collective-permute-start.110 = (bf16[352,384]{1,0:T(8,128)(2,1)}, bf16[352,384]{1,0:T(8,128)(2,1)S(1)}, u32[]{:S(2)}, u32[]{:S(2)}) collective-permute-start(bf16[352,384]{1,0:T(8,128)(2,1)} %get-tuple-element.351), channel_id=1, source_target_pairs={{0,16},{8,24},{16,0},{24,8},{1,17},{9,25},{17,1},{25,9},{2,18},{10... | collective-permute-start | bytes 811016 | tf_op jit(solution)/shard_map/ppermute | solution.py:930
  1005.2 247.2 %collective-permute-start.101 = (bf16[192,2944]{1,0:T(8,128)(2,1)}, bf16[192,2944]{1,0:T(8,128)(2,1)}, u32[]{:S(2)}, u32[]{:S(2)}) collective-permute-start(bf16[192,2944]{1,0:T(8,128)(2,1)} %pack_kernel.7.refs_0_), channel_id=1, source_target_pairs={{0,8},{8,0},{16,24},{24,16},{1,9},{9,1},{17,25},{25,17},{2,10},{10... | collective-permute-start | bytes 3391496 | tf_op jit(solution)/shard_map/ppermute | solution.py:930
  1110.2 126.9 %collective-permute-start.79 = (bf16[352,1024]{1,0:T(8,128)(2,1)}, bf16[352,1024]{1,0:T(8,128)(2,1)}, u32[]{:S(2)}, u32[]{:S(2)}) collective-permute-start(bf16[352,1024]{1,0:T(8,128)(2,1)} %get-tuple-element.404), channel_id=1, source_target_pairs={{0,16},{8,24},{16,0},{24,8},{1,17},{9,25},{17,1},{25,9},{2,18},{10... | collective-permute-start | bytes 2162696 | tf_op jit(solution)/shard_map/ppermute | solution.py:930
  1119.1 122.5 %collective-permute-start.112 = (bf16[176,384]{1,0:T(8,128)(2,1)}, bf16[176,384]{1,0:T(8,128)(2,1)}, u32[]{:S(2)}, u32[]{:S(2)}) collective-permute-start(bf16[176,384]{1,0:T(8,128)(2,1)} %add_convert_fusion.18), channel_id=1, source_target_pairs={{0,16},{8,24},{16,0},{24,8},{1,17},{9,25},{17,1},{25,9},{2,18},{10... | collective-permute-start | bytes 405512 | tf_op jit(solution)/shard_map/ppermute | solution.py:930
  (277 other events, 4164.1 us)
Sparse Core Ops, SparseCore 0:
  10.2 40.9 all-gather.14
  53.5 37.9 all-gather.18
  93.7 41.0 all-gather.16
  136.9 47.7 all-gather.20
  186.7 47.1 all-gather.28
  236.0 37.9 all-gather.22
  275.6 77.1 all-gather.12
  354.4 39.7 all-gather.24
  395.8 45.3 all-gather.26
  442.7 47.1 all-gather.30
  531.7 48.9 reduce-scatter.11
  583.5 49.3 reduce-scatter.13
  691.4 31.9 reduce-scatter.15
  725.5 39.3 reduce-scatter.19
  787.1 48.5 reduce-scatter.17
  838.5 49.3 reduce-scatter.29
  890.7 94.9 reduce-scatter.31
  988.1 122.0 reduce-scatter.27
  1112.5 121.3 reduce-scatter.23
  1236.7 32.6 reduce-scatter.25
  1272.3 39.1 reduce-scatter.21

commit v10 on v9

--- a/solution.py
+++ b/solution.py
@@ -644,6 +644,82 @@
     )[0]
 
 
+def spread_outer_kernel(count, groups, half, scalars_ref, *refs):
+    rows_refs, branch_refs, refs = refs[:groups], refs[groups : 2 * groups], refs[2 * groups :]
+    out_refs, (turned_ref, stack_ref) = refs[:-2], refs[-2:]
+    width = stack_ref.shape[2]
+    stride = padded_width(width)
+    odd = scalars_ref[2 * count]
+    for g in range(groups):
+        at = slice(g * stride, g * stride + width)
+        turned_ref[...] = rows_refs[g][...].T
+        for a in range(count):
+            stack_ref[a] = branch_refs[g][:, a * width : (a + 1) * width]
+        out_refs[0][:, at] = dot_nn(turned_ref[...], stack_ref[scalars_ref[0]]).astype(BF16)
+        for i in range(1, count):
+            if not half:
+                out_refs[i][:, at] = dot_nn(turned_ref[...], stack_ref[scalars_ref[i]]).astype(BF16)
+                continue
+            for k in range(2):
+                low = pl.multiple_of((odd if k == 0 else 1 - odd) * half, half)
+                found = dot_nn(turned_ref[pl.ds(low, half), :], stack_ref[scalars_ref[i]])
+                out_refs[2 * i - 1 + k][:, at] = found.astype(BF16)
+    if stride > width:
+        for ref in out_refs:
+            for g in range(groups):
+                ref[:, g * stride + width : (g + 1) * stride] = jnp.zeros(
+                    (ref.shape[0], stride - width), BF16
+                )
+
+
+def spread_outer(scalars, rows, branches, deps=()):
+    count = lax.axis_size("seq")
+    tokens, width = branches[0].shape[0], branches[0].shape[1] // count
+    groups, columns = len(rows), rows[0].shape[1]
+    stride = padded_width(width)
+    half = columns // 2 if count == 4 else 0
+    shapes = [((columns, groups * stride), BF16)]
+    if half:
+        shapes += [((half, groups * stride), BF16)] * (2 * (count - 1))
+    else:
+        shapes = shapes * count
+    return list(
+        call(
+            functools.partial(spread_outer_kernel, count, groups, half),
+            shapes,
+            [pltpu.VMEM((columns, tokens), BF16), pltpu.VMEM((count, tokens, width), BF16)],
+            3.5 * groups,
+            *rows,
+            *branches,
+            scalars=scalars,
+            deps=deps,
+        )
+    )
+
+
+def join_kernel(count, scalars_ref, own_ref, mine_ref, other_ref, out_ref):
+    odd = scalars_ref[2 * count]
+    half = mine_ref.shape[0]
+    for ref, place in ((mine_ref, odd), (other_ref, 1 - odd)):
+        at = pl.ds(pl.multiple_of(place * half, half), half)
+        out_ref[at, :] = (own_ref[at, :].astype(F32) + ref[...].astype(F32)).astype(BF16)
+
+
+def join_halves(scalars, own, mine, other):
+    count = lax.axis_size("seq")
+    (found,) = call(
+        functools.partial(join_kernel, count),
+        [(own.shape, BF16)],
+        [],
+        4,
+        own,
+        mine,
+        other,
+        scalars=scalars,
+    )
+    return found
+
+
 def fold_kernel(count, groups, scalars_ref, shard_ref, own_ref, *refs):
     piece_refs, stack_ref = refs[:-1], refs[-1]
     stride = stack_ref.shape[2] // groups
@@ -1102,6 +1178,32 @@
         activated,
     )
     return (saved, square_parts, mlp_parts, held)
+
+
+def unspread_first(blocks, ready):
+    own, first_mine, first_other, second_mine, second_other, corner_mine, corner_other = blocks
+    from_corner, to_other = swap_core(corner_other), swap_core(second_mine)
+    to_mine = swap_core(second_other)
+    sums = [add_bf16(corner_mine, from_corner), add_bf16(first_other, to_other)]
+    sums = gate(sums, ready)
+    hops = [swap_by_core(sums[0], 2, 1), swap_by_core(sums[1], 1, 2)]
+    return own, hops, [first_mine, to_mine], sums
+
+
+def unspread_next(first, ready):
+    own, hops, terms, _ = first
+    passed, other = gate(hops, ready)
+    return own, swap_by_core(add_bf16(*terms, passed), 1, 2), other
+
+
+def unspread_last(scalars, second, ready):
+    own, mine, other = second
+    (mine,) = gate([mine], ready)
+    return join_halves(scalars, own, mine, other)
+
+
+def unspread_any(blocks):
+    return add_bf16(blocks[0], *[swap_seq(m, j + 1) for j, m in enumerate(blocks[1:])])
 
 
 def sum_shard(scalars, shard, groups, ready=None):
@@ -1321,13 +1423,14 @@
         grad_qkv = dot_tn(saved[0], grad_triples).astype(BF16)
         (grad_qkv,) = gate([grad_qkv], first[:2])
         held["last"] = first[:2]
-        squares = outer(
+        squares = spread_outer(
+            scalars,
             [saved[2], saved[4], saved[6]],
             [self_branch, query_branch, cross_branch],
             (grad_triples,),
         )
-        held["outer"] = squares
-        square_shard = scatter_fsdp(gate([squares], first[:2])[0])
+        held["outer"] = squares[0]
+        squares = gate(squares, first[:2])
         pair_terms = gate(pair_terms, first[:2])
         grad_pairs = add_bf16(own_pairs, *pair_terms)
         kv_part = kv_both[:, 2 * block * padded_columns : 2 * (block + 1) * padded_columns]
@@ -1338,7 +1441,7 @@
             grad_after_self,
             gain_grads,
             grad_text,
-            square_shard,
+            squares,
             grad_qkv,
             grad_triples,
             (scatter_fsdp(grad_qkv), kv_shard, up_shard, down_shard),
@@ -1359,7 +1462,7 @@
         grad_after_self,
         gain_grads,
         text_second,
-        square_shard,
+        squares,
         grad_qkv,
         grad_triples,
         (qkv_shard, kv_shard, up_shard, down_shard),
@@ -1386,6 +1489,9 @@
     vectors_second = jnp.concatenate([vectors[:2], gain_grads, vectors[2:]], axis=0)
     first_hops = gather_first(first_round)
     first_parts = gather_last(first_hops)
+    fours = seq_count == 4
+    if fours:
+        squares = unspread_first(squares, first_parts[-2:])
     own_terms = scatter_last(held["own"], held["own_hops"], terms[-2:])
     output = close_forward(own_terms, saved_second[7])
     skip_outer = outer([joined_norm], [skip_branch], tuple(first_hops[1:]))
@@ -1415,7 +1521,7 @@
         grad_after_self,
         gain_grads,
         text_first,
-        first_square_shard,
+        first_squares,
         grad_qkv,
         grad_triples,
         (first_qkv_shard, first_kv_shard, first_up_shard, first_down_shard),
@@ -1427,14 +1533,20 @@
         (lead_first, squares_first, pairs_first, up_first, down_first),
         None,
         (
-            (skip_outer,),
+            (skip_outer,) + (tuple(squares[3]) if fours else ()),
             first_middle,
             first_self,
-            (),
+            squares[1] if fours else (),
         ),
     )
     early_hops = gather_first(pack([entry[0] for entry in early], held["last"]))
-    square_sum = sum_shard(scalars, square_shard, 3, held["last"])
+    if fours:
+        joined = unspread_last(scalars, unspread_next(squares, held["last"]), terms[-2:])
+        first_squares = unspread_next(unspread_first(first_squares, terms[3:4]), terms[-2:])
+        first_joined = unspread_last(scalars, first_squares, terms[-2:])
+    else:
+        joined, first_joined = unspread_any(squares), unspread_any(first_squares)
+    square_sum = scatter_fsdp(joined)
     skip_sum = sum_shard(scalars, skip_shard, 1, held["last"])
     early, _ = entries(
         (first_qkv_shard, first_qkv_shard, first_kv_shard, first_up_shard, first_down_shard)
@@ -1446,7 +1558,7 @@
     vectors_first = jnp.concatenate([vectors, gain_grads], axis=0)
     first_layer = (
         first_qkv_shard,
-        sum_shard(scalars, first_square_shard, 3),
+        scatter_fsdp(first_joined),
         first_kv_shard,
         first_up_shard,
         first_down_shard,

time: 1400 us -> 1300 us (0.929)
  waiting for transfers between devices: 641 us -> 533 us
    reduce_scatter x11, waiting for transfers between devices: 209 us -> 0.11 us  [scatter_fsdp(): lax.psum_scatter(full.astype(BF16), 'fsdp', scatter_dimension=0, tiled=True)]
    ppermute x4 -> x10, waiting for transfers between devices: 5.01 us -> 64.7 us  [swap_by_core(): return lax.ppermute(block, ('seq', 'fsdp'), pairs)]
    ppermute x106 -> x98, waiting for transfers between devices: 306 us -> 348 us  [swap_seq(): return lax.ppermute(block, 'seq', [(i, i ^ bits) for i in range(seq_count)])]
    ppermute x106 -> x98, starting transfers between devices: 120 us -> 110 us  [swap_seq(): return lax.ppermute(block, 'seq', [(i, i ^ bits) for i in range(seq_count)])]
    pallas_call x33 -> x31, Pallas kernels: 366 us -> 367 us  [call(): pl.pallas_call(run, name=getattr(kernel, 'func', kernel).__name__, out_sh...]
  transfers between devices with their start and end apart: 140 -> 144, of which waited for: 65 -> 69; matrix products, arithmetic and copies ran while one was open for 11% -> 12% of each run, Pallas kernels for 28% -> 30%
where the time goes in v10:
time: 1300 us; the launch traced here: 1290 us
  waiting for transfers between devices  533 us (41%)
  Pallas kernels  396 us (30%)
  starting transfers between devices  133 us (10%)
  local copies, waits for them, and re-layouts  100 us (8%)
  matrix products  69.3 us (5%)
  other arithmetic  34.7 us (3%)
  between operations  16.9 us (1%)
    pallas_call x31, Pallas kernels, call(): pl.pallas_call(run, name=getattr(kernel, 'func', kernel).__name__, out_sh...  367 us
    ppermute x98, waiting for transfers between devices, swap_seq(): return lax.ppermute(block, 'seq', [(i, i ^ bits) for i in range(seq_count)])  348 us
    ppermute x98, starting transfers between devices, swap_seq(): return lax.ppermute(block, 'seq', [(i, i ^ bits) for i in range(seq_count)])  110 us
    all_gather x10, waiting for transfers between devices, gather_fsdp(): return lax.all_gather(shard, 'fsdp', axis=0, tiled=True)  83.6 us
    ppermute x10, waiting for transfers between devices, swap_by_core(): return lax.ppermute(block, ('seq', 'fsdp'), pairs)  64.7 us
    dot_general x8, matrix products, dot_tn(): lax.dot_general(a, b, (((0,), (0,)), ((), ())), preferred_element_type=F32)  54.9 us
    unnamed x335, local copies, waits for them, and re-layouts  47 us
    pallas_call x5, Pallas kernels, settle(): pl.pallas_call(functools.partial(settle_kernel, count, len(blocks), plan)...  28.7 us
  transfers between devices with their start and end apart: 144, of which 69 were waited for; matrix products, arithmetic and copies ran while one was open for 12% of the time, Pallas kernels for 30%

profile of v10, /device:TPU:0, one launch (start us, length us, event | category | flops | bytes accessed | tf_op | source)
XLA Modules:
  0.0 1293.0 jit_solution(1694634262688615479)
XLA Ops:
  63.9 23.1 %collective-permute-done.4.refs_1_.refs_11_.refs_7_ = bf16[352,1536]{1,0:T(8,128)(2,1)S(1)} collective-permute-done((bf16[352,1536]{1,0:T(8,128)(2,1)S(1)}, bf16[352,1536]{1,0:T(8,128)(2,1)S(1)}, u32[]{:S(2)}, u32[]{:S(2)}) %collective-permute-start.4) | collective-permute-done | bytes 1081376 | tf_op jit(solution)/shard_map/ppermute | solution.py:1006
  136.4 18.5 %self_forward_kernel.2 = (bf16[1024,1408]{1,0:T(8,128)(2,1)}, bf16[1024,1152]{1,0:T(8,128)(2,1)}, bf16[256,352]{1,0:T(8,128)(2,1)}, bf16[256,352]{1,0:T(8,128)(2...) custom-call(bf16[256,1408]{1,0:T(8,128)(2,1)} %bitcast.168, bf16[256,1408]{1,0:T(8,128)(2,1)} %copy-done.71, ...), custom_call_target="tpu_custom_call" | custom-call | flops 24000 | bytes 1000 | tf_op jit(solution)/shard_map/self_forward_kernel/pallas_call | solution.py:50
  185.3 20.4 %middle_forward_kernel.2 = (bf16[256,1408]{1,0:T(8,128)(2,1)}, f32[256,1408]{1,0:T(8,128)}, bf16[256,1408]{1,0:T(8,128)(2,1)}, bf16[4,256,352]{2,1,0:T(8,128)(2,...) custom-call(s32[10]{0:T(128)} %stack.83.refs_0_.scalars_ref, ...), custom_call_target="tpu_custom_call" | custom-call | flops 23000 | bytes 1000 | tf_op jit(solution)/shard_map/middle_forward_kernel/pallas_call | solution.py:50
  209.0 14.7 %collective-permute-done.16.refs_2_ = bf16[256,1408]{1,0:T(8,128)(2,1)S(1)} collective-permute-done((bf16[256,1408]{1,0:T(8,128)(2,1)}, bf16[256,1408]{1,0:T(8,128)(2,1)S(1)}, u32[]{:S(2)}, u32[]{:S(2)}) %collective-permute-start.16) | collective-permute-done | bytes 720928 | tf_op jit(solution)/shard_map/ppermute | solution.py:1006
  238.5 12.6 mlp_up_kernel.2
  262.4 14.5 %collective-permute-done.19.refs_1_.refs_2_ = bf16[256,1408]{1,0:T(8,128)(2,1)S(1)} collective-permute-done((bf16[256,1408]{1,0:T(8,128)(2,1)}, bf16[256,1408]{1,0:T(8,128)(2,1)S(1)}, u32[]{:S(2)}, u32[]{:S(2)}) %collective-permute-start.19) | collective-permute-done | bytes 720928 | tf_op jit(solution)/shard_map/ppermute | solution.py:1006
  287.2 65.6 %all-gather.13.cloned.1.call-done.refs_0_ = bf16[2816,1408]{1,0:T(8,128)(2,1)} async-done(((bf16[352,1408]{1,0:T(8,128)(2,1)}), bf16[2816,1408]{1,0:T(8,128)(2,1)}) %all-gather.13.cloned.1.call-update) | async-done | bytes 7929872 | tf_op jit(solution)/shard_map/all_gather | solution.py:1132
  366.1 15.5 %collective-permute-done.23.refs_1_ = bf16[256,1408]{1,0:T(8,128)(2,1)S(1)} collective-permute-done((bf16[256,1408]{1,0:T(8,128)(2,1)}, bf16[256,1408]{1,0:T(8,128)(2,1)S(1)}, u32[]{:S(2)}, u32[]{:S(2)}) %collective-permute-start.23) | collective-permute-done | bytes 720928 | tf_op jit(solution)/shard_map/ppermute | solution.py:1006
  400.5 15.0 %collective-permute-done.26.refs_4_ = bf16[128,1408]{1,0:T(8,128)(2,1)S(1)} collective-permute-done((bf16[128,1408]{1,0:T(8,128)(2,1)}, bf16[128,1408]{1,0:T(8,128)(2,1)S(1)}, u32[]{:S(2)}, u32[]{:S(2)}) %collective-permute-start.26) | collective-permute-done | bytes 360480 | tf_op jit(solution)/shard_map/ppermute | solution.py:1006
  416.2 18.2 %self_forward_kernel.3 = (bf16[1024,1408]{1,0:T(8,128)(2,1)}, bf16[1024,1152]{1,0:T(8,128)(2,1)}, bf16[256,352]{1,0:T(8,128)(2,1)}, bf16[256,352]{1,0:T(8,128)(2...) custom-call(bf16[256,1408]{1,0:T(8,128)(2,1)} %get-tuple-element.229.refs_0_, bf16[256,1408]{1,0:T(8,128)(2,1)} %copy-done.56, ...), custom_call_target="tpu_custom_call" | custom-call | flops 24000 | bytes 1000 | tf_op jit(solution)/shard_map/self_forward_kernel/pallas_call | solution.py:50
  452.0 21.6 %middle_forward_kernel.3 = (bf16[256,1408]{1,0:T(8,128)(2,1)}, f32[256,1408]{1,0:T(8,128)}, bf16[256,1408]{1,0:T(8,128)(2,1)}, bf16[4,256,352]{2,1,0:T(8,128)(2,...) custom-call(s32[10]{0:T(128)} %stack.83.refs_0_.scalars_ref, ...), custom_call_target="tpu_custom_call" | custom-call | flops 23000 | bytes 1000 | tf_op jit(solution)/shard_map/middle_forward_kernel/pallas_call | solution.py:50
  510.3 12.6 mlp_up_kernel.3
  531.8 20.5 %mlp_backward_kernel.2 = (bf16[1024,1408]{1,0:T(8,128)(2,1)}, bf16[1024,1536]{1,0:T(8,128)(2,1)}, f32[256,1408]{1,0:T(8,128)}, bf16[256,1408]{1,0:T(8,128)(2,1)}...) custom-call(bf16[1024,1408]{1,0:T(8,128)(2,1)} %stack_kernel.1.refs_0_, ...), custom_call_target="tpu_custom_call" | custom-call | flops 22000 | bytes 1000 | tf_op jit(solution)/shard_map/mlp_backward_kernel/pallas_call | solution.py:50
  585.2 27.5 %middle_backward_kernel.2 = (f32[256,1408]{1,0:T(8,128)}, bf16[256,1408]{1,0:T(8,128)(2,1)}, bf16[256,1408]{1,0:T(8,128)(2,1)}, bf16[256,1408]{1,0:T(8,128)(2,1)...) custom-call(s32[10]{0:T(128)} %stack.83.refs_0_.scalars_ref, ...), custom_call_target="tpu_custom_call" | custom-call | flops 37000 | bytes 1000 | tf_op jit(solution)/shard_map/middle_backward_kernel/pallas_call | solution.py:50
  641.6 28.7 %self_backward_kernel.2 = (bf16[1024,1152]{1,0:T(8,128)(2,1)}, f32[256,1408]{1,0:T(8,128)}, bf16[256,1408]{1,0:T(8,128)(2,1)}, bf16[256,1408]{1,0:T(8,128)(2,1)}...) custom-call(bf16[1024,1152]{1,0:T(8,128)(2,1)} %get-tuple-element.252.refs_0_, ...), custom_call_target="tpu_custom_call" | custom-call | flops 32000 | bytes 1000 | tf_op jit(solution)/shard_map/self_backward_kernel/pallas_call | solution.py:50
  730.1 15.8 %collective-permute-done.61.refs_3_.refs_2_ = bf16[256,1408]{1,0:T(8,128)(2,1)S(1)} collective-permute-done((bf16[256,1408]{1,0:T(8,128)(2,1)S(1)}, bf16[256,1408]{1,0:T(8,128)(2,1)S(1)}, u32[]{:S(2)}, u32[]{:S(2)}) %collective-permute-start.61) | collective-permute-done | bytes 720928 | tf_op jit(solution)/shard_map/ppermute | solution.py:1006
  766.0 20.0 %mlp_backward_kernel.3 = (bf16[1024,1408]{1,0:T(8,128)(2,1)}, bf16[1024,1536]{1,0:T(8,128)(2,1)}, f32[256,1408]{1,0:T(8,128)}, bf16[256,1408]{1,0:T(8,128)(2,1)}...) custom-call(bf16[256,1408]{1,0:T(8,128)(2,1)} %get-tuple-element.296.refs_0_, ...), custom_call_target="tpu_custom_call" | custom-call | flops 22000 | bytes 1000 | tf_op jit(solution)/shard_map/mlp_backward_kernel/pallas_call | solution.py:50
  831.8 27.7 %middle_backward_kernel.3 = (f32[256,1408]{1,0:T(8,128)}, bf16[256,1408]{1,0:T(8,128)(2,1)}, bf16[256,1408]{1,0:T(8,128)(2,1)}, bf16[256,1408]{1,0:T(8,128)(2,1)...) custom-call(s32[10]{0:T(128)} %stack.83.refs_0_.scalars_ref, ...), custom_call_target="tpu_custom_call" | custom-call | flops 37000 | bytes 1000 | tf_op jit(solution)/shard_map/middle_backward_kernel/pallas_call | solution.py:50
  874.4 28.8 %self_backward_kernel.3 = (bf16[1024,1152]{1,0:T(8,128)(2,1)}, f32[256,1408]{1,0:T(8,128)}, bf16[256,1408]{1,0:T(8,128)(2,1)}, bf16[256,1408]{1,0:T(8,128)(2,1)}...) custom-call(bf16[1024,1152]{1,0:T(8,128)(2,1)} %get-tuple-element.284.refs_0_, ...), custom_call_target="tpu_custom_call" | custom-call | flops 32000 | bytes 1000 | tf_op jit(solution)/shard_map/self_backward_kernel/pallas_call | solution.py:50
  990.5 35.8 %collective-permute-done.92.refs_0_ = bf16[704,1152]{1,0:T(8,128)(2,1)} collective-permute-done((bf16[704,1152]{1,0:T(8,128)(2,1)}, bf16[704,1152]{1,0:T(8,128)(2,1)}, u32[]{:S(2)}, u32[]{:S(2)}) %collective-permute-start.92) | collective-permute-done | bytes 1622048 | tf_op jit(solution)/shard_map/ppermute | solution.py:1025
  1034.2 17.2 %collective-permute-done.94.refs_0_ = bf16[704,1152]{1,0:T(8,128)(2,1)S(1)} collective-permute-done((bf16[704,1152]{1,0:T(8,128)(2,1)}, bf16[704,1152]{1,0:T(8,128)(2,1)S(1)}, u32[]{:S(2)}, u32[]{:S(2)}) %collective-permute-start.94) | collective-permute-done | bytes 1622048 | tf_op jit(solution)/shard_map/ppermute | solution.py:1025
  1100.1 24.6 %collective-permute-done.88 = f32[4,10,1408]{2,1,0:T(8,128)S(1)} collective-permute-done((f32[4,10,1408]{2,1,0:T(8,128)S(1)}, f32[4,10,1408]{2,1,0:T(8,128)S(1)}, u32[]{:S(2)}, u32[]{:S(2)}) %collective-permute-start.88) | collective-permute-done | bytes 225312 | tf_op jit(solution)/shard_map/ppermute | solution.py:1011
  1141.4 16.0 %collective-permute-done.114.refs_2_ = bf16[352,384]{1,0:T(8,128)(2,1)S(1)} collective-permute-done((bf16[352,384]{1,0:T(8,128)(2,1)}, bf16[352,384]{1,0:T(8,128)(2,1)S(1)}, u32[]{:S(2)}, u32[]{:S(2)}) %collective-permute-start.114) | collective-permute-done | bytes 270368 | tf_op jit(solution)/shard_map/ppermute | solution.py:1006
  1202.9 17.5 %collective-permute-done.117.refs_1_ = bf16[352,384]{1,0:T(8,128)(2,1)S(1)} collective-permute-done((bf16[352,384]{1,0:T(8,128)(2,1)S(1)}, bf16[352,384]{1,0:T(8,128)(2,1)S(1)}, u32[]{:S(2)}, u32[]{:S(2)}) %collective-permute-start.117) | collective-permute-done | bytes 270368 | tf_op jit(solution)/shard_map/ppermute | solution.py:1006
  (823 shorter events, 743.7 us)
Async XLA Ops:
  9.8 81.6 %all-gather.19.cloned.1.call-start = ((), (), s32[]{:S(2)}) async-start(), calls=%async_computation.17 | async-start | bytes 3649536 | tf_op jit(solution)/shard_map/all_gather | solution.py:1132
  51.3 85.1 %all-gather.17.cloned.1.call-start = ((), (), s32[]{:S(2)}) async-start(), calls=%async_computation.16 | async-start | bytes 3649536 | tf_op jit(solution)/shard_map/all_gather | solution.py:1132
  52.0 186.5 %all-gather.21.cloned.1.call-start = ((), (), s32[]{:S(2)}) async-start(), calls=%async_computation.18 | async-start | bytes 4866048 | tf_op jit(solution)/shard_map/all_gather | solution.py:1132
  57.6 193.6 %all-gather.29.cloned.1.call-start = ((), (), s32[]{:S(2)}) async-start(), calls=%async_computation.33 | async-start | bytes 4866048 | tf_op jit(solution)/shard_map/all_gather | solution.py:1132
  116.1 161.4 %all-gather.23.cloned.1.call-start = ((), (), s32[]{:S(2)}) async-start(), calls=%async_computation.19 | async-start | bytes 3649536 | tf_op jit(solution)/shard_map/all_gather | solution.py:1132
  234.6 118.1 %all-gather.13.cloned.1.call-start = ((), (), s32[]{:S(2)}) async-start(), calls=%async_computation.14 | async-start | bytes 8921088 | tf_op jit(solution)/shard_map/all_gather | solution.py:1132
  235.4 158.8 %all-gather.25.cloned.1.call-start = ((), (), s32[]{:S(2)}) async-start(), calls=%async_computation.20 | async-start | bytes 3649536 | tf_op jit(solution)/shard_map/all_gather | solution.py:1132
  237.2 270.1 %all-gather.27.cloned.1.call-start = ((), (), s32[]{:S(2)}) async-start(), calls=%async_computation.21 | async-start | bytes 4866048 | tf_op jit(solution)/shard_map/all_gather | solution.py:1132
  238.4 293.3 %all-gather.31.cloned.1.call-start = ((), (), s32[]{:S(2)}) async-start(), calls=%async_computation.34 | async-start | bytes 4866048 | tf_op jit(solution)/shard_map/all_gather | solution.py:1132
  278.3 104.6 %collective-permute-start.27 = (bf16[1408,1152]{1,0:T(8,128)(2,1)}, bf16[1408,1152]{1,0:T(8,128)(2,1)}, u32[]{:S(2)}, u32[]{:S(2)}) collective-permute-start(bf16[1408,1152]{1,0:T(8,128)(2,1)} %shard_map.296.refs_11_.refs_5_.refs_1_), channel_id=1, source_target_pairs={{0,8},{1,17},{2,10},{3,19},{4,12},{5,21},{6,14},{7,23},{8,0},{9,25... | collective-permute-start | bytes 9732104 | tf_op jit(solution)/shard_map/ppermute | solution.py:1025
  281.4 359.1 %reduce-scatter.12.cloned.1.call-start = ((), (), s32[]{:S(2)}) async-start(), calls=%async_computation.22 | async-start | bytes 4866048 | tf_op jit(solution)/shard_map/reduce_scatter | solution.py:1136
  283.0 69.7 %collective-permute-start.22 = (bf16[128,1408]{1,0:T(8,128)(2,1)S(1)}, bf16[128,1408]{1,0:T(8,128)(2,1)S(1)}, u32[]{:S(2)}, u32[]{:S(2)}) collective-permute-start(bf16[128,1408]{1,0:T(8,128)(2,1)S(1)} %add_convert_fusion.18), channel_id=1, source_target_pairs={{0,16},{8,24},{16,0},{24,8},{1,17},{9,25},{17,1},{25,9},{2,18},{10... | collective-permute-start | bytes 1081352 | tf_op jit(solution)/shard_map/ppermute | solution.py:1006
  531.5 182.4 %reduce-scatter.14.cloned.1.call-start = ((), (), s32[]{:S(2)}) async-start(), calls=%async_computation.23 | async-start | bytes 4866048 | tf_op jit(solution)/shard_map/reduce_scatter | solution.py:1136
  571.4 253.4 %reduce-scatter.16.cloned.1.call-start = ((), (), s32[]{:S(2)}) async-start(), calls=%async_computation.24 | async-start | bytes 1769472 | tf_op jit(solution)/shard_map/reduce_scatter | solution.py:1136
  691.4 183.1 %reduce-scatter.20.cloned.1.call-start = ((), (), s32[]{:S(2)}) async-start(), calls=%async_computation.26 | async-start | bytes 3649536 | tf_op jit(solution)/shard_map/reduce_scatter | solution.py:1136
  698.9 175.5 %reduce-scatter.18.cloned.1.call-start = ((), (), s32[]{:S(2)}) async-start(), calls=%async_computation.25 | async-start | bytes 4866048 | tf_op jit(solution)/shard_map/reduce_scatter | solution.py:1136
  811.6 276.4 %reduce-scatter.30.cloned.1.call-start = ((), (), s32[]{:S(2)}) async-start(), calls=%async_computation.31 | async-start | bytes 4866048 | tf_op jit(solution)/shard_map/reduce_scatter | solution.py:1136
  821.3 307.6 %reduce-scatter.32.cloned.1.call-start = ((), (), s32[]{:S(2)}) async-start(), calls=%async_computation.32 | async-start | bytes 8921088 | tf_op jit(solution)/shard_map/reduce_scatter | solution.py:1136
  821.9 348.8 %reduce-scatter.28.cloned.1.call-start = ((), (), s32[]{:S(2)}) async-start(), calls=%async_computation.30 | async-start | bytes 3649536 | tf_op jit(solution)/shard_map/reduce_scatter | solution.py:1136
  824.8 94.9 %collective-permute-start.99 = (bf16[704,1152]{1,0:T(8,128)(2,1)}, bf16[704,1152]{1,0:T(8,128)(2,1)}, u32[]{:S(2)}, u32[]{:S(2)}) collective-permute-start(bf16[704,1152]{1,0:T(8,128)(2,1)} %get-tuple-element.392), channel_id=1, source_target_pairs={{0,1},{1,0},{2,3},{3,2},{4,5},{5,4},{6,7},{7,6},{8,9},{9,8},{10,11... | collective-permute-start | bytes 4866056 | tf_op jit(solution)/shard_map/ppermute | solution.py:1011
  955.3 265.8 %reduce-scatter.26.cloned.1.call-start = ((), (), s32[]{:S(2)}) async-start(), calls=%async_computation.29 | async-start | bytes 1769472 | tf_op jit(solution)/shard_map/reduce_scatter | solution.py:1136
  961.3 259.9 %reduce-scatter.22.cloned.1.call-start = ((), (), s32[]{:S(2)}) async-start(), calls=%async_computation.27 | async-start | bytes 3649536 | tf_op jit(solution)/shard_map/reduce_scatter | solution.py:1136
  981.8 239.4 %reduce-scatter.24.cloned.1.call-start = ((), (), s32[]{:S(2)}) async-start(), calls=%async_computation.28 | async-start | bytes 3649536 | tf_op jit(solution)/shard_map/reduce_scatter | solution.py:1136
  1090.3 94.5 %collective-permute-start.106 = (bf16[192,2944]{1,0:T(8,128)(2,1)}, bf16[192,2944]{1,0:T(8,128)(2,1)}, u32[]{:S(2)}, u32[]{:S(2)}) collective-permute-start(bf16[192,2944]{1,0:T(8,128)(2,1)} %pack_kernel.7.refs_0_), channel_id=1, source_target_pairs={{0,16},{8,24},{16,0},{24,8},{1,17},{9,25},{17,1},{25,9},{2,18},{10... | collective-permute-start | bytes 3391496 | tf_op jit(solution)/shard_map/ppermute | solution.py:1006
  (281 other events, 3595.8 us)
Sparse Core Ops, SparseCore 0:
  10.2 40.9 all-gather.14
  53.5 37.9 all-gather.18
  93.7 41.0 all-gather.16
  136.9 47.7 all-gather.20
  186.7 47.1 all-gather.28
  236.0 37.9 all-gather.22
  275.6 77.1 all-gather.12
  355.0 39.1 all-gather.24
  395.8 45.7 all-gather.26
  443.1 47.1 all-gather.30
  531.6 48.9 reduce-scatter.11
  583.5 49.3 reduce-scatter.13
  691.5 31.5 reduce-scatter.15
  725.2 39.4 reduce-scatter.19
  811.8 48.4 reduce-scatter.17
  863.0 49.3 reduce-scatter.29
  915.3 83.4 reduce-scatter.31
  1001.0 39.6 reduce-scatter.27
  1043.0 32.9 reduce-scatter.25
  1078.8 52.2 reduce-scatter.21
  1133.5 43.9 reduce-scatter.23
